TPU v7x, 128 devices: a whole 4x4x4 slice. The times are simulated.
128 devices in a mesh: particle: 16 (over x, z), tensor: 8 (over y, core).
Axes of the slice: x: 4, y: 4, z: 4, core: 2. Of those that a mesh axis runs over, the one named last changes fastest.
Arguments:
- inputs: bfloat16 [256, 2, 8192], P('particle'), may hold values from -6 to 6
- norm_gain: float32 [8192], replicated, may hold values from 0.125 to 2
- query_proj: bfloat16 [256, 2, 8192], P('particle', None, 'tensor'), may hold values from -6 to 6
- w_key: bfloat16 [8192, 1024], P(None, 'tensor'), may hold values from -0.5 to 0.5
- w_value: bfloat16 [8192, 1024], P(None, 'tensor'), may hold values from -0.125 to 0.125
- w_out: bfloat16 [8192, 8192], P('tensor'), may hold values from -0.0625 to 0.0625
- kv_cache: bfloat16 [256, 8, 512, 256], P('particle', 'tensor'), may hold values from -200 to 200
- ancestors: int32 [256], P('particle'), may hold values from 0 to 255, as said below
Outputs:
- attn_out: bfloat16 [256, 2, 8192], P('particle', None, 'tensor')
Inputs may be any that keep to these rules, and one draw needn't show every extreme that they name: The 16 particles of one device (aligned blocks of ancestors) take their ancestors from exactly 8 distinct devices, 2 particles from each; two of them may share an ancestor.
All inputs are finite; a program needn't handle non-finite values.
Results may differ from a plain program's by a relative error of at most 0.019.
Values may be sent and summed in bfloat16 or wider, within the bound.
No kernel may reach another device: no remote copies, remote signals or barrier semaphores. Data moves between devices by JAX's collectives and lax.ppermute only.
A program may use at most 128 MiB of HBM per device.

v0:
```python
import jax
import jax.numpy as jnp
from jax import lax
from jax.sharding import PartitionSpec as P

PAIR = 2


theta_base = 500000.0
epsilon = 1e-05


def rotate(values, offset):
    half = values.shape[-1] // 2
    step_count = values.shape[1]
    freqs = theta_base ** (-jnp.arange(half, dtype=jnp.float32) * 2.0 / values.shape[-1])
    position = (offset + jnp.arange(step_count, dtype=jnp.float32)).reshape(1, step_count, 1, 1)
    angles = position * freqs
    cosine = jnp.cos(angles)
    sine = jnp.sin(angles)
    first = values[..., :half]
    second = values[..., half:]
    return jnp.concatenate([first * cosine - second * sine, second * cosine + first * sine], -1)


def cache_part(questions, caches):
    head_dim = caches.shape[-1] // 2
    keys = caches[..., :head_dim]
    vals = caches[..., head_dim:]
    scores = jnp.einsum(
        "rskgd,rkcd->rskgc", questions, keys, preferred_element_type=jnp.float32
    ) * head_dim ** (-0.5)
    top_score = jnp.max(scores, -1)
    expo = jnp.exp(scores - top_score[..., None])
    total = jnp.sum(expo, -1)
    vector = jnp.einsum(
        "rskgc,rkcd->rskgd", expo.astype(jnp.bfloat16), vals, preferred_element_type=jnp.float32
    )
    return (vector, total, top_score)


def shards(inputs, norm_gain, query_proj, w_key, w_value, w_out, kv_cache, ancestors):
    local_rows, step_count, width = inputs.shape
    kv_local = kv_cache.shape[1]
    context = kv_cache.shape[2]
    head_dim = kv_cache.shape[3] // 2
    query_local = query_proj.shape[2] // head_dim
    group = query_local // kv_local
    floats = inputs.astype(jnp.float32)
    normed = (
        floats * lax.rsqrt(jnp.mean(floats * floats, -1, keepdims=True) + epsilon) * norm_gain
    ).astype(jnp.bfloat16)
    flat = normed.reshape(local_rows * step_count, width)
    offset = jnp.float32(context)
    queries = rotate(
        query_proj.astype(jnp.float32).reshape(local_rows, step_count, query_local, head_dim),
        offset,
    ).astype(jnp.bfloat16)
    queries = queries.reshape(local_rows, step_count, kv_local, group, head_dim)
    new_keys = rotate(
        jnp.dot(flat, w_key, preferred_element_type=jnp.float32).reshape(
            local_rows, step_count, kv_local, head_dim
        ),
        offset,
    ).astype(jnp.bfloat16)
    new_values = (
        jnp.dot(flat, w_value, preferred_element_type=jnp.float32)
        .astype(jnp.bfloat16)
        .reshape(local_rows, step_count, kv_local, head_dim)
    )
    devices_count = lax.axis_size("particle")
    source = ancestors // local_rows
    order = jnp.arange(local_rows)
    earlier = (source[:, None] == source[None, :]) & (order[None, :] < order[:, None])
    rank_own = jnp.sum(earlier.astype(jnp.int32), 1)
    row_of = source * PAIR + rank_own
    slot_range = jnp.arange(PAIR)
    myself = lax.axis_index("particle")
    lineage = lax.all_gather(ancestors, "particle", axis=0, tiled=True).reshape(
        devices_count, local_rows
    )
    owner = lineage // local_rows
    spot = lineage % local_rows
    mine = owner == myself
    rank = jnp.cumsum(mine.astype(jnp.int32), 1) - 1
    picked = mine[:, None, :] & (rank[:, None, :] == slot_range[None, :, None])
    index = jnp.sum(jnp.where(picked, spot[:, None, :], 0), -1).reshape(-1)
    outgoing = jnp.take(kv_cache, index, axis=0).reshape(
        devices_count, PAIR, kv_local, context, 2 * head_dim
    )
    incoming = lax.all_to_all(
        outgoing, "particle", split_axis=0, concat_axis=0, tiled=True
    ).reshape(devices_count * PAIR, kv_local, context, 2 * head_dim)
    resampled = jnp.take(incoming, row_of, axis=0)
    cache_vec, cache_sum, cache_max = cache_part(queries, resampled)
    fresh = jnp.einsum(
        "rskgd,rtkd->rskgt", queries, new_keys, preferred_element_type=jnp.float32
    ) * head_dim ** (-0.5)
    allowed = (jnp.arange(step_count)[:, None] >= jnp.arange(step_count)[None, :]).reshape(
        1, step_count, 1, 1, step_count
    )
    fresh = jnp.where(allowed, fresh, jnp.float32(-1e30))
    fresh_max = jnp.max(fresh, -1)
    fresh_exp = jnp.exp(fresh - fresh_max[..., None])
    fresh_sum = jnp.sum(fresh_exp, -1)
    fresh_vec = jnp.einsum(
        "rskgt,rtkd->rskgd",
        fresh_exp.astype(jnp.bfloat16),
        new_values,
        preferred_element_type=jnp.float32,
    )
    highest = jnp.maximum(cache_max, fresh_max)
    cache_factor = jnp.exp(cache_max - highest)
    fresh_factor = jnp.exp(fresh_max - highest)
    heads = (cache_vec * cache_factor[..., None] + fresh_vec * fresh_factor[..., None]) / (
        cache_sum * cache_factor + fresh_sum * fresh_factor
    )[..., None]
    heads = heads.astype(jnp.bfloat16).reshape(local_rows * step_count, query_local * head_dim)
    partial_value = jnp.dot(heads, w_out, preferred_element_type=jnp.float32).reshape(
        local_rows, step_count, width
    )
    return lax.psum_scatter(
        partial_value.astype(jnp.bfloat16), "tensor", scatter_dimension=2, tiled=True
    )


def solution(mesh):
    in_specs = (
        P("particle", None, None),
        P(),
        P("particle", None, "tensor"),
        P(None, "tensor"),
        P(None, "tensor"),
        P("tensor", None),
        P("particle", "tensor", None, None),
        P("particle"),
    )
    out_specs = P("particle", None, "tensor")
    return jax.shard_map(shards, mesh=mesh, in_specs=in_specs, out_specs=out_specs, check_vma=False)
```

profile of v0, /device:TPU:1, one launch (start us, length us, event | category | flops | bytes accessed | tf_op | source)
XLA Modules:
  0.0 220.7 jit_solution(7291520843611630537)
XLA Ops:
  6.5 0.0 copy-start
  6.5 1.4 dynamic-slice
  8.6 0.9 dynamic-update-slice
  9.4 14.5 %all-reduce = s32[256]{0:T(256)S(1)} all-reduce(s32[256]{0:T(256)S(1)} %dynamic-update-slice), channel_id=1, replica_groups=mesh['particle'=16,'tensor'=8] {'particle'}, use_global_device_ids=true, to_apply=%add | all-reduce | flops 256 | bytes 2048
  24.0 0.1 reshape.379
  24.1 0.2 reduce_window_sum.11
  24.3 0.1 select_reduce_fusion
  24.4 0.1 copy.35
  24.5 0.1 reshape.380
  24.6 0.1 copy.34
  24.7 7.1 %gather_fusion = bf16[32,512,256]{2,1,0:T(8,128)(2,1)} fusion(bf16[16,512,256]{2,1,0:T(8,128)(2,1)} %bitcast.102, s32[1024]{0:T(1024)S(1)} %pad_clamp_fusion.1), kind=kCustom, calls=%fused_computation | custom fusion | bytes 16777344 | tf_op jit(solution)/shard_map/jit(_take)/gather | solution.py:88
  31.8 7.5 %broadcast_select_fusion = bf16[16,2,1,512,256]{4,3,1,2,0:T(8,128)(2,1)} fusion(bf16[16,2,1,512,256]{4,3,1,2,0:T(8,128)(2,1)} %bitcast.101, pred[16,2]{1,0:T(8,128)(4,1)S(1)} %copy.34), kind=kLoop, calls=%fused_computation.5 | loop fusion | flops 4194304 | bytes 16777248 | tf_op jit(solution)/shard_map/jit(_take)/select_n | solution.py:88
  39.3 0.0 copy-start.2
  39.3 0.0 copy-start.1
  39.3 0.0 copy-start.3
  39.3 0.0 copy-start.4
  39.3 4.9 %all-to-all-start = ((bf16[16,2,1,512,256]{4,3,1,2,0:T(8,128)(2,1)}), bf16[16,2,1,512,256]{4,3,1,2,0:T(8,128)(2,1)}, u32[]{:S(2)}, u32[]{:S(2)}) async-start(bf16[16,2,1,512,256]{4,3,1,2,0:T(8,128)(2,1)} %broadcast_select_fusion), calls=%async_computation | async-start | bytes 16777216 | tf_op jit(solution)/shard_map/all_to_all | solution.py:91
  44.2 0.0 reduce-scatter.2.cloned.1.call-start
  44.2 0.0 copy-done.2
  44.3 0.0 copy-done.1
  44.3 0.6 fusion.23
  44.9 0.0 copy-done.3
  44.9 0.7 fusion.25
  45.6 0.2 reshape.387
  45.8 0.0 copy-done.4
  45.9 0.2 convert_reduce_fusion
  46.1 0.1 multiply_cosine_fusion
  46.2 0.0 copy-done
  46.2 0.6 fusion.19
  46.8 0.1 fusion.42
  46.8 0.1 maximum_bitcast_fusion
  46.9 0.1 subtract_convert_fusion
  47.0 0.5 fusion.56
  47.5 0.1 fusion.33
  47.6 2.0 convolution_convert_fusion
  49.6 104.2 %all-to-all-done = bf16[16,2,1,512,256]{4,3,1,2,0:T(8,128)(2,1)} async-done(((bf16[16,2,1,512,256]{4,3,1,2,0:T(8,128)(2,1)}), bf16[16,2,1,512,256]{4,3,1,2,0:T(8,128)(2,1)}, u32[]{:S(2)}, u32[]{:S(2)}) %all-to-all-start) | async-done | bytes 8388640 | tf_op jit(solution)/shard_map/all_to_all | solution.py:91
  153.9 6.2 %gather_fusion.1 = bf16[16,512,256]{2,1,0:T(8,128)(2,1)} fusion(bf16[32,512,256]{2,1,0:T(8,128)(2,1)} %bitcast.4, s32[1024]{0:T(1024)S(1)} %pad_clamp_fusion), kind=kCustom, calls=%fused_computation.1 | custom fusion | bytes 8388672 | tf_op jit(solution)/shard_map/jit(_take)/gather | solution.py:94
  160.1 2.6 %bitcast_select_fusion = bf16[16,1,512,256]{3,2,0,1:T(8,128)(2,1)S(1)} fusion(bf16[16,512,256]{2,1,0:T(8,128)(2,1)} %gather_fusion.1, pred[16]{0:T(512)(128)(4,1)S(1)} %get-tuple-element.8), kind=kLoop, calls=%fused_computation.6 | loop fusion | flops 2097152 | bytes 8388624 | tf_op jit(solution)/shard_map/jit(_take)/select_n | solution.py:94
  162.7 0.8 fusion.55
  163.5 0.3 fusion.27
  163.8 0.4 fusion.15
  164.2 0.2 fusion.17
  164.5 9.5 %fusion.2 = bf16[16,2,8192]{2,0,1:T(8,128)(2,1)} fusion(bf16[1024,8192]{1,0:T(8,128)(2,1)} %param.13, bf16[16,2,1024]{2,1,0:T(2,128)(2,1)S(1)} %dot_general.38), kind=kOutput, calls=%fused_computation.4 | convolution fusion | flops 537133056 | bytes 17367040 | tf_op jit(solution)/shard_map/dot_general | solution.py:119
  174.1 0.0 reduce-scatter.2.cloned.1.call-update
  174.1 38.2 %reduce-scatter.2.cloned.1.call-done = bf16[16,2,1024]{2,0,1:T(8,128)(2,1)} async-done(((bf16[16,2,8192]{2,0,1:T(8,128)(2,1)}), bf16[16,2,1024]{2,0,1:T(8,128)(2,1)}) %reduce-scatter.2.cloned.1.call-update) | async-done | bytes 65552 | tf_op jit(solution)/shard_map/reduce_scatter | solution.py:122
  212.3 1.5 copy.41
  (16 shorter events, 0.2 us)
Async XLA Ops:
  6.5 39.7 %copy-start = (bf16[8192,128]{1,0:T(8,128)(2,1)S(1)}, bf16[8192,128]{1,0:T(8,128)(2,1)}, u32[]{:S(2)}) copy-start(bf16[8192,128]{1,0:T(8,128)(2,1)} %param.11) | copy-start | bytes 6291460
  39.3 5.0 %copy-start.2 = (bf16[16,2,1024]{2,1,0:T(2,128)(2,1)S(1)}, bf16[16,2,1024]{2,1,0:T(2,128)(2,1)}, u32[]{:S(2)}) copy-start(bf16[16,2,1024]{2,1,0:T(2,128)(2,1)} %param.10) | copy-start | bytes 196612
  39.3 5.0 %copy-start.1 = (bf16[16,2,8192]{2,1,0:T(2,128)(2,1)S(1)}, bf16[16,2,8192]{2,1,0:T(2,128)(2,1)}, u32[]{:S(2)}) copy-start(bf16[16,2,8192]{2,1,0:T(2,128)(2,1)} %param.8) | copy-start | bytes 1572868
  39.3 5.7 %copy-start.3 = (f32[8192]{0:T(1024)S(1)}, f32[8192]{0:T(1024)}, u32[]{:S(2)}) copy-start(f32[8192]{0:T(1024)} %param.9) | copy-start | bytes 98308
  39.3 6.6 %copy-start.4 = (s32[16]{0:T(128)S(1)}, s32[16]{0:T(128)}, u32[]{:S(2)}) copy-start(s32[16]{0:T(128)} %param.15) | copy-start | bytes 196
  39.3 114.6 %all-to-all-start = ((bf16[16,2,1,512,256]{4,3,1,2,0:T(8,128)(2,1)}), bf16[16,2,1,512,256]{4,3,1,2,0:T(8,128)(2,1)}, u32[]{:S(2)}, u32[]{:S(2)}) async-start(bf16[16,2,1,512,256]{4,3,1,2,0:T(8,128)(2,1)} %broadcast_select_fusion), calls=%async_computation | async-start | bytes 16777216 | tf_op jit(solution)/shard_map/all_to_all | solution.py:91
  44.2 168.1 %reduce-scatter.2.cloned.1.call-start = ((), (), s32[]{:S(2)}) async-start(), calls=%async_computation.2 | async-start | bytes 589824 | tf_op jit(solution)/shard_map/reduce_scatter | solution.py:122
Sparse Core Ops, SparseCore 0:
  174.2 38.0 reduce-scatter.1
where the time goes:
time: 223 us; the launch traced here: 221 us
  waiting for transfers between devices  142 us (64%)
  local copies, waits for them, and re-layouts  17.7 us (8%)
  blocking collectives  14.5 us (7%)
  between operations  14.2 us (6%)
  matrix products  14.1 us (6%)
  other arithmetic  12.7 us (6%)
  starting transfers between devices  4.92 us (2%)
    all_to_all x1, waiting for transfers between devices, shards(): lax.all_to_all(outgoing, 'particle', split_axis=0, concat_axis=0, tiled=T...  104 us
    reduce_scatter x1, waiting for transfers between devices, shards(): lax.psum_scatter(partial_value.astype(jnp.bfloat16), 'tensor', scatter_di...  38.2 us
    unnamed x1, blocking collectives  14.5 us
    dot_general x1, matrix products, shards(): jnp.dot(heads, w_out, preferred_element_type=jnp.float32)  9.55 us
    select_n x2, other arithmetic, shards(): jnp.take(kv_cache, index, axis=0)  7.46 us
    gather x1, local copies, waits for them, and re-layouts, shards(): jnp.take(kv_cache, index, axis=0)  7.11 us
    gather x1, local copies, waits for them, and re-layouts, shards(): resampled = jnp.take(incoming, row_of, axis=0)  6.17 us
    all_to_all x1, starting transfers between devices, shards(): lax.all_to_all(outgoing, 'particle', split_axis=0, concat_axis=0, tiled=T...  4.88 us
  transfers between devices with their start and end apart: 2, of which 2 were waited for; matrix products, arithmetic and copies ran while one was open for 2% of the time, Pallas kernels for 0%

commit v1 on v0

v1 whole, which is shorter than its diff:
```python
import functools

import jax
import jax.numpy as jnp
import numpy as np
from jax import lax
from jax.experimental import pallas as pl
from jax.experimental.pallas import tpu as pltpu
from jax.sharding import PartitionSpec as P

PAIR = 2
THETA = 500000.0
EPSILON = 1e-05
F32 = jnp.float32
BF16 = jnp.bfloat16
MIB = 1 << 20
NT = (((1,), (1,)), ((), ()))


def rotary_tables(context, steps, head_dim):
    half = head_dim // 2
    freqs = np.float32(THETA) ** (-np.arange(half, dtype=np.float32) * np.float32(2.0) / np.float32(head_dim))
    position = (np.float32(context) + np.arange(steps, dtype=np.float32)).reshape(steps, 1)
    angles = (position * freqs.astype(np.float32)).astype(np.float32)
    cosine, sine = np.cos(angles), np.sin(angles)
    return (
        np.concatenate([cosine, cosine], 1).astype(np.float32),
        np.concatenate([-sine, sine], 1).astype(np.float32),
    )


def slot_of(anc, row, rows, count):
    source = lax.div(anc[row], rows)
    rank = count[source]
    count[source] = rank + 1
    return source, rank


def pack_kernel(anc, qp, cosine, sine, send, queries, grid_ref, count, spots):
    rows, steps, width = qp.shape
    head_dim = cosine.shape[1]
    heads = width // head_dim
    devices = send.shape[0]
    for h in range(heads):
        grid_ref[:, steps * h : steps * (h + 1), :] = qp[:, :, head_dim * h : head_dim * (h + 1)].astype(F32)
    flat = grid_ref[...].reshape(rows * heads * steps, head_dim)
    swapped = pltpu.roll(flat, head_dim // 2, 1)
    shape = (rows, heads * steps, head_dim)
    turned = flat.reshape(shape) * cosine[...][None] + swapped.reshape(shape) * sine[...][None]
    queries[...] = turned.astype(BF16)
    send[...] = jnp.zeros(send.shape, BF16)
    for d in range(devices):
        count[d] = 0
        for j in range(PAIR):
            spots[PAIR * d + j] = 0
    for r in range(rows):
        source, rank = slot_of(anc, r, rows, count)
        spots[source * PAIR + rank] = lax.rem(anc[r], rows)
        send[source, rank] = queries[r]
    lane = lax.broadcasted_iota(jnp.int32, (heads * steps, head_dim), 1)
    for d in range(devices):
        send[d, PAIR] = jnp.where(
            lane < head_dim // 2, spots[PAIR * d].astype(F32), spots[PAIR * d + 1].astype(F32)
        ).astype(BF16)


def fresh_kernel(x, gain, wk, wv, queries, cosine, sine, vec, stat):
    tokens = x.shape[0]
    head_dim = wk.shape[1]
    rows, per_row, _ = queries.shape
    steps = tokens // rows
    floats = x[...].astype(F32)
    mean = jnp.mean(floats * floats, -1, keepdims=True)
    normed = (floats * lax.rsqrt(mean + EPSILON) * gain[...]).astype(BF16)
    keys = jnp.dot(normed, wk[...], preferred_element_type=F32)
    keys = (keys * cosine[...] + pltpu.roll(keys, head_dim // 2, 1) * sine[...]).astype(BF16)
    vals = jnp.dot(normed, wv[...], preferred_element_type=F32).astype(BF16)
    flat = queries[...].reshape(rows * per_row, head_dim)
    scores = lax.dot_general(flat, keys, NT, preferred_element_type=F32) * head_dim ** (-0.5)
    row = lax.broadcasted_iota(jnp.int32, scores.shape, 0)
    col = lax.broadcasted_iota(jnp.int32, scores.shape, 1)
    seen = (lax.div(row, per_row) == lax.div(col, steps)) & (lax.rem(col, steps) <= lax.rem(row, steps))
    top = jnp.max(jnp.where(seen, scores, -jnp.inf), -1, keepdims=True)
    expo = jnp.where(seen, jnp.exp(jnp.where(seen, scores - top, 0.0)), 0.0)
    vec[...] = jnp.dot(expo.astype(BF16), vals, preferred_element_type=F32)
    lane = lax.broadcasted_iota(jnp.int32, stat.shape, 1)
    stat[...] = jnp.where(lane == 0, top, jnp.sum(expo, -1, keepdims=True))


def cache_kernel(recv, kv, back):
    devices, _, per_row, head_dim = recv.shape
    lane = lax.broadcasted_iota(jnp.int32, (per_row, head_dim), 1)
    for d in range(devices):
        spot = recv[d, PAIR].astype(F32)
        stat = jnp.zeros((per_row, head_dim), F32)
        for j in range(PAIR):
            base = j * (head_dim // PAIR)
            at = spot[0, base].astype(jnp.int32)
            keys = kv[at, 0, :, :head_dim]
            vals = kv[at, 0, :, head_dim:]
            scores = lax.dot_general(recv[d, j], keys, NT, preferred_element_type=F32) * head_dim ** (-0.5)
            top = jnp.max(scores, -1, keepdims=True)
            expo = jnp.exp(scores - top)
            total = jnp.sum(expo, -1, keepdims=True)
            vector = jnp.dot(expo.astype(BF16), vals, preferred_element_type=F32)
            back[d, j] = (vector / total).astype(BF16)
            at_lane = base
            for value, parts in ((top, 3), (total, 2)):
                for _ in range(parts):
                    part = value.astype(BF16).astype(F32)
                    stat = jnp.where(lane == at_lane, part, stat)
                    value = value - part
                    at_lane += 1
        back[d, PAIR] = stat.astype(BF16)


def project(heads, w, out, place):
    out[place] = jnp.dot(heads[...], w[...], preferred_element_type=F32).astype(BF16)


def merge_kernel(scalars, recv, vec, stat, w, out, heads, grid_ref, sums, count):
    rows = recv.shape[0]
    _, _, per_row, head_dim = recv.shape
    steps = heads.shape[0] // rows
    step = pl.program_id(0)

    @pl.when(step == 0)
    def _():
        for d in range(recv.shape[0]):
            count[d] = 0
        for r in range(rows):
            source, rank = slot_of(scalars, r, rows, count)
            grid_ref[pl.ds(r * per_row, per_row), :] = recv[source, rank].astype(F32)
            both = recv[source, PAIR].astype(F32)
            sums[pl.ds(r * per_row, per_row), :] = jnp.where(rank == 0, both, pltpu.roll(both, head_dim // 2, 1))
        parts = sums[...]
        top_c = parts[:, 0:1] + parts[:, 1:2] + parts[:, 2:3]
        sum_c = parts[:, 3:4] + parts[:, 4:5]
        fresh = stat[...]
        top_f, sum_f = fresh[:, 0:1], fresh[:, 1:2]
        top = jnp.maximum(top_c, top_f)
        factor_c = sum_c * jnp.exp(top_c - top)
        factor_f = jnp.exp(top_f - top)
        share = 1.0 / (factor_c + sum_f * factor_f)
        grid_ref[...] = grid_ref[...] * (factor_c * share) + vec[...] * (factor_f * share)
        for h in range(per_row // steps):
            for s in range(steps):
                heads[pl.ds(s * rows, rows), pl.ds(h * head_dim, head_dim)] = grid_ref[
                    pl.ds(h * steps + s, rows, stride=per_row), :
                ].astype(BF16)

    project(heads, w, out, step)


def second_kernel(scalars, heads, w, out):
    project(heads, w, out, pl.program_id(0))


def whole(shape):
    return pl.BlockSpec(shape, lambda *_: (0,) * len(shape))


def shards(inputs, norm_gain, query_proj, w_key, w_value, w_out, kv_cache, ancestors):
    rows, steps, width = inputs.shape
    context = kv_cache.shape[2]
    head_dim = kv_cache.shape[3] // 2
    local = query_proj.shape[2]
    heads = local // head_dim
    per_row = heads * steps
    devices = lax.axis_size("particle")
    tensor = lax.axis_size("tensor")
    column = width // tensor
    cosine, sine = rotary_tables(context, steps, head_dim)
    smem = pl.BlockSpec(memory_space=pltpu.SMEM)
    vmem = pl.BlockSpec(memory_space=pltpu.VMEM)

    packed = (devices, PAIR + 1, per_row, head_dim)
    send, queries = pl.pallas_call(
        pack_kernel,
        out_shape=(
            jax.ShapeDtypeStruct(packed, BF16),
            jax.ShapeDtypeStruct((rows, per_row, head_dim), BF16),
        ),
        in_specs=[smem, vmem, vmem, vmem],
        out_specs=(vmem, vmem),
        scratch_shapes=[
            pltpu.VMEM((rows, per_row, head_dim), F32),
            pltpu.SMEM((devices,), jnp.int32),
            pltpu.SMEM((devices * PAIR,), jnp.int32),
        ],
        compiler_params=pltpu.CompilerParams(vmem_limit_bytes=8 * MIB),
        name="pack_queries",
    )(ancestors, query_proj, np.tile(cosine, (heads, 1)), np.tile(sine, (heads, 1)))

    recv = lax.all_to_all(send, "particle", split_axis=0, concat_axis=0, tiled=True)

    vec, stat = pl.pallas_call(
        fresh_kernel,
        out_shape=(
            jax.ShapeDtypeStruct((rows * per_row, head_dim), F32),
            jax.ShapeDtypeStruct((rows * per_row, head_dim), F32),
        ),
        in_specs=[vmem] * 7,
        out_specs=(vmem, vmem),
        compiler_params=pltpu.CompilerParams(vmem_limit_bytes=16 * MIB),
        cost_estimate=pl.CostEstimate(
            flops=4 * rows * steps * width * head_dim, bytes_accessed=5 * MIB, transcendentals=0
        ),
        name="new_tokens",
    )(
        inputs.reshape(rows * steps, width),
        norm_gain.reshape(1, width),
        w_key,
        w_value,
        queries,
        np.tile(cosine, (rows, 1)),
        np.tile(sine, (rows, 1)),
    )

    back = pl.pallas_call(
        cache_kernel,
        out_shape=jax.ShapeDtypeStruct(packed, BF16),
        in_specs=[vmem, vmem],
        out_specs=vmem,
        compiler_params=pltpu.CompilerParams(vmem_limit_bytes=12 * MIB),
        cost_estimate=pl.CostEstimate(
            flops=4 * devices * PAIR * per_row * context * head_dim, bytes_accessed=5 * MIB, transcendentals=0
        ),
        name="cache_attention",
    )(recv, kv_cache)
    home = lax.all_to_all(back, "particle", split_axis=0, concat_axis=0, tiled=True)

    place = lax.axis_index("tensor")
    y, core = place // 2, place % 2
    scalars = jnp.concatenate([ancestors, jnp.stack([y, core]).astype(jnp.int32)])
    groups = tensor // 2
    w_spec = lambda own: pl.BlockSpec(
        (local, column),
        lambda i, sc: (0, 2 * lax.rem(sc[rows] + i, groups) + (sc[rows + 1] if own else 1 - sc[rows + 1])),
    )
    block = (groups, rows * steps, column)
    params = pltpu.CompilerParams(vmem_limit_bytes=16 * MIB)
    cost = pl.CostEstimate(
        flops=rows * steps * local * width, bytes_accessed=local * width, transcendentals=0
    )
    other, heads_out = pl.pallas_call(
        merge_kernel,
        out_shape=(
            jax.ShapeDtypeStruct(block, BF16),
            jax.ShapeDtypeStruct((rows * steps, local), BF16),
        ),
        grid_spec=pltpu.PrefetchScalarGridSpec(
            num_scalar_prefetch=1,
            grid=(groups,),
            in_specs=[whole(packed), whole(vec.shape), whole(stat.shape), w_spec(False)],
            out_specs=(whole(block), whole((rows * steps, local))),
            scratch_shapes=[
                pltpu.VMEM((rows * per_row, head_dim), F32),
                pltpu.VMEM((rows * per_row, head_dim), F32),
                pltpu.SMEM((devices,), jnp.int32),
            ],
        ),
        compiler_params=params,
        cost_estimate=cost,
        name="merge_project_sibling",
    )(scalars, home, vec, stat, w_out)
    given = lax.ppermute(other, "tensor", [(i, i ^ 1) for i in range(tensor)])
    mine = pl.pallas_call(
        second_kernel,
        out_shape=jax.ShapeDtypeStruct(block, BF16),
        grid_spec=pltpu.PrefetchScalarGridSpec(
            num_scalar_prefetch=1,
            grid=(groups,),
            in_specs=[whole((rows * steps, local)), w_spec(True)],
            out_specs=whole(block),
        ),
        compiler_params=params,
        cost_estimate=cost,
        name="project_own",
    )(scalars, heads_out, w_out)
    pair = [(mine[k].astype(F32) + given[k].astype(F32)) for k in range(groups)]
    total = pair[0]
    for k in range(1, groups):
        ring = [(i, ((i // 2 + k) % groups) * 2 + i % 2) for i in range(tensor)]
        total = total + lax.ppermute(pair[k].astype(BF16), "tensor", ring).astype(F32)
    return total.astype(BF16).reshape(steps, rows, column).swapaxes(0, 1)


def solution(mesh):
    in_specs = (
        P("particle", None, None),
        P(),
        P("particle", None, "tensor"),
        P(None, "tensor"),
        P(None, "tensor"),
        P("tensor", None),
        P("particle", "tensor", None, None),
        P("particle"),
    )
    out_specs = P("particle", None, "tensor")
    return jax.shard_map(shards, mesh=mesh, in_specs=in_specs, out_specs=out_specs, check_vma=False)
```

time: 223 us -> 67.1 us (0.30)
  the two profiles are of different devices: /device:TPU:1 before, /device:TPU:0 now
where the time goes in v1:
time: 67.1 us; the launch traced here: 66.5 us
  Pallas kernels  17.1 us (25%)
  local copies, waits for them, and re-layouts  16.5 us (25%)
  blocking collectives  15.9 us (24%)
  starting transfers between devices  9.06 us (14%)
  waiting for transfers between devices  7.7 us (11%)
    all_to_all x1, blocking collectives, shards(): lax.all_to_all(send, 'particle', split_axis=0, concat_axis=0, tiled=True)  15.9 us
    unnamed x26, local copies, waits for them, and re-layouts  14.5 us
    pallas_call x1, Pallas kernels, shards(): pl.pallas_call(cache_kernel, out_shape=jax.ShapeDtypeStruct(packed, BF16)...  8.48 us
    ppermute x3, starting transfers between devices, shards(): lax.ppermute(pair[k].astype(BF16), 'tensor', ring).astype(F32)  5.29 us
    all_to_all x1, waiting for transfers between devices, shards(): lax.all_to_all(back, 'particle', split_axis=0, concat_axis=0, tiled=True)  3.92 us
    ppermute x3, waiting for transfers between devices, shards(): lax.ppermute(pair[k].astype(BF16), 'tensor', ring).astype(F32)  3.78 us
    all_to_all x1, starting transfers between devices, shards(): lax.all_to_all(back, 'particle', split_axis=0, concat_axis=0, tiled=True)  3.75 us
    pallas_call x1, Pallas kernels, shards(): pl.pallas_call(merge_kernel, out_shape=(jax.ShapeDtypeStruct(block, BF16)...  3.66 us
  transfers between devices with their start and end apart: 5, of which 3 were waited for; matrix products, arithmetic and copies ran while one was open for 2% of the time, Pallas kernels for 6%

profile of v1, /device:TPU:0, one launch (start us, length us, event | category | flops | bytes accessed | tf_op | source)
XLA Modules:
  0.0 66.5 jit_solution(3159933371263354074)
XLA Ops:
  0.0 0.0 copy-start.5
  0.0 0.8 %copy-done.5 = bf16[16,2,1024]{2,1,0:T(2,128)(2,1)S(1)} copy-done((bf16[16,2,1024]{2,1,0:T(2,128)(2,1)S(1)}, bf16[16,2,1024]{2,1,0:T(2,128)(2,1)}, u32[]{:S(2)}) %copy-start.5) | copy-done | bytes 65560
  0.8 0.0 copy-start.9
  0.8 0.7 %copy-done.9 = f32[16,128]{1,0:T(8,128)S(1)} copy-done((f32[16,128]{1,0:T(8,128)S(1)}, f32[16,128]{1,0:T(8,128)}, u32[]{:S(2)}) %copy-start.9) | copy-done | bytes 8216
  1.5 0.0 copy-start.10
  1.5 0.7 %copy-done.10 = f32[16,128]{1,0:T(8,128)S(1)} copy-done((f32[16,128]{1,0:T(8,128)S(1)}, f32[16,128]{1,0:T(8,128)}, u32[]{:S(2)}) %copy-start.10) | copy-done | bytes 8216
  2.2 0.0 copy-start.11
  2.2 0.7 copy-done.11
  2.9 0.0 copy-start.6
  2.9 0.0 copy-start.7
  2.9 0.0 copy-start.8
  2.9 0.7 %pack_queries.1 = (bf16[16,3,16,128]{3,2,1,0:T(8,128)(2,1)S(1)}, bf16[16,16,128]{2,1,0:T(8,128)(2,1)S(1)}) custom-call(s32[16]{0:T(128)S(1)} %copy-done.11, bf16[16,2,1024]{2,1,0:T(2,128)(2,1)S(1)} %copy-done.5, f32[16,128]{1,0:T(8,128)S(1)} %copy-done.10, f32[16,128]{1,0:T(8,128)S(1)} %copy-done.9), custom_call_target="tpu_custom_call" | custom-call | tf_op jit(solution)/shard_map/pack_queries/pallas_call | solution.py:178
  3.6 15.9 %all_to_all.10.recv = bf16[16,3,16,128]{3,2,1,0:T(8,128)(2,1)S(1)} all-to-all(bf16[16,3,16,128]{3,2,1,0:T(8,128)(2,1)S(1)} %get-tuple-element.11), channel_id=1, replica_groups=mesh['particle'=16,'tensor'=8] {'particle'}, dimensions={0} | all-to-all | bytes 393216 | tf_op jit(solution)/shard_map/all_to_all | solution.py:195
  19.6 0.0 copy-start.2
  19.6 2.2 %copy-done.2 = bf16[16,1,512,256]{3,2,1,0:T(8,128)(2,1)S(1)} copy-done((bf16[16,1,512,256]{3,2,1,0:T(8,128)(2,1)S(1)}, bf16[16,1,512,256]{3,2,1,0:T(8,128)(2,1)}, u32[]{:S(2)}) %copy-start.2) | copy-done | bytes 4194328
  21.8 0.0 copy-start.3
  21.8 8.5 %cache_attention.1 = bf16[16,3,16,128]{3,2,1,0:T(8,128)(2,1)} custom-call(bf16[16,3,16,128]{3,2,1,0:T(8,128)(2,1)S(1)} %all_to_all.10.recv, bf16[16,1,512,256]{3,2,1,0:T(8,128)(2,1)S(1)} %copy-done.2), custom_call_target="tpu_custom_call" | custom-call | flops 134217728 | bytes 5242880 | tf_op jit(solution)/shard_map/cache_attention/pallas_call | solution.py:220
  30.2 0.0 copy-start.12
  30.3 3.7 %all-to-all-start.1 = ((bf16[16,3,16,128]{3,2,1,0:T(8,128)(2,1)}), bf16[16,3,16,128]{3,2,1,0:T(8,128)(2,1)S(1)}, u32[]{:S(2)}, u32[]{:S(2)}) async-start(bf16[16,3,16,128]{3,2,1,0:T(8,128)(2,1)} %cache_attention.1), calls=%async_computation.1 | async-start | bytes 393216 | tf_op jit(solution)/shard_map/all_to_all | solution.py:231
  34.0 1.2 %reshape.24.x = bf16[32,8192]{1,0:T(8,128)(2,1)S(1)} reshape(bf16[16,2,8192]{2,1,0:T(2,128)(2,1)} %param.12) | data formatting | bytes 1048576 | tf_op jit(solution)/shard_map/reshape | solution.py:211
  35.3 0.0 copy-done.6
  35.3 0.0 copy-done.7
  35.3 0.0 copy-done.8
  35.3 0.0 copy-done.3
  35.3 0.0 copy-start.4
  35.3 1.6 %copy-done.4 = bf16[8192,128]{1,0:T(8,128)(2,1)S(1)} copy-done((bf16[8192,128]{1,0:T(8,128)(2,1)S(1)}, bf16[8192,128]{1,0:T(8,128)(2,1)}, u32[]{:S(2)}) %copy-start.4) | copy-done | bytes 2097176
  36.9 1.2 %new_tokens.1 = (f32[256,128]{1,0:T(8,128)S(1)}, f32[256,128]{1,0:T(8,128)S(1)}) custom-call(bf16[32,8192]{1,0:T(8,128)(2,1)S(1)} %reshape.24.x, f32[1,8192]{1,0:T(1,128)S(1)} %bitcast.21, bf16[8192,128]{1,0:T(8,128)(2,1)S(1)} %copy-done.3, bf16[8192,128]{1,0:T(8,128)(2,1)S(1)} %copy-done.4, bf16[16,16,128]{2,1,0:T(8,128)(2,1)S(1)} %get-tuple-element.12.queries, ...), custom_call_target="tpu_custom_call" | custom-call | flops 134217728 | bytes 5242880 | tf_op jit(solution)/shard_map/new_tokens/pallas_call | solution.py:197
  38.1 0.0 copy-done.12
  38.1 0.1 pad_add_fusion.scalars
  38.2 3.9 %all-to-all-done.1.recv = bf16[16,3,16,128]{3,2,1,0:T(8,128)(2,1)S(1)} async-done(((bf16[16,3,16,128]{3,2,1,0:T(8,128)(2,1)}), bf16[16,3,16,128]{3,2,1,0:T(8,128)(2,1)S(1)}, u32[]{:S(2)}, u32[]{:S(2)}) %all-to-all-start.1) | async-done | bytes 196640 | tf_op jit(solution)/shard_map/all_to_all | solution.py:231
  42.1 0.0 copy-start
  42.1 5.8 %copy-done = bf16[1024,8192]{1,0:T(8,128)(2,1)S(1)} copy-done((bf16[1024,8192]{1,0:T(8,128)(2,1)S(1)}, bf16[1024,8192]{1,0:T(8,128)(2,1)}, u32[]{:S(2)}) %copy-start) | copy-done | bytes 16777240
  47.9 0.0 copy-start.1
  47.9 3.7 %merge_project_sibling.1 = (bf16[4,32,1024]{2,1,0:T(8,128)(2,1)S(1)}, bf16[32,1024]{1,0:T(8,128)(2,1)S(1)}) custom-call(s32[18]{0:T(128)S(1)} %pad_add_fusion.scalars, bf16[16,3,16,128]{3,2,1,0:T(8,128)(2,1)S(1)} %all-to-all-done.1.recv, f32[256,128]{1,0:T(8,128)S(1)} %get-tuple-element.13.vec, f32[256,128]{1,0:T(8,128)S(1)} %get-tuple-element.14.stat, ...), custom_call_target="tpu_custom_call" | custom-call | flops 268435456 | bytes 8388608 | tf_op jit(solution)/shard_map/merge_project_sibling/pallas_call | solution.py:246
  51.5 0.0 collective-permute-start
  51.5 2.1 %copy-done.1 = bf16[1024,8192]{1,0:T(8,128)(2,1)S(1)} copy-done((bf16[1024,8192]{1,0:T(8,128)(2,1)S(1)}, bf16[1024,8192]{1,0:T(8,128)(2,1)}, u32[]{:S(2)}) %copy-start.1) | copy-done | bytes 16777240
  53.6 3.0 %project_own.1 = bf16[4,32,1024]{2,1,0:T(8,128)(2,1)S(1)} custom-call(s32[18]{0:T(128)S(1)} %pad_add_fusion.scalars, bf16[32,1024]{1,0:T(8,128)(2,1)S(1)} %get-tuple-element.15.heads, bf16[1024,8192]{1,0:T(8,128)(2,1)S(1)} %copy-done.1), custom_call_target="tpu_custom_call" | custom-call | flops 268435456 | bytes 8388608 | tf_op jit(solution)/shard_map/project_own/pallas_call | solution.py:268
  56.6 0.0 collective-permute-done
  56.7 0.1 fusion.3
  56.7 1.6 %collective-permute-start.1 = (bf16[32,1024]{1,0:T(8,128)(2,1)S(1)}, bf16[32,1024]{1,0:T(8,128)(2,1)S(1)}, u32[]{:S(2)}, u32[]{:S(2)}) collective-permute-start(bf16[32,1024]{1,0:T(8,128)(2,1)S(1)} %get-tuple-element.17), channel_id=1, source_target_pairs={{0,2},{1,3},{2,4},{3,5},{4,6},{5,7},{6,0},{7,1},{8,10},{9,11},{10,... | collective-permute-start | bytes 196616 | tf_op jit(solution)/shard_map/ppermute | solution.py:285
  58.4 1.7 %collective-permute-start.3 = (bf16[32,1024]{1,0:T(8,128)(2,1)S(1)}, bf16[32,1024]{1,0:T(8,128)(2,1)S(1)}, u32[]{:S(2)}, u32[]{:S(2)}) collective-permute-start(bf16[32,1024]{1,0:T(8,128)(2,1)S(1)} %get-tuple-element.18), channel_id=1, source_target_pairs={{0,6},{1,7},{2,0},{3,1},{4,2},{5,3},{6,4},{7,5},{8,14},{9,15},{10,... | collective-permute-start | bytes 196616 | tf_op jit(solution)/shard_map/ppermute | solution.py:285
  60.0 2.0 %collective-permute-start.2 = (bf16[32,1024]{1,0:T(8,128)(2,1)S(1)}, bf16[32,1024]{1,0:T(8,128)(2,1)S(1)}, u32[]{:S(2)}, u32[]{:S(2)}) collective-permute-start(bf16[32,1024]{1,0:T(8,128)(2,1)S(1)} %get-tuple-element.19), channel_id=1, source_target_pairs={{0,4},{1,5},{2,6},{3,7},{4,0},{5,1},{6,2},{7,3},{8,12},{9,13},{10,... | collective-permute-start | bytes 196616 | tf_op jit(solution)/shard_map/ppermute | solution.py:285
  62.0 1.0 %collective-permute-done.1 = bf16[32,1024]{1,0:T(8,128)(2,1)S(1)} collective-permute-done((bf16[32,1024]{1,0:T(8,128)(2,1)S(1)}, bf16[32,1024]{1,0:T(8,128)(2,1)S(1)}, u32[]{:S(2)}, u32[]{:S(2)}) %collective-permute-start.1) | collective-permute-done | bytes 65568 | tf_op jit(solution)/shard_map/ppermute | solution.py:285
  63.0 0.0 collective-permute-done.3
  63.0 2.8 %collective-permute-done.2 = bf16[32,1024]{1,0:T(8,128)(2,1)S(1)} collective-permute-done((bf16[32,1024]{1,0:T(8,128)(2,1)S(1)}, bf16[32,1024]{1,0:T(8,128)(2,1)S(1)}, u32[]{:S(2)}, u32[]{:S(2)}) %collective-permute-start.2) | collective-permute-done | bytes 65568 | tf_op jit(solution)/shard_map/ppermute | solution.py:285
  65.8 0.1 fusion.2
  65.8 0.7 %copy.15 = bf16[2,16,1024]{2,0,1:T(2,128)(2,1)} copy(bf16[2,16,1024]{2,1,0:T(8,128)(2,1)S(1)} %bitcast.22) | data formatting | bytes 131072 | tf_op jit(solution)/shard_map/reshape | solution.py:286
Async XLA Ops:
  0.0 0.8 %copy-start.5 = (bf16[16,2,1024]{2,1,0:T(2,128)(2,1)S(1)}, bf16[16,2,1024]{2,1,0:T(2,128)(2,1)}, u32[]{:S(2)}) copy-start(bf16[16,2,1024]{2,1,0:T(2,128)(2,1)} %qp.1) | copy-start | bytes 196612
  0.8 0.7 %copy-start.9 = (f32[16,128]{1,0:T(8,128)S(1)}, f32[16,128]{1,0:T(8,128)}, u32[]{:S(2)}) copy-start(f32[16,128]{1,0:T(8,128)} %constant.37.clone.sine) | copy-start | bytes 24580
  1.5 0.7 %copy-start.10 = (f32[16,128]{1,0:T(8,128)S(1)}, f32[16,128]{1,0:T(8,128)}, u32[]{:S(2)}) copy-start(f32[16,128]{1,0:T(8,128)} %constant.36.clone.cosine) | copy-start | bytes 24580
  2.2 0.7 copy-start.11
  2.9 32.4 %copy-start.6 = (f32[8192]{0:T(1024)S(1)}, f32[8192]{0:T(1024)}, u32[]{:S(2)}) copy-start(f32[8192]{0:T(1024)} %param.13) | copy-start | bytes 98308
  2.9 32.4 %copy-start.7 = (f32[32,128]{1,0:T(8,128)S(1)}, f32[32,128]{1,0:T(8,128)}, u32[]{:S(2)}) copy-start(f32[32,128]{1,0:T(8,128)} %constant.39.clone.sine) | copy-start | bytes 49156
  2.9 32.4 %copy-start.8 = (f32[32,128]{1,0:T(8,128)S(1)}, f32[32,128]{1,0:T(8,128)}, u32[]{:S(2)}) copy-start(f32[32,128]{1,0:T(8,128)} %constant.38.clone.cosine) | copy-start | bytes 49156
  19.6 2.2 %copy-start.2 = (bf16[16,1,512,256]{3,2,1,0:T(8,128)(2,1)S(1)}, bf16[16,1,512,256]{3,2,1,0:T(8,128)(2,1)}, u32[]{:S(2)}) copy-start(bf16[16,1,512,256]{3,2,1,0:T(8,128)(2,1)} %kv.1) | copy-start | bytes 12582916
  21.8 13.5 %copy-start.3 = (bf16[8192,128]{1,0:T(8,128)(2,1)S(1)}, bf16[8192,128]{1,0:T(8,128)(2,1)}, u32[]{:S(2)}) copy-start(bf16[8192,128]{1,0:T(8,128)(2,1)} %wk.1) | copy-start | bytes 6291460
  30.2 7.8 %copy-start.12 = (s32[16]{0:T(128)S(1)}, s32[16]{0:T(128)}, u32[]{:S(2)}) copy-start(s32[16]{0:T(128)} %anc.1) | copy-start | bytes 196
  30.3 11.8 %all-to-all-start.1 = ((bf16[16,3,16,128]{3,2,1,0:T(8,128)(2,1)}), bf16[16,3,16,128]{3,2,1,0:T(8,128)(2,1)S(1)}, u32[]{:S(2)}, u32[]{:S(2)}) async-start(bf16[16,3,16,128]{3,2,1,0:T(8,128)(2,1)} %cache_attention.1), calls=%async_computation.1 | async-start | bytes 393216 | tf_op jit(solution)/shard_map/all_to_all | solution.py:231
  35.3 1.6 %copy-start.4 = (bf16[8192,128]{1,0:T(8,128)(2,1)S(1)}, bf16[8192,128]{1,0:T(8,128)(2,1)}, u32[]{:S(2)}) copy-start(bf16[8192,128]{1,0:T(8,128)(2,1)} %wv.1) | copy-start | bytes 6291460
  42.1 5.8 %copy-start = (bf16[1024,8192]{1,0:T(8,128)(2,1)S(1)}, bf16[1024,8192]{1,0:T(8,128)(2,1)}, u32[]{:S(2)}) copy-start(bf16[1024,8192]{1,0:T(8,128)(2,1)} %w.3) | copy-start | bytes 50331652
  47.9 5.8 %copy-start.1 = (bf16[1024,8192]{1,0:T(8,128)(2,1)S(1)}, bf16[1024,8192]{1,0:T(8,128)(2,1)}, u32[]{:S(2)}) copy-start(bf16[1024,8192]{1,0:T(8,128)(2,1)} %w.3) | copy-start | bytes 50331652
  51.5 5.1 %collective-permute-start = (bf16[4,32,1024]{2,1,0:T(8,128)(2,1)S(1)}, bf16[4,32,1024]{2,1,0:T(8,128)(2,1)S(1)}, u32[]{:S(2)}, u32[]{:S(2)}) collective-permute-start(bf16[4,32,1024]{2,1,0:T(8,128)(2,1)S(1)} %get-tuple-element.16), channel_id=1, source_target_pairs={{0,1},{1,0},{2,3},{3,2},{4,5},{5,4},{6,7},{7,6},{8,9},{9,8},{10,11... | collective-permute-start | bytes 786440 | tf_op jit(solution)/shard_map/ppermute | solution.py:267
  56.7 6.2 %collective-permute-start.1 = (bf16[32,1024]{1,0:T(8,128)(2,1)S(1)}, bf16[32,1024]{1,0:T(8,128)(2,1)S(1)}, u32[]{:S(2)}, u32[]{:S(2)}) collective-permute-start(bf16[32,1024]{1,0:T(8,128)(2,1)S(1)} %get-tuple-element.17), channel_id=1, source_target_pairs={{0,2},{1,3},{2,4},{3,5},{4,6},{5,7},{6,0},{7,1},{8,10},{9,11},{10,... | collective-permute-start | bytes 196616 | tf_op jit(solution)/shard_map/ppermute | solution.py:285
  58.4 4.6 %collective-permute-start.3 = (bf16[32,1024]{1,0:T(8,128)(2,1)S(1)}, bf16[32,1024]{1,0:T(8,128)(2,1)S(1)}, u32[]{:S(2)}, u32[]{:S(2)}) collective-permute-start(bf16[32,1024]{1,0:T(8,128)(2,1)S(1)} %get-tuple-element.18), channel_id=1, source_target_pairs={{0,6},{1,7},{2,0},{3,1},{4,2},{5,3},{6,4},{7,5},{8,14},{9,15},{10,... | collective-permute-start | bytes 196616 | tf_op jit(solution)/shard_map/ppermute | solution.py:285
  60.0 5.8 %collective-permute-start.2 = (bf16[32,1024]{1,0:T(8,128)(2,1)S(1)}, bf16[32,1024]{1,0:T(8,128)(2,1)S(1)}, u32[]{:S(2)}, u32[]{:S(2)}) collective-permute-start(bf16[32,1024]{1,0:T(8,128)(2,1)S(1)} %get-tuple-element.19), channel_id=1, source_target_pairs={{0,4},{1,5},{2,6},{3,7},{4,0},{5,1},{6,2},{7,3},{8,12},{9,13},{10,... | collective-permute-start | bytes 196616 | tf_op jit(solution)/shard_map/ppermute | solution.py:285

commit v2 on v1

v2 whole, which is shorter than its diff:
```python
import jax
import jax.numpy as jnp
import numpy as np
from jax import lax
from jax.experimental import pallas as pl
from jax.experimental.pallas import tpu as pltpu
from jax.sharding import PartitionSpec as P

PAIR = 2
THETA = 500000.0
EPSILON = 1e-05
F32 = jnp.float32
BF16 = jnp.bfloat16
MIB = 1 << 20
NT = (((1,), (1,)), ((), ()))


def rotary_tables(context, steps, head_dim):
    half = head_dim // 2
    freqs = np.float32(THETA) ** (-np.arange(half, dtype=np.float32) * np.float32(2.0) / np.float32(head_dim))
    position = (np.float32(context) + np.arange(steps, dtype=np.float32)).reshape(steps, 1)
    angles = (position * freqs.astype(np.float32)).astype(np.float32)
    cosine, sine = np.cos(angles), np.sin(angles)
    return (
        np.concatenate([cosine, cosine], 1).astype(np.float32),
        np.concatenate([-sine, sine], 1).astype(np.float32),
    )


def slot_of(anc, row, rows, count):
    source = lax.div(anc[row], rows)
    rank = count[source]
    count[source] = rank + 1
    return source, rank


def pack_kernel(anc_hbm, qp_hbm, tables_hbm, send, queries, grid_ref, qp, tables, anc, count, spots, sems):
    copies = [
        pltpu.make_async_copy(src, dst, sems.at[i])
        for i, (src, dst) in enumerate(((qp_hbm, qp), (tables_hbm, tables), (anc_hbm, anc)))
    ]
    for copy in copies:
        copy.start()
    rows, steps, width = qp.shape
    _, per_row, head_dim = tables.shape
    devices = send.shape[0]
    send[...] = jnp.zeros(send.shape, BF16)
    for d in range(devices):
        count[d] = 0
        for j in range(PAIR):
            spots[PAIR * d + j] = 0
    for copy in copies:
        copy.wait()
    for h in range(width // head_dim):
        grid_ref[:, steps * h : steps * (h + 1), :] = qp[:, :, head_dim * h : head_dim * (h + 1)].astype(F32)
    flat = grid_ref[...].reshape(rows * per_row, head_dim)
    swapped = pltpu.roll(flat, head_dim // 2, 1)
    shape = (rows, per_row, head_dim)
    turned = flat.reshape(shape) * tables[0][None] + swapped.reshape(shape) * tables[1][None]
    queries[...] = turned.astype(BF16)
    for r in range(rows):
        source, rank = slot_of(anc, r, rows, count)
        spots[source * PAIR + rank] = lax.rem(anc[r], rows)
        send[source, rank] = queries[r]
    lane = lax.broadcasted_iota(jnp.int32, (per_row, head_dim), 1)
    for d in range(devices):
        send[d, PAIR] = jnp.where(
            lane < head_dim // 2, spots[PAIR * d].astype(F32), spots[PAIR * d + 1].astype(F32)
        ).astype(BF16)


def fresh_kernel(
    x, gain_hbm, wk_hbm, wv_hbm, queries, tables_hbm, kv_hbm, vec, stat, old, wk, wv, gain, tables, sems
):
    copies = [
        pltpu.make_async_copy(src, dst, sems.at[i])
        for i, (src, dst) in enumerate(
            ((gain_hbm, gain), (tables_hbm, tables), (wk_hbm, wk), (wv_hbm, wv), (kv_hbm.at[:, 0, :, : wk.shape[1]], old))
        )
    ]
    for copy in copies:
        copy.start()
    tokens = x.shape[0]
    rows, per_row, head_dim = queries.shape
    steps = tokens // rows
    floats = x[...].astype(F32)
    inverse = lax.rsqrt(jnp.mean(floats * floats, -1, keepdims=True) + EPSILON)
    copies[0].wait()
    normed = (floats * inverse * gain[...]).astype(BF16)
    for copy in copies[1:3]:
        copy.wait()
    repeat = tokens // per_row
    cosine, sine = (jnp.concatenate([tables[i]] * repeat, 0) for i in range(2))
    keys = jnp.dot(normed, wk[...], preferred_element_type=F32)
    keys = (keys * cosine + pltpu.roll(keys, head_dim // 2, 1) * sine).astype(BF16)
    copies[3].wait()
    vals = jnp.dot(normed, wv[...], preferred_element_type=F32).astype(BF16)
    flat = queries[...].reshape(rows * per_row, head_dim)
    scores = lax.dot_general(flat, keys, NT, preferred_element_type=F32) * head_dim ** (-0.5)
    row = lax.broadcasted_iota(jnp.int32, scores.shape, 0)
    col = lax.broadcasted_iota(jnp.int32, scores.shape, 1)
    seen = (lax.div(row, per_row) == lax.div(col, steps)) & (lax.rem(col, steps) <= lax.rem(row, steps))
    top = jnp.max(jnp.where(seen, scores, -jnp.inf), -1, keepdims=True)
    expo = jnp.where(seen, jnp.exp(jnp.where(seen, scores - top, 0.0)), 0.0)
    vec[...] = jnp.dot(expo.astype(BF16), vals, preferred_element_type=F32)
    lane = lax.broadcasted_iota(jnp.int32, stat.shape, 1)
    stat[...] = jnp.where(lane == 0, top, jnp.sum(expo, -1, keepdims=True))
    copies[4].wait()


def cache_kernel(recv, keys, kv_hbm, back, scores, expos, tops, sums, values, sem):
    devices, _, per_row, head_dim = recv.shape
    copy = pltpu.make_async_copy(kv_hbm.at[:, 0, :, keys.shape[2] :], values, sem)
    copy.start()
    slots = [(d, j) for d in range(devices) for j in range(PAIR)]
    lane = lax.broadcasted_iota(jnp.int32, (per_row, head_dim), 1)
    spots = []
    for d in range(devices):
        spot = recv[d, PAIR].astype(F32)
        for j in range(PAIR):
            spots.append(spot[0, j * (head_dim // PAIR)].astype(jnp.int32))
    for i, (d, j) in enumerate(slots):
        scores[i] = lax.dot_general(
            recv[d, j], keys[spots[i]], NT, preferred_element_type=F32
        ) * head_dim ** (-0.5)
    for i in range(len(slots)):
        score = scores[i]
        top = jnp.max(score, -1, keepdims=True)
        expo = jnp.exp(score - top)
        expos[i] = expo.astype(BF16)
        tops[i] = jnp.broadcast_to(top, lane.shape)
        sums[i] = jnp.broadcast_to(jnp.sum(expo, -1, keepdims=True), lane.shape)
    copy.wait()
    for i, (d, j) in enumerate(slots):
        vector = jnp.dot(expos[i], values[spots[i]], preferred_element_type=F32)
        back[d, j] = (vector / sums[i]).astype(BF16)
    for d in range(devices):
        stat = jnp.zeros(lane.shape, F32)
        for j in range(PAIR):
            at_lane = j * (head_dim // PAIR)
            for value, parts in ((tops[d * PAIR + j], 3), (sums[d * PAIR + j], 2)):
                for _ in range(parts):
                    part = value.astype(BF16).astype(F32)
                    stat = jnp.where(lane == at_lane, part, stat)
                    value = value - part
                    at_lane += 1
        back[d, PAIR] = stat.astype(BF16)


def project(heads, w, out, own):
    index = lax.axis_index("tensor")
    first, core = lax.div(index, 2), lax.rem(index, 2)
    core = core if own else 1 - core
    groups, _, column = out.shape
    for k in range(groups):
        block = 2 * lax.rem(first + k, groups) + core
        at = pl.multiple_of(block * column, column)
        out[k] = jnp.dot(heads[...], w[:, pl.ds(at, column)], preferred_element_type=F32).astype(BF16)


def merge_kernel(anc, recv, vec, stat, w, out, heads, grid_ref, sums, lined, count):
    devices, _, per_row, head_dim = recv.shape
    rows = vec.shape[0] // per_row
    steps = heads.shape[0] // rows
    for d in range(devices):
        count[d] = 0
    for r in range(rows):
        source, rank = slot_of(anc, r, rows, count)
        grid_ref[pl.ds(r * per_row, per_row), :] = recv[source, rank].astype(F32)
        both = recv[source, PAIR].astype(F32)
        sums[pl.ds(r * per_row, per_row), :] = jnp.where(rank == 0, both, pltpu.roll(both, head_dim // 2, 1))
    parts = sums[...]
    top_c = parts[:, 0:1] + parts[:, 1:2] + parts[:, 2:3]
    sum_c = parts[:, 3:4] + parts[:, 4:5]
    top_f, sum_f = stat[:, 0:1], stat[:, 1:2]
    top = jnp.maximum(top_c, top_f)
    factor_c = sum_c * jnp.exp(top_c - top)
    factor_f = jnp.exp(top_f - top)
    share = 1.0 / (factor_c + sum_f * factor_f)
    grid_ref[...] = grid_ref[...] * (factor_c * share) + vec[...] * (factor_f * share)
    for h in range(per_row // steps):
        for s in range(steps):
            lined[h, pl.ds(s, rows, stride=steps), :] = grid_ref[pl.ds(h * steps + s, rows, stride=per_row), :]
        heads[:, pl.ds(h * head_dim, head_dim)] = lined[h].astype(BF16)
    project(heads, w, out, False)


def second_kernel(heads, w, out):
    project(heads, w, out, True)


def shards(inputs, norm_gain, query_proj, w_key, w_value, w_out, kv_cache, ancestors):
    rows, steps, width = inputs.shape
    context = kv_cache.shape[2]
    head_dim = kv_cache.shape[3] // 2
    local = query_proj.shape[2]
    heads = local // head_dim
    per_row = heads * steps
    devices = lax.axis_size("particle")
    tensor = lax.axis_size("tensor")
    column = width // tensor
    cosine, sine = rotary_tables(context, steps, head_dim)
    tables = np.stack([np.tile(cosine, (heads, 1)), np.tile(sine, (heads, 1))])
    smem = pl.BlockSpec(memory_space=pltpu.SMEM)
    vmem = pl.BlockSpec(memory_space=pltpu.VMEM)
    stay = pl.BlockSpec(memory_space=pl.ANY)
    hbm = lambda x: pltpu.with_memory_space_constraint(x, pltpu.HBM)
    tables = hbm(jnp.asarray(tables))

    packed = (devices, PAIR + 1, per_row, head_dim)
    send, queries = pl.pallas_call(
        pack_kernel,
        out_shape=(
            jax.ShapeDtypeStruct(packed, BF16),
            jax.ShapeDtypeStruct((rows, per_row, head_dim), BF16),
        ),
        in_specs=[stay] * 3,
        out_specs=(vmem, vmem),
        scratch_shapes=[
            pltpu.VMEM((rows, per_row, head_dim), F32),
            pltpu.VMEM((rows, steps, local), BF16),
            pltpu.VMEM((2, per_row, head_dim), F32),
            pltpu.SMEM((rows,), jnp.int32),
            pltpu.SMEM((devices,), jnp.int32),
            pltpu.SMEM((devices * PAIR,), jnp.int32),
            pltpu.SemaphoreType.DMA((3,)),
        ],
        compiler_params=pltpu.CompilerParams(vmem_limit_bytes=4 * MIB),
        cost_estimate=pl.CostEstimate(flops=10_000_000_000, bytes_accessed=MIB, transcendentals=0),
        name="pack_queries",
    )(hbm(ancestors), hbm(query_proj), tables)

    recv = lax.all_to_all(send, "particle", split_axis=0, concat_axis=0, tiled=True)

    vec, stat, cached_keys = pl.pallas_call(
        fresh_kernel,
        out_shape=(
            jax.ShapeDtypeStruct((rows * per_row, head_dim), F32),
            jax.ShapeDtypeStruct((rows * per_row, head_dim), F32),
            pltpu.VMEM((rows, context, head_dim), BF16),
        ),
        in_specs=[vmem, stay, stay, stay, vmem, stay, stay],
        out_specs=(vmem, vmem, vmem),
        scratch_shapes=[
            pltpu.VMEM((width, head_dim), BF16),
            pltpu.VMEM((width, head_dim), BF16),
            pltpu.VMEM((1, width), F32),
            pltpu.VMEM((2, per_row, head_dim), F32),
            pltpu.SemaphoreType.DMA((5,)),
        ],
        compiler_params=pltpu.CompilerParams(vmem_limit_bytes=16 * MIB),
        cost_estimate=pl.CostEstimate(
            flops=4_000_000_000, bytes_accessed=5 * MIB, transcendentals=0
        ),
        name="new_tokens",
    )(
        inputs.reshape(rows * steps, width),
        hbm(norm_gain.reshape(1, width)),
        hbm(w_key),
        hbm(w_value),
        queries,
        tables,
        hbm(kv_cache),
    )

    slots = devices * PAIR
    back = pl.pallas_call(
        cache_kernel,
        out_shape=jax.ShapeDtypeStruct(packed, BF16),
        in_specs=[vmem, vmem, stay],
        out_specs=vmem,
        scratch_shapes=[
            pltpu.VMEM((slots, per_row, context), F32),
            pltpu.VMEM((slots, per_row, context), BF16),
            pltpu.VMEM((slots, per_row, head_dim), F32),
            pltpu.VMEM((slots, per_row, head_dim), F32),
            pltpu.VMEM((rows, context, head_dim), BF16),
            pltpu.SemaphoreType.DMA(()),
        ],
        compiler_params=pltpu.CompilerParams(vmem_limit_bytes=8 * MIB),
        cost_estimate=pl.CostEstimate(
            flops=10_000_000_000, bytes_accessed=5 * MIB, transcendentals=0
        ),
        name="cache_attention",
    )(recv, cached_keys, hbm(kv_cache))
    home = lax.all_to_all(back, "particle", split_axis=0, concat_axis=0, tiled=True)

    groups = tensor // 2
    block = (groups, rows * steps, column)
    params = pltpu.CompilerParams(vmem_limit_bytes=8 * MIB)
    cost = pl.CostEstimate(
        flops=rows * steps * local * width, bytes_accessed=local * width, transcendentals=0
    )
    other, heads_out = pl.pallas_call(
        merge_kernel,
        out_shape=(
            jax.ShapeDtypeStruct(block, BF16),
            jax.ShapeDtypeStruct((rows * steps, local), BF16),
        ),
        in_specs=[smem, vmem, vmem, vmem, vmem],
        out_specs=(vmem, vmem),
        scratch_shapes=[
            pltpu.VMEM((rows * per_row, head_dim), F32),
            pltpu.VMEM((rows * per_row, head_dim), F32),
            pltpu.VMEM((heads, rows * steps, head_dim), F32),
            pltpu.SMEM((devices,), jnp.int32),
        ],
        compiler_params=params,
        cost_estimate=cost,
        name="merge_project_sibling",
    )(ancestors, home, vec, stat, w_out)
    given = lax.ppermute(other, "tensor", [(i, i ^ 1) for i in range(tensor)])
    mine = pl.pallas_call(
        second_kernel,
        out_shape=jax.ShapeDtypeStruct(block, BF16),
        in_specs=[vmem, vmem],
        out_specs=vmem,
        compiler_params=params,
        cost_estimate=cost,
        name="project_own",
    )(heads_out, w_out)
    pair = [(mine[k].astype(F32) + given[k].astype(F32)) for k in range(groups)]
    total = pair[0]
    for k in range(1, groups):
        ring = [(i, ((i // 2 + k) % groups) * 2 + i % 2) for i in range(tensor)]
        total = total + lax.ppermute(pair[k].astype(BF16), "tensor", ring).astype(F32)
    return total.astype(BF16).reshape(rows, steps, column)


def solution(mesh):
    in_specs = (
        P("particle", None, None),
        P(),
        P("particle", None, "tensor"),
        P(None, "tensor"),
        P(None, "tensor"),
        P("tensor", None),
        P("particle", "tensor", None, None),
        P("particle"),
    )
    out_specs = P("particle", None, "tensor")
    return jax.shard_map(shards, mesh=mesh, in_specs=in_specs, out_specs=out_specs, check_vma=False)
```

time: 67.1 us -> 48.2 us (0.72)
  the two profiles are of different devices: /device:TPU:0 before, /device:TPU:1 now
where the time goes in v2:
time: 48.2 us; the launch traced here: 47.8 us
  starting transfers between devices  16.1 us (33%)
  Pallas kernels  13.2 us (27%)
  blocking collectives  10.6 us (22%)
  waiting for transfers between devices  6.89 us (14%)
  local copies, waits for them, and re-layouts  0.88 us (2%)
    all_to_all x1, blocking collectives, shards(): lax.all_to_all(back, 'particle', split_axis=0, concat_axis=0, tiled=True)  10.6 us
    all_to_all x1, starting transfers between devices, shards(): lax.all_to_all(send, 'particle', split_axis=0, concat_axis=0, tiled=True)  8.44 us
    ppermute x3, starting transfers between devices, shards(): lax.ppermute(pair[k].astype(BF16), 'tensor', ring).astype(F32)  4.45 us
    pallas_call x1, Pallas kernels, shards(): pl.pallas_call(cache_kernel, out_shape=jax.ShapeDtypeStruct(packed, BF16)...  4.08 us
    all_to_all x1, waiting for transfers between devices, shards(): lax.all_to_all(send, 'particle', split_axis=0, concat_axis=0, tiled=True)  3.83 us
    ppermute x1, starting transfers between devices, shards(): given = lax.ppermute(other, 'tensor', [(i, i ^ 1) for i in range(tensor)])  3.17 us
    pallas_call x1, Pallas kernels, shards(): pl.pallas_call(fresh_kernel, out_shape=(jax.ShapeDtypeStruct((rows * per_...  3.09 us
    ppermute x3, waiting for transfers between devices, shards(): lax.ppermute(pair[k].astype(BF16), 'tensor', ring).astype(F32)  3.06 us
  transfers between devices with their start and end apart: 5, of which 3 were waited for; matrix products, arithmetic and copies ran while one was open for 0% of the time, Pallas kernels for 10%

profile of v2, /device:TPU:1, one launch (start us, length us, event | category | flops | bytes accessed | tf_op | source)
XLA Modules:
  0.0 47.8 jit_solution(10836494206147756426)
XLA Ops:
  0.0 0.0 copy-start.1
  0.0 1.8 %pack_queries.1 = (bf16[16,3,16,128]{3,2,1,0:T(8,128)(2,1)}, bf16[16,16,128]{2,1,0:T(8,128)(2,1)S(1)}) custom-call(s32[16]{0:T(128)} %anc.1, bf16[16,2,1024]{2,1,0:T(2,128)(2,1)} %qp_hbm.1, f32[2,16,128]{2,1,0:T(8,128)} %constant.2.clone.tables_hbm), custom_call_target="tpu_custom_call" | custom-call | flops 10000000000 | bytes 1048576 | tf_op jit(solution)/shard_map/pack_queries/pallas_call | solution.py:211
  1.8 8.4 %all-to-all-start = ((bf16[16,3,16,128]{3,2,1,0:T(8,128)(2,1)}), bf16[16,3,16,128]{3,2,1,0:T(8,128)(2,1)S(1)}, u32[]{:S(2)}, u32[]{:S(2)}) async-start(bf16[16,3,16,128]{3,2,1,0:T(8,128)(2,1)} %get-tuple-element.12), calls=%async_computation | async-start | bytes 393216 | tf_op jit(solution)/shard_map/all_to_all | solution.py:233
  10.3 0.0 copy-done.1
  10.3 0.2 reshape.24.x
  10.5 3.1 %new_tokens.1 = (f32[256,128]{1,0:T(8,128)S(1)}, f32[256,128]{1,0:T(8,128)S(1)}, bf16[16,512,128]{2,1,0:T(8,128)(2,1)S(1)}) custom-call(bf16[32,8192]{1,0:T(8,128)(2,1)S(1)} %reshape.24.x, f32[1,8192]{1,0:T(1,128)} %bitcast.17, bf16[8192,128]{1,0:T(8,128)(2,1)} %wk_hbm.1, bf16[8192,128]{1,0:T(8,128)(2,1)} %wv_hbm.1, ...), custom_call_target="tpu_custom_call" | custom-call | flops 4000000000 | bytes 5242880 | tf_op jit(solution)/shard_map/new_tokens/pallas_call | solution.py:235
  13.6 3.8 %all-to-all-done.recv = bf16[16,3,16,128]{3,2,1,0:T(8,128)(2,1)S(1)} async-done(((bf16[16,3,16,128]{3,2,1,0:T(8,128)(2,1)}), bf16[16,3,16,128]{3,2,1,0:T(8,128)(2,1)S(1)}, u32[]{:S(2)}, u32[]{:S(2)}) %all-to-all-start) | async-done | bytes 196640 | tf_op jit(solution)/shard_map/all_to_all | solution.py:233
  17.4 0.0 slice-start
  17.4 0.0 slice-start.1
  17.4 0.0 slice-start.2
  17.4 0.0 slice-start.3
  17.4 0.0 copy-start
  17.4 4.1 %cache_attention.1 = bf16[16,3,16,128]{3,2,1,0:T(8,128)(2,1)S(1)} custom-call(bf16[16,3,16,128]{3,2,1,0:T(8,128)(2,1)S(1)} %all-to-all-done.recv, bf16[16,512,128]{2,1,0:T(8,128)(2,1)S(1)} %get-tuple-element.14.keys, bf16[16,1,512,256]{3,2,1,0:T(8,128)(2,1)} %kv_hbm.3), custom_call_target="tpu_custom_call" | custom-call | flops 10000000000 | bytes 5242880 | tf_op jit(solution)/shard_map/cache_attention/pallas_call | solution.py:267
  21.5 10.6 %all_to_all.10.recv = bf16[16,3,16,128]{3,2,1,0:T(8,128)(2,1)S(1)} all-to-all(bf16[16,3,16,128]{3,2,1,0:T(8,128)(2,1)S(1)} %cache_attention.1), channel_id=1, replica_groups=mesh['particle'=16,'tensor'=8] {'particle'}, dimensions={0} | all-to-all | bytes 393216 | tf_op jit(solution)/shard_map/all_to_all | solution.py:286
  32.2 0.0 slice-done
  32.2 0.0 slice-done.1
  32.2 0.0 slice-done.2
  32.2 0.0 slice-done.3
  32.2 0.0 copy-done
  32.2 2.6 %merge_project_sibling.1 = (bf16[4,32,1024]{2,1,0:T(8,128)(2,1)S(1)}, bf16[32,1024]{1,0:T(8,128)(2,1)S(1)}) custom-call(s32[16]{0:T(128)S(1)} %copy-done, bf16[16,3,16,128]{3,2,1,0:T(8,128)(2,1)S(1)} %all_to_all.10.recv, f32[256,128]{1,0:T(8,128)S(1)} %get-tuple-element.15.vec, f32[256,128]{1,0:T(8,128)S(1)} %get-tuple-element.16.stat, ...), custom_call_target="tpu_custom_call" | custom-call | flops 268435456 | bytes 8388608 | tf_op jit(solution)/shard_map/merge_project_sibling/pallas_call | solution.py:294
  34.8 3.2 %collective-permute-start = (bf16[4,32,1024]{2,1,0:T(8,128)(2,1)S(1)}, bf16[4,32,1024]{2,1,0:T(8,128)(2,1)S(1)}, u32[]{:S(2)}, u32[]{:S(2)}) collective-permute-start(bf16[4,32,1024]{2,1,0:T(8,128)(2,1)S(1)} %get-tuple-element.18), channel_id=1, source_target_pairs={{0,1},{1,0},{2,3},{3,2},{4,5},{5,4},{6,7},{7,6},{8,9},{9,8},{10,11... | collective-permute-start | bytes 786440 | tf_op jit(solution)/shard_map/ppermute | solution.py:312
  38.0 1.5 %project_own.1 = bf16[4,32,1024]{2,1,0:T(8,128)(2,1)S(1)} custom-call(bf16[32,1024]{1,0:T(8,128)(2,1)S(1)} %get-tuple-element.17.heads, bf16[1024,8192]{1,0:T(8,128)(2,1)S(1)} %bitcast.16), custom_call_target="tpu_custom_call" | custom-call | flops 268435456 | bytes 8388608 | tf_op jit(solution)/shard_map/project_own/pallas_call | solution.py:313
  39.5 0.0 collective-permute-done
  39.6 0.1 fusion.3
  39.6 1.4 %collective-permute-start.1 = (bf16[32,1024]{1,0:T(8,128)(2,1)S(1)}, bf16[32,1024]{1,0:T(8,128)(2,1)S(1)}, u32[]{:S(2)}, u32[]{:S(2)}) collective-permute-start(bf16[32,1024]{1,0:T(8,128)(2,1)S(1)} %get-tuple-element.19), channel_id=1, source_target_pairs={{0,2},{1,3},{2,4},{3,5},{4,6},{5,7},{6,0},{7,1},{8,10},{9,11},{10,... | collective-permute-start | bytes 196616 | tf_op jit(solution)/shard_map/ppermute | solution.py:326
  41.0 1.5 %collective-permute-start.3 = (bf16[32,1024]{1,0:T(8,128)(2,1)S(1)}, bf16[32,1024]{1,0:T(8,128)(2,1)S(1)}, u32[]{:S(2)}, u32[]{:S(2)}) collective-permute-start(bf16[32,1024]{1,0:T(8,128)(2,1)S(1)} %get-tuple-element.20), channel_id=1, source_target_pairs={{0,6},{1,7},{2,0},{3,1},{4,2},{5,3},{6,4},{7,5},{8,14},{9,15},{10,... | collective-permute-start | bytes 196616 | tf_op jit(solution)/shard_map/ppermute | solution.py:326
  42.5 1.6 %collective-permute-start.2 = (bf16[32,1024]{1,0:T(8,128)(2,1)S(1)}, bf16[32,1024]{1,0:T(8,128)(2,1)S(1)}, u32[]{:S(2)}, u32[]{:S(2)}) collective-permute-start(bf16[32,1024]{1,0:T(8,128)(2,1)S(1)} %get-tuple-element.21), channel_id=1, source_target_pairs={{0,4},{1,5},{2,6},{3,7},{4,0},{5,1},{6,2},{7,3},{8,12},{9,13},{10,... | collective-permute-start | bytes 196616 | tf_op jit(solution)/shard_map/ppermute | solution.py:326
  44.1 0.7 %collective-permute-done.1 = bf16[32,1024]{1,0:T(8,128)(2,1)S(1)} collective-permute-done((bf16[32,1024]{1,0:T(8,128)(2,1)S(1)}, bf16[32,1024]{1,0:T(8,128)(2,1)S(1)}, u32[]{:S(2)}, u32[]{:S(2)}) %collective-permute-start.1) | collective-permute-done | bytes 65568 | tf_op jit(solution)/shard_map/ppermute | solution.py:326
  44.7 0.0 collective-permute-done.3
  44.7 2.4 %collective-permute-done.2 = bf16[32,1024]{1,0:T(8,128)(2,1)S(1)} collective-permute-done((bf16[32,1024]{1,0:T(8,128)(2,1)S(1)}, bf16[32,1024]{1,0:T(8,128)(2,1)S(1)}, u32[]{:S(2)}, u32[]{:S(2)}) %collective-permute-start.2) | collective-permute-done | bytes 65568 | tf_op jit(solution)/shard_map/ppermute | solution.py:326
  47.1 0.1 fusion.2
  47.2 0.7 %reshape.26 = bf16[16,2,1024]{2,1,0:T(2,128)(2,1)} reshape(bf16[32,1024]{1,0:T(8,128)(2,1)S(1)} %fusion.2) | data formatting | bytes 131072 | tf_op jit(solution)/shard_map/reshape | solution.py:327
  (1 shorter events, 0.0 us)
Async XLA Ops:
  0.0 10.3 %copy-start.1 = (bf16[16,2,8192]{2,1,0:T(2,128)(2,1)S(1)}, bf16[16,2,8192]{2,1,0:T(2,128)(2,1)}, u32[]{:S(2)}) copy-start(bf16[16,2,8192]{2,1,0:T(2,128)(2,1)} %param.9) | copy-start | bytes 1572868
  1.8 15.6 %all-to-all-start = ((bf16[16,3,16,128]{3,2,1,0:T(8,128)(2,1)}), bf16[16,3,16,128]{3,2,1,0:T(8,128)(2,1)S(1)}, u32[]{:S(2)}, u32[]{:S(2)}) async-start(bf16[16,3,16,128]{3,2,1,0:T(8,128)(2,1)} %get-tuple-element.12), calls=%async_computation | async-start | bytes 393216 | tf_op jit(solution)/shard_map/all_to_all | solution.py:233
  17.4 14.7 %slice-start = ((s8[16777216]{0:T(1024)(128)(4,1)}), s8[4194304]{0:T(1024)(128)(4,1)S(1)}, s32[]{:S(2)}) async-start(s8[16777216]{0:T(1024)(128)(4,1)} %bitcast.15), calls=%async_computation.2 | async-start | bytes 8388608
  17.4 14.7 %slice-start.1 = ((s8[16777216]{0:T(1024)(128)(4,1)}), s8[4194304]{0:T(1024)(128)(4,1)S(1)}, s32[]{:S(2)}) async-start(s8[16777216]{0:T(1024)(128)(4,1)} %bitcast.15), calls=%async_computation.3 | async-start | bytes 8388608
  17.4 14.7 %slice-start.2 = ((s8[16777216]{0:T(1024)(128)(4,1)}), s8[4194304]{0:T(1024)(128)(4,1)S(1)}, s32[]{:S(2)}) async-start(s8[16777216]{0:T(1024)(128)(4,1)} %bitcast.15), calls=%async_computation.4 | async-start | bytes 8388608
  17.4 14.7 %slice-start.3 = ((s8[16777216]{0:T(1024)(128)(4,1)}), s8[4194304]{0:T(1024)(128)(4,1)S(1)}, s32[]{:S(2)}) async-start(s8[16777216]{0:T(1024)(128)(4,1)} %bitcast.15), calls=%async_computation.5 | async-start | bytes 8388608
  17.4 14.8 %copy-start = (s32[16]{0:T(128)S(1)}, s32[16]{0:T(128)}, u32[]{:S(2)}) copy-start(s32[16]{0:T(128)} %anc.1) | copy-start | bytes 196
  34.8 4.7 %collective-permute-start = (bf16[4,32,1024]{2,1,0:T(8,128)(2,1)S(1)}, bf16[4,32,1024]{2,1,0:T(8,128)(2,1)S(1)}, u32[]{:S(2)}, u32[]{:S(2)}) collective-permute-start(bf16[4,32,1024]{2,1,0:T(8,128)(2,1)S(1)} %get-tuple-element.18), channel_id=1, source_target_pairs={{0,1},{1,0},{2,3},{3,2},{4,5},{5,4},{6,7},{7,6},{8,9},{9,8},{10,11... | collective-permute-start | bytes 786440 | tf_op jit(solution)/shard_map/ppermute | solution.py:312
  39.6 5.1 %collective-permute-start.1 = (bf16[32,1024]{1,0:T(8,128)(2,1)S(1)}, bf16[32,1024]{1,0:T(8,128)(2,1)S(1)}, u32[]{:S(2)}, u32[]{:S(2)}) collective-permute-start(bf16[32,1024]{1,0:T(8,128)(2,1)S(1)} %get-tuple-element.19), channel_id=1, source_target_pairs={{0,2},{1,3},{2,4},{3,5},{4,6},{5,7},{6,0},{7,1},{8,10},{9,11},{10,... | collective-permute-start | bytes 196616 | tf_op jit(solution)/shard_map/ppermute | solution.py:326
  41.0 3.7 %collective-permute-start.3 = (bf16[32,1024]{1,0:T(8,128)(2,1)S(1)}, bf16[32,1024]{1,0:T(8,128)(2,1)S(1)}, u32[]{:S(2)}, u32[]{:S(2)}) collective-permute-start(bf16[32,1024]{1,0:T(8,128)(2,1)S(1)} %get-tuple-element.20), channel_id=1, source_target_pairs={{0,6},{1,7},{2,0},{3,1},{4,2},{5,3},{6,4},{7,5},{8,14},{9,15},{10,... | collective-permute-start | bytes 196616 | tf_op jit(solution)/shard_map/ppermute | solution.py:326
  42.5 4.6 %collective-permute-start.2 = (bf16[32,1024]{1,0:T(8,128)(2,1)S(1)}, bf16[32,1024]{1,0:T(8,128)(2,1)S(1)}, u32[]{:S(2)}, u32[]{:S(2)}) collective-permute-start(bf16[32,1024]{1,0:T(8,128)(2,1)S(1)} %get-tuple-element.21), channel_id=1, source_target_pairs={{0,4},{1,5},{2,6},{3,7},{4,0},{5,1},{6,2},{7,3},{8,12},{9,13},{10,... | collective-permute-start | bytes 196616 | tf_op jit(solution)/shard_map/ppermute | solution.py:326

commit v3 on v2

--- a/solution.py
+++ b/solution.py
@@ -108,7 +108,7 @@
     copies[4].wait()
 
 
-def cache_kernel(recv, keys, kv_hbm, back, scores, expos, tops, sums, values, sem):
+def cache_kernel(recv, keys, kv_hbm, vectors, tops, sums, scores, expos, values, sem):
     devices, _, per_row, head_dim = recv.shape
     copy = pltpu.make_async_copy(kv_hbm.at[:, 0, :, keys.shape[2] :], values, sem)
     copy.start()
@@ -131,10 +131,15 @@
         tops[i] = jnp.broadcast_to(top, lane.shape)
         sums[i] = jnp.broadcast_to(jnp.sum(expo, -1, keepdims=True), lane.shape)
     copy.wait()
-    for i, (d, j) in enumerate(slots):
-        vector = jnp.dot(expos[i], values[spots[i]], preferred_element_type=F32)
-        back[d, j] = (vector / sums[i]).astype(BF16)
-    for d in range(devices):
+    for i in range(len(slots)):
+        vectors[i] = jnp.dot(expos[i], values[spots[i]], preferred_element_type=F32)
+
+def return_kernel(vectors, tops, sums, back):
+    devices, _, per_row, head_dim = back.shape
+    lane = lax.broadcasted_iota(jnp.int32, (per_row, head_dim), 1)
+    for d in range(devices):
+        for j in range(PAIR):
+            back[d, j] = (vectors[d * PAIR + j] / sums[d * PAIR + j]).astype(BF16)
         stat = jnp.zeros(lane.shape, F32)
         for j in range(PAIR):
             at_lane = j * (head_dim // PAIR)
@@ -151,11 +156,12 @@
     index = lax.axis_index("tensor")
     first, core = lax.div(index, 2), lax.rem(index, 2)
     core = core if own else 1 - core
-    groups, _, column = out.shape
+    groups, tokens, column = out.shape
+    wide = jnp.concatenate([heads[...]] * max(1, 128 // tokens), 0)
     for k in range(groups):
         block = 2 * lax.rem(first + k, groups) + core
         at = pl.multiple_of(block * column, column)
-        out[k] = jnp.dot(heads[...], w[:, pl.ds(at, column)], preferred_element_type=F32).astype(BF16)
+        out[k] = jnp.dot(wide, w[:, pl.ds(at, column)], preferred_element_type=F32)[:tokens].astype(BF16)
 
 
 def merge_kernel(anc, recv, vec, stat, w, out, heads, grid_ref, sums, lined, count):
@@ -264,25 +270,33 @@
     )
 
     slots = devices * PAIR
-    back = pl.pallas_call(
+    partial_result = jax.ShapeDtypeStruct((slots, per_row, head_dim), F32)
+    found = pl.pallas_call(
         cache_kernel,
-        out_shape=jax.ShapeDtypeStruct(packed, BF16),
+        out_shape=(partial_result,) * 3,
         in_specs=[vmem, vmem, stay],
-        out_specs=vmem,
+        out_specs=(vmem,) * 3,
         scratch_shapes=[
             pltpu.VMEM((slots, per_row, context), F32),
             pltpu.VMEM((slots, per_row, context), BF16),
-            pltpu.VMEM((slots, per_row, head_dim), F32),
-            pltpu.VMEM((slots, per_row, head_dim), F32),
             pltpu.VMEM((rows, context, head_dim), BF16),
             pltpu.SemaphoreType.DMA(()),
         ],
         compiler_params=pltpu.CompilerParams(vmem_limit_bytes=8 * MIB),
         cost_estimate=pl.CostEstimate(
-            flops=10_000_000_000, bytes_accessed=5 * MIB, transcendentals=0
+            flops=4 * slots * per_row * context * head_dim, bytes_accessed=5 * MIB, transcendentals=0
         ),
         name="cache_attention",
     )(recv, cached_keys, hbm(kv_cache))
+    back = pl.pallas_call(
+        return_kernel,
+        out_shape=jax.ShapeDtypeStruct(packed, BF16),
+        in_specs=[vmem] * 3,
+        out_specs=vmem,
+        compiler_params=pltpu.CompilerParams(vmem_limit_bytes=2 * MIB),
+        cost_estimate=pl.CostEstimate(flops=10_000_000_000, bytes_accessed=MIB, transcendentals=0),
+        name="pack_results",
+    )(*found)
     home = lax.all_to_all(back, "particle", split_axis=0, concat_axis=0, tiled=True)
 
     groups = tensor // 2
@@ -321,7 +335,7 @@
     )(heads_out, w_out)
     pair = [(mine[k].astype(F32) + given[k].astype(F32)) for k in range(groups)]
     total = pair[0]
-    for k in range(1, groups):
+    for k in (2, 1, 3):
         ring = [(i, ((i // 2 + k) % groups) * 2 + i % 2) for i in range(tensor)]
         total = total + lax.ppermute(pair[k].astype(BF16), "tensor", ring).astype(F32)
     return total.astype(BF16).reshape(rows, steps, column)

time: 48.2 us -> 48.4 us (level)
  Pallas kernels: 13.2 us -> 12.3 us
  waiting for transfers between devices: 6.89 us -> 7.47 us
    ppermute x3, waiting for transfers between devices: 3.06 us -> 3.63 us  [shards(): lax.ppermute(pair[k].astype(BF16), 'tensor', ring).astype(F32)]
    pallas_call x1 -> x2, Pallas kernels: 4.08 us -> 3.79 us  [the longest x1 3.63 us: shards(): pl.pallas_call(cache_kernel, out_shape=(partial_result,) * 3, in_specs=[v...]
  transfers between devices with their start and end apart: 5 -> 5, of which waited for: 3 -> 4; matrix products, arithmetic and copies ran while one was open for 0% -> 0% of each run, Pallas kernels for 10% -> 9%
where the time goes in v3:
time: 48.4 us; the launch traced here: 47.7 us
  starting transfers between devices  16.1 us (33%)
  Pallas kernels  12.3 us (25%)
  blocking collectives  10.6 us (22%)
  waiting for transfers between devices  7.47 us (15%)
  local copies, waits for them, and re-layouts  0.89 us (2%)
    all_to_all x1, blocking collectives, shards(): lax.all_to_all(back, 'particle', split_axis=0, concat_axis=0, tiled=True)  10.6 us
    all_to_all x1, starting transfers between devices, shards(): lax.all_to_all(send, 'particle', split_axis=0, concat_axis=0, tiled=True)  8.44 us
    ppermute x3, starting transfers between devices, shards(): lax.ppermute(pair[k].astype(BF16), 'tensor', ring).astype(F32)  4.46 us
    all_to_all x1, waiting for transfers between devices, shards(): lax.all_to_all(send, 'particle', split_axis=0, concat_axis=0, tiled=True)  3.83 us
    ppermute x3, waiting for transfers between devices, shards(): lax.ppermute(pair[k].astype(BF16), 'tensor', ring).astype(F32)  3.63 us
    pallas_call x1, Pallas kernels, shards(): pl.pallas_call(cache_kernel, out_shape=(partial_result,) * 3, in_specs=[v...  3.63 us
    ppermute x1, starting transfers between devices, shards(): given = lax.ppermute(other, 'tensor', [(i, i ^ 1) for i in range(tensor)])  3.2 us
    pallas_call x1, Pallas kernels, shards(): pl.pallas_call(fresh_kernel, out_shape=(jax.ShapeDtypeStruct((rows * per_...  3.09 us
  transfers between devices with their start and end apart: 5, of which 4 were waited for; matrix products, arithmetic and copies ran while one was open for 0% of the time, Pallas kernels for 9%

profile of v3, /device:TPU:1, one launch (start us, length us, event | category | flops | bytes accessed | tf_op | source)
XLA Modules:
  0.0 47.7 jit_solution(12101352328585212597)
XLA Ops:
  0.0 0.0 copy-start.1
  0.0 1.8 %pack_queries.1 = (bf16[16,3,16,128]{3,2,1,0:T(8,128)(2,1)}, bf16[16,16,128]{2,1,0:T(8,128)(2,1)S(1)}) custom-call(s32[16]{0:T(128)} %anc.1, bf16[16,2,1024]{2,1,0:T(2,128)(2,1)} %qp_hbm.1, f32[2,16,128]{2,1,0:T(8,128)} %constant.2.clone.tables_hbm), custom_call_target="tpu_custom_call" | custom-call | flops 10000000000 | bytes 1048576 | tf_op jit(solution)/shard_map/pack_queries/pallas_call | solution.py:217
  1.8 8.4 %all-to-all-start = ((bf16[16,3,16,128]{3,2,1,0:T(8,128)(2,1)}), bf16[16,3,16,128]{3,2,1,0:T(8,128)(2,1)S(1)}, u32[]{:S(2)}, u32[]{:S(2)}) async-start(bf16[16,3,16,128]{3,2,1,0:T(8,128)(2,1)} %get-tuple-element.15), calls=%async_computation | async-start | bytes 393216 | tf_op jit(solution)/shard_map/all_to_all | solution.py:239
  10.3 0.0 copy-done.1
  10.3 0.2 reshape.24.x
  10.5 3.1 %new_tokens.1 = (f32[256,128]{1,0:T(8,128)S(1)}, f32[256,128]{1,0:T(8,128)S(1)}, bf16[16,512,128]{2,1,0:T(8,128)(2,1)S(1)}) custom-call(bf16[32,8192]{1,0:T(8,128)(2,1)S(1)} %reshape.24.x, f32[1,8192]{1,0:T(1,128)} %bitcast.17, bf16[8192,128]{1,0:T(8,128)(2,1)} %wk_hbm.1, bf16[8192,128]{1,0:T(8,128)(2,1)} %wv_hbm.1, ...), custom_call_target="tpu_custom_call" | custom-call | flops 4000000000 | bytes 5242880 | tf_op jit(solution)/shard_map/new_tokens/pallas_call | solution.py:241
  13.6 3.8 %all-to-all-done.recv = bf16[16,3,16,128]{3,2,1,0:T(8,128)(2,1)S(1)} async-done(((bf16[16,3,16,128]{3,2,1,0:T(8,128)(2,1)}), bf16[16,3,16,128]{3,2,1,0:T(8,128)(2,1)S(1)}, u32[]{:S(2)}, u32[]{:S(2)}) %all-to-all-start) | async-done | bytes 196640 | tf_op jit(solution)/shard_map/all_to_all | solution.py:239
  17.4 3.6 %cache_attention.1 = (f32[32,16,128]{2,1,0:T(8,128)S(1)}, f32[32,16,128]{2,1,0:T(8,128)S(1)}, f32[32,16,128]{2,1,0:T(8,128)S(1)}) custom-call(bf16[16,3,16,128]{3,2,1,0:T(8,128)(2,1)S(1)} %all-to-all-done.recv, bf16[16,512,128]{2,1,0:T(8,128)(2,1)S(1)} %get-tuple-element.17.keys, bf16[16,1,512,256]{3,2,1,0:T(8,128)(2,1)} %kv_hbm.3), custom_call_target="tpu_custom_call" | custom-call | flops 134217728 | bytes 5242880 | tf_op jit(solution)/shard_map/cache_attention/pallas_call | solution.py:274
  21.0 0.0 slice-start
  21.1 0.0 slice-start.1
  21.1 0.0 slice-start.2
  21.1 0.0 slice-start.3
  21.1 0.0 copy-start
  21.1 0.2 pack_results.1
  21.3 10.6 %all_to_all.10.recv = bf16[16,3,16,128]{3,2,1,0:T(8,128)(2,1)S(1)} all-to-all(bf16[16,3,16,128]{3,2,1,0:T(8,128)(2,1)S(1)} %pack_results.1), channel_id=1, replica_groups=mesh['particle'=16,'tensor'=8] {'particle'}, dimensions={0} | all-to-all | bytes 393216 | tf_op jit(solution)/shard_map/all_to_all | solution.py:300
  31.9 0.0 slice-done
  31.9 0.0 slice-done.1
  31.9 0.0 slice-done.2
  31.9 0.0 slice-done.3
  31.9 0.0 copy-done
  31.9 2.4 %merge_project_sibling.1 = (bf16[4,32,1024]{2,1,0:T(8,128)(2,1)S(1)}, bf16[32,1024]{1,0:T(8,128)(2,1)S(1)}) custom-call(s32[16]{0:T(128)S(1)} %copy-done, bf16[16,3,16,128]{3,2,1,0:T(8,128)(2,1)S(1)} %all_to_all.10.recv, f32[256,128]{1,0:T(8,128)S(1)} %get-tuple-element.21.vec, f32[256,128]{1,0:T(8,128)S(1)} %get-tuple-element.22.stat, ...), custom_call_target="tpu_custom_call" | custom-call | flops 268435456 | bytes 8388608 | tf_op jit(solution)/shard_map/merge_project_sibling/pallas_call | solution.py:308
  34.3 3.2 %collective-permute-start = (bf16[4,32,1024]{2,1,0:T(8,128)(2,1)S(1)}, bf16[4,32,1024]{2,1,0:T(8,128)(2,1)S(1)}, u32[]{:S(2)}, u32[]{:S(2)}) collective-permute-start(bf16[4,32,1024]{2,1,0:T(8,128)(2,1)S(1)} %get-tuple-element.24), channel_id=1, source_target_pairs={{0,1},{1,0},{2,3},{3,2},{4,5},{5,4},{6,7},{7,6},{8,9},{9,8},{10,11... | collective-permute-start | bytes 786440 | tf_op jit(solution)/shard_map/ppermute | solution.py:326
  37.5 1.3 %project_own.1 = bf16[4,32,1024]{2,1,0:T(8,128)(2,1)S(1)} custom-call(bf16[32,1024]{1,0:T(8,128)(2,1)S(1)} %get-tuple-element.23.heads, bf16[1024,8192]{1,0:T(8,128)(2,1)S(1)} %bitcast.16), custom_call_target="tpu_custom_call" | custom-call | flops 268435456 | bytes 8388608 | tf_op jit(solution)/shard_map/project_own/pallas_call | solution.py:327
  38.8 0.0 collective-permute-done
  38.8 0.1 fusion.3
  38.9 3.0 %collective-permute-start.1 = (bf16[32,1024]{1,0:T(8,128)(2,1)S(1)}, bf16[32,1024]{1,0:T(8,128)(2,1)S(1)}, u32[]{:S(2)}, u32[]{:S(2)}) collective-permute-start(bf16[32,1024]{1,0:T(8,128)(2,1)S(1)} %get-tuple-element.25), channel_id=1, source_target_pairs={{0,4},{1,5},{2,6},{3,7},{4,0},{5,1},{6,2},{7,3},{8,12},{9,13},{10,... | collective-permute-start | bytes 196616 | tf_op jit(solution)/shard_map/ppermute | solution.py:340
  41.9 0.8 %collective-permute-start.3 = (bf16[32,1024]{1,0:T(8,128)(2,1)S(1)}, bf16[32,1024]{1,0:T(8,128)(2,1)S(1)}, u32[]{:S(2)}, u32[]{:S(2)}) collective-permute-start(bf16[32,1024]{1,0:T(8,128)(2,1)S(1)} %get-tuple-element.26), channel_id=1, source_target_pairs={{0,6},{1,7},{2,0},{3,1},{4,2},{5,3},{6,4},{7,5},{8,14},{9,15},{10,... | collective-permute-start | bytes 196616 | tf_op jit(solution)/shard_map/ppermute | solution.py:340
  42.6 0.7 %collective-permute-start.2 = (bf16[32,1024]{1,0:T(8,128)(2,1)S(1)}, bf16[32,1024]{1,0:T(8,128)(2,1)S(1)}, u32[]{:S(2)}, u32[]{:S(2)}) collective-permute-start(bf16[32,1024]{1,0:T(8,128)(2,1)S(1)} %get-tuple-element.27), channel_id=1, source_target_pairs={{0,2},{1,3},{2,4},{3,5},{4,6},{5,7},{6,0},{7,1},{8,10},{9,11},{10,... | collective-permute-start | bytes 196616 | tf_op jit(solution)/shard_map/ppermute | solution.py:340
  43.3 0.2 collective-permute-done.1
  43.6 2.1 %collective-permute-done.3 = bf16[32,1024]{1,0:T(8,128)(2,1)S(1)} collective-permute-done((bf16[32,1024]{1,0:T(8,128)(2,1)S(1)}, bf16[32,1024]{1,0:T(8,128)(2,1)S(1)}, u32[]{:S(2)}, u32[]{:S(2)}) %collective-permute-start.3) | collective-permute-done | bytes 65568 | tf_op jit(solution)/shard_map/ppermute | solution.py:340
  45.7 1.3 %collective-permute-done.2 = bf16[32,1024]{1,0:T(8,128)(2,1)S(1)} collective-permute-done((bf16[32,1024]{1,0:T(8,128)(2,1)S(1)}, bf16[32,1024]{1,0:T(8,128)(2,1)S(1)}, u32[]{:S(2)}, u32[]{:S(2)}) %collective-permute-start.2) | collective-permute-done | bytes 65568 | tf_op jit(solution)/shard_map/ppermute | solution.py:340
  47.0 0.1 fusion.2
  47.0 0.7 %reshape.26 = bf16[16,2,1024]{2,1,0:T(2,128)(2,1)} reshape(bf16[32,1024]{1,0:T(8,128)(2,1)S(1)} %fusion.2) | data formatting | bytes 131072 | tf_op jit(solution)/shard_map/reshape | solution.py:341
  (1 shorter events, 0.0 us)
Async XLA Ops:
  0.0 10.3 %copy-start.1 = (bf16[16,2,8192]{2,1,0:T(2,128)(2,1)S(1)}, bf16[16,2,8192]{2,1,0:T(2,128)(2,1)}, u32[]{:S(2)}) copy-start(bf16[16,2,8192]{2,1,0:T(2,128)(2,1)} %param.9) | copy-start | bytes 1572868
  1.8 15.6 %all-to-all-start = ((bf16[16,3,16,128]{3,2,1,0:T(8,128)(2,1)}), bf16[16,3,16,128]{3,2,1,0:T(8,128)(2,1)S(1)}, u32[]{:S(2)}, u32[]{:S(2)}) async-start(bf16[16,3,16,128]{3,2,1,0:T(8,128)(2,1)} %get-tuple-element.15), calls=%async_computation | async-start | bytes 393216 | tf_op jit(solution)/shard_map/all_to_all | solution.py:239
  21.0 10.8 %slice-start = ((s8[16777216]{0:T(1024)(128)(4,1)}), s8[4194304]{0:T(1024)(128)(4,1)S(1)}, s32[]{:S(2)}) async-start(s8[16777216]{0:T(1024)(128)(4,1)} %bitcast.15), calls=%async_computation.2 | async-start | bytes 8388608
  21.1 10.8 %slice-start.1 = ((s8[16777216]{0:T(1024)(128)(4,1)}), s8[4194304]{0:T(1024)(128)(4,1)S(1)}, s32[]{:S(2)}) async-start(s8[16777216]{0:T(1024)(128)(4,1)} %bitcast.15), calls=%async_computation.3 | async-start | bytes 8388608
  21.1 10.8 %slice-start.2 = ((s8[16777216]{0:T(1024)(128)(4,1)}), s8[4194304]{0:T(1024)(128)(4,1)S(1)}, s32[]{:S(2)}) async-start(s8[16777216]{0:T(1024)(128)(4,1)} %bitcast.15), calls=%async_computation.4 | async-start | bytes 8388608
  21.1 10.8 %slice-start.3 = ((s8[16777216]{0:T(1024)(128)(4,1)}), s8[4194304]{0:T(1024)(128)(4,1)S(1)}, s32[]{:S(2)}) async-start(s8[16777216]{0:T(1024)(128)(4,1)} %bitcast.15), calls=%async_computation.5 | async-start | bytes 8388608
  21.1 10.8 %copy-start = (s32[16]{0:T(128)S(1)}, s32[16]{0:T(128)}, u32[]{:S(2)}) copy-start(s32[16]{0:T(128)} %anc.1) | copy-start | bytes 196
  34.3 4.5 %collective-permute-start = (bf16[4,32,1024]{2,1,0:T(8,128)(2,1)S(1)}, bf16[4,32,1024]{2,1,0:T(8,128)(2,1)S(1)}, u32[]{:S(2)}, u32[]{:S(2)}) collective-permute-start(bf16[4,32,1024]{2,1,0:T(8,128)(2,1)S(1)} %get-tuple-element.24), channel_id=1, source_target_pairs={{0,1},{1,0},{2,3},{3,2},{4,5},{5,4},{6,7},{7,6},{8,9},{9,8},{10,11... | collective-permute-start | bytes 786440 | tf_op jit(solution)/shard_map/ppermute | solution.py:326
  38.9 4.7 %collective-permute-start.1 = (bf16[32,1024]{1,0:T(8,128)(2,1)S(1)}, bf16[32,1024]{1,0:T(8,128)(2,1)S(1)}, u32[]{:S(2)}, u32[]{:S(2)}) collective-permute-start(bf16[32,1024]{1,0:T(8,128)(2,1)S(1)} %get-tuple-element.25), channel_id=1, source_target_pairs={{0,4},{1,5},{2,6},{3,7},{4,0},{5,1},{6,2},{7,3},{8,12},{9,13},{10,... | collective-permute-start | bytes 196616 | tf_op jit(solution)/shard_map/ppermute | solution.py:340
  41.9 3.8 %collective-permute-start.3 = (bf16[32,1024]{1,0:T(8,128)(2,1)S(1)}, bf16[32,1024]{1,0:T(8,128)(2,1)S(1)}, u32[]{:S(2)}, u32[]{:S(2)}) collective-permute-start(bf16[32,1024]{1,0:T(8,128)(2,1)S(1)} %get-tuple-element.26), channel_id=1, source_target_pairs={{0,6},{1,7},{2,0},{3,1},{4,2},{5,3},{6,4},{7,5},{8,14},{9,15},{10,... | collective-permute-start | bytes 196616 | tf_op jit(solution)/shard_map/ppermute | solution.py:340
  42.6 4.3 %collective-permute-start.2 = (bf16[32,1024]{1,0:T(8,128)(2,1)S(1)}, bf16[32,1024]{1,0:T(8,128)(2,1)S(1)}, u32[]{:S(2)}, u32[]{:S(2)}) collective-permute-start(bf16[32,1024]{1,0:T(8,128)(2,1)S(1)} %get-tuple-element.27), channel_id=1, source_target_pairs={{0,2},{1,3},{2,4},{3,5},{4,6},{5,7},{6,0},{7,1},{8,10},{9,11},{10,... | collective-permute-start | bytes 196616 | tf_op jit(solution)/shard_map/ppermute | solution.py:340

commit v4 on v3

--- a/solution.py
+++ b/solution.py
@@ -103,36 +103,44 @@
     top = jnp.max(jnp.where(seen, scores, -jnp.inf), -1, keepdims=True)
     expo = jnp.where(seen, jnp.exp(jnp.where(seen, scores - top, 0.0)), 0.0)
     vec[...] = jnp.dot(expo.astype(BF16), vals, preferred_element_type=F32)
-    lane = lax.broadcasted_iota(jnp.int32, stat.shape, 1)
-    stat[...] = jnp.where(lane == 0, top, jnp.sum(expo, -1, keepdims=True))
+    stat[0] = jnp.broadcast_to(top, stat.shape[1:])
+    stat[1] = jnp.broadcast_to(jnp.sum(expo, -1, keepdims=True), stat.shape[1:])
     copies[4].wait()
 
 
-def cache_kernel(recv, keys, kv_hbm, vectors, tops, sums, scores, expos, values, sem):
+def cache_kernel(recv, keys, kv_hbm, vectors, tops, sums, scores, expos, values, spots, sem):
     devices, _, per_row, head_dim = recv.shape
-    copy = pltpu.make_async_copy(kv_hbm.at[:, 0, :, keys.shape[2] :], values, sem)
+    lane = lax.broadcasted_iota(jnp.int32, (per_row, head_dim), 1)
+    copy = pltpu.make_async_copy(kv_hbm.at[:, 0, :, head_dim:], values, sem)
     copy.start()
-    slots = [(d, j) for d in range(devices) for j in range(PAIR)]
-    lane = lax.broadcasted_iota(jnp.int32, (per_row, head_dim), 1)
-    spots = []
-    for d in range(devices):
-        spot = recv[d, PAIR].astype(F32)
-        for j in range(PAIR):
-            spots.append(spot[0, j * (head_dim // PAIR)].astype(jnp.int32))
-    for i, (d, j) in enumerate(slots):
-        scores[i] = lax.dot_general(
-            recv[d, j], keys[spots[i]], NT, preferred_element_type=F32
-        ) * head_dim ** (-0.5)
-    for i in range(len(slots)):
-        score = scores[i]
-        top = jnp.max(score, -1, keepdims=True)
-        expo = jnp.exp(score - top)
+    half = devices // 2
+
+    def score(part, _):
+        chosen = []
+        for k in range(half):
+            spot = recv[part * half + k, PAIR].astype(F32)
+            for j in range(PAIR):
+                chosen.append(spot[0, j * (head_dim // PAIR)].astype(jnp.int32))
+                spots[(part * half + k) * PAIR + j] = chosen[-1]
+        for k in range(half):
+            for j in range(PAIR):
+                d = part * half + k
+                scores[d * PAIR + j] = lax.dot_general(
+                    recv[d, j], keys[chosen[k * PAIR + j]], NT, preferred_element_type=F32
+                ) * head_dim ** (-0.5)
+        return 0
+
+    lax.fori_loop(0, 2, score, 0)
+    for i in range(devices * PAIR):
+        top = jnp.max(scores[i], -1, keepdims=True)
+        expo = jnp.exp(scores[i] - top)
         expos[i] = expo.astype(BF16)
         tops[i] = jnp.broadcast_to(top, lane.shape)
         sums[i] = jnp.broadcast_to(jnp.sum(expo, -1, keepdims=True), lane.shape)
     copy.wait()
-    for i in range(len(slots)):
+    for i in range(devices * PAIR):
         vectors[i] = jnp.dot(expos[i], values[spots[i]], preferred_element_type=F32)
+
 
 def return_kernel(vectors, tops, sums, back):
     devices, _, per_row, head_dim = back.shape
@@ -168,22 +176,28 @@
     devices, _, per_row, head_dim = recv.shape
     rows = vec.shape[0] // per_row
     steps = heads.shape[0] // rows
+    half = head_dim // PAIR
     for d in range(devices):
         count[d] = 0
+    lane = lax.broadcasted_iota(jnp.int32, (per_row, head_dim), 1)
     for r in range(rows):
         source, rank = slot_of(anc, r, rows, count)
         grid_ref[pl.ds(r * per_row, per_row), :] = recv[source, rank].astype(F32)
-        both = recv[source, PAIR].astype(F32)
-        sums[pl.ds(r * per_row, per_row), :] = jnp.where(rank == 0, both, pltpu.roll(both, head_dim // 2, 1))
-    parts = sums[...]
-    top_c = parts[:, 0:1] + parts[:, 1:2] + parts[:, 2:3]
-    sum_c = parts[:, 3:4] + parts[:, 4:5]
-    top_f, sum_f = stat[:, 0:1], stat[:, 1:2]
+        parts = recv[source, PAIR].astype(F32)
+        sums[pl.ds(r * per_row, per_row), :] = jnp.where(lax.div(lane, half) == rank, parts, 0.0).astype(BF16)
+    lane_from = lax.rem(lax.broadcasted_iota(jnp.int32, (head_dim, 2 * head_dim), 0), half)
+    lane_to = lax.broadcasted_iota(jnp.int32, (head_dim, 2 * head_dim), 1)
+    first = jnp.where(lane_from < 3, 1.0, 0.0)
+    second = jnp.where((lane_from >= 3) & (lane_from < 5), 1.0, 0.0)
+    spread = jnp.where(lane_to < head_dim, first, second)
+    both = jnp.dot(sums[...], spread.astype(BF16), preferred_element_type=F32)
+    top_c, sum_c = both[:, :head_dim], both[:, head_dim:]
+    top_f, sum_f = stat[0], stat[1]
     top = jnp.maximum(top_c, top_f)
     factor_c = sum_c * jnp.exp(top_c - top)
     factor_f = jnp.exp(top_f - top)
     share = 1.0 / (factor_c + sum_f * factor_f)
-    grid_ref[...] = grid_ref[...] * (factor_c * share) + vec[...] * (factor_f * share)
+    grid_ref[...] = (grid_ref[...] * factor_c + vec[...] * factor_f) * share
     for h in range(per_row // steps):
         for s in range(steps):
             lined[h, pl.ds(s, rows, stride=steps), :] = grid_ref[pl.ds(h * steps + s, rows, stride=per_row), :]
@@ -242,7 +256,7 @@
         fresh_kernel,
         out_shape=(
             jax.ShapeDtypeStruct((rows * per_row, head_dim), F32),
-            jax.ShapeDtypeStruct((rows * per_row, head_dim), F32),
+            jax.ShapeDtypeStruct((2, rows * per_row, head_dim), F32),
             pltpu.VMEM((rows, context, head_dim), BF16),
         ),
         in_specs=[vmem, stay, stay, stay, vmem, stay, stay],
@@ -280,6 +294,7 @@
             pltpu.VMEM((slots, per_row, context), F32),
             pltpu.VMEM((slots, per_row, context), BF16),
             pltpu.VMEM((rows, context, head_dim), BF16),
+            pltpu.SMEM((slots,), jnp.int32),
             pltpu.SemaphoreType.DMA(()),
         ],
         compiler_params=pltpu.CompilerParams(vmem_limit_bytes=8 * MIB),
@@ -315,7 +330,7 @@
         out_specs=(vmem, vmem),
         scratch_shapes=[
             pltpu.VMEM((rows * per_row, head_dim), F32),
-            pltpu.VMEM((rows * per_row, head_dim), F32),
+            pltpu.VMEM((rows * per_row, head_dim), BF16),
             pltpu.VMEM((heads, rows * steps, head_dim), F32),
             pltpu.SMEM((devices,), jnp.int32),
         ],
@@ -335,7 +350,7 @@
     )(heads_out, w_out)
     pair = [(mine[k].astype(F32) + given[k].astype(F32)) for k in range(groups)]
     total = pair[0]
-    for k in (2, 1, 3):
+    for k in range(1, groups):
         ring = [(i, ((i // 2 + k) % groups) * 2 + i % 2) for i in range(tensor)]
         total = total + lax.ppermute(pair[k].astype(BF16), "tensor", ring).astype(F32)
     return total.astype(BF16).reshape(rows, steps, column)

time: 48.4 us -> 46.3 us (0.957)
  Pallas kernels: 12.3 us -> 10.9 us
  waiting for transfers between devices: 7.47 us -> 6.89 us
    pallas_call x1, Pallas kernels: 3.63 us -> 2.53 us  [shards(): pl.pallas_call(cache_kernel, out_shape=(partial_result,) * 3, in_specs=[v...]
    ppermute x3, waiting for transfers between devices: 3.63 us -> 3.06 us  [shards(): lax.ppermute(pair[k].astype(BF16), 'tensor', ring).astype(F32)]
  transfers between devices with their start and end apart: 5 -> 5, of which waited for: 4 -> 3; matrix products, arithmetic and copies ran while one was open for 0% -> 0% of each run, Pallas kernels for 9% -> 10%
where the time goes in v4:
time: 46.3 us; the launch traced here: 45.6 us
  starting transfers between devices  16.1 us (35%)
  Pallas kernels  10.9 us (24%)
  blocking collectives  10.6 us (23%)
  waiting for transfers between devices  6.89 us (15%)
  local copies, waits for them, and re-layouts  0.89 us (2%)
    all_to_all x1, blocking collectives, shards(): lax.all_to_all(back, 'particle', split_axis=0, concat_axis=0, tiled=True)  10.6 us
    all_to_all x1, starting transfers between devices, shards(): lax.all_to_all(send, 'particle', split_axis=0, concat_axis=0, tiled=True)  8.44 us
    ppermute x3, starting transfers between devices, shards(): lax.ppermute(pair[k].astype(BF16), 'tensor', ring).astype(F32)  4.45 us
    all_to_all x1, waiting for transfers between devices, shards(): lax.all_to_all(send, 'particle', split_axis=0, concat_axis=0, tiled=True)  3.83 us
    ppermute x1, starting transfers between devices, shards(): given = lax.ppermute(other, 'tensor', [(i, i ^ 1) for i in range(tensor)])  3.18 us
    pallas_call x1, Pallas kernels, shards(): pl.pallas_call(fresh_kernel, out_shape=(jax.ShapeDtypeStruct((rows * per_...  3.09 us
    ppermute x3, waiting for transfers between devices, shards(): lax.ppermute(pair[k].astype(BF16), 'tensor', ring).astype(F32)  3.06 us
    pallas_call x1, Pallas kernels, shards(): pl.pallas_call(cache_kernel, out_shape=(partial_result,) * 3, in_specs=[v...  2.53 us
  transfers between devices with their start and end apart: 5, of which 3 were waited for; matrix products, arithmetic and copies ran while one was open for 0% of the time, Pallas kernels for 10%

profile of v4, /device:TPU:1, one launch (start us, length us, event | category | flops | bytes accessed | tf_op | source)
XLA Modules:
  0.0 45.6 jit_solution(5090650792879548961)
XLA Ops:
  0.0 0.0 copy-start.1
  0.0 1.8 %pack_queries.1 = (bf16[16,3,16,128]{3,2,1,0:T(8,128)(2,1)}, bf16[16,16,128]{2,1,0:T(8,128)(2,1)S(1)}) custom-call(s32[16]{0:T(128)} %anc.1, bf16[16,2,1024]{2,1,0:T(2,128)(2,1)} %qp_hbm.1, f32[2,16,128]{2,1,0:T(8,128)} %constant.2.clone.tables_hbm), custom_call_target="tpu_custom_call" | custom-call | flops 10000000000 | bytes 1048576 | tf_op jit(solution)/shard_map/pack_queries/pallas_call | solution.py:231
  1.8 8.4 %all-to-all-start = ((bf16[16,3,16,128]{3,2,1,0:T(8,128)(2,1)}), bf16[16,3,16,128]{3,2,1,0:T(8,128)(2,1)S(1)}, u32[]{:S(2)}, u32[]{:S(2)}) async-start(bf16[16,3,16,128]{3,2,1,0:T(8,128)(2,1)} %get-tuple-element.15), calls=%async_computation | async-start | bytes 393216 | tf_op jit(solution)/shard_map/all_to_all | solution.py:253
  10.3 0.0 copy-done.1
  10.3 0.2 reshape.24.x
  10.5 3.1 %new_tokens.1 = (f32[256,128]{1,0:T(8,128)S(1)}, f32[2,256,128]{2,1,0:T(8,128)S(1)}, bf16[16,512,128]{2,1,0:T(8,128)(2,1)S(1)}) custom-call(bf16[32,8192]{1,0:T(8,128)(2,1)S(1)} %reshape.24.x, f32[1,8192]{1,0:T(1,128)} %bitcast.17, bf16[8192,128]{1,0:T(8,128)(2,1)} %wk_hbm.1, bf16[8192,128]{1,0:T(8,128)(2,1)} %wv_hbm.1, ...), custom_call_target="tpu_custom_call" | custom-call | flops 4000000000 | bytes 5242880 | tf_op jit(solution)/shard_map/new_tokens/pallas_call | solution.py:255
  13.6 3.8 %all-to-all-done.recv = bf16[16,3,16,128]{3,2,1,0:T(8,128)(2,1)S(1)} async-done(((bf16[16,3,16,128]{3,2,1,0:T(8,128)(2,1)}), bf16[16,3,16,128]{3,2,1,0:T(8,128)(2,1)S(1)}, u32[]{:S(2)}, u32[]{:S(2)}) %all-to-all-start) | async-done | bytes 196640 | tf_op jit(solution)/shard_map/all_to_all | solution.py:253
  17.4 2.5 %cache_attention.1 = (f32[32,16,128]{2,1,0:T(8,128)S(1)}, f32[32,16,128]{2,1,0:T(8,128)S(1)}, f32[32,16,128]{2,1,0:T(8,128)S(1)}) custom-call(bf16[16,3,16,128]{3,2,1,0:T(8,128)(2,1)S(1)} %all-to-all-done.recv, bf16[16,512,128]{2,1,0:T(8,128)(2,1)S(1)} %get-tuple-element.17.keys, bf16[16,1,512,256]{3,2,1,0:T(8,128)(2,1)} %kv_hbm.3), custom_call_target="tpu_custom_call" | custom-call | flops 134217728 | bytes 5242880 | tf_op jit(solution)/shard_map/cache_attention/pallas_call | solution.py:288
  19.9 0.0 slice-start
  20.0 0.0 slice-start.1
  20.0 0.0 slice-start.2
  20.0 0.0 slice-start.3
  20.0 0.0 copy-start
  20.0 0.2 pack_results.1
  20.2 10.6 %all_to_all.10.recv = bf16[16,3,16,128]{3,2,1,0:T(8,128)(2,1)S(1)} all-to-all(bf16[16,3,16,128]{3,2,1,0:T(8,128)(2,1)S(1)} %pack_results.1), channel_id=1, replica_groups=mesh['particle'=16,'tensor'=8] {'particle'}, dimensions={0} | all-to-all | bytes 393216 | tf_op jit(solution)/shard_map/all_to_all | solution.py:315
  30.8 0.0 slice-done
  30.8 0.0 slice-done.1
  30.8 0.0 slice-done.2
  30.8 0.0 slice-done.3
  30.8 0.0 copy-done
  30.8 2.1 %merge_project_sibling.1 = (bf16[4,32,1024]{2,1,0:T(8,128)(2,1)S(1)}, bf16[32,1024]{1,0:T(8,128)(2,1)S(1)}) custom-call(s32[16]{0:T(128)S(1)} %copy-done, bf16[16,3,16,128]{3,2,1,0:T(8,128)(2,1)S(1)} %all_to_all.10.recv, f32[256,128]{1,0:T(8,128)S(1)} %get-tuple-element.21.vec, f32[2,256,128]{2,1,0:T(8,128)S(1)} %get-tuple-element.22.stat, ...), custom_call_target="tpu_custom_call" | custom-call | flops 268435456 | bytes 8388608 | tf_op jit(solution)/shard_map/merge_project_sibling/pallas_call | solution.py:323
  32.9 3.2 %collective-permute-start = (bf16[4,32,1024]{2,1,0:T(8,128)(2,1)S(1)}, bf16[4,32,1024]{2,1,0:T(8,128)(2,1)S(1)}, u32[]{:S(2)}, u32[]{:S(2)}) collective-permute-start(bf16[4,32,1024]{2,1,0:T(8,128)(2,1)S(1)} %get-tuple-element.24), channel_id=1, source_target_pairs={{0,1},{1,0},{2,3},{3,2},{4,5},{5,4},{6,7},{7,6},{8,9},{9,8},{10,11... | collective-permute-start | bytes 786440 | tf_op jit(solution)/shard_map/ppermute | solution.py:341
  36.1 1.3 %project_own.1 = bf16[4,32,1024]{2,1,0:T(8,128)(2,1)S(1)} custom-call(bf16[32,1024]{1,0:T(8,128)(2,1)S(1)} %get-tuple-element.23.heads, bf16[1024,8192]{1,0:T(8,128)(2,1)S(1)} %bitcast.16), custom_call_target="tpu_custom_call" | custom-call | flops 268435456 | bytes 8388608 | tf_op jit(solution)/shard_map/project_own/pallas_call | solution.py:342
  37.3 0.0 collective-permute-done
  37.4 0.1 fusion.3
  37.4 1.4 %collective-permute-start.1 = (bf16[32,1024]{1,0:T(8,128)(2,1)S(1)}, bf16[32,1024]{1,0:T(8,128)(2,1)S(1)}, u32[]{:S(2)}, u32[]{:S(2)}) collective-permute-start(bf16[32,1024]{1,0:T(8,128)(2,1)S(1)} %get-tuple-element.25), channel_id=1, source_target_pairs={{0,2},{1,3},{2,4},{3,5},{4,6},{5,7},{6,0},{7,1},{8,10},{9,11},{10,... | collective-permute-start | bytes 196616 | tf_op jit(solution)/shard_map/ppermute | solution.py:355
  38.8 1.5 %collective-permute-start.3 = (bf16[32,1024]{1,0:T(8,128)(2,1)S(1)}, bf16[32,1024]{1,0:T(8,128)(2,1)S(1)}, u32[]{:S(2)}, u32[]{:S(2)}) collective-permute-start(bf16[32,1024]{1,0:T(8,128)(2,1)S(1)} %get-tuple-element.26), channel_id=1, source_target_pairs={{0,6},{1,7},{2,0},{3,1},{4,2},{5,3},{6,4},{7,5},{8,14},{9,15},{10,... | collective-permute-start | bytes 196616 | tf_op jit(solution)/shard_map/ppermute | solution.py:355
  40.3 1.6 %collective-permute-start.2 = (bf16[32,1024]{1,0:T(8,128)(2,1)S(1)}, bf16[32,1024]{1,0:T(8,128)(2,1)S(1)}, u32[]{:S(2)}, u32[]{:S(2)}) collective-permute-start(bf16[32,1024]{1,0:T(8,128)(2,1)S(1)} %get-tuple-element.27), channel_id=1, source_target_pairs={{0,4},{1,5},{2,6},{3,7},{4,0},{5,1},{6,2},{7,3},{8,12},{9,13},{10,... | collective-permute-start | bytes 196616 | tf_op jit(solution)/shard_map/ppermute | solution.py:355
  41.9 0.4 collective-permute-done.1
  42.3 0.0 collective-permute-done.3
  42.3 2.7 %collective-permute-done.2 = bf16[32,1024]{1,0:T(8,128)(2,1)S(1)} collective-permute-done((bf16[32,1024]{1,0:T(8,128)(2,1)S(1)}, bf16[32,1024]{1,0:T(8,128)(2,1)S(1)}, u32[]{:S(2)}, u32[]{:S(2)}) %collective-permute-start.2) | collective-permute-done | bytes 65568 | tf_op jit(solution)/shard_map/ppermute | solution.py:355
  44.9 0.1 fusion.2
  45.0 0.7 %reshape.26 = bf16[16,2,1024]{2,1,0:T(2,128)(2,1)} reshape(bf16[32,1024]{1,0:T(8,128)(2,1)S(1)} %fusion.2) | data formatting | bytes 131072 | tf_op jit(solution)/shard_map/reshape | solution.py:356
  (1 shorter events, 0.0 us)
Async XLA Ops:
  0.0 10.3 %copy-start.1 = (bf16[16,2,8192]{2,1,0:T(2,128)(2,1)S(1)}, bf16[16,2,8192]{2,1,0:T(2,128)(2,1)}, u32[]{:S(2)}) copy-start(bf16[16,2,8192]{2,1,0:T(2,128)(2,1)} %param.9) | copy-start | bytes 1572868
  1.8 15.6 %all-to-all-start = ((bf16[16,3,16,128]{3,2,1,0:T(8,128)(2,1)}), bf16[16,3,16,128]{3,2,1,0:T(8,128)(2,1)S(1)}, u32[]{:S(2)}, u32[]{:S(2)}) async-start(bf16[16,3,16,128]{3,2,1,0:T(8,128)(2,1)} %get-tuple-element.15), calls=%async_computation | async-start | bytes 393216 | tf_op jit(solution)/shard_map/all_to_all | solution.py:253
  19.9 10.8 %slice-start = ((s8[16777216]{0:T(1024)(128)(4,1)}), s8[4194304]{0:T(1024)(128)(4,1)S(1)}, s32[]{:S(2)}) async-start(s8[16777216]{0:T(1024)(128)(4,1)} %bitcast.15), calls=%async_computation.2 | async-start | bytes 8388608
  20.0 10.8 %slice-start.1 = ((s8[16777216]{0:T(1024)(128)(4,1)}), s8[4194304]{0:T(1024)(128)(4,1)S(1)}, s32[]{:S(2)}) async-start(s8[16777216]{0:T(1024)(128)(4,1)} %bitcast.15), calls=%async_computation.3 | async-start | bytes 8388608
  20.0 10.8 %slice-start.2 = ((s8[16777216]{0:T(1024)(128)(4,1)}), s8[4194304]{0:T(1024)(128)(4,1)S(1)}, s32[]{:S(2)}) async-start(s8[16777216]{0:T(1024)(128)(4,1)} %bitcast.15), calls=%async_computation.4 | async-start | bytes 8388608
  20.0 10.8 %slice-start.3 = ((s8[16777216]{0:T(1024)(128)(4,1)}), s8[4194304]{0:T(1024)(128)(4,1)S(1)}, s32[]{:S(2)}) async-start(s8[16777216]{0:T(1024)(128)(4,1)} %bitcast.15), calls=%async_computation.5 | async-start | bytes 8388608
  20.0 10.8 %copy-start = (s32[16]{0:T(128)S(1)}, s32[16]{0:T(128)}, u32[]{:S(2)}) copy-start(s32[16]{0:T(128)} %anc.1) | copy-start | bytes 196
  32.9 4.4 %collective-permute-start = (bf16[4,32,1024]{2,1,0:T(8,128)(2,1)S(1)}, bf16[4,32,1024]{2,1,0:T(8,128)(2,1)S(1)}, u32[]{:S(2)}, u32[]{:S(2)}) collective-permute-start(bf16[4,32,1024]{2,1,0:T(8,128)(2,1)S(1)} %get-tuple-element.24), channel_id=1, source_target_pairs={{0,1},{1,0},{2,3},{3,2},{4,5},{5,4},{6,7},{7,6},{8,9},{9,8},{10,11... | collective-permute-start | bytes 786440 | tf_op jit(solution)/shard_map/ppermute | solution.py:341
  37.4 4.8 %collective-permute-start.1 = (bf16[32,1024]{1,0:T(8,128)(2,1)S(1)}, bf16[32,1024]{1,0:T(8,128)(2,1)S(1)}, u32[]{:S(2)}, u32[]{:S(2)}) collective-permute-start(bf16[32,1024]{1,0:T(8,128)(2,1)S(1)} %get-tuple-element.25), channel_id=1, source_target_pairs={{0,2},{1,3},{2,4},{3,5},{4,6},{5,7},{6,0},{7,1},{8,10},{9,11},{10,... | collective-permute-start | bytes 196616 | tf_op jit(solution)/shard_map/ppermute | solution.py:355
  38.8 3.5 %collective-permute-start.3 = (bf16[32,1024]{1,0:T(8,128)(2,1)S(1)}, bf16[32,1024]{1,0:T(8,128)(2,1)S(1)}, u32[]{:S(2)}, u32[]{:S(2)}) collective-permute-start(bf16[32,1024]{1,0:T(8,128)(2,1)S(1)} %get-tuple-element.26), channel_id=1, source_target_pairs={{0,6},{1,7},{2,0},{3,1},{4,2},{5,3},{6,4},{7,5},{8,14},{9,15},{10,... | collective-permute-start | bytes 196616 | tf_op jit(solution)/shard_map/ppermute | solution.py:355
  40.3 4.6 %collective-permute-start.2 = (bf16[32,1024]{1,0:T(8,128)(2,1)S(1)}, bf16[32,1024]{1,0:T(8,128)(2,1)S(1)}, u32[]{:S(2)}, u32[]{:S(2)}) collective-permute-start(bf16[32,1024]{1,0:T(8,128)(2,1)S(1)} %get-tuple-element.27), channel_id=1, source_target_pairs={{0,4},{1,5},{2,6},{3,7},{4,0},{5,1},{6,2},{7,3},{8,12},{9,13},{10,... | collective-permute-start | bytes 196616 | tf_op jit(solution)/shard_map/ppermute | solution.py:355

commit v5 on v4

--- a/solution.py
+++ b/solution.py
@@ -34,34 +34,36 @@
     return source, rank
 
 
-def pack_kernel(anc_hbm, qp_hbm, tables_hbm, send, queries, grid_ref, qp, tables, anc, count, spots, sems):
-    copies = [
-        pltpu.make_async_copy(src, dst, sems.at[i])
-        for i, (src, dst) in enumerate(((qp_hbm, qp), (tables_hbm, tables), (anc_hbm, anc)))
-    ]
+def pack_kernel(
+    anc_hbm, qp_hbm, tables_hbm, gain_hbm, send, queries, tables, gain, grid_ref, qp, anc, count, spots, sems
+):
+    pairs = ((anc_hbm, anc), (qp_hbm, qp), (tables_hbm, tables), (gain_hbm, gain))
+    copies = [pltpu.make_async_copy(src, dst, sems.at[i]) for i, (src, dst) in enumerate(pairs)]
     for copy in copies:
         copy.start()
     rows, steps, width = qp.shape
     _, per_row, head_dim = tables.shape
     devices = send.shape[0]
-    send[...] = jnp.zeros(send.shape, BF16)
-    for d in range(devices):
+
+    def clear(d, _):
+        send[d] = jnp.zeros(send.shape[1:], BF16)
         count[d] = 0
         for j in range(PAIR):
             spots[PAIR * d + j] = 0
+        return 0
+
+    lax.fori_loop(0, devices, clear, 0)
     for copy in copies:
         copy.wait()
     for h in range(width // head_dim):
         grid_ref[:, steps * h : steps * (h + 1), :] = qp[:, :, head_dim * h : head_dim * (h + 1)].astype(F32)
-    flat = grid_ref[...].reshape(rows * per_row, head_dim)
-    swapped = pltpu.roll(flat, head_dim // 2, 1)
-    shape = (rows, per_row, head_dim)
-    turned = flat.reshape(shape) * tables[0][None] + swapped.reshape(shape) * tables[1][None]
-    queries[...] = turned.astype(BF16)
     for r in range(rows):
         source, rank = slot_of(anc, r, rows, count)
         spots[source * PAIR + rank] = lax.rem(anc[r], rows)
-        send[source, rank] = queries[r]
+        plain = grid_ref[r]
+        turned = (plain * tables[0] + pltpu.roll(plain, head_dim // 2, 1) * tables[1]).astype(BF16)
+        queries[r] = turned
+        send[source, rank] = turned
     lane = lax.broadcasted_iota(jnp.int32, (per_row, head_dim), 1)
     for d in range(devices):
         send[d, PAIR] = jnp.where(
@@ -69,77 +71,49 @@
         ).astype(BF16)
 
 
-def fresh_kernel(
-    x, gain_hbm, wk_hbm, wv_hbm, queries, tables_hbm, kv_hbm, vec, stat, old, wk, wv, gain, tables, sems
+def attend_kernel(
+    recv, kv, x, gain, wk, wv, queries, tables, vectors, tops, sums, vec, stat, *scratch
 ):
-    copies = [
-        pltpu.make_async_copy(src, dst, sems.at[i])
-        for i, (src, dst) in enumerate(
-            ((gain_hbm, gain), (tables_hbm, tables), (wk_hbm, wk), (wv_hbm, wv), (kv_hbm.at[:, 0, :, : wk.shape[1]], old))
-        )
-    ]
-    for copy in copies:
-        copy.start()
-    tokens = x.shape[0]
-    rows, per_row, head_dim = queries.shape
-    steps = tokens // rows
-    floats = x[...].astype(F32)
-    inverse = lax.rsqrt(jnp.mean(floats * floats, -1, keepdims=True) + EPSILON)
-    copies[0].wait()
-    normed = (floats * inverse * gain[...]).astype(BF16)
-    for copy in copies[1:3]:
-        copy.wait()
-    repeat = tokens // per_row
-    cosine, sine = (jnp.concatenate([tables[i]] * repeat, 0) for i in range(2))
-    keys = jnp.dot(normed, wk[...], preferred_element_type=F32)
-    keys = (keys * cosine + pltpu.roll(keys, head_dim // 2, 1) * sine).astype(BF16)
-    copies[3].wait()
-    vals = jnp.dot(normed, wv[...], preferred_element_type=F32).astype(BF16)
-    flat = queries[...].reshape(rows * per_row, head_dim)
-    scores = lax.dot_general(flat, keys, NT, preferred_element_type=F32) * head_dim ** (-0.5)
-    row = lax.broadcasted_iota(jnp.int32, scores.shape, 0)
-    col = lax.broadcasted_iota(jnp.int32, scores.shape, 1)
-    seen = (lax.div(row, per_row) == lax.div(col, steps)) & (lax.rem(col, steps) <= lax.rem(row, steps))
-    top = jnp.max(jnp.where(seen, scores, -jnp.inf), -1, keepdims=True)
-    expo = jnp.where(seen, jnp.exp(jnp.where(seen, scores - top, 0.0)), 0.0)
-    vec[...] = jnp.dot(expo.astype(BF16), vals, preferred_element_type=F32)
-    stat[0] = jnp.broadcast_to(top, stat.shape[1:])
-    stat[1] = jnp.broadcast_to(jnp.sum(expo, -1, keepdims=True), stat.shape[1:])
-    copies[4].wait()
-
-
-def cache_kernel(recv, keys, kv_hbm, vectors, tops, sums, scores, expos, values, spots, sem):
+    scores, expos, normed = scratch
     devices, _, per_row, head_dim = recv.shape
     lane = lax.broadcasted_iota(jnp.int32, (per_row, head_dim), 1)
-    copy = pltpu.make_async_copy(kv_hbm.at[:, 0, :, head_dim:], values, sem)
-    copy.start()
-    half = devices // 2
-
-    def score(part, _):
-        chosen = []
-        for k in range(half):
-            spot = recv[part * half + k, PAIR].astype(F32)
-            for j in range(PAIR):
-                chosen.append(spot[0, j * (head_dim // PAIR)].astype(jnp.int32))
-                spots[(part * half + k) * PAIR + j] = chosen[-1]
-        for k in range(half):
-            for j in range(PAIR):
-                d = part * half + k
-                scores[d * PAIR + j] = lax.dot_general(
-                    recv[d, j], keys[chosen[k * PAIR + j]], NT, preferred_element_type=F32
-                ) * head_dim ** (-0.5)
-        return 0
-
-    lax.fori_loop(0, 2, score, 0)
+    spots = []
+    for d in range(devices):
+        spot = recv[d, PAIR].astype(F32)
+        for j in range(PAIR):
+            spots.append(spot[0, j * (head_dim // PAIR)].astype(jnp.int32))
+    for i in range(devices * PAIR):
+        scores[i] = lax.dot_general(
+            recv[i // PAIR, i % PAIR], kv[spots[i], 0, :, :head_dim], NT, preferred_element_type=F32
+        ) * head_dim ** (-0.5)
     for i in range(devices * PAIR):
         top = jnp.max(scores[i], -1, keepdims=True)
         expo = jnp.exp(scores[i] - top)
         expos[i] = expo.astype(BF16)
         tops[i] = jnp.broadcast_to(top, lane.shape)
         sums[i] = jnp.broadcast_to(jnp.sum(expo, -1, keepdims=True), lane.shape)
-    copy.wait()
     for i in range(devices * PAIR):
-        vectors[i] = jnp.dot(expos[i], values[spots[i]], preferred_element_type=F32)
+        vectors[i] = jnp.dot(expos[i], kv[spots[i], 0, :, head_dim:], preferred_element_type=F32)
+    rows, steps, width = x.shape
+    tokens = rows * steps
+    floats = x[...].reshape(tokens, width).astype(F32)
+    inverse = lax.rsqrt(jnp.mean(floats * floats, -1, keepdims=True) + EPSILON)
+    normed[...] = (floats * inverse * gain[...]).astype(BF16)
+    repeat = tokens // per_row
+    cosine, sine = (jnp.concatenate([tables[i]] * repeat, 0) for i in range(2))
+    keys = jnp.dot(normed[...], wk[...], preferred_element_type=F32)
+    keys = (keys * cosine + pltpu.roll(keys, head_dim // 2, 1) * sine).astype(BF16)
+    vals = jnp.dot(normed[...], wv[...], preferred_element_type=F32).astype(BF16)
+    flat = queries[...].reshape(rows * per_row, head_dim)
+    fresh = lax.dot_general(flat, keys, NT, preferred_element_type=F32) * head_dim ** (-0.5)
+    row = lax.broadcasted_iota(jnp.int32, fresh.shape, 0)
+    col = lax.broadcasted_iota(jnp.int32, fresh.shape, 1)
+    seen = (lax.div(row, per_row) == lax.div(col, steps)) & (lax.rem(col, steps) <= lax.rem(row, steps))
+    top = jnp.max(jnp.where(seen, fresh, -jnp.inf), -1, keepdims=True)
+    expo = jnp.where(seen, jnp.exp(jnp.where(seen, fresh - top, 0.0)), 0.0)
+    vec[...] = jnp.dot(expo.astype(BF16), vals, preferred_element_type=F32)
+    stat[0] = jnp.broadcast_to(top, stat.shape[1:])
+    stat[1] = jnp.broadcast_to(jnp.sum(expo, -1, keepdims=True), stat.shape[1:])
 
 
 def return_kernel(vectors, tops, sums, back):
@@ -225,84 +199,65 @@
     vmem = pl.BlockSpec(memory_space=pltpu.VMEM)
     stay = pl.BlockSpec(memory_space=pl.ANY)
     hbm = lambda x: pltpu.with_memory_space_constraint(x, pltpu.HBM)
-    tables = hbm(jnp.asarray(tables))
+    tables = jnp.asarray(tables)
 
     packed = (devices, PAIR + 1, per_row, head_dim)
-    send, queries = pl.pallas_call(
+    send, queries, tables, gain = pl.pallas_call(
         pack_kernel,
         out_shape=(
             jax.ShapeDtypeStruct(packed, BF16),
             jax.ShapeDtypeStruct((rows, per_row, head_dim), BF16),
+            jax.ShapeDtypeStruct((2, per_row, head_dim), F32),
+            jax.ShapeDtypeStruct((1, width), F32),
         ),
-        in_specs=[stay] * 3,
-        out_specs=(vmem, vmem),
+        in_specs=[stay] * 4,
+        out_specs=(vmem,) * 4,
         scratch_shapes=[
             pltpu.VMEM((rows, per_row, head_dim), F32),
             pltpu.VMEM((rows, steps, local), BF16),
-            pltpu.VMEM((2, per_row, head_dim), F32),
             pltpu.SMEM((rows,), jnp.int32),
             pltpu.SMEM((devices,), jnp.int32),
             pltpu.SMEM((devices * PAIR,), jnp.int32),
-            pltpu.SemaphoreType.DMA((3,)),
+            pltpu.SemaphoreType.DMA((4,)),
         ],
         compiler_params=pltpu.CompilerParams(vmem_limit_bytes=4 * MIB),
         cost_estimate=pl.CostEstimate(flops=10_000_000_000, bytes_accessed=MIB, transcendentals=0),
         name="pack_queries",
-    )(hbm(ancestors), hbm(query_proj), tables)
+    )(hbm(ancestors), hbm(query_proj), hbm(tables), hbm(norm_gain.reshape(1, width)))
 
     recv = lax.all_to_all(send, "particle", split_axis=0, concat_axis=0, tiled=True)
 
-    vec, stat, cached_keys = pl.pallas_call(
-        fresh_kernel,
-        out_shape=(
+    slots = devices * PAIR
+    partial_result = jax.ShapeDtypeStruct((slots, per_row, head_dim), F32)
+    *found, vec, stat = pl.pallas_call(
+        attend_kernel,
+        out_shape=(partial_result,) * 3
+        + (
             jax.ShapeDtypeStruct((rows * per_row, head_dim), F32),
             jax.ShapeDtypeStruct((2, rows * per_row, head_dim), F32),
-            pltpu.VMEM((rows, context, head_dim), BF16),
         ),
-        in_specs=[vmem, stay, stay, stay, vmem, stay, stay],
-        out_specs=(vmem, vmem, vmem),
-        scratch_shapes=[
-            pltpu.VMEM((width, head_dim), BF16),
-            pltpu.VMEM((width, head_dim), BF16),
-            pltpu.VMEM((1, width), F32),
-            pltpu.VMEM((2, per_row, head_dim), F32),
-            pltpu.SemaphoreType.DMA((5,)),
-        ],
-        compiler_params=pltpu.CompilerParams(vmem_limit_bytes=16 * MIB),
-        cost_estimate=pl.CostEstimate(
-            flops=4_000_000_000, bytes_accessed=5 * MIB, transcendentals=0
-        ),
-        name="new_tokens",
-    )(
-        inputs.reshape(rows * steps, width),
-        hbm(norm_gain.reshape(1, width)),
-        hbm(w_key),
-        hbm(w_value),
-        queries,
-        tables,
-        hbm(kv_cache),
-    )
-
-    slots = devices * PAIR
-    partial_result = jax.ShapeDtypeStruct((slots, per_row, head_dim), F32)
-    found = pl.pallas_call(
-        cache_kernel,
-        out_shape=(partial_result,) * 3,
-        in_specs=[vmem, vmem, stay],
-        out_specs=(vmem,) * 3,
+        in_specs=[vmem] * 8,
+        out_specs=(vmem,) * 5,
         scratch_shapes=[
             pltpu.VMEM((slots, per_row, context), F32),
             pltpu.VMEM((slots, per_row, context), BF16),
-            pltpu.VMEM((rows, context, head_dim), BF16),
-            pltpu.SMEM((slots,), jnp.int32),
-            pltpu.SemaphoreType.DMA(()),
+            pltpu.VMEM((rows * steps, width), BF16),
         ],
-        compiler_params=pltpu.CompilerParams(vmem_limit_bytes=8 * MIB),
+        compiler_params=pltpu.CompilerParams(vmem_limit_bytes=12 * MIB),
         cost_estimate=pl.CostEstimate(
             flops=4 * slots * per_row * context * head_dim, bytes_accessed=5 * MIB, transcendentals=0
         ),
-        name="cache_attention",
-    )(recv, cached_keys, hbm(kv_cache))
+        name="attention",
+    )(
+        recv,
+        kv_cache,
+        inputs,
+        gain,
+        w_key,
+        w_value,
+        queries,
+        tables,
+    )
     back = pl.pallas_call(
         return_kernel,
         out_shape=jax.ShapeDtypeStruct(packed, BF16),

time: 46.3 us -> 46 us (level)
  blocking collectives: 10.6 us -> 26.3 us
  starting transfers between devices: 16.1 us -> 7.65 us
  waiting for transfers between devices: 6.89 us -> 3.06 us
  Pallas kernels: 10.9 us -> 7.55 us
    all_to_all x0 -> x1, blocking collectives: none -> 15.6 us  [shards(): lax.all_to_all(send, 'particle', split_axis=0, concat_axis=0, tiled=True)]
    all_to_all x1 -> x0, starting transfers between devices: 8.44 us -> none  [shards(): lax.all_to_all(send, 'particle', split_axis=0, concat_axis=0, tiled=True)]
    all_to_all x1 -> x0, waiting for transfers between devices: 3.83 us -> none  [shards(): lax.all_to_all(send, 'particle', split_axis=0, concat_axis=0, tiled=True)]
    pallas_call x2 -> x1, Pallas kernels: 5.62 us -> 2.88 us  [shards(): pl.pallas_call(attend_kernel, out_shape=(partial_result,) * 3 + (jax.Shap...]
    pallas_call x1, Pallas kernels: 1.8 us -> 1.2 us  [shards(): pl.pallas_call(pack_kernel, out_shape=(jax.ShapeDtypeStruct(packed, BF16)...]
  transfers between devices with their start and end apart: 5 -> 4, of which waited for: 3 -> 2; matrix products, arithmetic and copies ran while one was open for 0% -> 0% of each run, Pallas kernels for 10% -> 3%
where the time goes in v5:
time: 46 us; the launch traced here: 45.5 us
  blocking collectives  26.3 us (57%)
  starting transfers between devices  7.65 us (17%)
  Pallas kernels  7.55 us (16%)
  waiting for transfers between devices  3.06 us (7%)
  local copies, waits for them, and re-layouts  0.7 us (2%)
    all_to_all x1, blocking collectives, shards(): lax.all_to_all(send, 'particle', split_axis=0, concat_axis=0, tiled=True)  15.6 us
    all_to_all x1, blocking collectives, shards(): lax.all_to_all(back, 'particle', split_axis=0, concat_axis=0, tiled=True)  10.6 us
    ppermute x3, starting transfers between devices, shards(): lax.ppermute(pair[k].astype(BF16), 'tensor', ring).astype(F32)  4.46 us
    ppermute x1, starting transfers between devices, shards(): given = lax.ppermute(other, 'tensor', [(i, i ^ 1) for i in range(tensor)])  3.19 us
    ppermute x3, waiting for transfers between devices, shards(): lax.ppermute(pair[k].astype(BF16), 'tensor', ring).astype(F32)  3.06 us
    pallas_call x1, Pallas kernels, shards(): pl.pallas_call(attend_kernel, out_shape=(partial_result,) * 3 + (jax.Shap...  2.88 us
    pallas_call x1, Pallas kernels, shards(): pl.pallas_call(merge_kernel, out_shape=(jax.ShapeDtypeStruct(block, BF16)...  2.06 us
    pallas_call x1, Pallas kernels, shards(): pl.pallas_call(second_kernel, out_shape=jax.ShapeDtypeStruct(block, BF16)...  1.26 us
  transfers between devices with their start and end apart: 4, of which 2 were waited for; matrix products, arithmetic and copies ran while one was open for 0% of the time, Pallas kernels for 3%

profile of v5, /device:TPU:1, one launch (start us, length us, event | category | flops | bytes accessed | tf_op | source)
XLA Modules:
  0.0 45.5 jit_solution(15180641034496790919)
XLA Ops:
  0.0 0.0 copy-start
  0.0 0.0 copy-start.1
  0.0 0.0 copy-start.2
  0.0 0.0 copy-start.3
  0.0 1.2 %pack_queries.1 = (bf16[16,3,16,128]{3,2,1,0:T(8,128)(2,1)S(1)}, bf16[16,16,128]{2,1,0:T(8,128)(2,1)S(1)}, f32[2,16,128]{2,1,0:T(8,128)S(1)}, f32[1,8192]{1,0:T(1,128)S(1)}) custom-call(s32[16]{0:T(128)} %anc.1, bf16[16,2,1024]{2,1,0:T(2,128)(2,1)} %qp_hbm.1, f32[2,16,128]{2,1,0:T(8,128)} %constant.2.clone.tables_hbm, f32[1,8192]{1,0:T(1,128)} %bitcast.17), custom_call_target="tpu_custom_call" | custom-call | flops 10000000000 | bytes 1048576 | tf_op jit(solution)/shard_map/pack_queries/pallas_call | solution.py:205
  1.2 15.6 %all_to_all.10.recv = bf16[16,3,16,128]{3,2,1,0:T(8,128)(2,1)S(1)} all-to-all(bf16[16,3,16,128]{3,2,1,0:T(8,128)(2,1)S(1)} %get-tuple-element.16), channel_id=1, replica_groups=mesh['particle'=16,'tensor'=8] {'particle'}, dimensions={0} | all-to-all | bytes 393216 | tf_op jit(solution)/shard_map/all_to_all | solution.py:228
  16.9 0.0 copy-done
  16.9 0.0 copy-done.1
  16.9 0.0 copy-done.2
  16.9 0.0 copy-done.3
  16.9 2.9 %attention.1 = (f32[32,16,128]{2,1,0:T(8,128)S(1)}, f32[32,16,128]{2,1,0:T(8,128)S(1)}, f32[32,16,128]{2,1,0:T(8,128)S(1)}, f32[256,128]{1,0:T(8,128)S(1)}, f32[2,256,128]{2,1,0:T(8,128)S(1)}) custom-call(bf16[16,3,16,128]{3,2,1,0:T(8,128)(2,1)S(1)} %all_to_all.10.recv, bf16[16,1,512,256]{3,2,1,0:T(8,128)(2,1)S(1)} %copy-done, ...), custom_call_target="tpu_custom_call" | custom-call | flops 134217728 | bytes 5242880 | tf_op jit(solution)/shard_map/attention/pallas_call | solution.py:232
  19.8 0.0 slice-start
  19.8 0.0 slice-start.1
  19.8 0.0 slice-start.2
  19.8 0.0 slice-start.3
  19.8 0.0 copy-start.4
  19.8 0.1 pack_results.1
  20.0 10.6 %all_to_all.11.recv = bf16[16,3,16,128]{3,2,1,0:T(8,128)(2,1)S(1)} all-to-all(bf16[16,3,16,128]{3,2,1,0:T(8,128)(2,1)S(1)} %pack_results.1), channel_id=1, replica_groups=mesh['particle'=16,'tensor'=8] {'particle'}, dimensions={0} | all-to-all | bytes 393216 | tf_op jit(solution)/shard_map/all_to_all | solution.py:270
  30.6 0.0 slice-done
  30.6 0.0 slice-done.1
  30.6 0.0 slice-done.2
  30.6 0.0 slice-done.3
  30.6 0.0 copy-done.4
  30.6 2.1 %merge_project_sibling.1 = (bf16[4,32,1024]{2,1,0:T(8,128)(2,1)S(1)}, bf16[32,1024]{1,0:T(8,128)(2,1)S(1)}) custom-call(s32[16]{0:T(128)S(1)} %copy-done.4, bf16[16,3,16,128]{3,2,1,0:T(8,128)(2,1)S(1)} %all_to_all.11.recv, f32[256,128]{1,0:T(8,128)S(1)} %get-tuple-element.23.vec, f32[2,256,128]{2,1,0:T(8,128)S(1)} %get-tuple-element.24.stat, ...), custom_call_target="tpu_custom_call" | custom-call | flops 268435456 | bytes 8388608 | tf_op jit(solution)/shard_map/merge_project_sibling/pallas_call | solution.py:278
  32.7 3.2 %collective-permute-start = (bf16[4,32,1024]{2,1,0:T(8,128)(2,1)S(1)}, bf16[4,32,1024]{2,1,0:T(8,128)(2,1)S(1)}, u32[]{:S(2)}, u32[]{:S(2)}) collective-permute-start(bf16[4,32,1024]{2,1,0:T(8,128)(2,1)S(1)} %get-tuple-element.26), channel_id=1, source_target_pairs={{0,1},{1,0},{2,3},{3,2},{4,5},{5,4},{6,7},{7,6},{8,9},{9,8},{10,11... | collective-permute-start | bytes 786440 | tf_op jit(solution)/shard_map/ppermute | solution.py:296
  35.9 1.3 %project_own.1 = bf16[4,32,1024]{2,1,0:T(8,128)(2,1)S(1)} custom-call(bf16[32,1024]{1,0:T(8,128)(2,1)S(1)} %get-tuple-element.25.heads, bf16[1024,8192]{1,0:T(8,128)(2,1)S(1)} %bitcast.16), custom_call_target="tpu_custom_call" | custom-call | flops 268435456 | bytes 8388608 | tf_op jit(solution)/shard_map/project_own/pallas_call | solution.py:297
  37.2 0.0 collective-permute-done
  37.2 0.1 fusion.3
  37.2 1.4 %collective-permute-start.1 = (bf16[32,1024]{1,0:T(8,128)(2,1)S(1)}, bf16[32,1024]{1,0:T(8,128)(2,1)S(1)}, u32[]{:S(2)}, u32[]{:S(2)}) collective-permute-start(bf16[32,1024]{1,0:T(8,128)(2,1)S(1)} %get-tuple-element.27), channel_id=1, source_target_pairs={{0,2},{1,3},{2,4},{3,5},{4,6},{5,7},{6,0},{7,1},{8,10},{9,11},{10,... | collective-permute-start | bytes 196616 | tf_op jit(solution)/shard_map/ppermute | solution.py:310
  38.6 1.5 %collective-permute-start.3 = (bf16[32,1024]{1,0:T(8,128)(2,1)S(1)}, bf16[32,1024]{1,0:T(8,128)(2,1)S(1)}, u32[]{:S(2)}, u32[]{:S(2)}) collective-permute-start(bf16[32,1024]{1,0:T(8,128)(2,1)S(1)} %get-tuple-element.28), channel_id=1, source_target_pairs={{0,6},{1,7},{2,0},{3,1},{4,2},{5,3},{6,4},{7,5},{8,14},{9,15},{10,... | collective-permute-start | bytes 196616 | tf_op jit(solution)/shard_map/ppermute | solution.py:310
  40.1 1.6 %collective-permute-start.2 = (bf16[32,1024]{1,0:T(8,128)(2,1)S(1)}, bf16[32,1024]{1,0:T(8,128)(2,1)S(1)}, u32[]{:S(2)}, u32[]{:S(2)}) collective-permute-start(bf16[32,1024]{1,0:T(8,128)(2,1)S(1)} %get-tuple-element.29), channel_id=1, source_target_pairs={{0,4},{1,5},{2,6},{3,7},{4,0},{5,1},{6,2},{7,3},{8,12},{9,13},{10,... | collective-permute-start | bytes 196616 | tf_op jit(solution)/shard_map/ppermute | solution.py:310
  41.7 0.4 collective-permute-done.1
  42.1 0.0 collective-permute-done.3
  42.1 2.6 %collective-permute-done.2 = bf16[32,1024]{1,0:T(8,128)(2,1)S(1)} collective-permute-done((bf16[32,1024]{1,0:T(8,128)(2,1)S(1)}, bf16[32,1024]{1,0:T(8,128)(2,1)S(1)}, u32[]{:S(2)}, u32[]{:S(2)}) %collective-permute-start.2) | collective-permute-done | bytes 65568 | tf_op jit(solution)/shard_map/ppermute | solution.py:310
  44.8 0.1 fusion.2
  44.8 0.7 %reshape.22 = bf16[16,2,1024]{2,1,0:T(2,128)(2,1)} reshape(bf16[32,1024]{1,0:T(8,128)(2,1)S(1)} %fusion.2) | data formatting | bytes 131072 | tf_op jit(solution)/shard_map/reshape | solution.py:311
  (1 shorter events, 0.0 us)
Async XLA Ops:
  0.0 16.9 %copy-start = (bf16[16,1,512,256]{3,2,1,0:T(8,128)(2,1)S(1)}, bf16[16,1,512,256]{3,2,1,0:T(8,128)(2,1)}, u32[]{:S(2)}) copy-start(bf16[16,1,512,256]{3,2,1,0:T(8,128)(2,1)} %kv.1) | copy-start | bytes 12582916
  0.0 16.9 %copy-start.1 = (bf16[8192,128]{1,0:T(8,128)(2,1)S(1)}, bf16[8192,128]{1,0:T(8,128)(2,1)}, u32[]{:S(2)}) copy-start(bf16[8192,128]{1,0:T(8,128)(2,1)} %wk.1) | copy-start | bytes 6291460
  0.0 16.9 %copy-start.2 = (bf16[8192,128]{1,0:T(8,128)(2,1)S(1)}, bf16[8192,128]{1,0:T(8,128)(2,1)}, u32[]{:S(2)}) copy-start(bf16[8192,128]{1,0:T(8,128)(2,1)} %wv.1) | copy-start | bytes 6291460
  0.0 16.9 %copy-start.3 = (bf16[16,2,8192]{2,1,0:T(2,128)(2,1)S(1)}, bf16[16,2,8192]{2,1,0:T(2,128)(2,1)}, u32[]{:S(2)}) copy-start(bf16[16,2,8192]{2,1,0:T(2,128)(2,1)} %x.1) | copy-start | bytes 1572868
  19.8 10.8 %slice-start = ((s8[16777216]{0:T(1024)(128)(4,1)}), s8[4194304]{0:T(1024)(128)(4,1)S(1)}, s32[]{:S(2)}) async-start(s8[16777216]{0:T(1024)(128)(4,1)} %bitcast.15), calls=%async_computation.2 | async-start | bytes 8388608
  19.8 10.8 %slice-start.1 = ((s8[16777216]{0:T(1024)(128)(4,1)}), s8[4194304]{0:T(1024)(128)(4,1)S(1)}, s32[]{:S(2)}) async-start(s8[16777216]{0:T(1024)(128)(4,1)} %bitcast.15), calls=%async_computation.3 | async-start | bytes 8388608
  19.8 10.8 %slice-start.2 = ((s8[16777216]{0:T(1024)(128)(4,1)}), s8[4194304]{0:T(1024)(128)(4,1)S(1)}, s32[]{:S(2)}) async-start(s8[16777216]{0:T(1024)(128)(4,1)} %bitcast.15), calls=%async_computation.4 | async-start | bytes 8388608
  19.8 10.8 %slice-start.3 = ((s8[16777216]{0:T(1024)(128)(4,1)}), s8[4194304]{0:T(1024)(128)(4,1)S(1)}, s32[]{:S(2)}) async-start(s8[16777216]{0:T(1024)(128)(4,1)} %bitcast.15), calls=%async_computation.5 | async-start | bytes 8388608
  19.8 10.8 %copy-start.4 = (s32[16]{0:T(128)S(1)}, s32[16]{0:T(128)}, u32[]{:S(2)}) copy-start(s32[16]{0:T(128)} %anc.1) | copy-start | bytes 196
  32.7 4.5 %collective-permute-start = (bf16[4,32,1024]{2,1,0:T(8,128)(2,1)S(1)}, bf16[4,32,1024]{2,1,0:T(8,128)(2,1)S(1)}, u32[]{:S(2)}, u32[]{:S(2)}) collective-permute-start(bf16[4,32,1024]{2,1,0:T(8,128)(2,1)S(1)} %get-tuple-element.26), channel_id=1, source_target_pairs={{0,1},{1,0},{2,3},{3,2},{4,5},{5,4},{6,7},{7,6},{8,9},{9,8},{10,11... | collective-permute-start | bytes 786440 | tf_op jit(solution)/shard_map/ppermute | solution.py:296
  37.2 4.9 %collective-permute-start.1 = (bf16[32,1024]{1,0:T(8,128)(2,1)S(1)}, bf16[32,1024]{1,0:T(8,128)(2,1)S(1)}, u32[]{:S(2)}, u32[]{:S(2)}) collective-permute-start(bf16[32,1024]{1,0:T(8,128)(2,1)S(1)} %get-tuple-element.27), channel_id=1, source_target_pairs={{0,2},{1,3},{2,4},{3,5},{4,6},{5,7},{6,0},{7,1},{8,10},{9,11},{10,... | collective-permute-start | bytes 196616 | tf_op jit(solution)/shard_map/ppermute | solution.py:310
  38.6 3.5 %collective-permute-start.3 = (bf16[32,1024]{1,0:T(8,128)(2,1)S(1)}, bf16[32,1024]{1,0:T(8,128)(2,1)S(1)}, u32[]{:S(2)}, u32[]{:S(2)}) collective-permute-start(bf16[32,1024]{1,0:T(8,128)(2,1)S(1)} %get-tuple-element.28), channel_id=1, source_target_pairs={{0,6},{1,7},{2,0},{3,1},{4,2},{5,3},{6,4},{7,5},{8,14},{9,15},{10,... | collective-permute-start | bytes 196616 | tf_op jit(solution)/shard_map/ppermute | solution.py:310
  40.1 4.6 %collective-permute-start.2 = (bf16[32,1024]{1,0:T(8,128)(2,1)S(1)}, bf16[32,1024]{1,0:T(8,128)(2,1)S(1)}, u32[]{:S(2)}, u32[]{:S(2)}) collective-permute-start(bf16[32,1024]{1,0:T(8,128)(2,1)S(1)} %get-tuple-element.29), channel_id=1, source_target_pairs={{0,4},{1,5},{2,6},{3,7},{4,0},{5,1},{6,2},{7,3},{8,12},{9,13},{10,... | collective-permute-start | bytes 196616 | tf_op jit(solution)/shard_map/ppermute | solution.py:310

commit v6 on v0

v6 whole, which is shorter than its diff:
```python
import functools

import jax
import jax.numpy as jnp
import numpy as np
from jax import lax
from jax.experimental import pallas as pl
from jax.experimental.pallas import tpu as pltpu
from jax.sharding import PartitionSpec as P

PAIR = 2
THETA = 500000.0
EPSILON = 1e-05
F32 = jnp.float32
BF16 = jnp.bfloat16
MIB = 1 << 20
NT = (((1,), (1,)), ((), ()))


def rotary_tables(context, steps, head_dim):
    half = head_dim // 2
    freqs = np.float32(THETA) ** (-np.arange(half, dtype=np.float32) * np.float32(2.0) / np.float32(head_dim))
    position = (np.float32(context) + np.arange(steps, dtype=np.float32)).reshape(steps, 1)
    angles = (position * freqs.astype(np.float32)).astype(np.float32)
    cosine, sine = np.cos(angles), np.sin(angles)
    return (
        np.concatenate([cosine, cosine], 1).astype(np.float32),
        np.concatenate([-sine, sine], 1).astype(np.float32),
    )


def slot_of(anc, row, rows, count):
    source = lax.div(anc[row], rows)
    rank = count[source]
    count[source] = rank + 1
    return source, rank


def prepare_kernel(*refs):
    sources, (queries, blocks), scratch = refs[:7], refs[7:9], refs[9:]
    anc, qp, tables, gain, x, wk, wv, grid_ref, normed, fresh, sems = scratch
    targets = (anc, qp, tables, gain, x, wk, wv)
    copies = [pltpu.make_async_copy(src, dst, sems.at[i]) for i, (src, dst) in enumerate(zip(sources, targets))]
    for copy in copies:
        copy.start()
    rows, steps, local = qp.shape
    width = x.shape[2]
    tokens = rows * steps
    _, per_row, head_dim = tables.shape
    for copy in copies[:5]:
        copy.wait()
    for h in range(local // head_dim):
        grid_ref[:, steps * h : steps * (h + 1), :] = qp[:, :, head_dim * h : head_dim * (h + 1)].astype(F32)
    for r in range(rows):
        plain = grid_ref[r]
        queries[r] = (plain * tables[0] + pltpu.roll(plain, head_dim // 2, 1) * tables[1]).astype(BF16)
    floats = x[...].reshape(tokens, width).astype(F32)
    inverse = lax.rsqrt(jnp.mean(floats * floats, -1, keepdims=True) + EPSILON)
    normed[...] = (floats * inverse * gain[...]).astype(BF16)
    repeat = tokens // per_row
    cosine, sine = (jnp.concatenate([tables[i]] * repeat, 0) for i in range(2))
    copies[5].wait()
    keys = jnp.dot(normed[...], wk[...], preferred_element_type=F32)
    fresh[0] = (keys * cosine + pltpu.roll(keys, head_dim // 2, 1) * sine).astype(BF16).astype(F32)
    copies[6].wait()
    fresh[1] = jnp.dot(normed[...], wv[...], preferred_element_type=F32).astype(BF16).astype(F32)
    for r in range(rows):
        blocks[r, 0:steps] = fresh[0, steps * r : steps * (r + 1)]
        blocks[r, steps : 2 * steps] = fresh[1, steps * r : steps * (r + 1)]
        blocks[r, 2 * steps :] = jnp.full(
            (blocks.shape[1] - 2 * steps, head_dim), lax.rem(anc[r], rows).astype(F32), F32
        )


def send_kernel(anc, queries, blocks, send, tiles, count):
    rows = queries.shape[0]
    devices = send.shape[0]
    eight = blocks.shape[1]
    send[...] = jnp.zeros(send.shape, BF16)
    tiles[...] = jnp.zeros(tiles.shape, F32)
    for d in range(devices):
        count[d] = 0
    for r in range(rows):
        source, rank = slot_of(anc, r, rows, count)
        send[source, rank] = queries[r]
        tiles[source, pl.ds(pl.multiple_of(rank * eight, eight), eight), :] = blocks[r]
    for d in range(devices):
        send[d, PAIR] = tiles[d].astype(BF16)


def attend_kernel(recv, kv, heads, scores, expos, tops, sums, vectors, extra, lined):
    devices, _, per_row, head_dim = recv.shape
    slots = devices * PAIR
    steps = heads.shape[0] // slots
    eight = per_row // PAIR
    spots = []
    for d in range(devices):
        tile = recv[d, PAIR].astype(F32)
        extra[pl.ds(d * per_row, per_row), :] = tile
        for j in range(PAIR):
            spots.append(tile[j * eight + 2 * steps, 0].astype(jnp.int32))
    for i in range(slots):
        scores[i] = lax.dot_general(
            recv[i // PAIR, i % PAIR], kv[spots[i], 0, :, :head_dim], NT, preferred_element_type=F32
        ) * head_dim ** (-0.5)
    for i in range(slots):
        top = jnp.max(scores[i], -1, keepdims=True)
        expo = jnp.exp(scores[i] - top)
        expos[i] = expo.astype(BF16)
        at = pl.ds(i * per_row, per_row)
        tops[at, :] = jnp.broadcast_to(top, (per_row, head_dim))
        sums[at, :] = jnp.broadcast_to(jnp.sum(expo, -1, keepdims=True), (per_row, head_dim))
    for i in range(slots):
        vectors[pl.ds(i * per_row, per_row), :] = jnp.dot(
            expos[i], kv[spots[i], 0, :, head_dim:], preferred_element_type=F32
        )
    count = devices * per_row
    extra[count:, :] = jnp.zeros((extra.shape[0] - count, head_dim), F32)
    asked = jnp.concatenate([recv[i // PAIR, i % PAIR] for i in range(slots)], 0)
    fresh = lax.dot_general(
        asked, extra[:count, :].astype(BF16), NT, preferred_element_type=F32
    ) * head_dim ** (-0.5)
    row = lax.broadcasted_iota(jnp.int32, fresh.shape, 0)
    col = lax.broadcasted_iota(jnp.int32, fresh.shape, 1)
    ahead = lax.rem(row, steps) - (col - lax.div(row, per_row) * eight)
    seen = (ahead >= 0) & (ahead <= lax.rem(row, steps))
    top_f = jnp.max(jnp.where(seen, fresh, -jnp.inf), -1, keepdims=True)
    expo = jnp.where(seen, jnp.exp(jnp.where(seen, fresh - top_f, 0.0)), 0.0)
    sum_f = jnp.sum(expo, -1, keepdims=True)
    vec_f = jnp.dot(expo.astype(BF16), extra[steps : count + steps, :].astype(BF16), preferred_element_type=F32)
    top_c = tops[...]
    top = jnp.maximum(top_c, top_f)
    factor_c = jnp.exp(top_c - top)
    factor_f = jnp.exp(top_f - top)
    vectors[...] = (vectors[...] * factor_c + vec_f * factor_f) / (sums[...] * factor_c + sum_f * factor_f)
    for h in range(per_row // steps):
        for s in range(steps):
            lined[h, pl.ds(s, slots, stride=steps), :] = vectors[pl.ds(h * steps + s, slots, stride=per_row), :]
        heads[:, pl.ds(h * head_dim, head_dim)] = lined[h].astype(BF16)


def project_kernel(own, heads, w, out):
    groups, tokens, column = out.shape
    core = lax.rem(lax.axis_index("tensor"), 2)
    core = core if own else 1 - core
    wide = jnp.concatenate([heads[...]] * max(1, 128 // tokens), 0)
    for k in range(groups):
        at = pl.multiple_of((2 * k + core) * column, column)
        out[k] = jnp.dot(wide, w[:, pl.ds(at, column)], preferred_element_type=F32)[:tokens].astype(BF16)


def arrange_kernel(mine, given, out):
    devices, groups, pair, steps, column = out.shape
    for k in range(groups):
        total = mine[k].astype(F32) + given[k].astype(F32)
        out[:, k] = total.reshape(devices, pair, steps, column).astype(BF16)


def collect_kernel(anc, parts, out, count):
    rows = out.shape[0]
    devices = parts.shape[0]
    for d in range(devices):
        count[d] = 0
    for r in range(rows):
        source, rank = slot_of(anc, r, rows, count)
        total = parts[source, 0, rank].astype(F32)
        for k in range(1, parts.shape[1]):
            total = total + parts[source, k, rank].astype(F32)
        out[r] = total.astype(BF16)


def shards(inputs, norm_gain, query_proj, w_key, w_value, w_out, kv_cache, ancestors):
    rows, steps, width = inputs.shape
    context = kv_cache.shape[2]
    head_dim = kv_cache.shape[3] // 2
    local = query_proj.shape[2]
    heads = local // head_dim
    per_row = heads * steps
    devices = lax.axis_size("particle")
    tensor = lax.axis_size("tensor")
    groups = tensor // 2
    column = width // tensor
    slots = devices * PAIR
    eight = per_row // PAIR
    cosine, sine = rotary_tables(context, steps, head_dim)
    tables = jnp.asarray(np.stack([np.tile(cosine, (heads, 1)), np.tile(sine, (heads, 1))]))
    smem = pl.BlockSpec(memory_space=pltpu.SMEM)
    vmem = pl.BlockSpec(memory_space=pltpu.VMEM)
    stay = pl.BlockSpec(memory_space=pl.ANY)
    shape = jax.ShapeDtypeStruct
    packed = (devices, PAIR + 1, per_row, head_dim)

    def call(kernel, out, ins, operands, name, mib, scratch=(), flops=0, moved=MIB):
        return pl.pallas_call(
            kernel,
            out_shape=out,
            in_specs=ins,
            out_specs=jax.tree.map(lambda _: vmem, out),
            scratch_shapes=scratch,
            compiler_params=pltpu.CompilerParams(vmem_limit_bytes=mib * MIB),
            cost_estimate=pl.CostEstimate(flops=flops, bytes_accessed=moved, transcendentals=0),
            name=name,
        )(*operands)

    fetched = [ancestors, query_proj, tables, norm_gain.reshape(1, width), inputs, w_key, w_value]
    queries, blocks = call(
        prepare_kernel,
        (shape((rows, per_row, head_dim), BF16), shape((rows, eight, head_dim), F32)),
        [stay] * 7,
        [pltpu.with_memory_space_constraint(x, pltpu.HBM) for x in fetched],
        "prepare",
        12,
        [pltpu.SMEM(fetched[0].shape, jnp.int32)]
        + [pltpu.VMEM(x.shape, x.dtype) for x in fetched[1:]]
        + [
            pltpu.VMEM((rows, per_row, head_dim), F32),
            pltpu.VMEM((rows * steps, width), BF16),
            pltpu.VMEM((2, rows * steps, head_dim), F32),
            pltpu.SemaphoreType.DMA((7,)),
        ],
    )
    send = call(
        send_kernel,
        shape(packed, BF16),
        [smem, vmem, vmem],
        [ancestors, queries, blocks],
        "pack_queries",
        4,
        [pltpu.VMEM((devices, per_row, head_dim), F32), pltpu.SMEM((devices,), jnp.int32)],
        flops=20_000_000_000,
    )
    recv = lax.all_to_all(send, "particle", split_axis=0, concat_axis=0, tiled=True)
    heads_out = call(
        attend_kernel,
        shape((slots * steps, local), BF16),
        [vmem, vmem],
        [recv, kv_cache],
        "attention",
        12,
        [
            pltpu.VMEM((slots, per_row, context), F32),
            pltpu.VMEM((slots, per_row, context), BF16),
            pltpu.VMEM((slots * per_row, head_dim), F32),
            pltpu.VMEM((slots * per_row, head_dim), F32),
            pltpu.VMEM((slots * per_row, head_dim), F32),
            pltpu.VMEM((devices * per_row + 8, head_dim), F32),
            pltpu.VMEM((heads, slots * steps, head_dim), F32),
        ],
        flops=4 * slots * per_row * context * head_dim,
        moved=5 * MIB,
    )
    block = shape((groups, slots * steps, column), BF16)
    cost = dict(flops=2 * slots * steps * local * width, moved=local * width)
    other, mine = (
        call(functools.partial(project_kernel, own), block, [vmem, vmem], [heads_out, w_out], name, 8, **cost)
        for own, name in ((False, "project_sibling"), (True, "project_own"))
    )
    given = lax.ppermute(other, "tensor", [(i, i ^ 1) for i in range(tensor)])
    parts = call(
        arrange_kernel,
        shape((devices, groups, PAIR, steps, column), BF16),
        [vmem, vmem],
        [mine, given],
        "add_sibling",
        8,
    )
    same_core = [[p * tensor + 2 * y + core for p in range(devices) for y in range(groups)] for core in range(2)]
    parts = lax.all_to_all(
        parts.reshape(devices * groups, PAIR, steps, column),
        ("particle", "tensor"),
        split_axis=0,
        concat_axis=0,
        axis_index_groups=same_core,
        tiled=True,
    ).reshape(devices, groups, PAIR, steps, column)
    return call(
        collect_kernel,
        shape((rows, steps, column), BF16),
        [smem, vmem],
        [ancestors, parts],
        "collect",
        4,
        [pltpu.SMEM((devices,), jnp.int32)],
    )


def solution(mesh):
    in_specs = (
        P("particle", None, None),
        P(),
        P("particle", None, "tensor"),
        P(None, "tensor"),
        P(None, "tensor"),
        P("tensor", None),
        P("particle", "tensor", None, None),
        P("particle"),
    )
    out_specs = P("particle", None, "tensor")
    return jax.shard_map(shards, mesh=mesh, in_specs=in_specs, out_specs=out_specs, check_vma=False)
```

time: 223 us -> 48.2 us (0.22)
  waiting for transfers between devices: 142 us -> 0.27 us
  blocking collectives: 14.5 us -> 34.3 us
  local copies, waits for them, and re-layouts: 17.7 us -> 0.03 us
  matrix products: 14.1 us -> 0 us
  between operations: 14.2 us -> 0.12 us
  other arithmetic: 12.7 us -> 0.01 us
  Pallas kernels: 0 us -> 10.6 us
  starting transfers between devices: 4.92 us -> 2.06 us
    all_to_all x1 -> x0, waiting for transfers between devices: 104 us -> none  [shards(): lax.all_to_all(outgoing, 'particle', split_axis=0, concat_axis=0, tiled=T...]
    reduce_scatter x1 -> x0, waiting for transfers between devices: 38.2 us -> none  [shards(): lax.psum_scatter(partial_value.astype(jnp.bfloat16), 'tensor', scatter_di...]
    all_to_all x0 -> x2, blocking collectives: none -> 34.3 us  [the longest x1 18.7 us: shards(): lax.all_to_all(parts.reshape(devices * groups, PAIR, steps, column), ('pa...]
    unnamed x1 -> x0, blocking collectives: 14.5 us -> none
    dot_general x7 -> x0, matrix products: 14.1 us -> none  [the longest x1 9.55 us: shards(): jnp.dot(heads, w_out, preferred_element_type=jnp.float32)]
    gather x2 -> x0, local copies, waits for them, and re-layouts: 13.3 us -> none  [the longest x1 7.11 us: shards(): jnp.take(kv_cache, index, axis=0)]
    pallas_call x0 -> x7, Pallas kernels: none -> 10.6 us  [call(): pl.pallas_call(kernel, out_shape=out, in_specs=ins, out_specs=jax.tree.ma...]
    select_n x5 -> x0, other arithmetic: 10.1 us -> none  [the longest x2 7.46 us: shards(): jnp.take(kv_cache, index, axis=0)]
  transfers between devices with their start and end apart: 2 -> 1, of which waited for: 2 -> 1; matrix products, arithmetic and copies ran while one was open for 2% -> 0% of each run, Pallas kernels for 0% -> 3%
where the time goes in v6:
time: 48.2 us; the launch traced here: 47.4 us
  blocking collectives  34.3 us (71%)
  Pallas kernels  10.6 us (22%)
  starting transfers between devices  2.06 us (4%)
    all_to_all x1, blocking collectives, shards(): lax.all_to_all(parts.reshape(devices * groups, PAIR, steps, column), ('pa...  18.7 us
    all_to_all x1, blocking collectives, shards(): lax.all_to_all(send, 'particle', split_axis=0, concat_axis=0, tiled=True)  15.6 us
    pallas_call x7, Pallas kernels, call(): pl.pallas_call(kernel, out_shape=out, in_specs=ins, out_specs=jax.tree.ma...  10.6 us
    ppermute x1, starting transfers between devices, shards(): given = lax.ppermute(other, 'tensor', [(i, i ^ 1) for i in range(tensor)])  2.06 us
  transfers between devices with their start and end apart: 1, of which 1 were waited for; matrix products, arithmetic and copies ran while one was open for 0% of the time, Pallas kernels for 3%

profile of v6, /device:TPU:1, one launch (start us, length us, event | category | flops | bytes accessed | tf_op | source)
XLA Modules:
  0.0 47.4 jit_solution(1827735879697329480)
XLA Ops:
  0.0 0.0 copy-start.1
  0.0 3.0 %prepare.1 = (bf16[16,16,128]{2,1,0:T(8,128)(2,1)S(1)}, f32[16,8,128]{2,1,0:T(8,128)S(1)}) custom-call(s32[16]{0:T(128)} %anc.3, bf16[16,2,1024]{2,1,0:T(2,128)(2,1)} %refs_1_.1, f32[2,16,128]{2,1,0:T(8,128)} %constant.2.clone.refs_2_, f32[1,8192]{1,0:T(1,128)} %bitcast.7, bf16[16,2,8192]{2,1,0:T(2,128)(2,1)} %refs_4_.1, bf16[8192,128]{1,0:T(8,128)(2,1)} %refs_5_.1, ...), custom_call_target="tpu_custom_call" | custom-call | bytes 1048576 | tf_op jit(solution)/shard_map/prepare/pallas_call | solution.py:194
  3.0 0.0 slice-start
  3.0 0.0 copy-done.1
  3.0 0.0 copy-start
  3.0 0.0 slice-start.1
  3.0 0.0 slice-start.2
  3.0 0.0 slice-start.3
  3.0 0.7 %pack_queries.1 = bf16[16,3,16,128]{3,2,1,0:T(8,128)(2,1)S(1)} custom-call(s32[16]{0:T(128)S(1)} %copy-done.1, bf16[16,16,128]{2,1,0:T(8,128)(2,1)S(1)} %get-tuple-element.7.queries, f32[16,8,128]{2,1,0:T(8,128)S(1)} %get-tuple-element.8.blocks), custom_call_target="tpu_custom_call" | custom-call | flops 20000000000 | bytes 1048576 | tf_op jit(solution)/shard_map/pack_queries/pallas_call | solution.py:194
  3.7 15.6 %all_to_all.10.recv = bf16[16,3,16,128]{3,2,1,0:T(8,128)(2,1)S(1)} all-to-all(bf16[16,3,16,128]{3,2,1,0:T(8,128)(2,1)S(1)} %pack_queries.1), channel_id=1, replica_groups=mesh['particle'=16,'tensor'=8] {'particle'}, dimensions={0} | all-to-all | bytes 393216 | tf_op jit(solution)/shard_map/all_to_all | solution.py:232
  19.3 0.0 copy-done
  19.3 2.6 %attention.1.heads = bf16[64,1024]{1,0:T(8,128)(2,1)S(1)} custom-call(bf16[16,3,16,128]{3,2,1,0:T(8,128)(2,1)S(1)} %all_to_all.10.recv, bf16[16,1,512,256]{3,2,1,0:T(8,128)(2,1)S(1)} %copy-done), custom_call_target="tpu_custom_call" | custom-call | flops 134217728 | bytes 5242880 | tf_op jit(solution)/shard_map/attention/pallas_call | solution.py:194
  21.9 0.0 slice-done
  21.9 0.0 slice-done.1
  21.9 0.0 slice-done.2
  22.0 0.0 slice-done.3
  22.0 1.3 %project_sibling.1 = bf16[4,64,1024]{2,1,0:T(8,128)(2,1)S(1)} custom-call(bf16[64,1024]{1,0:T(8,128)(2,1)S(1)} %attention.1.heads, bf16[1024,8192]{1,0:T(8,128)(2,1)S(1)} %bitcast.4), custom_call_target="tpu_custom_call" | custom-call | flops 1073741824 | bytes 8388608 | tf_op jit(solution)/shard_map/project_sibling/pallas_call | solution.py:194
  23.3 2.1 %collective-permute-start = (bf16[4,64,1024]{2,1,0:T(8,128)(2,1)S(1)}, bf16[4,64,1024]{2,1,0:T(8,128)(2,1)S(1)}, u32[]{:S(2)}, u32[]{:S(2)}) collective-permute-start(bf16[4,64,1024]{2,1,0:T(8,128)(2,1)S(1)} %project_sibling.1), channel_id=1, source_target_pairs={{0,1},{1,0},{2,3},{3,2},{4,5},{5,4},{6,7},{7,6},{8,9},{9,8},{10,11... | collective-permute-start | bytes 1572872 | tf_op jit(solution)/shard_map/ppermute | solution.py:258
  25.3 1.3 %project_own.1.mine = bf16[4,64,1024]{2,1,0:T(8,128)(2,1)S(1)} custom-call(bf16[64,1024]{1,0:T(8,128)(2,1)S(1)} %attention.1.heads, bf16[1024,8192]{1,0:T(8,128)(2,1)S(1)} %bitcast.4), custom_call_target="tpu_custom_call" | custom-call | flops 1073741824 | bytes 8388608 | tf_op jit(solution)/shard_map/project_own/pallas_call | solution.py:194
  26.6 0.3 collective-permute-done.given
  26.9 0.6 %add_sibling.1 = bf16[16,4,2,2,1024]{4,3,2,1,0:T(2,128)(2,1)S(1)} custom-call(bf16[4,64,1024]{2,1,0:T(8,128)(2,1)S(1)} %project_own.1.mine, bf16[4,64,1024]{2,1,0:T(8,128)(2,1)S(1)} %collective-permute-done.given), custom_call_target="tpu_custom_call" | custom-call | bytes 1048576 | tf_op jit(solution)/shard_map/add_sibling/pallas_call | solution.py:194
  27.4 18.7 %all_to_all.11 = bf16[64,2,2,1024]{3,2,1,0:T(2,128)(2,1)S(1)} all-to-all(bf16[64,2,2,1024]{3,2,1,0:T(2,128)(2,1)S(1)} %bitcast.5), channel_id=1, replica_groups={{0,2,4,6,8,10,12,14,16,18,20,22,24,26,28,30,32,34,36,38,40,42,44,46,48,..., dimensions={0} | all-to-all | bytes 1048576 | tf_op jit(solution)/shard_map/all_to_all | solution.py:268
  46.1 1.3 %collect.1 = bf16[16,2,1024]{2,1,0:T(2,128)(2,1)} custom-call(s32[16]{0:T(128)S(1)} %copy-done.1, bf16[16,4,2,2,1024]{4,3,2,1,0:T(2,128)(2,1)S(1)} %bitcast.6), custom_call_target="tpu_custom_call" | custom-call | bytes 1048576 | tf_op jit(solution)/shard_map/collect/pallas_call | solution.py:194
  (1 shorter events, 0.0 us)
Async XLA Ops:
  0.0 3.0 %copy-start.1 = (s32[16]{0:T(128)S(1)}, s32[16]{0:T(128)}, u32[]{:S(2)}) copy-start(s32[16]{0:T(128)} %anc.3) | copy-start | bytes 196
  3.0 19.0 %slice-start = ((s8[16777216]{0:T(1024)(128)(4,1)}), s8[4194304]{0:T(1024)(128)(4,1)S(1)}, s32[]{:S(2)}) async-start(s8[16777216]{0:T(1024)(128)(4,1)} %bitcast.3), calls=%async_computation.2 | async-start | bytes 8388608
  3.0 16.3 %copy-start = (bf16[16,1,512,256]{3,2,1,0:T(8,128)(2,1)S(1)}, bf16[16,1,512,256]{3,2,1,0:T(8,128)(2,1)}, u32[]{:S(2)}) copy-start(bf16[16,1,512,256]{3,2,1,0:T(8,128)(2,1)} %kv.1) | copy-start | bytes 12582916
  3.0 18.9 %slice-start.1 = ((s8[16777216]{0:T(1024)(128)(4,1)}), s8[4194304]{0:T(1024)(128)(4,1)S(1)}, s32[]{:S(2)}) async-start(s8[16777216]{0:T(1024)(128)(4,1)} %bitcast.3), calls=%async_computation.3 | async-start | bytes 8388608
  3.0 18.9 %slice-start.2 = ((s8[16777216]{0:T(1024)(128)(4,1)}), s8[4194304]{0:T(1024)(128)(4,1)S(1)}, s32[]{:S(2)}) async-start(s8[16777216]{0:T(1024)(128)(4,1)} %bitcast.3), calls=%async_computation.4 | async-start | bytes 8388608
  3.0 18.9 %slice-start.3 = ((s8[16777216]{0:T(1024)(128)(4,1)}), s8[4194304]{0:T(1024)(128)(4,1)S(1)}, s32[]{:S(2)}) async-start(s8[16777216]{0:T(1024)(128)(4,1)} %bitcast.3), calls=%async_computation.5 | async-start | bytes 8388608
  23.3 3.6 %collective-permute-start = (bf16[4,64,1024]{2,1,0:T(8,128)(2,1)S(1)}, bf16[4,64,1024]{2,1,0:T(8,128)(2,1)S(1)}, u32[]{:S(2)}, u32[]{:S(2)}) collective-permute-start(bf16[4,64,1024]{2,1,0:T(8,128)(2,1)S(1)} %project_sibling.1), channel_id=1, source_target_pairs={{0,1},{1,0},{2,3},{3,2},{4,5},{5,4},{6,7},{7,6},{8,9},{9,8},{10,11... | collective-permute-start | bytes 1572872 | tf_op jit(solution)/shard_map/ppermute | solution.py:258

commit v7 on v5

--- a/solution.py
+++ b/solution.py
@@ -134,14 +134,19 @@
         back[d, PAIR] = stat.astype(BF16)
 
 
-def project(heads, w, out, own):
+def units(own, groups):
     index = lax.axis_index("tensor")
-    first, core = lax.div(index, 2), lax.rem(index, 2)
+    y, core = lax.div(index, 2), lax.rem(index, 2)
     core = core if own else 1 - core
-    groups, tokens, column = out.shape
+    near = lax.rem(y + 1 + (groups - 2) * core, groups)
+    far = lax.rem(y + 2, groups)
+    return 2 * near + core, 2 * near + 1 - core, 2 * far + core, 2 * y + core
+
+
+def project(heads, w, out, blocks):
+    tokens, column = out.shape[-2:]
     wide = jnp.concatenate([heads[...]] * max(1, 128 // tokens), 0)
-    for k in range(groups):
-        block = 2 * lax.rem(first + k, groups) + core
+    for k, block in enumerate(blocks):
         at = pl.multiple_of(block * column, column)
         out[k] = jnp.dot(wide, w[:, pl.ds(at, column)], preferred_element_type=F32)[:tokens].astype(BF16)
 
@@ -176,11 +181,21 @@
         for s in range(steps):
             lined[h, pl.ds(s, rows, stride=steps), :] = grid_ref[pl.ds(h * steps + s, rows, stride=per_row), :]
         heads[:, pl.ds(h * head_dim, head_dim)] = lined[h].astype(BF16)
-    project(heads, w, out, False)
+    project(heads, w, out, units(False, w.shape[1] // out.shape[-1] // 2)[:3])
 
 
 def second_kernel(heads, w, out):
-    project(heads, w, out, True)
+    project(heads, w, out, units(True, w.shape[1] // out.shape[-1] // 2)[:3])
+
+
+def add_kernel(mine, given, near, far):
+    near[...] = (mine[:2].astype(F32) + given[:2].astype(F32)).astype(BF16)
+    far[...] = (mine[2].astype(F32) + given[2].astype(F32)).astype(BF16)
+
+
+def last_kernel(heads, w, out):
+    groups = w.shape[1] // out.shape[-1] // 2
+    project(heads, w, out, (units(True, groups)[3], units(False, groups)[3]))
 
 
 def shards(inputs, norm_gain, query_proj, w_key, w_value, w_out, kv_cache, ancestors):
@@ -270,7 +285,7 @@
     home = lax.all_to_all(back, "particle", split_axis=0, concat_axis=0, tiled=True)
 
     groups = tensor // 2
-    block = (groups, rows * steps, column)
+    block = jax.ShapeDtypeStruct((3, rows * steps, column), BF16)
     params = pltpu.CompilerParams(vmem_limit_bytes=8 * MIB)
     cost = pl.CostEstimate(
         flops=rows * steps * local * width, bytes_accessed=local * width, transcendentals=0
@@ -278,7 +293,7 @@
     other, heads_out = pl.pallas_call(
         merge_kernel,
         out_shape=(
-            jax.ShapeDtypeStruct(block, BF16),
+            block,
             jax.ShapeDtypeStruct((rows * steps, local), BF16),
         ),
         in_specs=[smem, vmem, vmem, vmem, vmem],
@@ -293,21 +308,44 @@
         cost_estimate=cost,
         name="merge_project_sibling",
     )(ancestors, home, vec, stat, w_out)
-    given = lax.ppermute(other, "tensor", [(i, i ^ 1) for i in range(tensor)])
+    sibling = [(i, i ^ 1) for i in range(tensor)]
+    given = lax.ppermute(other, "tensor", sibling)
     mine = pl.pallas_call(
         second_kernel,
-        out_shape=jax.ShapeDtypeStruct(block, BF16),
+        out_shape=block,
         in_specs=[vmem, vmem],
         out_specs=vmem,
         compiler_params=params,
         cost_estimate=cost,
         name="project_own",
     )(heads_out, w_out)
-    pair = [(mine[k].astype(F32) + given[k].astype(F32)) for k in range(groups)]
-    total = pair[0]
-    for k in range(1, groups):
-        ring = [(i, ((i // 2 + k) % groups) * 2 + i % 2) for i in range(tensor)]
-        total = total + lax.ppermute(pair[k].astype(BF16), "tensor", ring).astype(F32)
+    near, far = pl.pallas_call(
+        add_kernel,
+        out_shape=(
+            jax.ShapeDtypeStruct((2, rows * steps, column), BF16),
+            jax.ShapeDtypeStruct((rows * steps, column), BF16),
+        ),
+        in_specs=[vmem, vmem],
+        out_specs=(vmem, vmem),
+        compiler_params=params,
+        name="add_sibling",
+    )(mine, given)
+    ring = [(i, 2 * ((i // 2 + (1 if i % 2 == 0 else groups - 1)) % groups) + i % 2) for i in range(tensor)]
+    across = [(i, 2 * ((i // 2 + 2) % groups) + i % 2) for i in range(tensor)]
+    from_near = lax.ppermute(near, "tensor", ring)
+    from_far = lax.ppermute(far, "tensor", across)
+    last = pl.pallas_call(
+        last_kernel,
+        out_shape=jax.ShapeDtypeStruct((2, rows * steps, column), BF16),
+        in_specs=[vmem, vmem],
+        out_specs=vmem,
+        compiler_params=params,
+        cost_estimate=cost,
+        name="project_last",
+    )(heads_out, w_out)
+    crossing = (from_near[1].astype(F32) + last[1].astype(F32)).astype(BF16)
+    crossed = lax.ppermute(crossing, "tensor", sibling)
+    total = last[0].astype(F32) + from_near[0].astype(F32) + from_far.astype(F32) + crossed.astype(F32)
     return total.astype(BF16).reshape(rows, steps, column)
 
 

time: 46 us -> 46.2 us (level)
  starting transfers between devices: 7.65 us -> 8.36 us
    ppermute x4, starting transfers between devices: 7.65 us -> 8.36 us  [the longest x1 3.19 us: shards(): given = lax.ppermute(other, 'tensor', sibling)]
    pallas_call x2 -> x4, Pallas kernels: 3.32 us -> 3.54 us  [the longest x1 1.79 us: shards(): pl.pallas_call(merge_kernel, out_shape=(block, jax.ShapeDtypeStruct((rows...]
  transfers between devices with their start and end apart: 4 -> 4, of which waited for: 2 -> 3; matrix products, arithmetic and copies ran while one was open for 0% -> 0% of each run, Pallas kernels for 3% -> 4%
where the time goes in v7:
time: 46.2 us; the launch traced here: 46.1 us
  blocking collectives  26.3 us (57%)
  starting transfers between devices  8.36 us (18%)
  Pallas kernels  7.77 us (17%)
  waiting for transfers between devices  2.76 us (6%)
  local copies, waits for them, and re-layouts  0.7 us (2%)
    all_to_all x1, blocking collectives, shards(): lax.all_to_all(send, 'particle', split_axis=0, concat_axis=0, tiled=True)  15.6 us
    all_to_all x1, blocking collectives, shards(): lax.all_to_all(back, 'particle', split_axis=0, concat_axis=0, tiled=True)  10.6 us
    ppermute x1, starting transfers between devices, shards(): given = lax.ppermute(other, 'tensor', sibling)  3.19 us
    pallas_call x1, Pallas kernels, shards(): pl.pallas_call(attend_kernel, out_shape=(partial_result,) * 3 + (jax.Shap...  2.88 us
    ppermute x1, starting transfers between devices, shards(): from_near = lax.ppermute(near, 'tensor', ring)  2.81 us
    ppermute x1, starting transfers between devices, shards(): crossed = lax.ppermute(crossing, 'tensor', sibling)  1.94 us
    ppermute x1, waiting for transfers between devices, shards(): from_far = lax.ppermute(far, 'tensor', across)  1.89 us
    pallas_call x1, Pallas kernels, shards(): pl.pallas_call(merge_kernel, out_shape=(block, jax.ShapeDtypeStruct((rows...  1.79 us
  transfers between devices with their start and end apart: 4, of which 3 were waited for; matrix products, arithmetic and copies ran while one was open for 0% of the time, Pallas kernels for 4%

profile of v7, /device:TPU:1, one launch (start us, length us, event | category | flops | bytes accessed | tf_op | source)
XLA Modules:
  0.0 46.1 jit_solution(18179644963812641465)
XLA Ops:
  0.0 0.0 copy-start
  0.0 0.0 copy-start.1
  0.0 0.0 copy-start.2
  0.0 0.0 copy-start.3
  0.0 1.2 %pack_queries.1 = (bf16[16,3,16,128]{3,2,1,0:T(8,128)(2,1)S(1)}, bf16[16,16,128]{2,1,0:T(8,128)(2,1)S(1)}, f32[2,16,128]{2,1,0:T(8,128)S(1)}, f32[1,8192]{1,0:T(1,128)S(1)}) custom-call(s32[16]{0:T(128)} %anc.1, bf16[16,2,1024]{2,1,0:T(2,128)(2,1)} %qp_hbm.1, f32[2,16,128]{2,1,0:T(8,128)} %constant.2.clone.tables_hbm, f32[1,8192]{1,0:T(1,128)} %bitcast.11), custom_call_target="tpu_custom_call" | custom-call | flops 10000000000 | bytes 1048576 | tf_op jit(solution)/shard_map/pack_queries/pallas_call | solution.py:220
  1.2 15.6 %all_to_all.10.recv = bf16[16,3,16,128]{3,2,1,0:T(8,128)(2,1)S(1)} all-to-all(bf16[16,3,16,128]{3,2,1,0:T(8,128)(2,1)S(1)} %get-tuple-element.18), channel_id=1, replica_groups=mesh['particle'=16,'tensor'=8] {'particle'}, dimensions={0} | all-to-all | bytes 393216 | tf_op jit(solution)/shard_map/all_to_all | solution.py:243
  16.9 0.0 copy-done
  16.9 0.0 copy-done.1
  16.9 0.0 copy-done.2
  16.9 0.0 copy-done.3
  16.9 2.9 %attention.1 = (f32[32,16,128]{2,1,0:T(8,128)S(1)}, f32[32,16,128]{2,1,0:T(8,128)S(1)}, f32[32,16,128]{2,1,0:T(8,128)S(1)}, f32[256,128]{1,0:T(8,128)S(1)}, f32[2,256,128]{2,1,0:T(8,128)S(1)}) custom-call(bf16[16,3,16,128]{3,2,1,0:T(8,128)(2,1)S(1)} %all_to_all.10.recv, bf16[16,1,512,256]{3,2,1,0:T(8,128)(2,1)S(1)} %copy-done, ...), custom_call_target="tpu_custom_call" | custom-call | flops 134217728 | bytes 5242880 | tf_op jit(solution)/shard_map/attention/pallas_call | solution.py:247
  19.8 0.0 slice-start
  19.8 0.0 slice-start.1
  19.8 0.0 slice-start.2
  19.8 0.0 slice-start.3
  19.8 0.0 copy-start.4
  19.8 0.1 pack_results.1
  20.0 10.6 %all_to_all.11.recv = bf16[16,3,16,128]{3,2,1,0:T(8,128)(2,1)S(1)} all-to-all(bf16[16,3,16,128]{3,2,1,0:T(8,128)(2,1)S(1)} %pack_results.1), channel_id=1, replica_groups=mesh['particle'=16,'tensor'=8] {'particle'}, dimensions={0} | all-to-all | bytes 393216 | tf_op jit(solution)/shard_map/all_to_all | solution.py:285
  30.6 0.0 slice-done
  30.6 0.0 slice-done.1
  30.6 0.0 slice-done.2
  30.6 0.0 slice-done.3
  30.6 0.0 copy-done.4
  30.6 1.8 %merge_project_sibling.1 = (bf16[3,32,1024]{2,1,0:T(8,128)(2,1)S(1)}, bf16[32,1024]{1,0:T(8,128)(2,1)S(1)}) custom-call(s32[16]{0:T(128)S(1)} %copy-done.4, bf16[16,3,16,128]{3,2,1,0:T(8,128)(2,1)S(1)} %all_to_all.11.recv, f32[256,128]{1,0:T(8,128)S(1)} %get-tuple-element.25.vec, f32[2,256,128]{2,1,0:T(8,128)S(1)} %get-tuple-element.26.stat, ...), custom_call_target="tpu_custom_call" | custom-call | flops 268435456 | bytes 8388608 | tf_op jit(solution)/shard_map/merge_project_sibling/pallas_call | solution.py:293
  32.4 3.2 %collective-permute-start = (bf16[3,32,1024]{2,1,0:T(8,128)(2,1)S(1)}, bf16[3,32,1024]{2,1,0:T(8,128)(2,1)S(1)}, u32[]{:S(2)}, u32[]{:S(2)}) collective-permute-start(bf16[3,32,1024]{2,1,0:T(8,128)(2,1)S(1)} %get-tuple-element.28), channel_id=1, source_target_pairs={{0,1},{1,0},{2,3},{3,2},{4,5},{5,4},{6,7},{7,6},{8,9},{9,8},{10,11... | collective-permute-start | bytes 589832 | tf_op jit(solution)/shard_map/ppermute | solution.py:312
  35.6 1.0 %project_own.1.mine = bf16[3,32,1024]{2,1,0:T(8,128)(2,1)S(1)} custom-call(bf16[32,1024]{1,0:T(8,128)(2,1)S(1)} %get-tuple-element.27.heads, bf16[1024,8192]{1,0:T(8,128)(2,1)S(1)} %bitcast.10), custom_call_target="tpu_custom_call" | custom-call | flops 268435456 | bytes 8388608 | tf_op jit(solution)/shard_map/project_own/pallas_call | solution.py:313
  36.6 0.1 collective-permute-done.given
  36.7 2.8 %collective-permute-start.1 = (bf16[2,32,1024]{2,1,0:T(8,128)(2,1)S(1)}, bf16[2,32,1024]{2,1,0:T(8,128)(2,1)S(1)}, u32[]{:S(2)}, u32[]{:S(2)}) collective-permute-start(bf16[2,32,1024]{2,1,0:T(8,128)(2,1)S(1)} %get-tuple-element.29), channel_id=1, source_target_pairs={{0,2},{1,7},{2,4},{3,1},{4,6},{5,3},{6,0},{7,5},{8,10},{9,15},{10,... | collective-permute-start | bytes 393224 | tf_op jit(solution)/shard_map/ppermute | solution.py:335
  39.6 0.7 %project_last.1 = bf16[2,32,1024]{2,1,0:T(8,128)(2,1)S(1)} custom-call(bf16[32,1024]{1,0:T(8,128)(2,1)S(1)} %get-tuple-element.27.heads, bf16[1024,8192]{1,0:T(8,128)(2,1)S(1)} %bitcast.10), custom_call_target="tpu_custom_call" | custom-call | flops 268435456 | bytes 8388608 | tf_op jit(solution)/shard_map/project_last/pallas_call | solution.py:337
  40.3 0.4 collective-permute-start.2
  40.7 0.8 %collective-permute-done.1 = bf16[2,32,1024]{2,1,0:T(8,128)(2,1)S(1)} collective-permute-done((bf16[2,32,1024]{2,1,0:T(8,128)(2,1)S(1)}, bf16[2,32,1024]{2,1,0:T(8,128)(2,1)S(1)}, u32[]{:S(2)}, u32[]{:S(2)}) %collective-permute-start.1) | collective-permute-done | bytes 131104 | tf_op jit(solution)/shard_map/ppermute | solution.py:335
  41.5 1.9 %collective-permute-start.3 = (bf16[32,1024]{1,0:T(8,128)(2,1)S(1)}, bf16[32,1024]{1,0:T(8,128)(2,1)S(1)}, u32[]{:S(2)}, u32[]{:S(2)}) collective-permute-start(bf16[32,1024]{1,0:T(8,128)(2,1)S(1)} %fusion.2), channel_id=1, source_target_pairs={{0,1},{1,0},{2,3},{3,2},{4,5},{5,4},{6,7},{7,6},{8,9},{9,8},{10,11... | collective-permute-start | bytes 196616 | tf_op jit(solution)/shard_map/ppermute | solution.py:347
  43.5 1.9 %collective-permute-done.2 = bf16[32,1024]{1,0:T(8,128)(2,1)S(1)} collective-permute-done((bf16[32,1024]{1,0:T(8,128)(2,1)S(1)}, bf16[32,1024]{1,0:T(8,128)(2,1)S(1)}, u32[]{:S(2)}, u32[]{:S(2)}) %collective-permute-start.2) | collective-permute-done | bytes 65568 | tf_op jit(solution)/shard_map/ppermute | solution.py:336
  45.4 0.0 collective-permute-done.3
  45.4 0.7 %reshape.14 = bf16[16,2,1024]{2,1,0:T(2,128)(2,1)} reshape(bf16[32,1024]{1,0:T(8,128)(2,1)S(1)} %fusion.1) | data formatting | bytes 131072 | tf_op jit(solution)/shard_map/reshape | solution.py:349
  (4 shorter events, 0.1 us)
Async XLA Ops:
  0.0 16.9 %copy-start = (bf16[16,1,512,256]{3,2,1,0:T(8,128)(2,1)S(1)}, bf16[16,1,512,256]{3,2,1,0:T(8,128)(2,1)}, u32[]{:S(2)}) copy-start(bf16[16,1,512,256]{3,2,1,0:T(8,128)(2,1)} %kv.1) | copy-start | bytes 12582916
  0.0 16.9 %copy-start.1 = (bf16[8192,128]{1,0:T(8,128)(2,1)S(1)}, bf16[8192,128]{1,0:T(8,128)(2,1)}, u32[]{:S(2)}) copy-start(bf16[8192,128]{1,0:T(8,128)(2,1)} %wk.1) | copy-start | bytes 6291460
  0.0 16.9 %copy-start.2 = (bf16[8192,128]{1,0:T(8,128)(2,1)S(1)}, bf16[8192,128]{1,0:T(8,128)(2,1)}, u32[]{:S(2)}) copy-start(bf16[8192,128]{1,0:T(8,128)(2,1)} %wv.1) | copy-start | bytes 6291460
  0.0 16.9 %copy-start.3 = (bf16[16,2,8192]{2,1,0:T(2,128)(2,1)S(1)}, bf16[16,2,8192]{2,1,0:T(2,128)(2,1)}, u32[]{:S(2)}) copy-start(bf16[16,2,8192]{2,1,0:T(2,128)(2,1)} %x.1) | copy-start | bytes 1572868
  19.8 10.8 %slice-start = ((s8[16777216]{0:T(1024)(128)(4,1)}), s8[4194304]{0:T(1024)(128)(4,1)S(1)}, s32[]{:S(2)}) async-start(s8[16777216]{0:T(1024)(128)(4,1)} %bitcast.9), calls=%async_computation.2 | async-start | bytes 8388608
  19.8 10.8 %slice-start.1 = ((s8[16777216]{0:T(1024)(128)(4,1)}), s8[4194304]{0:T(1024)(128)(4,1)S(1)}, s32[]{:S(2)}) async-start(s8[16777216]{0:T(1024)(128)(4,1)} %bitcast.9), calls=%async_computation.3 | async-start | bytes 8388608
  19.8 10.8 %slice-start.2 = ((s8[16777216]{0:T(1024)(128)(4,1)}), s8[4194304]{0:T(1024)(128)(4,1)S(1)}, s32[]{:S(2)}) async-start(s8[16777216]{0:T(1024)(128)(4,1)} %bitcast.9), calls=%async_computation.4 | async-start | bytes 8388608
  19.8 10.8 %slice-start.3 = ((s8[16777216]{0:T(1024)(128)(4,1)}), s8[4194304]{0:T(1024)(128)(4,1)S(1)}, s32[]{:S(2)}) async-start(s8[16777216]{0:T(1024)(128)(4,1)} %bitcast.9), calls=%async_computation.5 | async-start | bytes 8388608
  19.8 10.8 %copy-start.4 = (s32[16]{0:T(128)S(1)}, s32[16]{0:T(128)}, u32[]{:S(2)}) copy-start(s32[16]{0:T(128)} %anc.1) | copy-start | bytes 196
  32.4 4.3 %collective-permute-start = (bf16[3,32,1024]{2,1,0:T(8,128)(2,1)S(1)}, bf16[3,32,1024]{2,1,0:T(8,128)(2,1)S(1)}, u32[]{:S(2)}, u32[]{:S(2)}) collective-permute-start(bf16[3,32,1024]{2,1,0:T(8,128)(2,1)S(1)} %get-tuple-element.28), channel_id=1, source_target_pairs={{0,1},{1,0},{2,3},{3,2},{4,5},{5,4},{6,7},{7,6},{8,9},{9,8},{10,11... | collective-permute-start | bytes 589832 | tf_op jit(solution)/shard_map/ppermute | solution.py:312
  36.7 4.8 %collective-permute-start.1 = (bf16[2,32,1024]{2,1,0:T(8,128)(2,1)S(1)}, bf16[2,32,1024]{2,1,0:T(8,128)(2,1)S(1)}, u32[]{:S(2)}, u32[]{:S(2)}) collective-permute-start(bf16[2,32,1024]{2,1,0:T(8,128)(2,1)S(1)} %get-tuple-element.29), channel_id=1, source_target_pairs={{0,2},{1,7},{2,4},{3,1},{4,6},{5,3},{6,0},{7,5},{8,10},{9,15},{10,... | collective-permute-start | bytes 393224 | tf_op jit(solution)/shard_map/ppermute | solution.py:335
  40.3 5.1 %collective-permute-start.2 = (bf16[32,1024]{1,0:T(8,128)(2,1)S(1)}, bf16[32,1024]{1,0:T(8,128)(2,1)S(1)}, u32[]{:S(2)}, u32[]{:S(2)}) collective-permute-start(bf16[32,1024]{1,0:T(8,128)(2,1)S(1)} %get-tuple-element.30), channel_id=1, source_target_pairs={{0,4},{1,5},{2,6},{3,7},{4,0},{5,1},{6,2},{7,3},{8,12},{9,13},{10,... | collective-permute-start | bytes 196616 | tf_op jit(solution)/shard_map/ppermute | solution.py:336
  41.5 3.8 %collective-permute-start.3 = (bf16[32,1024]{1,0:T(8,128)(2,1)S(1)}, bf16[32,1024]{1,0:T(8,128)(2,1)S(1)}, u32[]{:S(2)}, u32[]{:S(2)}) collective-permute-start(bf16[32,1024]{1,0:T(8,128)(2,1)S(1)} %fusion.2), channel_id=1, source_target_pairs={{0,1},{1,0},{2,3},{3,2},{4,5},{5,4},{6,7},{7,6},{8,9},{9,8},{10,11... | collective-permute-start | bytes 196616 | tf_op jit(solution)/shard_map/ppermute | solution.py:347

commit v8 on v7

--- a/solution.py
+++ b/solution.py
@@ -193,9 +193,14 @@
     far[...] = (mine[2].astype(F32) + given[2].astype(F32)).astype(BF16)
 
 
-def last_kernel(heads, w, out):
-    groups = w.shape[1] // out.shape[-1] // 2
-    project(heads, w, out, (units(True, groups)[3], units(False, groups)[3]))
+def last_kernel(heads, w, arrived, keep, crossing):
+    tokens, column = keep.shape
+    mine, given = units(True, w.shape[1] // column // 2)[3], units(False, w.shape[1] // column // 2)[3]
+    wide = jnp.concatenate([heads[...]] * max(1, 128 // tokens), 0)
+    for k, (out, block) in enumerate(((keep, mine), (crossing, given))):
+        at = pl.multiple_of(block * column, column)
+        product = jnp.dot(wide, w[:, pl.ds(at, column)], preferred_element_type=F32)[:tokens]
+        out[...] = (product + arrived[k].astype(F32)).astype(out.dtype)
 
 
 def shards(inputs, norm_gain, query_proj, w_key, w_value, w_out, kv_cache, ancestors):
@@ -334,18 +339,20 @@
     across = [(i, 2 * ((i // 2 + 2) % groups) + i % 2) for i in range(tensor)]
     from_near = lax.ppermute(near, "tensor", ring)
     from_far = lax.ppermute(far, "tensor", across)
-    last = pl.pallas_call(
+    keep, crossing = pl.pallas_call(
         last_kernel,
-        out_shape=jax.ShapeDtypeStruct((2, rows * steps, column), BF16),
-        in_specs=[vmem, vmem],
-        out_specs=vmem,
+        out_shape=(
+            jax.ShapeDtypeStruct((rows * steps, column), F32),
+            jax.ShapeDtypeStruct((rows * steps, column), BF16),
+        ),
+        in_specs=[vmem, vmem, vmem],
+        out_specs=(vmem, vmem),
         compiler_params=params,
         cost_estimate=cost,
         name="project_last",
-    )(heads_out, w_out)
-    crossing = (from_near[1].astype(F32) + last[1].astype(F32)).astype(BF16)
+    )(heads_out, w_out, from_near)
     crossed = lax.ppermute(crossing, "tensor", sibling)
-    total = last[0].astype(F32) + from_near[0].astype(F32) + from_far.astype(F32) + crossed.astype(F32)
+    total = keep + from_far.astype(F32) + crossed.astype(F32)
     return total.astype(BF16).reshape(rows, steps, column)
 
 

time: 46.2 us -> 46 us (level)
  starting transfers between devices: 8.36 us -> 6.91 us
  waiting for transfers between devices: 2.76 us -> 4.03 us
    ppermute x1, waiting for transfers between devices: 0.8 us -> 2.97 us  [shards(): from_near = lax.ppermute(near, 'tensor', ring)]
    ppermute x1, starting transfers between devices: 1.94 us -> 0.58 us  [shards(): crossed = lax.ppermute(crossing, 'tensor', sibling)]
    ppermute x1, waiting for transfers between devices: 1.89 us -> 0.98 us  [shards(): from_far = lax.ppermute(far, 'tensor', across)]
where the time goes in v8:
time: 46 us; the launch traced here: 45.9 us
  blocking collectives  26.3 us (57%)
  Pallas kernels  7.78 us (17%)
  starting transfers between devices  6.91 us (15%)
  waiting for transfers between devices  4.03 us (9%)
  local copies, waits for them, and re-layouts  0.7 us (2%)
    all_to_all x1, blocking collectives, shards(): lax.all_to_all(send, 'particle', split_axis=0, concat_axis=0, tiled=True)  15.6 us
    all_to_all x1, blocking collectives, shards(): lax.all_to_all(back, 'particle', split_axis=0, concat_axis=0, tiled=True)  10.6 us
    ppermute x1, starting transfers between devices, shards(): given = lax.ppermute(other, 'tensor', sibling)  3.18 us
    ppermute x1, waiting for transfers between devices, shards(): from_near = lax.ppermute(near, 'tensor', ring)  2.97 us
    pallas_call x1, Pallas kernels, shards(): pl.pallas_call(attend_kernel, out_shape=(partial_result,) * 3 + (jax.Shap...  2.88 us
    ppermute x1, starting transfers between devices, shards(): from_near = lax.ppermute(near, 'tensor', ring)  2.81 us
    pallas_call x1, Pallas kernels, shards(): pl.pallas_call(merge_kernel, out_shape=(block, jax.ShapeDtypeStruct((rows...  1.8 us
    pallas_call x1, Pallas kernels, shards(): pl.pallas_call(pack_kernel, out_shape=(jax.ShapeDtypeStruct(packed, BF16)...  1.2 us
  transfers between devices with their start and end apart: 4, of which 3 were waited for; matrix products, arithmetic and copies ran while one was open for 0% of the time, Pallas kernels for 4%

profile of v8, /device:TPU:1, one launch (start us, length us, event | category | flops | bytes accessed | tf_op | source)
XLA Modules:
  0.0 45.9 jit_solution(2619399858103555416)
XLA Ops:
  0.0 0.0 copy-start
  0.0 0.0 copy-start.1
  0.0 0.0 copy-start.2
  0.0 0.0 copy-start.3
  0.0 1.2 %pack_queries.1 = (bf16[16,3,16,128]{3,2,1,0:T(8,128)(2,1)S(1)}, bf16[16,16,128]{2,1,0:T(8,128)(2,1)S(1)}, f32[2,16,128]{2,1,0:T(8,128)S(1)}, f32[1,8192]{1,0:T(1,128)S(1)}) custom-call(s32[16]{0:T(128)} %anc.1, bf16[16,2,1024]{2,1,0:T(2,128)(2,1)} %qp_hbm.1, f32[2,16,128]{2,1,0:T(8,128)} %constant.2.clone.tables_hbm, f32[1,8192]{1,0:T(1,128)} %bitcast.3), custom_call_target="tpu_custom_call" | custom-call | flops 10000000000 | bytes 1048576 | tf_op jit(solution)/shard_map/pack_queries/pallas_call | solution.py:225
  1.2 15.6 %all_to_all.10.recv = bf16[16,3,16,128]{3,2,1,0:T(8,128)(2,1)S(1)} all-to-all(bf16[16,3,16,128]{3,2,1,0:T(8,128)(2,1)S(1)} %get-tuple-element.20), channel_id=1, replica_groups=mesh['particle'=16,'tensor'=8] {'particle'}, dimensions={0} | all-to-all | bytes 393216 | tf_op jit(solution)/shard_map/all_to_all | solution.py:248
  16.9 0.0 copy-done
  16.9 0.0 copy-done.1
  16.9 0.0 copy-done.2
  16.9 0.0 copy-done.3
  16.9 2.9 %attention.1 = (f32[32,16,128]{2,1,0:T(8,128)S(1)}, f32[32,16,128]{2,1,0:T(8,128)S(1)}, f32[32,16,128]{2,1,0:T(8,128)S(1)}, f32[256,128]{1,0:T(8,128)S(1)}, f32[2,256,128]{2,1,0:T(8,128)S(1)}) custom-call(bf16[16,3,16,128]{3,2,1,0:T(8,128)(2,1)S(1)} %all_to_all.10.recv, bf16[16,1,512,256]{3,2,1,0:T(8,128)(2,1)S(1)} %copy-done, ...), custom_call_target="tpu_custom_call" | custom-call | flops 134217728 | bytes 5242880 | tf_op jit(solution)/shard_map/attention/pallas_call | solution.py:252
  19.8 0.0 slice-start
  19.8 0.0 slice-start.1
  19.8 0.0 slice-start.2
  19.8 0.0 slice-start.3
  19.8 0.0 copy-start.4
  19.8 0.1 pack_results.1
  20.0 10.6 %all_to_all.11.recv = bf16[16,3,16,128]{3,2,1,0:T(8,128)(2,1)S(1)} all-to-all(bf16[16,3,16,128]{3,2,1,0:T(8,128)(2,1)S(1)} %pack_results.1), channel_id=1, replica_groups=mesh['particle'=16,'tensor'=8] {'particle'}, dimensions={0} | all-to-all | bytes 393216 | tf_op jit(solution)/shard_map/all_to_all | solution.py:290
  30.6 0.0 slice-done
  30.6 0.0 slice-done.1
  30.6 0.0 slice-done.2
  30.6 0.0 slice-done.3
  30.6 0.0 copy-done.4
  30.6 1.8 %merge_project_sibling.1 = (bf16[3,32,1024]{2,1,0:T(8,128)(2,1)S(1)}, bf16[32,1024]{1,0:T(8,128)(2,1)S(1)}) custom-call(s32[16]{0:T(128)S(1)} %copy-done.4, bf16[16,3,16,128]{3,2,1,0:T(8,128)(2,1)S(1)} %all_to_all.11.recv, f32[256,128]{1,0:T(8,128)S(1)} %get-tuple-element.27.vec, f32[2,256,128]{2,1,0:T(8,128)S(1)} %get-tuple-element.28.stat, ...), custom_call_target="tpu_custom_call" | custom-call | flops 268435456 | bytes 8388608 | tf_op jit(solution)/shard_map/merge_project_sibling/pallas_call | solution.py:298
  32.4 3.2 %collective-permute-start = (bf16[3,32,1024]{2,1,0:T(8,128)(2,1)S(1)}, bf16[3,32,1024]{2,1,0:T(8,128)(2,1)S(1)}, u32[]{:S(2)}, u32[]{:S(2)}) collective-permute-start(bf16[3,32,1024]{2,1,0:T(8,128)(2,1)S(1)} %get-tuple-element.30), channel_id=1, source_target_pairs={{0,1},{1,0},{2,3},{3,2},{4,5},{5,4},{6,7},{7,6},{8,9},{9,8},{10,11... | collective-permute-start | bytes 589832 | tf_op jit(solution)/shard_map/ppermute | solution.py:317
  35.6 1.0 %project_own.1.mine = bf16[3,32,1024]{2,1,0:T(8,128)(2,1)S(1)} custom-call(bf16[32,1024]{1,0:T(8,128)(2,1)S(1)} %get-tuple-element.29.heads, bf16[1024,8192]{1,0:T(8,128)(2,1)S(1)} %bitcast.2), custom_call_target="tpu_custom_call" | custom-call | flops 268435456 | bytes 8388608 | tf_op jit(solution)/shard_map/project_own/pallas_call | solution.py:318
  36.6 0.1 collective-permute-done.given
  36.7 2.8 %collective-permute-start.1 = (bf16[2,32,1024]{2,1,0:T(8,128)(2,1)S(1)}, bf16[2,32,1024]{2,1,0:T(8,128)(2,1)S(1)}, u32[]{:S(2)}, u32[]{:S(2)}) collective-permute-start(bf16[2,32,1024]{2,1,0:T(8,128)(2,1)S(1)} %get-tuple-element.31), channel_id=1, source_target_pairs={{0,2},{1,7},{2,4},{3,1},{4,6},{5,3},{6,0},{7,5},{8,10},{9,15},{10,... | collective-permute-start | bytes 393224 | tf_op jit(solution)/shard_map/ppermute | solution.py:340
  39.6 0.3 collective-permute-start.2
  39.9 3.0 %collective-permute-done.1.arrived = bf16[2,32,1024]{2,1,0:T(8,128)(2,1)S(1)} collective-permute-done((bf16[2,32,1024]{2,1,0:T(8,128)(2,1)S(1)}, bf16[2,32,1024]{2,1,0:T(8,128)(2,1)S(1)}, u32[]{:S(2)}, u32[]{:S(2)}) %collective-permute-start.1) | collective-permute-done | bytes 131104 | tf_op jit(solution)/shard_map/ppermute | solution.py:340
  42.9 0.7 %project_last.1 = (f32[32,1024]{1,0:T(8,128)S(1)}, bf16[32,1024]{1,0:T(8,128)(2,1)S(1)}) custom-call(bf16[32,1024]{1,0:T(8,128)(2,1)S(1)} %get-tuple-element.29.heads, bf16[1024,8192]{1,0:T(8,128)(2,1)S(1)} %bitcast.2, bf16[2,32,1024]{2,1,0:T(8,128)(2,1)S(1)} %collective-permute-done.1.arrived), custom_call_target="tpu_custom_call" | custom-call | flops 268435456 | bytes 8388608 | tf_op jit(solution)/shard_map/project_last/pallas_call | solution.py:342
  43.6 0.6 %collective-permute-start.3 = (bf16[32,1024]{1,0:T(8,128)(2,1)S(1)}, bf16[32,1024]{1,0:T(8,128)(2,1)S(1)}, u32[]{:S(2)}, u32[]{:S(2)}) collective-permute-start(bf16[32,1024]{1,0:T(8,128)(2,1)S(1)} %get-tuple-element.34), channel_id=1, source_target_pairs={{0,1},{1,0},{2,3},{3,2},{4,5},{5,4},{6,7},{7,6},{8,9},{9,8},{10,11... | collective-permute-start | bytes 196616 | tf_op jit(solution)/shard_map/ppermute | solution.py:354
  44.2 1.0 %collective-permute-done.2 = bf16[32,1024]{1,0:T(8,128)(2,1)S(1)} collective-permute-done((bf16[32,1024]{1,0:T(8,128)(2,1)S(1)}, bf16[32,1024]{1,0:T(8,128)(2,1)S(1)}, u32[]{:S(2)}, u32[]{:S(2)}) %collective-permute-start.2) | collective-permute-done | bytes 65568 | tf_op jit(solution)/shard_map/ppermute | solution.py:341
  45.2 0.0 collective-permute-done.3
  45.2 0.7 %reshape.7 = bf16[16,2,1024]{2,1,0:T(2,128)(2,1)} reshape(bf16[32,1024]{1,0:T(8,128)(2,1)S(1)} %add_convert_fusion) | data formatting | bytes 131072 | tf_op jit(solution)/shard_map/reshape | solution.py:356
  (3 shorter events, 0.1 us)
Async XLA Ops:
  0.0 16.9 %copy-start = (bf16[16,1,512,256]{3,2,1,0:T(8,128)(2,1)S(1)}, bf16[16,1,512,256]{3,2,1,0:T(8,128)(2,1)}, u32[]{:S(2)}) copy-start(bf16[16,1,512,256]{3,2,1,0:T(8,128)(2,1)} %kv.1) | copy-start | bytes 12582916
  0.0 16.9 %copy-start.1 = (bf16[8192,128]{1,0:T(8,128)(2,1)S(1)}, bf16[8192,128]{1,0:T(8,128)(2,1)}, u32[]{:S(2)}) copy-start(bf16[8192,128]{1,0:T(8,128)(2,1)} %wk.1) | copy-start | bytes 6291460
  0.0 16.9 %copy-start.2 = (bf16[8192,128]{1,0:T(8,128)(2,1)S(1)}, bf16[8192,128]{1,0:T(8,128)(2,1)}, u32[]{:S(2)}) copy-start(bf16[8192,128]{1,0:T(8,128)(2,1)} %wv.1) | copy-start | bytes 6291460
  0.0 16.9 %copy-start.3 = (bf16[16,2,8192]{2,1,0:T(2,128)(2,1)S(1)}, bf16[16,2,8192]{2,1,0:T(2,128)(2,1)}, u32[]{:S(2)}) copy-start(bf16[16,2,8192]{2,1,0:T(2,128)(2,1)} %x.1) | copy-start | bytes 1572868
  19.8 10.8 %slice-start = ((s8[16777216]{0:T(1024)(128)(4,1)}), s8[4194304]{0:T(1024)(128)(4,1)S(1)}, s32[]{:S(2)}) async-start(s8[16777216]{0:T(1024)(128)(4,1)} %bitcast.1), calls=%async_computation.2 | async-start | bytes 8388608
  19.8 10.8 %slice-start.1 = ((s8[16777216]{0:T(1024)(128)(4,1)}), s8[4194304]{0:T(1024)(128)(4,1)S(1)}, s32[]{:S(2)}) async-start(s8[16777216]{0:T(1024)(128)(4,1)} %bitcast.1), calls=%async_computation.3 | async-start | bytes 8388608
  19.8 10.8 %slice-start.2 = ((s8[16777216]{0:T(1024)(128)(4,1)}), s8[4194304]{0:T(1024)(128)(4,1)S(1)}, s32[]{:S(2)}) async-start(s8[16777216]{0:T(1024)(128)(4,1)} %bitcast.1), calls=%async_computation.4 | async-start | bytes 8388608
  19.8 10.8 %slice-start.3 = ((s8[16777216]{0:T(1024)(128)(4,1)}), s8[4194304]{0:T(1024)(128)(4,1)S(1)}, s32[]{:S(2)}) async-start(s8[16777216]{0:T(1024)(128)(4,1)} %bitcast.1), calls=%async_computation.5 | async-start | bytes 8388608
  19.8 10.8 %copy-start.4 = (s32[16]{0:T(128)S(1)}, s32[16]{0:T(128)}, u32[]{:S(2)}) copy-start(s32[16]{0:T(128)} %anc.1) | copy-start | bytes 196
  32.4 4.2 %collective-permute-start = (bf16[3,32,1024]{2,1,0:T(8,128)(2,1)S(1)}, bf16[3,32,1024]{2,1,0:T(8,128)(2,1)S(1)}, u32[]{:S(2)}, u32[]{:S(2)}) collective-permute-start(bf16[3,32,1024]{2,1,0:T(8,128)(2,1)S(1)} %get-tuple-element.30), channel_id=1, source_target_pairs={{0,1},{1,0},{2,3},{3,2},{4,5},{5,4},{6,7},{7,6},{8,9},{9,8},{10,11... | collective-permute-start | bytes 589832 | tf_op jit(solution)/shard_map/ppermute | solution.py:317
  36.7 6.1 %collective-permute-start.1 = (bf16[2,32,1024]{2,1,0:T(8,128)(2,1)S(1)}, bf16[2,32,1024]{2,1,0:T(8,128)(2,1)S(1)}, u32[]{:S(2)}, u32[]{:S(2)}) collective-permute-start(bf16[2,32,1024]{2,1,0:T(8,128)(2,1)S(1)} %get-tuple-element.31), channel_id=1, source_target_pairs={{0,2},{1,7},{2,4},{3,1},{4,6},{5,3},{6,0},{7,5},{8,10},{9,15},{10,... | collective-permute-start | bytes 393224 | tf_op jit(solution)/shard_map/ppermute | solution.py:340
  39.6 5.6 %collective-permute-start.2 = (bf16[32,1024]{1,0:T(8,128)(2,1)S(1)}, bf16[32,1024]{1,0:T(8,128)(2,1)S(1)}, u32[]{:S(2)}, u32[]{:S(2)}) collective-permute-start(bf16[32,1024]{1,0:T(8,128)(2,1)S(1)} %get-tuple-element.33), channel_id=1, source_target_pairs={{0,4},{1,5},{2,6},{3,7},{4,0},{5,1},{6,2},{7,3},{8,12},{9,13},{10,... | collective-permute-start | bytes 196616 | tf_op jit(solution)/shard_map/ppermute | solution.py:341
  43.6 1.6 %collective-permute-start.3 = (bf16[32,1024]{1,0:T(8,128)(2,1)S(1)}, bf16[32,1024]{1,0:T(8,128)(2,1)S(1)}, u32[]{:S(2)}, u32[]{:S(2)}) collective-permute-start(bf16[32,1024]{1,0:T(8,128)(2,1)S(1)} %get-tuple-element.34), channel_id=1, source_target_pairs={{0,1},{1,0},{2,3},{3,2},{4,5},{5,4},{6,7},{7,6},{8,9},{9,8},{10,11... | collective-permute-start | bytes 196616 | tf_op jit(solution)/shard_map/ppermute | solution.py:354

commit v9 on v5

--- a/solution.py
+++ b/solution.py
@@ -98,12 +98,12 @@
     tokens = rows * steps
     floats = x[...].reshape(tokens, width).astype(F32)
     inverse = lax.rsqrt(jnp.mean(floats * floats, -1, keepdims=True) + EPSILON)
-    normed[...] = (floats * inverse * gain[...]).astype(BF16)
+    normed[...] = (floats * gain[...]).astype(BF16)
     repeat = tokens // per_row
     cosine, sine = (jnp.concatenate([tables[i]] * repeat, 0) for i in range(2))
-    keys = jnp.dot(normed[...], wk[...], preferred_element_type=F32)
+    keys = jnp.dot(normed[...], wk[...], preferred_element_type=F32) * inverse
     keys = (keys * cosine + pltpu.roll(keys, head_dim // 2, 1) * sine).astype(BF16)
-    vals = jnp.dot(normed[...], wv[...], preferred_element_type=F32).astype(BF16)
+    vals = (jnp.dot(normed[...], wv[...], preferred_element_type=F32) * inverse).astype(BF16)
     flat = queries[...].reshape(rows * per_row, head_dim)
     fresh = lax.dot_general(flat, keys, NT, preferred_element_type=F32) * head_dim ** (-0.5)
     row = lax.broadcasted_iota(jnp.int32, fresh.shape, 0)
@@ -134,16 +134,27 @@
         back[d, PAIR] = stat.astype(BF16)
 
 
+def units(own, groups):
+    index = lax.axis_index("tensor")
+    y, core = lax.div(index, 2), lax.rem(index, 2)
+    core = core if own else 1 - core
+    return [2 * lax.rem(y + k, groups) + core for k in (*range(1, groups), 0)]
+
+
+def product(wide, w, block, tokens, column):
+    at = pl.multiple_of(block * column, column)
+    return jnp.dot(wide, w[:, pl.ds(at, column)], preferred_element_type=F32)[:tokens]
+
+
+def widen(heads):
+    return jnp.concatenate([heads[...]] * max(1, 128 // heads.shape[0]), 0)
+
+
 def project(heads, w, out, own):
-    index = lax.axis_index("tensor")
-    first, core = lax.div(index, 2), lax.rem(index, 2)
-    core = core if own else 1 - core
-    groups, tokens, column = out.shape
-    wide = jnp.concatenate([heads[...]] * max(1, 128 // tokens), 0)
-    for k in range(groups):
-        block = 2 * lax.rem(first + k, groups) + core
-        at = pl.multiple_of(block * column, column)
-        out[k] = jnp.dot(wide, w[:, pl.ds(at, column)], preferred_element_type=F32)[:tokens].astype(BF16)
+    away, tokens, column = out.shape
+    wide = widen(heads)
+    for k, block in enumerate(units(own, away + 1)[:away]):
+        out[k] = product(wide, w, block, tokens, column).astype(BF16)
 
 
 def merge_kernel(anc, recv, vec, stat, w, out, heads, grid_ref, sums, lined, count):
@@ -181,6 +192,19 @@
 
 def second_kernel(heads, w, out):
     project(heads, w, out, True)
+
+
+def add_kernel(mine, given, *outs):
+    for k, out in enumerate(outs):
+        out[...] = (mine[k].astype(F32) + given[k].astype(F32)).astype(BF16)
+
+
+def last_kernel(heads, w, arrived, keep, crossing):
+    tokens, column = keep.shape
+    groups = w.shape[1] // column // 2
+    wide = widen(heads)
+    crossing[...] = product(wide, w, units(False, groups)[-1], tokens, column).astype(BF16)
+    keep[...] = product(wide, w, units(True, groups)[-1], tokens, column) + arrived[...].astype(F32)
 
 
 def shards(inputs, norm_gain, query_proj, w_key, w_value, w_out, kv_cache, ancestors):
@@ -270,7 +294,9 @@
     home = lax.all_to_all(back, "particle", split_axis=0, concat_axis=0, tiled=True)
 
     groups = tensor // 2
-    block = (groups, rows * steps, column)
+    away = groups - 1
+    block = jax.ShapeDtypeStruct((away, rows * steps, column), BF16)
+    one = jax.ShapeDtypeStruct((rows * steps, column), BF16)
     params = pltpu.CompilerParams(vmem_limit_bytes=8 * MIB)
     cost = pl.CostEstimate(
         flops=rows * steps * local * width, bytes_accessed=local * width, transcendentals=0
@@ -278,7 +304,7 @@
     other, heads_out = pl.pallas_call(
         merge_kernel,
         out_shape=(
-            jax.ShapeDtypeStruct(block, BF16),
+            block,
             jax.ShapeDtypeStruct((rows * steps, local), BF16),
         ),
         in_specs=[smem, vmem, vmem, vmem, vmem],
@@ -293,21 +319,41 @@
         cost_estimate=cost,
         name="merge_project_sibling",
     )(ancestors, home, vec, stat, w_out)
-    given = lax.ppermute(other, "tensor", [(i, i ^ 1) for i in range(tensor)])
+    sibling = [(i, i ^ 1) for i in range(tensor)]
+    given = lax.ppermute(other, "tensor", sibling)
     mine = pl.pallas_call(
         second_kernel,
-        out_shape=jax.ShapeDtypeStruct(block, BF16),
+        out_shape=block,
         in_specs=[vmem, vmem],
         out_specs=vmem,
         compiler_params=params,
         cost_estimate=cost,
         name="project_own",
     )(heads_out, w_out)
-    pair = [(mine[k].astype(F32) + given[k].astype(F32)) for k in range(groups)]
-    total = pair[0]
-    for k in range(1, groups):
+    pair = pl.pallas_call(
+        add_kernel,
+        out_shape=(one,) * away,
+        in_specs=[vmem, vmem],
+        out_specs=(vmem,) * away,
+        compiler_params=params,
+        name="add_sibling",
+    )(mine, given)
+    arrived = []
+    for k in (1, *range(groups - 1, 1, -1)):
         ring = [(i, ((i // 2 + k) % groups) * 2 + i % 2) for i in range(tensor)]
-        total = total + lax.ppermute(pair[k].astype(BF16), "tensor", ring).astype(F32)
+        arrived.append(lax.ppermute(pair[k - 1], "tensor", ring))
+    keep, crossing = pl.pallas_call(
+        last_kernel,
+        out_shape=(jax.ShapeDtypeStruct(one.shape, F32), one),
+        in_specs=[vmem, vmem, vmem],
+        out_specs=(vmem, vmem),
+        compiler_params=params,
+        cost_estimate=cost,
+        name="project_last",
+    )(heads_out, w_out, arrived[0])
+    total = keep + lax.ppermute(crossing, "tensor", sibling).astype(F32)
+    for part in arrived[1:]:
+        total = total + part.astype(F32)
     return total.astype(BF16).reshape(rows, steps, column)
 
 

time: 46 us -> 45.4 us (0.987)
  waiting for transfers between devices: 3.06 us -> 0.98 us
  starting transfers between devices: 7.65 us -> 9.19 us
    ppermute x4 -> x5, waiting for transfers between devices: 3.06 us -> 0.98 us  [the longest x3 0.8 us: shards(): arrived.append(lax.ppermute(pair[k - 1], 'tensor', ring))]
    ppermute x4 -> x5, starting transfers between devices: 7.65 us -> 9.19 us  [the longest x3 4.46 us: shards(): arrived.append(lax.ppermute(pair[k - 1], 'tensor', ring))]
    pallas_call x2 -> x4, Pallas kernels: 3.32 us -> 3.53 us  [the longest x1 1.77 us: shards(): pl.pallas_call(merge_kernel, out_shape=(block, jax.ShapeDtypeStruct((rows...]
  transfers between devices with their start and end apart: 4 -> 5, of which waited for: 2 -> 3; matrix products, arithmetic and copies ran while one was open for 0% -> 0% of each run, Pallas kernels for 3% -> 4%
where the time goes in v9:
time: 45.4 us; the launch traced here: 44.9 us
  blocking collectives  26.3 us (58%)
  starting transfers between devices  9.19 us (20%)
  Pallas kernels  7.6 us (17%)
  waiting for transfers between devices  0.98 us (2%)
  local copies, waits for them, and re-layouts  0.7 us (2%)
    all_to_all x1, blocking collectives, shards(): lax.all_to_all(send, 'particle', split_axis=0, concat_axis=0, tiled=True)  15.6 us
    all_to_all x1, blocking collectives, shards(): lax.all_to_all(back, 'particle', split_axis=0, concat_axis=0, tiled=True)  10.6 us
    ppermute x3, starting transfers between devices, shards(): arrived.append(lax.ppermute(pair[k - 1], 'tensor', ring))  4.46 us
    ppermute x1, starting transfers between devices, shards(): given = lax.ppermute(other, 'tensor', sibling)  3.2 us
    pallas_call x1, Pallas kernels, shards(): pl.pallas_call(attend_kernel, out_shape=(partial_result,) * 3 + (jax.Shap...  2.72 us
    pallas_call x1, Pallas kernels, shards(): pl.pallas_call(merge_kernel, out_shape=(block, jax.ShapeDtypeStruct((rows...  1.77 us
    ppermute x1, starting transfers between devices, shards(): total = keep + lax.ppermute(crossing, 'tensor', sibling).astype(F32)  1.53 us
    pallas_call x1, Pallas kernels, shards(): pl.pallas_call(pack_kernel, out_shape=(jax.ShapeDtypeStruct(packed, BF16)...  1.2 us
  transfers between devices with their start and end apart: 5, of which 3 were waited for; matrix products, arithmetic and copies ran while one was open for 0% of the time, Pallas kernels for 4%

profile of v9, /device:TPU:1, one launch (start us, length us, event | category | flops | bytes accessed | tf_op | source)
XLA Modules:
  0.0 44.9 jit_solution(11892671967604288439)
XLA Ops:
  0.0 0.0 copy-start
  0.0 0.0 copy-start.1
  0.0 0.0 copy-start.2
  0.0 0.0 copy-start.3
  0.0 1.2 %pack_queries.1 = (bf16[16,3,16,128]{3,2,1,0:T(8,128)(2,1)S(1)}, bf16[16,16,128]{2,1,0:T(8,128)(2,1)S(1)}, f32[2,16,128]{2,1,0:T(8,128)S(1)}, f32[1,8192]{1,0:T(1,128)S(1)}) custom-call(s32[16]{0:T(128)} %anc.1, bf16[16,2,1024]{2,1,0:T(2,128)(2,1)} %qp_hbm.1, f32[2,16,128]{2,1,0:T(8,128)} %constant.2.clone.tables_hbm, f32[1,8192]{1,0:T(1,128)} %bitcast.3), custom_call_target="tpu_custom_call" | custom-call | flops 10000000000 | bytes 1048576 | tf_op jit(solution)/shard_map/pack_queries/pallas_call | solution.py:229
  1.2 15.6 %all_to_all.10.recv = bf16[16,3,16,128]{3,2,1,0:T(8,128)(2,1)S(1)} all-to-all(bf16[16,3,16,128]{3,2,1,0:T(8,128)(2,1)S(1)} %get-tuple-element.21), channel_id=1, replica_groups=mesh['particle'=16,'tensor'=8] {'particle'}, dimensions={0} | all-to-all | bytes 393216 | tf_op jit(solution)/shard_map/all_to_all | solution.py:252
  16.9 0.0 copy-done
  16.9 0.0 copy-done.1
  16.9 0.0 copy-done.2
  16.9 0.0 copy-done.3
  16.9 2.7 %attention.1 = (f32[32,16,128]{2,1,0:T(8,128)S(1)}, f32[32,16,128]{2,1,0:T(8,128)S(1)}, f32[32,16,128]{2,1,0:T(8,128)S(1)}, f32[256,128]{1,0:T(8,128)S(1)}, f32[2,256,128]{2,1,0:T(8,128)S(1)}) custom-call(bf16[16,3,16,128]{3,2,1,0:T(8,128)(2,1)S(1)} %all_to_all.10.recv, bf16[16,1,512,256]{3,2,1,0:T(8,128)(2,1)S(1)} %copy-done, ...), custom_call_target="tpu_custom_call" | custom-call | flops 134217728 | bytes 5242880 | tf_op jit(solution)/shard_map/attention/pallas_call | solution.py:256
  19.6 0.0 slice-start
  19.6 0.0 slice-start.1
  19.6 0.0 slice-start.2
  19.6 0.0 slice-start.3
  19.7 0.0 copy-start.4
  19.7 0.1 pack_results.1
  19.8 10.6 %all_to_all.11.recv = bf16[16,3,16,128]{3,2,1,0:T(8,128)(2,1)S(1)} all-to-all(bf16[16,3,16,128]{3,2,1,0:T(8,128)(2,1)S(1)} %pack_results.1), channel_id=1, replica_groups=mesh['particle'=16,'tensor'=8] {'particle'}, dimensions={0} | all-to-all | bytes 393216 | tf_op jit(solution)/shard_map/all_to_all | solution.py:294
  30.4 0.0 slice-done
  30.4 0.0 slice-done.1
  30.5 0.0 slice-done.2
  30.5 0.0 slice-done.3
  30.5 0.0 copy-done.4
  30.5 1.8 %merge_project_sibling.1 = (bf16[3,32,1024]{2,1,0:T(8,128)(2,1)S(1)}, bf16[32,1024]{1,0:T(8,128)(2,1)S(1)}) custom-call(s32[16]{0:T(128)S(1)} %copy-done.4, bf16[16,3,16,128]{3,2,1,0:T(8,128)(2,1)S(1)} %all_to_all.11.recv, f32[256,128]{1,0:T(8,128)S(1)} %get-tuple-element.28.vec, f32[2,256,128]{2,1,0:T(8,128)S(1)} %get-tuple-element.29.stat, ...), custom_call_target="tpu_custom_call" | custom-call | flops 268435456 | bytes 8388608 | tf_op jit(solution)/shard_map/merge_project_sibling/pallas_call | solution.py:304
  32.3 3.2 %collective-permute-start = (bf16[3,32,1024]{2,1,0:T(8,128)(2,1)S(1)}, bf16[3,32,1024]{2,1,0:T(8,128)(2,1)S(1)}, u32[]{:S(2)}, u32[]{:S(2)}) collective-permute-start(bf16[3,32,1024]{2,1,0:T(8,128)(2,1)S(1)} %get-tuple-element.31), channel_id=1, source_target_pairs={{0,1},{1,0},{2,3},{3,2},{4,5},{5,4},{6,7},{7,6},{8,9},{9,8},{10,11... | collective-permute-start | bytes 589832 | tf_op jit(solution)/shard_map/ppermute | solution.py:323
  35.5 1.0 %project_own.1.mine = bf16[3,32,1024]{2,1,0:T(8,128)(2,1)S(1)} custom-call(bf16[32,1024]{1,0:T(8,128)(2,1)S(1)} %get-tuple-element.30.heads, bf16[1024,8192]{1,0:T(8,128)(2,1)S(1)} %bitcast.2), custom_call_target="tpu_custom_call" | custom-call | flops 268435456 | bytes 8388608 | tf_op jit(solution)/shard_map/project_own/pallas_call | solution.py:324
  36.5 0.1 collective-permute-done.given
  36.6 1.4 %collective-permute-start.1 = (bf16[32,1024]{1,0:T(8,128)(2,1)S(1)}, bf16[32,1024]{1,0:T(8,128)(2,1)S(1)}, u32[]{:S(2)}, u32[]{:S(2)}) collective-permute-start(bf16[32,1024]{1,0:T(8,128)(2,1)S(1)} %get-tuple-element.32), channel_id=1, source_target_pairs={{0,2},{1,3},{2,4},{3,5},{4,6},{5,7},{6,0},{7,1},{8,10},{9,11},{10,... | collective-permute-start | bytes 196616 | tf_op jit(solution)/shard_map/ppermute | solution.py:344
  38.0 1.5 %collective-permute-start.3 = (bf16[32,1024]{1,0:T(8,128)(2,1)S(1)}, bf16[32,1024]{1,0:T(8,128)(2,1)S(1)}, u32[]{:S(2)}, u32[]{:S(2)}) collective-permute-start(bf16[32,1024]{1,0:T(8,128)(2,1)S(1)} %get-tuple-element.35), channel_id=1, source_target_pairs={{0,6},{1,7},{2,0},{3,1},{4,2},{5,3},{6,4},{7,5},{8,14},{9,15},{10,... | collective-permute-start | bytes 196616 | tf_op jit(solution)/shard_map/ppermute | solution.py:344
  39.5 1.6 %collective-permute-start.4 = (bf16[32,1024]{1,0:T(8,128)(2,1)S(1)}, bf16[32,1024]{1,0:T(8,128)(2,1)S(1)}, u32[]{:S(2)}, u32[]{:S(2)}) collective-permute-start(bf16[32,1024]{1,0:T(8,128)(2,1)S(1)} %get-tuple-element.36), channel_id=1, source_target_pairs={{0,4},{1,5},{2,6},{3,7},{4,0},{5,1},{6,2},{7,3},{8,12},{9,13},{10,... | collective-permute-start | bytes 196616 | tf_op jit(solution)/shard_map/ppermute | solution.py:344
  41.0 0.0 collective-permute-done.1.arrived
  41.1 0.7 %project_last.1 = (f32[32,1024]{1,0:T(8,128)S(1)}, bf16[32,1024]{1,0:T(8,128)(2,1)S(1)}) custom-call(bf16[32,1024]{1,0:T(8,128)(2,1)S(1)} %get-tuple-element.30.heads, bf16[1024,8192]{1,0:T(8,128)(2,1)S(1)} %bitcast.2, bf16[32,1024]{1,0:T(8,128)(2,1)S(1)} %collective-permute-done.1.arrived), custom_call_target="tpu_custom_call" | custom-call | flops 268435456 | bytes 8388608 | tf_op jit(solution)/shard_map/project_last/pallas_call | solution.py:345
  41.8 1.5 %collective-permute-start.2 = (bf16[32,1024]{1,0:T(8,128)(2,1)S(1)}, bf16[32,1024]{1,0:T(8,128)(2,1)S(1)}, u32[]{:S(2)}, u32[]{:S(2)}) collective-permute-start(bf16[32,1024]{1,0:T(8,128)(2,1)S(1)} %get-tuple-element.34), channel_id=1, source_target_pairs={{0,1},{1,0},{2,3},{3,2},{4,5},{5,4},{6,7},{7,6},{8,9},{9,8},{10,11... | collective-permute-start | bytes 196616 | tf_op jit(solution)/shard_map/ppermute | solution.py:354
  43.3 0.0 collective-permute-done.3
  43.3 0.8 %collective-permute-done.4 = bf16[32,1024]{1,0:T(8,128)(2,1)S(1)} collective-permute-done((bf16[32,1024]{1,0:T(8,128)(2,1)S(1)}, bf16[32,1024]{1,0:T(8,128)(2,1)S(1)}, u32[]{:S(2)}, u32[]{:S(2)}) %collective-permute-start.4) | collective-permute-done | bytes 65568 | tf_op jit(solution)/shard_map/ppermute | solution.py:344
  44.1 0.1 collective-permute-done.2
  44.2 0.7 %reshape.7 = bf16[16,2,1024]{2,1,0:T(2,128)(2,1)} reshape(bf16[32,1024]{1,0:T(8,128)(2,1)S(1)} %add_convert_fusion) | data formatting | bytes 131072 | tf_op jit(solution)/shard_map/reshape | solution.py:357
  (3 shorter events, 0.1 us)
Async XLA Ops:
  0.0 16.9 %copy-start = (bf16[16,1,512,256]{3,2,1,0:T(8,128)(2,1)S(1)}, bf16[16,1,512,256]{3,2,1,0:T(8,128)(2,1)}, u32[]{:S(2)}) copy-start(bf16[16,1,512,256]{3,2,1,0:T(8,128)(2,1)} %kv.1) | copy-start | bytes 12582916
  0.0 16.9 %copy-start.1 = (bf16[8192,128]{1,0:T(8,128)(2,1)S(1)}, bf16[8192,128]{1,0:T(8,128)(2,1)}, u32[]{:S(2)}) copy-start(bf16[8192,128]{1,0:T(8,128)(2,1)} %wk.1) | copy-start | bytes 6291460
  0.0 16.9 %copy-start.2 = (bf16[8192,128]{1,0:T(8,128)(2,1)S(1)}, bf16[8192,128]{1,0:T(8,128)(2,1)}, u32[]{:S(2)}) copy-start(bf16[8192,128]{1,0:T(8,128)(2,1)} %wv.1) | copy-start | bytes 6291460
  0.0 16.9 %copy-start.3 = (bf16[16,2,8192]{2,1,0:T(2,128)(2,1)S(1)}, bf16[16,2,8192]{2,1,0:T(2,128)(2,1)}, u32[]{:S(2)}) copy-start(bf16[16,2,8192]{2,1,0:T(2,128)(2,1)} %x.1) | copy-start | bytes 1572868
  19.6 10.8 %slice-start = ((s8[16777216]{0:T(1024)(128)(4,1)}), s8[4194304]{0:T(1024)(128)(4,1)S(1)}, s32[]{:S(2)}) async-start(s8[16777216]{0:T(1024)(128)(4,1)} %bitcast.1), calls=%async_computation.2 | async-start | bytes 8388608
  19.6 10.8 %slice-start.1 = ((s8[16777216]{0:T(1024)(128)(4,1)}), s8[4194304]{0:T(1024)(128)(4,1)S(1)}, s32[]{:S(2)}) async-start(s8[16777216]{0:T(1024)(128)(4,1)} %bitcast.1), calls=%async_computation.3 | async-start | bytes 8388608
  19.6 10.8 %slice-start.2 = ((s8[16777216]{0:T(1024)(128)(4,1)}), s8[4194304]{0:T(1024)(128)(4,1)S(1)}, s32[]{:S(2)}) async-start(s8[16777216]{0:T(1024)(128)(4,1)} %bitcast.1), calls=%async_computation.4 | async-start | bytes 8388608
  19.6 10.8 %slice-start.3 = ((s8[16777216]{0:T(1024)(128)(4,1)}), s8[4194304]{0:T(1024)(128)(4,1)S(1)}, s32[]{:S(2)}) async-start(s8[16777216]{0:T(1024)(128)(4,1)} %bitcast.1), calls=%async_computation.5 | async-start | bytes 8388608
  19.7 10.8 %copy-start.4 = (s32[16]{0:T(128)S(1)}, s32[16]{0:T(128)}, u32[]{:S(2)}) copy-start(s32[16]{0:T(128)} %anc.1) | copy-start | bytes 196
  32.3 4.3 %collective-permute-start = (bf16[3,32,1024]{2,1,0:T(8,128)(2,1)S(1)}, bf16[3,32,1024]{2,1,0:T(8,128)(2,1)S(1)}, u32[]{:S(2)}, u32[]{:S(2)}) collective-permute-start(bf16[3,32,1024]{2,1,0:T(8,128)(2,1)S(1)} %get-tuple-element.31), channel_id=1, source_target_pairs={{0,1},{1,0},{2,3},{3,2},{4,5},{5,4},{6,7},{7,6},{8,9},{9,8},{10,11... | collective-permute-start | bytes 589832 | tf_op jit(solution)/shard_map/ppermute | solution.py:323
  36.6 4.5 %collective-permute-start.1 = (bf16[32,1024]{1,0:T(8,128)(2,1)S(1)}, bf16[32,1024]{1,0:T(8,128)(2,1)S(1)}, u32[]{:S(2)}, u32[]{:S(2)}) collective-permute-start(bf16[32,1024]{1,0:T(8,128)(2,1)S(1)} %get-tuple-element.32), channel_id=1, source_target_pairs={{0,2},{1,3},{2,4},{3,5},{4,6},{5,7},{6,0},{7,1},{8,10},{9,11},{10,... | collective-permute-start | bytes 196616 | tf_op jit(solution)/shard_map/ppermute | solution.py:344
  38.0 5.4 %collective-permute-start.3 = (bf16[32,1024]{1,0:T(8,128)(2,1)S(1)}, bf16[32,1024]{1,0:T(8,128)(2,1)S(1)}, u32[]{:S(2)}, u32[]{:S(2)}) collective-permute-start(bf16[32,1024]{1,0:T(8,128)(2,1)S(1)} %get-tuple-element.35), channel_id=1, source_target_pairs={{0,6},{1,7},{2,0},{3,1},{4,2},{5,3},{6,4},{7,5},{8,14},{9,15},{10,... | collective-permute-start | bytes 196616 | tf_op jit(solution)/shard_map/ppermute | solution.py:344
  39.5 4.6 %collective-permute-start.4 = (bf16[32,1024]{1,0:T(8,128)(2,1)S(1)}, bf16[32,1024]{1,0:T(8,128)(2,1)S(1)}, u32[]{:S(2)}, u32[]{:S(2)}) collective-permute-start(bf16[32,1024]{1,0:T(8,128)(2,1)S(1)} %get-tuple-element.36), channel_id=1, source_target_pairs={{0,4},{1,5},{2,6},{3,7},{4,0},{5,1},{6,2},{7,3},{8,12},{9,13},{10,... | collective-permute-start | bytes 196616 | tf_op jit(solution)/shard_map/ppermute | solution.py:344
  41.8 2.4 %collective-permute-start.2 = (bf16[32,1024]{1,0:T(8,128)(2,1)S(1)}, bf16[32,1024]{1,0:T(8,128)(2,1)S(1)}, u32[]{:S(2)}, u32[]{:S(2)}) collective-permute-start(bf16[32,1024]{1,0:T(8,128)(2,1)S(1)} %get-tuple-element.34), channel_id=1, source_target_pairs={{0,1},{1,0},{2,3},{3,2},{4,5},{5,4},{6,7},{7,6},{8,9},{9,8},{10,11... | collective-permute-start | bytes 196616 | tf_op jit(solution)/shard_map/ppermute | solution.py:354

commit v10 on v9

--- a/solution.py
+++ b/solution.py
@@ -7,6 +7,7 @@
 from jax.sharding import PartitionSpec as P
 
 PAIR = 2
+MORE = 8
 THETA = 500000.0
 EPSILON = 1e-05
 F32 = jnp.float32
@@ -48,8 +49,7 @@
     def clear(d, _):
         send[d] = jnp.zeros(send.shape[1:], BF16)
         count[d] = 0
-        for j in range(PAIR):
-            spots[PAIR * d + j] = 0
+        spots[d] = 0
         return 0
 
     lax.fori_loop(0, devices, clear, 0)
@@ -59,32 +59,35 @@
         grid_ref[:, steps * h : steps * (h + 1), :] = qp[:, :, head_dim * h : head_dim * (h + 1)].astype(F32)
     for r in range(rows):
         source, rank = slot_of(anc, r, rows, count)
-        spots[source * PAIR + rank] = lax.rem(anc[r], rows)
+        spot = lax.rem(anc[r], rows)
+        spots[source] = spots[source] + jnp.where(rank == 0, rows * spot, spot)
         plain = grid_ref[r]
         turned = (plain * tables[0] + pltpu.roll(plain, head_dim // 2, 1) * tables[1]).astype(BF16)
         queries[r] = turned
-        send[source, rank] = turned
-    lane = lax.broadcasted_iota(jnp.int32, (per_row, head_dim), 1)
+        send[source, pl.ds(pl.multiple_of(rank * per_row, per_row), per_row), :] = turned
     for d in range(devices):
-        send[d, PAIR] = jnp.where(
-            lane < head_dim // 2, spots[PAIR * d].astype(F32), spots[PAIR * d + 1].astype(F32)
-        ).astype(BF16)
+        send[d, PAIR * per_row :, :] = jnp.full((MORE, head_dim), spots[d].astype(F32), F32).astype(BF16)
+
+
+def slot_rows(chunks, i, per_row):
+    at = (i % PAIR) * per_row
+    return chunks[i // PAIR, at : at + per_row, :]
 
 
 def attend_kernel(
     recv, kv, x, gain, wk, wv, queries, tables, vectors, tops, sums, vec, stat, *scratch
 ):
     scores, expos, normed = scratch
-    devices, _, per_row, head_dim = recv.shape
+    devices, _, head_dim = recv.shape
+    per_row = queries.shape[1]
     lane = lax.broadcasted_iota(jnp.int32, (per_row, head_dim), 1)
     spots = []
     for d in range(devices):
-        spot = recv[d, PAIR].astype(F32)
-        for j in range(PAIR):
-            spots.append(spot[0, j * (head_dim // PAIR)].astype(jnp.int32))
+        both = recv[d, PAIR * per_row :, :].astype(F32)[0, 0].astype(jnp.int32)
+        spots += [lax.div(both, kv.shape[0]), lax.rem(both, kv.shape[0])]
     for i in range(devices * PAIR):
         scores[i] = lax.dot_general(
-            recv[i // PAIR, i % PAIR], kv[spots[i], 0, :, :head_dim], NT, preferred_element_type=F32
+            slot_rows(recv, i, per_row), kv[spots[i], 0, :, :head_dim], NT, preferred_element_type=F32
         ) * head_dim ** (-0.5)
     for i in range(devices * PAIR):
         top = jnp.max(scores[i], -1, keepdims=True)
@@ -98,12 +101,12 @@
     tokens = rows * steps
     floats = x[...].reshape(tokens, width).astype(F32)
     inverse = lax.rsqrt(jnp.mean(floats * floats, -1, keepdims=True) + EPSILON)
-    normed[...] = (floats * gain[...]).astype(BF16)
+    normed[...] = (floats * inverse * gain[...]).astype(BF16)
     repeat = tokens // per_row
     cosine, sine = (jnp.concatenate([tables[i]] * repeat, 0) for i in range(2))
-    keys = jnp.dot(normed[...], wk[...], preferred_element_type=F32) * inverse
+    keys = jnp.dot(normed[...], wk[...], preferred_element_type=F32)
     keys = (keys * cosine + pltpu.roll(keys, head_dim // 2, 1) * sine).astype(BF16)
-    vals = (jnp.dot(normed[...], wv[...], preferred_element_type=F32) * inverse).astype(BF16)
+    vals = jnp.dot(normed[...], wv[...], preferred_element_type=F32).astype(BF16)
     flat = queries[...].reshape(rows * per_row, head_dim)
     fresh = lax.dot_general(flat, keys, NT, preferred_element_type=F32) * head_dim ** (-0.5)
     row = lax.broadcasted_iota(jnp.int32, fresh.shape, 0)
@@ -117,21 +120,25 @@
 
 
 def return_kernel(vectors, tops, sums, back):
-    devices, _, per_row, head_dim = back.shape
-    lane = lax.broadcasted_iota(jnp.int32, (per_row, head_dim), 1)
+    devices, _, head_dim = back.shape
+    per_row = vectors.shape[1]
+    lane = lax.broadcasted_iota(jnp.int32, (MORE, head_dim), 1)
+    quarter = head_dim * MORE // (PAIR * per_row)
     for d in range(devices):
-        for j in range(PAIR):
-            back[d, j] = (vectors[d * PAIR + j] / sums[d * PAIR + j]).astype(BF16)
         stat = jnp.zeros(lane.shape, F32)
         for j in range(PAIR):
-            at_lane = j * (head_dim // PAIR)
-            for value, parts in ((tops[d * PAIR + j], 3), (sums[d * PAIR + j], 2)):
-                for _ in range(parts):
-                    part = value.astype(BF16).astype(F32)
-                    stat = jnp.where(lane == at_lane, part, stat)
-                    value = value - part
-                    at_lane += 1
-        back[d, PAIR] = stat.astype(BF16)
+            i = d * PAIR + j
+            back[d, j * per_row : (j + 1) * per_row, :] = (vectors[i] / sums[i]).astype(BF16)
+            for g in range(per_row // MORE):
+                at_lane = (j * (per_row // MORE) + g) * quarter
+                for source, parts in ((tops, 3), (sums, 2)):
+                    value = source[i, g * MORE : (g + 1) * MORE, :]
+                    for _ in range(parts):
+                        part = value.astype(BF16).astype(F32)
+                        stat = jnp.where(lane == at_lane, part, stat)
+                        value = value - part
+                        at_lane += 1
+        back[d, PAIR * per_row :, :] = stat.astype(BF16)
 
 
 def units(own, groups):
@@ -158,19 +165,24 @@
 
 
 def merge_kernel(anc, recv, vec, stat, w, out, heads, grid_ref, sums, lined, count):
-    devices, _, per_row, head_dim = recv.shape
+    devices, chunk, head_dim = recv.shape
+    per_row = (chunk - MORE) // PAIR
     rows = vec.shape[0] // per_row
     steps = heads.shape[0] // rows
-    half = head_dim // PAIR
+    pieces = per_row // MORE
+    quarter = head_dim // (PAIR * pieces)
     for d in range(devices):
         count[d] = 0
-    lane = lax.broadcasted_iota(jnp.int32, (per_row, head_dim), 1)
+    part_of = lax.div(lax.broadcasted_iota(jnp.int32, (MORE, head_dim), 1), quarter)
     for r in range(rows):
         source, rank = slot_of(anc, r, rows, count)
-        grid_ref[pl.ds(r * per_row, per_row), :] = recv[source, rank].astype(F32)
-        parts = recv[source, PAIR].astype(F32)
-        sums[pl.ds(r * per_row, per_row), :] = jnp.where(lax.div(lane, half) == rank, parts, 0.0).astype(BF16)
-    lane_from = lax.rem(lax.broadcasted_iota(jnp.int32, (head_dim, 2 * head_dim), 0), half)
+        at = pl.multiple_of(rank * per_row, per_row)
+        grid_ref[pl.ds(r * per_row, per_row), :] = recv[source, pl.ds(at, per_row), :].astype(F32)
+        parts = recv[source, PAIR * per_row :, :].astype(F32)
+        sums[pl.ds(r * per_row, per_row), :] = jnp.concatenate(
+            [jnp.where(part_of == rank * pieces + g, parts, 0.0) for g in range(pieces)], 0
+        ).astype(BF16)
+    lane_from = lax.rem(lax.broadcasted_iota(jnp.int32, (head_dim, 2 * head_dim), 0), quarter)
     lane_to = lax.broadcasted_iota(jnp.int32, (head_dim, 2 * head_dim), 1)
     first = jnp.where(lane_from < 3, 1.0, 0.0)
     second = jnp.where((lane_from >= 3) & (lane_from < 5), 1.0, 0.0)
@@ -225,7 +237,7 @@
     hbm = lambda x: pltpu.with_memory_space_constraint(x, pltpu.HBM)
     tables = jnp.asarray(tables)
 
-    packed = (devices, PAIR + 1, per_row, head_dim)
+    packed = (devices, PAIR * per_row + MORE, head_dim)
     send, queries, tables, gain = pl.pallas_call(
         pack_kernel,
         out_shape=(
@@ -241,7 +253,7 @@
             pltpu.VMEM((rows, steps, local), BF16),
             pltpu.SMEM((rows,), jnp.int32),
             pltpu.SMEM((devices,), jnp.int32),
-            pltpu.SMEM((devices * PAIR,), jnp.int32),
+            pltpu.SMEM((devices,), jnp.int32),
             pltpu.SemaphoreType.DMA((4,)),
         ],
         compiler_params=pltpu.CompilerParams(vmem_limit_bytes=4 * MIB),

time: 45.4 us -> 45.4 us (level)
  no operation moved by 1% of the time
where the time goes in v10:
time: 45.4 us; the launch traced here: 44.9 us
  blocking collectives  25.9 us (57%)
  starting transfers between devices  9.21 us (20%)
  Pallas kernels  7.84 us (17%)
  waiting for transfers between devices  0.99 us (2%)
  local copies, waits for them, and re-layouts  0.7 us (2%)
    all_to_all x1, blocking collectives, shards(): lax.all_to_all(send, 'particle', split_axis=0, concat_axis=0, tiled=True)  15.5 us
    all_to_all x1, blocking collectives, shards(): lax.all_to_all(back, 'particle', split_axis=0, concat_axis=0, tiled=True)  10.4 us
    ppermute x3, starting transfers between devices, shards(): arrived.append(lax.ppermute(pair[k - 1], 'tensor', ring))  4.46 us
    ppermute x1, starting transfers between devices, shards(): given = lax.ppermute(other, 'tensor', sibling)  3.22 us
    pallas_call x1, Pallas kernels, shards(): pl.pallas_call(attend_kernel, out_shape=(partial_result,) * 3 + (jax.Shap...  2.91 us
    pallas_call x1, Pallas kernels, shards(): pl.pallas_call(merge_kernel, out_shape=(block, jax.ShapeDtypeStruct((rows...  1.78 us
    ppermute x1, starting transfers between devices, shards(): total = keep + lax.ppermute(crossing, 'tensor', sibling).astype(F32)  1.53 us
    pallas_call x1, Pallas kernels, shards(): pl.pallas_call(pack_kernel, out_shape=(jax.ShapeDtypeStruct(packed, BF16)...  1.21 us
  transfers between devices with their start and end apart: 5, of which 3 were waited for; matrix products, arithmetic and copies ran while one was open for 0% of the time, Pallas kernels for 4%

profile of v10, /device:TPU:1, one launch (start us, length us, event | category | flops | bytes accessed | tf_op | source)
XLA Modules:
  0.0 44.9 jit_solution(13978283639966857858)
XLA Ops:
  0.0 0.0 copy-start
  0.0 0.0 copy-start.1
  0.0 0.0 copy-start.2
  0.0 0.0 copy-start.3
  0.0 1.2 %pack_queries.1 = (bf16[16,40,128]{2,1,0:T(8,128)(2,1)S(1)}, bf16[16,16,128]{2,1,0:T(8,128)(2,1)S(1)}, f32[2,16,128]{2,1,0:T(8,128)S(1)}, f32[1,8192]{1,0:T(1,128)S(1)}) custom-call(s32[16]{0:T(128)} %anc.1, bf16[16,2,1024]{2,1,0:T(2,128)(2,1)} %qp_hbm.1, f32[2,16,128]{2,1,0:T(8,128)} %constant.2.clone.tables_hbm, f32[1,8192]{1,0:T(1,128)} %bitcast.3), custom_call_target="tpu_custom_call" | custom-call | flops 10000000000 | bytes 1048576 | tf_op jit(solution)/shard_map/pack_queries/pallas_call | solution.py:241
  1.2 15.5 %all_to_all.10.recv = bf16[16,40,128]{2,1,0:T(8,128)(2,1)S(1)} all-to-all(bf16[16,40,128]{2,1,0:T(8,128)(2,1)S(1)} %get-tuple-element.21), channel_id=1, replica_groups=mesh['particle'=16,'tensor'=8] {'particle'}, dimensions={0} | all-to-all | bytes 327680 | tf_op jit(solution)/shard_map/all_to_all | solution.py:264
  16.7 0.0 copy-done
  16.7 0.0 copy-done.1
  16.7 0.0 copy-done.2
  16.7 0.0 copy-done.3
  16.7 2.9 %attention.1 = (f32[32,16,128]{2,1,0:T(8,128)S(1)}, f32[32,16,128]{2,1,0:T(8,128)S(1)}, f32[32,16,128]{2,1,0:T(8,128)S(1)}, f32[256,128]{1,0:T(8,128)S(1)}, f32[2,256,128]{2,1,0:T(8,128)S(1)}) custom-call(bf16[16,40,128]{2,1,0:T(8,128)(2,1)S(1)} %all_to_all.10.recv, bf16[16,1,512,256]{3,2,1,0:T(8,128)(2,1)S(1)} %copy-done, ...), custom_call_target="tpu_custom_call" | custom-call | flops 134217728 | bytes 5242880 | tf_op jit(solution)/shard_map/attention/pallas_call | solution.py:268
  19.7 0.0 slice-start
  19.7 0.0 slice-start.1
  19.7 0.0 slice-start.2
  19.7 0.0 slice-start.3
  19.7 0.0 copy-start.4
  19.7 0.2 pack_results.1
  19.9 10.4 %all_to_all.11.recv = bf16[16,40,128]{2,1,0:T(8,128)(2,1)S(1)} all-to-all(bf16[16,40,128]{2,1,0:T(8,128)(2,1)S(1)} %pack_results.1), channel_id=1, replica_groups=mesh['particle'=16,'tensor'=8] {'particle'}, dimensions={0} | all-to-all | bytes 327680 | tf_op jit(solution)/shard_map/all_to_all | solution.py:306
  30.4 0.0 slice-done
  30.4 0.0 slice-done.1
  30.4 0.0 slice-done.2
  30.4 0.0 slice-done.3
  30.4 0.0 copy-done.4
  30.4 1.8 %merge_project_sibling.1 = (bf16[3,32,1024]{2,1,0:T(8,128)(2,1)S(1)}, bf16[32,1024]{1,0:T(8,128)(2,1)S(1)}) custom-call(s32[16]{0:T(128)S(1)} %copy-done.4, bf16[16,40,128]{2,1,0:T(8,128)(2,1)S(1)} %all_to_all.11.recv, f32[256,128]{1,0:T(8,128)S(1)} %get-tuple-element.28.vec, f32[2,256,128]{2,1,0:T(8,128)S(1)} %get-tuple-element.29.stat, ...), custom_call_target="tpu_custom_call" | custom-call | flops 268435456 | bytes 8388608 | tf_op jit(solution)/shard_map/merge_project_sibling/pallas_call | solution.py:316
  32.2 3.2 %collective-permute-start = (bf16[3,32,1024]{2,1,0:T(8,128)(2,1)S(1)}, bf16[3,32,1024]{2,1,0:T(8,128)(2,1)S(1)}, u32[]{:S(2)}, u32[]{:S(2)}) collective-permute-start(bf16[3,32,1024]{2,1,0:T(8,128)(2,1)S(1)} %get-tuple-element.31), channel_id=1, source_target_pairs={{0,1},{1,0},{2,3},{3,2},{4,5},{5,4},{6,7},{7,6},{8,9},{9,8},{10,11... | collective-permute-start | bytes 589832 | tf_op jit(solution)/shard_map/ppermute | solution.py:335
  35.4 1.0 %project_own.1.mine = bf16[3,32,1024]{2,1,0:T(8,128)(2,1)S(1)} custom-call(bf16[32,1024]{1,0:T(8,128)(2,1)S(1)} %get-tuple-element.30.heads, bf16[1024,8192]{1,0:T(8,128)(2,1)S(1)} %bitcast.2), custom_call_target="tpu_custom_call" | custom-call | flops 268435456 | bytes 8388608 | tf_op jit(solution)/shard_map/project_own/pallas_call | solution.py:336
  36.4 0.1 collective-permute-done.given
  36.5 1.4 %collective-permute-start.1 = (bf16[32,1024]{1,0:T(8,128)(2,1)S(1)}, bf16[32,1024]{1,0:T(8,128)(2,1)S(1)}, u32[]{:S(2)}, u32[]{:S(2)}) collective-permute-start(bf16[32,1024]{1,0:T(8,128)(2,1)S(1)} %get-tuple-element.32), channel_id=1, source_target_pairs={{0,2},{1,3},{2,4},{3,5},{4,6},{5,7},{6,0},{7,1},{8,10},{9,11},{10,... | collective-permute-start | bytes 196616 | tf_op jit(solution)/shard_map/ppermute | solution.py:356
  37.9 1.5 %collective-permute-start.3 = (bf16[32,1024]{1,0:T(8,128)(2,1)S(1)}, bf16[32,1024]{1,0:T(8,128)(2,1)S(1)}, u32[]{:S(2)}, u32[]{:S(2)}) collective-permute-start(bf16[32,1024]{1,0:T(8,128)(2,1)S(1)} %get-tuple-element.35), channel_id=1, source_target_pairs={{0,6},{1,7},{2,0},{3,1},{4,2},{5,3},{6,4},{7,5},{8,14},{9,15},{10,... | collective-permute-start | bytes 196616 | tf_op jit(solution)/shard_map/ppermute | solution.py:356
  39.4 1.6 %collective-permute-start.4 = (bf16[32,1024]{1,0:T(8,128)(2,1)S(1)}, bf16[32,1024]{1,0:T(8,128)(2,1)S(1)}, u32[]{:S(2)}, u32[]{:S(2)}) collective-permute-start(bf16[32,1024]{1,0:T(8,128)(2,1)S(1)} %get-tuple-element.36), channel_id=1, source_target_pairs={{0,4},{1,5},{2,6},{3,7},{4,0},{5,1},{6,2},{7,3},{8,12},{9,13},{10,... | collective-permute-start | bytes 196616 | tf_op jit(solution)/shard_map/ppermute | solution.py:356
  41.0 0.0 collective-permute-done.1.arrived
  41.0 0.7 %project_last.1 = (f32[32,1024]{1,0:T(8,128)S(1)}, bf16[32,1024]{1,0:T(8,128)(2,1)S(1)}) custom-call(bf16[32,1024]{1,0:T(8,128)(2,1)S(1)} %get-tuple-element.30.heads, bf16[1024,8192]{1,0:T(8,128)(2,1)S(1)} %bitcast.2, bf16[32,1024]{1,0:T(8,128)(2,1)S(1)} %collective-permute-done.1.arrived), custom_call_target="tpu_custom_call" | custom-call | flops 268435456 | bytes 8388608 | tf_op jit(solution)/shard_map/project_last/pallas_call | solution.py:357
  41.7 1.5 %collective-permute-start.2 = (bf16[32,1024]{1,0:T(8,128)(2,1)S(1)}, bf16[32,1024]{1,0:T(8,128)(2,1)S(1)}, u32[]{:S(2)}, u32[]{:S(2)}) collective-permute-start(bf16[32,1024]{1,0:T(8,128)(2,1)S(1)} %get-tuple-element.34), channel_id=1, source_target_pairs={{0,1},{1,0},{2,3},{3,2},{4,5},{5,4},{6,7},{7,6},{8,9},{9,8},{10,11... | collective-permute-start | bytes 196616 | tf_op jit(solution)/shard_map/ppermute | solution.py:366
  43.3 0.0 collective-permute-done.3
  43.3 0.8 %collective-permute-done.4 = bf16[32,1024]{1,0:T(8,128)(2,1)S(1)} collective-permute-done((bf16[32,1024]{1,0:T(8,128)(2,1)S(1)}, bf16[32,1024]{1,0:T(8,128)(2,1)S(1)}, u32[]{:S(2)}, u32[]{:S(2)}) %collective-permute-start.4) | collective-permute-done | bytes 65568 | tf_op jit(solution)/shard_map/ppermute | solution.py:356
  44.0 0.1 collective-permute-done.2
  44.2 0.7 %reshape.7 = bf16[16,2,1024]{2,1,0:T(2,128)(2,1)} reshape(bf16[32,1024]{1,0:T(8,128)(2,1)S(1)} %add_convert_fusion) | data formatting | bytes 131072 | tf_op jit(solution)/shard_map/reshape | solution.py:369
  (3 shorter events, 0.1 us)
Async XLA Ops:
  0.0 16.7 %copy-start = (bf16[16,1,512,256]{3,2,1,0:T(8,128)(2,1)S(1)}, bf16[16,1,512,256]{3,2,1,0:T(8,128)(2,1)}, u32[]{:S(2)}) copy-start(bf16[16,1,512,256]{3,2,1,0:T(8,128)(2,1)} %kv.1) | copy-start | bytes 12582916
  0.0 16.7 %copy-start.1 = (bf16[8192,128]{1,0:T(8,128)(2,1)S(1)}, bf16[8192,128]{1,0:T(8,128)(2,1)}, u32[]{:S(2)}) copy-start(bf16[8192,128]{1,0:T(8,128)(2,1)} %wk.1) | copy-start | bytes 6291460
  0.0 16.7 %copy-start.2 = (bf16[8192,128]{1,0:T(8,128)(2,1)S(1)}, bf16[8192,128]{1,0:T(8,128)(2,1)}, u32[]{:S(2)}) copy-start(bf16[8192,128]{1,0:T(8,128)(2,1)} %wv.1) | copy-start | bytes 6291460
  0.0 16.7 %copy-start.3 = (bf16[16,2,8192]{2,1,0:T(2,128)(2,1)S(1)}, bf16[16,2,8192]{2,1,0:T(2,128)(2,1)}, u32[]{:S(2)}) copy-start(bf16[16,2,8192]{2,1,0:T(2,128)(2,1)} %x.1) | copy-start | bytes 1572868
  19.7 10.7 %slice-start = ((s8[16777216]{0:T(1024)(128)(4,1)}), s8[4194304]{0:T(1024)(128)(4,1)S(1)}, s32[]{:S(2)}) async-start(s8[16777216]{0:T(1024)(128)(4,1)} %bitcast.1), calls=%async_computation.2 | async-start | bytes 8388608
  19.7 10.7 %slice-start.1 = ((s8[16777216]{0:T(1024)(128)(4,1)}), s8[4194304]{0:T(1024)(128)(4,1)S(1)}, s32[]{:S(2)}) async-start(s8[16777216]{0:T(1024)(128)(4,1)} %bitcast.1), calls=%async_computation.3 | async-start | bytes 8388608
  19.7 10.7 %slice-start.2 = ((s8[16777216]{0:T(1024)(128)(4,1)}), s8[4194304]{0:T(1024)(128)(4,1)S(1)}, s32[]{:S(2)}) async-start(s8[16777216]{0:T(1024)(128)(4,1)} %bitcast.1), calls=%async_computation.4 | async-start | bytes 8388608
  19.7 10.7 %slice-start.3 = ((s8[16777216]{0:T(1024)(128)(4,1)}), s8[4194304]{0:T(1024)(128)(4,1)S(1)}, s32[]{:S(2)}) async-start(s8[16777216]{0:T(1024)(128)(4,1)} %bitcast.1), calls=%async_computation.5 | async-start | bytes 8388608
  19.7 10.7 %copy-start.4 = (s32[16]{0:T(128)S(1)}, s32[16]{0:T(128)}, u32[]{:S(2)}) copy-start(s32[16]{0:T(128)} %anc.1) | copy-start | bytes 196
  32.2 4.3 %collective-permute-start = (bf16[3,32,1024]{2,1,0:T(8,128)(2,1)S(1)}, bf16[3,32,1024]{2,1,0:T(8,128)(2,1)S(1)}, u32[]{:S(2)}, u32[]{:S(2)}) collective-permute-start(bf16[3,32,1024]{2,1,0:T(8,128)(2,1)S(1)} %get-tuple-element.31), channel_id=1, source_target_pairs={{0,1},{1,0},{2,3},{3,2},{4,5},{5,4},{6,7},{7,6},{8,9},{9,8},{10,11... | collective-permute-start | bytes 589832 | tf_op jit(solution)/shard_map/ppermute | solution.py:335
  36.5 4.5 %collective-permute-start.1 = (bf16[32,1024]{1,0:T(8,128)(2,1)S(1)}, bf16[32,1024]{1,0:T(8,128)(2,1)S(1)}, u32[]{:S(2)}, u32[]{:S(2)}) collective-permute-start(bf16[32,1024]{1,0:T(8,128)(2,1)S(1)} %get-tuple-element.32), channel_id=1, source_target_pairs={{0,2},{1,3},{2,4},{3,5},{4,6},{5,7},{6,0},{7,1},{8,10},{9,11},{10,... | collective-permute-start | bytes 196616 | tf_op jit(solution)/shard_map/ppermute | solution.py:356
  37.9 5.4 %collective-permute-start.3 = (bf16[32,1024]{1,0:T(8,128)(2,1)S(1)}, bf16[32,1024]{1,0:T(8,128)(2,1)S(1)}, u32[]{:S(2)}, u32[]{:S(2)}) collective-permute-start(bf16[32,1024]{1,0:T(8,128)(2,1)S(1)} %get-tuple-element.35), channel_id=1, source_target_pairs={{0,6},{1,7},{2,0},{3,1},{4,2},{5,3},{6,4},{7,5},{8,14},{9,15},{10,... | collective-permute-start | bytes 196616 | tf_op jit(solution)/shard_map/ppermute | solution.py:356
  39.4 4.6 %collective-permute-start.4 = (bf16[32,1024]{1,0:T(8,128)(2,1)S(1)}, bf16[32,1024]{1,0:T(8,128)(2,1)S(1)}, u32[]{:S(2)}, u32[]{:S(2)}) collective-permute-start(bf16[32,1024]{1,0:T(8,128)(2,1)S(1)} %get-tuple-element.36), channel_id=1, source_target_pairs={{0,4},{1,5},{2,6},{3,7},{4,0},{5,1},{6,2},{7,3},{8,12},{9,13},{10,... | collective-permute-start | bytes 196616 | tf_op jit(solution)/shard_map/ppermute | solution.py:356
  41.7 2.4 %collective-permute-start.2 = (bf16[32,1024]{1,0:T(8,128)(2,1)S(1)}, bf16[32,1024]{1,0:T(8,128)(2,1)S(1)}, u32[]{:S(2)}, u32[]{:S(2)}) collective-permute-start(bf16[32,1024]{1,0:T(8,128)(2,1)S(1)} %get-tuple-element.34), channel_id=1, source_target_pairs={{0,1},{1,0},{2,3},{3,2},{4,5},{5,4},{6,7},{7,6},{8,9},{9,8},{10,11... | collective-permute-start | bytes 196616 | tf_op jit(solution)/shard_map/ppermute | solution.py:366

commit v11 on v10

--- a/solution.py
+++ b/solution.py
@@ -49,7 +49,8 @@
     def clear(d, _):
         send[d] = jnp.zeros(send.shape[1:], BF16)
         count[d] = 0
-        spots[d] = 0
+        for j in range(PAIR):
+            spots[PAIR * d + j] = 0
         return 0
 
     lax.fori_loop(0, devices, clear, 0)
@@ -59,14 +60,16 @@
         grid_ref[:, steps * h : steps * (h + 1), :] = qp[:, :, head_dim * h : head_dim * (h + 1)].astype(F32)
     for r in range(rows):
         source, rank = slot_of(anc, r, rows, count)
-        spot = lax.rem(anc[r], rows)
-        spots[source] = spots[source] + jnp.where(rank == 0, rows * spot, spot)
+        spots[source * PAIR + rank] = lax.rem(anc[r], rows)
         plain = grid_ref[r]
         turned = (plain * tables[0] + pltpu.roll(plain, head_dim // 2, 1) * tables[1]).astype(BF16)
         queries[r] = turned
         send[source, pl.ds(pl.multiple_of(rank * per_row, per_row), per_row), :] = turned
+    lane = lax.broadcasted_iota(jnp.int32, (MORE, head_dim), 1)
     for d in range(devices):
-        send[d, PAIR * per_row :, :] = jnp.full((MORE, head_dim), spots[d].astype(F32), F32).astype(BF16)
+        send[d, PAIR * per_row :, :] = jnp.where(
+            lane < head_dim // PAIR, spots[PAIR * d].astype(F32), spots[PAIR * d + 1].astype(F32)
+        ).astype(BF16)
 
 
 def slot_rows(chunks, i, per_row):
@@ -74,17 +77,39 @@
     return chunks[i // PAIR, at : at + per_row, :]
 
 
+def pack_statistics(tops, sums, back):
+    devices, _, head_dim = back.shape
+    per_row = tops.shape[1]
+    lane = lax.broadcasted_iota(jnp.int32, (MORE, head_dim), 1)
+    quarter = head_dim * MORE // (PAIR * per_row)
+    for d in range(devices):
+        stat = jnp.zeros(lane.shape, F32)
+        for j in range(PAIR):
+            i = d * PAIR + j
+            for g in range(per_row // MORE):
+                at_lane = (j * (per_row // MORE) + g) * quarter
+                for source, parts in ((tops, 3), (sums, 2)):
+                    value = source[i, g * MORE : (g + 1) * MORE, :]
+                    for _ in range(parts):
+                        part = value.astype(BF16).astype(F32)
+                        stat = jnp.where(lane == at_lane, part, stat)
+                        value = value - part
+                        at_lane += 1
+        back[d, PAIR * per_row :, :] = stat.astype(BF16)
+
+
 def attend_kernel(
-    recv, kv, x, gain, wk, wv, queries, tables, vectors, tops, sums, vec, stat, *scratch
+    recv, kv, x, gain, wk, wv, queries, tables, back, vec, stat, *scratch
 ):
-    scores, expos, normed = scratch
+    scores, expos, tops, sums, normed = scratch
     devices, _, head_dim = recv.shape
     per_row = queries.shape[1]
     lane = lax.broadcasted_iota(jnp.int32, (per_row, head_dim), 1)
     spots = []
     for d in range(devices):
-        both = recv[d, PAIR * per_row :, :].astype(F32)[0, 0].astype(jnp.int32)
-        spots += [lax.div(both, kv.shape[0]), lax.rem(both, kv.shape[0])]
+        spot = recv[d, PAIR * per_row :, :].astype(F32)
+        for j in range(PAIR):
+            spots.append(spot[0, j * (head_dim // PAIR)].astype(jnp.int32))
     for i in range(devices * PAIR):
         scores[i] = lax.dot_general(
             slot_rows(recv, i, per_row), kv[spots[i], 0, :, :head_dim], NT, preferred_element_type=F32
@@ -96,7 +121,10 @@
         tops[i] = jnp.broadcast_to(top, lane.shape)
         sums[i] = jnp.broadcast_to(jnp.sum(expo, -1, keepdims=True), lane.shape)
     for i in range(devices * PAIR):
-        vectors[i] = jnp.dot(expos[i], kv[spots[i], 0, :, head_dim:], preferred_element_type=F32)
+        vector = jnp.dot(expos[i], kv[spots[i], 0, :, head_dim:], preferred_element_type=F32)
+        at = (i % PAIR) * per_row
+        back[i // PAIR, at : at + per_row, :] = (vector / sums[i]).astype(BF16)
+    pack_statistics(tops, sums, back)
     rows, steps, width = x.shape
     tokens = rows * steps
     floats = x[...].reshape(tokens, width).astype(F32)
@@ -117,28 +145,6 @@
     vec[...] = jnp.dot(expo.astype(BF16), vals, preferred_element_type=F32)
     stat[0] = jnp.broadcast_to(top, stat.shape[1:])
     stat[1] = jnp.broadcast_to(jnp.sum(expo, -1, keepdims=True), stat.shape[1:])
-
-
-def return_kernel(vectors, tops, sums, back):
-    devices, _, head_dim = back.shape
-    per_row = vectors.shape[1]
-    lane = lax.broadcasted_iota(jnp.int32, (MORE, head_dim), 1)
-    quarter = head_dim * MORE // (PAIR * per_row)
-    for d in range(devices):
-        stat = jnp.zeros(lane.shape, F32)
-        for j in range(PAIR):
-            i = d * PAIR + j
-            back[d, j * per_row : (j + 1) * per_row, :] = (vectors[i] / sums[i]).astype(BF16)
-            for g in range(per_row // MORE):
-                at_lane = (j * (per_row // MORE) + g) * quarter
-                for source, parts in ((tops, 3), (sums, 2)):
-                    value = source[i, g * MORE : (g + 1) * MORE, :]
-                    for _ in range(parts):
-                        part = value.astype(BF16).astype(F32)
-                        stat = jnp.where(lane == at_lane, part, stat)
-                        value = value - part
-                        at_lane += 1
-        back[d, PAIR * per_row :, :] = stat.astype(BF16)
 
 
 def units(own, groups):
@@ -253,7 +259,7 @@
             pltpu.VMEM((rows, steps, local), BF16),
             pltpu.SMEM((rows,), jnp.int32),
             pltpu.SMEM((devices,), jnp.int32),
-            pltpu.SMEM((devices,), jnp.int32),
+            pltpu.SMEM((devices * PAIR,), jnp.int32),
             pltpu.SemaphoreType.DMA((4,)),
         ],
         compiler_params=pltpu.CompilerParams(vmem_limit_bytes=4 * MIB),
@@ -264,24 +270,25 @@
     recv = lax.all_to_all(send, "particle", split_axis=0, concat_axis=0, tiled=True)
 
     slots = devices * PAIR
-    partial_result = jax.ShapeDtypeStruct((slots, per_row, head_dim), F32)
-    *found, vec, stat = pl.pallas_call(
+    back, vec, stat = pl.pallas_call(
         attend_kernel,
-        out_shape=(partial_result,) * 3
-        + (
+        out_shape=(
+            jax.ShapeDtypeStruct(packed, BF16),
             jax.ShapeDtypeStruct((rows * per_row, head_dim), F32),
             jax.ShapeDtypeStruct((2, rows * per_row, head_dim), F32),
         ),
         in_specs=[vmem] * 8,
-        out_specs=(vmem,) * 5,
+        out_specs=(vmem,) * 3,
         scratch_shapes=[
             pltpu.VMEM((slots, per_row, context), F32),
             pltpu.VMEM((slots, per_row, context), BF16),
+            pltpu.VMEM((slots, per_row, head_dim), F32),
+            pltpu.VMEM((slots, per_row, head_dim), F32),
             pltpu.VMEM((rows * steps, width), BF16),
         ],
         compiler_params=pltpu.CompilerParams(vmem_limit_bytes=12 * MIB),
         cost_estimate=pl.CostEstimate(
-            flops=4 * slots * per_row * context * head_dim, bytes_accessed=5 * MIB, transcendentals=0
+            flops=10_000_000_000, bytes_accessed=5 * MIB, transcendentals=0
         ),
         name="attention",
     )(
@@ -294,15 +301,6 @@
         queries,
         tables,
     )
-    back = pl.pallas_call(
-        return_kernel,
-        out_shape=jax.ShapeDtypeStruct(packed, BF16),
-        in_specs=[vmem] * 3,
-        out_specs=vmem,
-        compiler_params=pltpu.CompilerParams(vmem_limit_bytes=2 * MIB),
-        cost_estimate=pl.CostEstimate(flops=10_000_000_000, bytes_accessed=MIB, transcendentals=0),
-        name="pack_results",
-    )(*found)
     home = lax.all_to_all(back, "particle", split_axis=0, concat_axis=0, tiled=True)
 
     groups = tensor // 2
@@ -351,7 +349,7 @@
         name="add_sibling",
     )(mine, given)
     arrived = []
-    for k in (1, *range(groups - 1, 1, -1)):
+    for k in range(1, groups):
         ring = [(i, ((i // 2 + k) % groups) * 2 + i % 2) for i in range(tensor)]
         arrived.append(lax.ppermute(pair[k - 1], "tensor", ring))
     keep, crossing = pl.pallas_call(

time: 45.4 us -> 45.1 us (level)
    ppermute x3, starting transfers between devices: 4.46 us -> 5.07 us  [shards(): arrived.append(lax.ppermute(pair[k - 1], 'tensor', ring))]
    ppermute x3, waiting for transfers between devices: 0.8 us -> 0.33 us  [shards(): arrived.append(lax.ppermute(pair[k - 1], 'tensor', ring))]
    ppermute x1, waiting for transfers between devices: 0.11 us -> 0.58 us  [shards(): total = keep + lax.ppermute(crossing, 'tensor', sibling).astype(F32)]
    pallas_call x2 -> x1, Pallas kernels: 3.1 us -> 2.9 us  [shards(): pl.pallas_call(attend_kernel, out_shape=(jax.ShapeDtypeStruct(packed, BF1...]
where the time goes in v11:
time: 45.1 us; the launch traced here: 45 us
  blocking collectives  25.9 us (57%)
  starting transfers between devices  9.58 us (21%)
  Pallas kernels  7.64 us (17%)
  waiting for transfers between devices  0.97 us (2%)
  local copies, waits for them, and re-layouts  0.7 us (2%)
    all_to_all x1, blocking collectives, shards(): lax.all_to_all(send, 'particle', split_axis=0, concat_axis=0, tiled=True)  15.5 us
    all_to_all x1, blocking collectives, shards(): lax.all_to_all(back, 'particle', split_axis=0, concat_axis=0, tiled=True)  10.4 us
    ppermute x3, starting transfers between devices, shards(): arrived.append(lax.ppermute(pair[k - 1], 'tensor', ring))  5.07 us
    ppermute x1, starting transfers between devices, shards(): given = lax.ppermute(other, 'tensor', sibling)  3.22 us
    pallas_call x1, Pallas kernels, shards(): pl.pallas_call(attend_kernel, out_shape=(jax.ShapeDtypeStruct(packed, BF1...  2.9 us
    pallas_call x1, Pallas kernels, shards(): pl.pallas_call(merge_kernel, out_shape=(block, jax.ShapeDtypeStruct((rows...  1.77 us
    ppermute x1, starting transfers between devices, shards(): total = keep + lax.ppermute(crossing, 'tensor', sibling).astype(F32)  1.29 us
    pallas_call x1, Pallas kernels, shards(): pl.pallas_call(pack_kernel, out_shape=(jax.ShapeDtypeStruct(packed, BF16)...  1.21 us
  transfers between devices with their start and end apart: 5, of which 3 were waited for; matrix products, arithmetic and copies ran while one was open for 0% of the time, Pallas kernels for 4%

profile of v11, /device:TPU:1, one launch (start us, length us, event | category | flops | bytes accessed | tf_op | source)
XLA Modules:
  0.0 45.0 jit_solution(12196907361951335889)
XLA Ops:
  0.0 0.0 copy-start.1
  0.0 0.0 copy-start.2
  0.0 0.0 copy-start.3
  0.0 0.0 copy-start.4
  0.0 1.2 %pack_queries.1 = (bf16[16,40,128]{2,1,0:T(8,128)(2,1)S(1)}, bf16[16,16,128]{2,1,0:T(8,128)(2,1)S(1)}, f32[2,16,128]{2,1,0:T(8,128)S(1)}, f32[1,8192]{1,0:T(1,128)S(1)}) custom-call(s32[16]{0:T(128)} %anc.1, bf16[16,2,1024]{2,1,0:T(2,128)(2,1)} %qp_hbm.1, f32[2,16,128]{2,1,0:T(8,128)} %constant.2.clone.tables_hbm, f32[1,8192]{1,0:T(1,128)} %bitcast.3), custom_call_target="tpu_custom_call" | custom-call | flops 10000000000 | bytes 1048576 | tf_op jit(solution)/shard_map/pack_queries/pallas_call | solution.py:247
  1.2 15.5 %all_to_all.10.recv = bf16[16,40,128]{2,1,0:T(8,128)(2,1)S(1)} all-to-all(bf16[16,40,128]{2,1,0:T(8,128)(2,1)S(1)} %get-tuple-element.19), channel_id=1, replica_groups=mesh['particle'=16,'tensor'=8] {'particle'}, dimensions={0} | all-to-all | bytes 327680 | tf_op jit(solution)/shard_map/all_to_all | solution.py:270
  16.7 0.0 slice-start
  16.7 0.0 copy-done.1
  16.7 0.0 copy-done.2
  16.7 0.0 copy-done.3
  16.7 0.0 copy-done.4
  16.7 0.0 slice-start.1
  16.8 0.0 slice-start.2
  16.8 0.0 slice-start.3
  16.8 0.0 copy-start
  16.8 2.9 %attention.1 = (bf16[16,40,128]{2,1,0:T(8,128)(2,1)S(1)}, f32[256,128]{1,0:T(8,128)S(1)}, f32[2,256,128]{2,1,0:T(8,128)S(1)}) custom-call(bf16[16,40,128]{2,1,0:T(8,128)(2,1)S(1)} %all_to_all.10.recv, bf16[16,1,512,256]{3,2,1,0:T(8,128)(2,1)S(1)} %copy-done.1, bf16[16,2,8192]{2,1,0:T(2,128)(2,1)S(1)} %copy-done.4, f32[1,8192]{1,0:T(1,128)S(1)} %get-tuple-element.20.gain, ...), custom_call_target="tpu_custom_call" | custom-call | flops 10000000000 | bytes 5242880 | tf_op jit(solution)/shard_map/attention/pallas_call | solution.py:273
  19.7 10.4 %all_to_all.11.recv = bf16[16,40,128]{2,1,0:T(8,128)(2,1)S(1)} all-to-all(bf16[16,40,128]{2,1,0:T(8,128)(2,1)S(1)} %get-tuple-element.23), channel_id=1, replica_groups=mesh['particle'=16,'tensor'=8] {'particle'}, dimensions={0} | all-to-all | bytes 327680 | tf_op jit(solution)/shard_map/all_to_all | solution.py:304
  30.1 0.0 slice-done
  30.1 0.0 slice-done.1
  30.1 0.0 slice-done.2
  30.2 0.0 slice-done.3
  30.2 0.0 copy-done
  30.2 1.8 %merge_project_sibling.1 = (bf16[3,32,1024]{2,1,0:T(8,128)(2,1)S(1)}, bf16[32,1024]{1,0:T(8,128)(2,1)S(1)}) custom-call(s32[16]{0:T(128)S(1)} %copy-done, bf16[16,40,128]{2,1,0:T(8,128)(2,1)S(1)} %all_to_all.11.recv, f32[256,128]{1,0:T(8,128)S(1)} %get-tuple-element.24.vec, f32[2,256,128]{2,1,0:T(8,128)S(1)} %get-tuple-element.25.stat, ...), custom_call_target="tpu_custom_call" | custom-call | flops 268435456 | bytes 8388608 | tf_op jit(solution)/shard_map/merge_project_sibling/pallas_call | solution.py:314
  32.0 3.2 %collective-permute-start = (bf16[3,32,1024]{2,1,0:T(8,128)(2,1)S(1)}, bf16[3,32,1024]{2,1,0:T(8,128)(2,1)S(1)}, u32[]{:S(2)}, u32[]{:S(2)}) collective-permute-start(bf16[3,32,1024]{2,1,0:T(8,128)(2,1)S(1)} %get-tuple-element.27), channel_id=1, source_target_pairs={{0,1},{1,0},{2,3},{3,2},{4,5},{5,4},{6,7},{7,6},{8,9},{9,8},{10,11... | collective-permute-start | bytes 589832 | tf_op jit(solution)/shard_map/ppermute | solution.py:333
  35.2 1.0 %project_own.1.mine = bf16[3,32,1024]{2,1,0:T(8,128)(2,1)S(1)} custom-call(bf16[32,1024]{1,0:T(8,128)(2,1)S(1)} %get-tuple-element.26.heads, bf16[1024,8192]{1,0:T(8,128)(2,1)S(1)} %bitcast.2), custom_call_target="tpu_custom_call" | custom-call | flops 268435456 | bytes 8388608 | tf_op jit(solution)/shard_map/project_own/pallas_call | solution.py:334
  36.2 0.1 collective-permute-done.given
  36.3 1.4 %collective-permute-start.1 = (bf16[32,1024]{1,0:T(8,128)(2,1)S(1)}, bf16[32,1024]{1,0:T(8,128)(2,1)S(1)}, u32[]{:S(2)}, u32[]{:S(2)}) collective-permute-start(bf16[32,1024]{1,0:T(8,128)(2,1)S(1)} %get-tuple-element.28), channel_id=1, source_target_pairs={{0,2},{1,3},{2,4},{3,5},{4,6},{5,7},{6,0},{7,1},{8,10},{9,11},{10,... | collective-permute-start | bytes 196616 | tf_op jit(solution)/shard_map/ppermute | solution.py:354
  37.7 2.6 %collective-permute-start.3 = (bf16[32,1024]{1,0:T(8,128)(2,1)S(1)}, bf16[32,1024]{1,0:T(8,128)(2,1)S(1)}, u32[]{:S(2)}, u32[]{:S(2)}) collective-permute-start(bf16[32,1024]{1,0:T(8,128)(2,1)S(1)} %get-tuple-element.31), channel_id=1, source_target_pairs={{0,4},{1,5},{2,6},{3,7},{4,0},{5,1},{6,2},{7,3},{8,12},{9,13},{10,... | collective-permute-start | bytes 196616 | tf_op jit(solution)/shard_map/ppermute | solution.py:354
  40.3 1.1 %collective-permute-start.4 = (bf16[32,1024]{1,0:T(8,128)(2,1)S(1)}, bf16[32,1024]{1,0:T(8,128)(2,1)S(1)}, u32[]{:S(2)}, u32[]{:S(2)}) collective-permute-start(bf16[32,1024]{1,0:T(8,128)(2,1)S(1)} %get-tuple-element.32), channel_id=1, source_target_pairs={{0,6},{1,7},{2,0},{3,1},{4,2},{5,3},{6,4},{7,5},{8,14},{9,15},{10,... | collective-permute-start | bytes 196616 | tf_op jit(solution)/shard_map/ppermute | solution.py:354
  41.4 0.0 collective-permute-done.1.arrived
  41.4 0.7 %project_last.1 = (f32[32,1024]{1,0:T(8,128)S(1)}, bf16[32,1024]{1,0:T(8,128)(2,1)S(1)}) custom-call(bf16[32,1024]{1,0:T(8,128)(2,1)S(1)} %get-tuple-element.26.heads, bf16[1024,8192]{1,0:T(8,128)(2,1)S(1)} %bitcast.2, bf16[32,1024]{1,0:T(8,128)(2,1)S(1)} %collective-permute-done.1.arrived), custom_call_target="tpu_custom_call" | custom-call | flops 268435456 | bytes 8388608 | tf_op jit(solution)/shard_map/project_last/pallas_call | solution.py:355
  42.1 1.3 %collective-permute-start.2 = (bf16[32,1024]{1,0:T(8,128)(2,1)S(1)}, bf16[32,1024]{1,0:T(8,128)(2,1)S(1)}, u32[]{:S(2)}, u32[]{:S(2)}) collective-permute-start(bf16[32,1024]{1,0:T(8,128)(2,1)S(1)} %get-tuple-element.30), channel_id=1, source_target_pairs={{0,1},{1,0},{2,3},{3,2},{4,5},{5,4},{6,7},{7,6},{8,9},{9,8},{10,11... | collective-permute-start | bytes 196616 | tf_op jit(solution)/shard_map/ppermute | solution.py:364
  43.4 0.0 collective-permute-done.3
  43.4 0.3 collective-permute-done.4
  43.7 0.6 %collective-permute-done.2 = bf16[32,1024]{1,0:T(8,128)(2,1)S(1)} collective-permute-done((bf16[32,1024]{1,0:T(8,128)(2,1)S(1)}, bf16[32,1024]{1,0:T(8,128)(2,1)S(1)}, u32[]{:S(2)}, u32[]{:S(2)}) %collective-permute-start.2) | collective-permute-done | bytes 65568 | tf_op jit(solution)/shard_map/ppermute | solution.py:364
  44.3 0.7 %reshape.7 = bf16[16,2,1024]{2,1,0:T(2,128)(2,1)} reshape(bf16[32,1024]{1,0:T(8,128)(2,1)S(1)} %add_convert_fusion) | data formatting | bytes 131072 | tf_op jit(solution)/shard_map/reshape | solution.py:367
  (3 shorter events, 0.1 us)
Async XLA Ops:
  0.0 16.7 %copy-start.1 = (bf16[16,1,512,256]{3,2,1,0:T(8,128)(2,1)S(1)}, bf16[16,1,512,256]{3,2,1,0:T(8,128)(2,1)}, u32[]{:S(2)}) copy-start(bf16[16,1,512,256]{3,2,1,0:T(8,128)(2,1)} %kv.1) | copy-start | bytes 12582916
  0.0 16.7 %copy-start.2 = (bf16[8192,128]{1,0:T(8,128)(2,1)S(1)}, bf16[8192,128]{1,0:T(8,128)(2,1)}, u32[]{:S(2)}) copy-start(bf16[8192,128]{1,0:T(8,128)(2,1)} %wk.1) | copy-start | bytes 6291460
  0.0 16.7 %copy-start.3 = (bf16[8192,128]{1,0:T(8,128)(2,1)S(1)}, bf16[8192,128]{1,0:T(8,128)(2,1)}, u32[]{:S(2)}) copy-start(bf16[8192,128]{1,0:T(8,128)(2,1)} %wv.1) | copy-start | bytes 6291460
  0.0 16.7 %copy-start.4 = (bf16[16,2,8192]{2,1,0:T(2,128)(2,1)S(1)}, bf16[16,2,8192]{2,1,0:T(2,128)(2,1)}, u32[]{:S(2)}) copy-start(bf16[16,2,8192]{2,1,0:T(2,128)(2,1)} %x.1) | copy-start | bytes 1572868
  16.7 13.4 %slice-start = ((s8[16777216]{0:T(1024)(128)(4,1)}), s8[4194304]{0:T(1024)(128)(4,1)S(1)}, s32[]{:S(2)}) async-start(s8[16777216]{0:T(1024)(128)(4,1)} %bitcast.1), calls=%async_computation.2 | async-start | bytes 8388608
  16.7 13.4 %slice-start.1 = ((s8[16777216]{0:T(1024)(128)(4,1)}), s8[4194304]{0:T(1024)(128)(4,1)S(1)}, s32[]{:S(2)}) async-start(s8[16777216]{0:T(1024)(128)(4,1)} %bitcast.1), calls=%async_computation.3 | async-start | bytes 8388608
  16.8 13.4 %slice-start.2 = ((s8[16777216]{0:T(1024)(128)(4,1)}), s8[4194304]{0:T(1024)(128)(4,1)S(1)}, s32[]{:S(2)}) async-start(s8[16777216]{0:T(1024)(128)(4,1)} %bitcast.1), calls=%async_computation.4 | async-start | bytes 8388608
  16.8 13.4 %slice-start.3 = ((s8[16777216]{0:T(1024)(128)(4,1)}), s8[4194304]{0:T(1024)(128)(4,1)S(1)}, s32[]{:S(2)}) async-start(s8[16777216]{0:T(1024)(128)(4,1)} %bitcast.1), calls=%async_computation.5 | async-start | bytes 8388608
  16.8 13.4 %copy-start = (s32[16]{0:T(128)S(1)}, s32[16]{0:T(128)}, u32[]{:S(2)}) copy-start(s32[16]{0:T(128)} %anc.1) | copy-start | bytes 196
  32.0 4.3 %collective-permute-start = (bf16[3,32,1024]{2,1,0:T(8,128)(2,1)S(1)}, bf16[3,32,1024]{2,1,0:T(8,128)(2,1)S(1)}, u32[]{:S(2)}, u32[]{:S(2)}) collective-permute-start(bf16[3,32,1024]{2,1,0:T(8,128)(2,1)S(1)} %get-tuple-element.27), channel_id=1, source_target_pairs={{0,1},{1,0},{2,3},{3,2},{4,5},{5,4},{6,7},{7,6},{8,9},{9,8},{10,11... | collective-permute-start | bytes 589832 | tf_op jit(solution)/shard_map/ppermute | solution.py:333
  36.3 5.1 %collective-permute-start.1 = (bf16[32,1024]{1,0:T(8,128)(2,1)S(1)}, bf16[32,1024]{1,0:T(8,128)(2,1)S(1)}, u32[]{:S(2)}, u32[]{:S(2)}) collective-permute-start(bf16[32,1024]{1,0:T(8,128)(2,1)S(1)} %get-tuple-element.28), channel_id=1, source_target_pairs={{0,2},{1,3},{2,4},{3,5},{4,6},{5,7},{6,0},{7,1},{8,10},{9,11},{10,... | collective-permute-start | bytes 196616 | tf_op jit(solution)/shard_map/ppermute | solution.py:354
  37.7 5.7 %collective-permute-start.3 = (bf16[32,1024]{1,0:T(8,128)(2,1)S(1)}, bf16[32,1024]{1,0:T(8,128)(2,1)S(1)}, u32[]{:S(2)}, u32[]{:S(2)}) collective-permute-start(bf16[32,1024]{1,0:T(8,128)(2,1)S(1)} %get-tuple-element.31), channel_id=1, source_target_pairs={{0,4},{1,5},{2,6},{3,7},{4,0},{5,1},{6,2},{7,3},{8,12},{9,13},{10,... | collective-permute-start | bytes 196616 | tf_op jit(solution)/shard_map/ppermute | solution.py:354
  40.3 3.4 %collective-permute-start.4 = (bf16[32,1024]{1,0:T(8,128)(2,1)S(1)}, bf16[32,1024]{1,0:T(8,128)(2,1)S(1)}, u32[]{:S(2)}, u32[]{:S(2)}) collective-permute-start(bf16[32,1024]{1,0:T(8,128)(2,1)S(1)} %get-tuple-element.32), channel_id=1, source_target_pairs={{0,6},{1,7},{2,0},{3,1},{4,2},{5,3},{6,4},{7,5},{8,14},{9,15},{10,... | collective-permute-start | bytes 196616 | tf_op jit(solution)/shard_map/ppermute | solution.py:354
  42.1 2.2 %collective-permute-start.2 = (bf16[32,1024]{1,0:T(8,128)(2,1)S(1)}, bf16[32,1024]{1,0:T(8,128)(2,1)S(1)}, u32[]{:S(2)}, u32[]{:S(2)}) collective-permute-start(bf16[32,1024]{1,0:T(8,128)(2,1)S(1)} %get-tuple-element.30), channel_id=1, source_target_pairs={{0,1},{1,0},{2,3},{3,2},{4,5},{5,4},{6,7},{7,6},{8,9},{9,8},{10,11... | collective-permute-start | bytes 196616 | tf_op jit(solution)/shard_map/ppermute | solution.py:364

commit v12 on v11

--- a/solution.py
+++ b/solution.py
@@ -7,6 +7,7 @@
 from jax.sharding import PartitionSpec as P
 
 PAIR = 2
+PARTNERS = (2, 3, 1)
 MORE = 8
 THETA = 500000.0
 EPSILON = 1e-05
@@ -147,11 +148,11 @@
     stat[1] = jnp.broadcast_to(jnp.sum(expo, -1, keepdims=True), stat.shape[1:])
 
 
-def units(own, groups):
+def units(own):
     index = lax.axis_index("tensor")
     y, core = lax.div(index, 2), lax.rem(index, 2)
     core = core if own else 1 - core
-    return [2 * lax.rem(y + k, groups) + core for k in (*range(1, groups), 0)]
+    return [2 * lax.bitwise_xor(y, k) + core for k in (*PARTNERS, 0)]
 
 
 def product(wide, w, block, tokens, column):
@@ -166,7 +167,7 @@
 def project(heads, w, out, own):
     away, tokens, column = out.shape
     wide = widen(heads)
-    for k, block in enumerate(units(own, away + 1)[:away]):
+    for k, block in enumerate(units(own)[:away]):
         out[k] = product(wide, w, block, tokens, column).astype(BF16)
 
 
@@ -219,10 +220,9 @@
 
 def last_kernel(heads, w, arrived, keep, crossing):
     tokens, column = keep.shape
-    groups = w.shape[1] // column // 2
     wide = widen(heads)
-    crossing[...] = product(wide, w, units(False, groups)[-1], tokens, column).astype(BF16)
-    keep[...] = product(wide, w, units(True, groups)[-1], tokens, column) + arrived[...].astype(F32)
+    crossing[...] = product(wide, w, units(False)[-1], tokens, column).astype(BF16)
+    keep[...] = product(wide, w, units(True)[-1], tokens, column) + arrived[...].astype(F32)
 
 
 def shards(inputs, norm_gain, query_proj, w_key, w_value, w_out, kv_cache, ancestors):
@@ -303,8 +303,7 @@
     )
     home = lax.all_to_all(back, "particle", split_axis=0, concat_axis=0, tiled=True)
 
-    groups = tensor // 2
-    away = groups - 1
+    away = len(PARTNERS)
     block = jax.ShapeDtypeStruct((away, rows * steps, column), BF16)
     one = jax.ShapeDtypeStruct((rows * steps, column), BF16)
     params = pltpu.CompilerParams(vmem_limit_bytes=8 * MIB)
@@ -349,9 +348,9 @@
         name="add_sibling",
     )(mine, given)
     arrived = []
-    for k in range(1, groups):
-        ring = [(i, ((i // 2 + k) % groups) * 2 + i % 2) for i in range(tensor)]
-        arrived.append(lax.ppermute(pair[k - 1], "tensor", ring))
+    for part, k in zip(pair, PARTNERS):
+        exchange = [(i, ((i // 2) ^ k) * 2 + i % 2) for i in range(tensor)]
+        arrived.append(lax.ppermute(part, "tensor", exchange))
     keep, crossing = pl.pallas_call(
         last_kernel,
         out_shape=(jax.ShapeDtypeStruct(one.shape, F32), one),

time: 45.1 us -> 45.1 us (level)
  starting transfers between devices: 9.58 us -> 8.59 us
  waiting for transfers between devices: 0.97 us -> 1.91 us
    ppermute x3, starting transfers between devices: 5.07 us -> 3.76 us  [shards(): arrived.append(lax.ppermute(part, 'tensor', exchange))]
    ppermute x3, waiting for transfers between devices: 0.33 us -> 1.22 us  [shards(): arrived.append(lax.ppermute(part, 'tensor', exchange))]
  transfers between devices with their start and end apart: 5 -> 5, of which waited for: 3 -> 4; matrix products, arithmetic and copies ran while one was open for 0% -> 0% of each run, Pallas kernels for 4% -> 4%
where the time goes in v12:
time: 45.1 us; the launch traced here: 44.9 us
  blocking collectives  25.9 us (57%)
  starting transfers between devices  8.59 us (19%)
  Pallas kernels  7.63 us (17%)
  waiting for transfers between devices  1.91 us (4%)
  local copies, waits for them, and re-layouts  0.7 us (2%)
    all_to_all x1, blocking collectives, shards(): lax.all_to_all(send, 'particle', split_axis=0, concat_axis=0, tiled=True)  15.5 us
    all_to_all x1, blocking collectives, shards(): lax.all_to_all(back, 'particle', split_axis=0, concat_axis=0, tiled=True)  10.4 us
    ppermute x3, starting transfers between devices, shards(): arrived.append(lax.ppermute(part, 'tensor', exchange))  3.76 us
    ppermute x1, starting transfers between devices, shards(): given = lax.ppermute(other, 'tensor', sibling)  3.23 us
    pallas_call x1, Pallas kernels, shards(): pl.pallas_call(attend_kernel, out_shape=(jax.ShapeDtypeStruct(packed, BF1...  2.9 us
    pallas_call x1, Pallas kernels, shards(): pl.pallas_call(merge_kernel, out_shape=(block, jax.ShapeDtypeStruct((rows...  1.77 us
    ppermute x1, starting transfers between devices, shards(): total = keep + lax.ppermute(crossing, 'tensor', sibling).astype(F32)  1.6 us
    ppermute x3, waiting for transfers between devices, shards(): arrived.append(lax.ppermute(part, 'tensor', exchange))  1.22 us
  transfers between devices with their start and end apart: 5, of which 4 were waited for; matrix products, arithmetic and copies ran while one was open for 0% of the time, Pallas kernels for 4%

profile of v12, /device:TPU:1, one launch (start us, length us, event | category | flops | bytes accessed | tf_op | source)
XLA Modules:
  0.0 44.9 jit_solution(3540068753784957630)
XLA Ops:
  0.0 0.0 copy-start.1
  0.0 0.0 copy-start.2
  0.0 0.0 copy-start.3
  0.0 0.0 copy-start.4
  0.0 1.2 %pack_queries.1 = (bf16[16,40,128]{2,1,0:T(8,128)(2,1)S(1)}, bf16[16,16,128]{2,1,0:T(8,128)(2,1)S(1)}, f32[2,16,128]{2,1,0:T(8,128)S(1)}, f32[1,8192]{1,0:T(1,128)S(1)}) custom-call(s32[16]{0:T(128)} %anc.1, bf16[16,2,1024]{2,1,0:T(2,128)(2,1)} %qp_hbm.1, f32[2,16,128]{2,1,0:T(8,128)} %constant.2.clone.tables_hbm, f32[1,8192]{1,0:T(1,128)} %bitcast.3), custom_call_target="tpu_custom_call" | custom-call | flops 10000000000 | bytes 1048576 | tf_op jit(solution)/shard_map/pack_queries/pallas_call | solution.py:247
  1.2 15.5 %all_to_all.10.recv = bf16[16,40,128]{2,1,0:T(8,128)(2,1)S(1)} all-to-all(bf16[16,40,128]{2,1,0:T(8,128)(2,1)S(1)} %get-tuple-element.19), channel_id=1, replica_groups=mesh['particle'=16,'tensor'=8] {'particle'}, dimensions={0} | all-to-all | bytes 327680 | tf_op jit(solution)/shard_map/all_to_all | solution.py:270
  16.7 0.0 slice-start
  16.7 0.0 copy-done.1
  16.7 0.0 copy-done.2
  16.7 0.0 copy-done.3
  16.7 0.0 copy-done.4
  16.7 0.0 slice-start.1
  16.8 0.0 slice-start.2
  16.8 0.0 slice-start.3
  16.8 0.0 copy-start
  16.8 2.9 %attention.1 = (bf16[16,40,128]{2,1,0:T(8,128)(2,1)S(1)}, f32[256,128]{1,0:T(8,128)S(1)}, f32[2,256,128]{2,1,0:T(8,128)S(1)}) custom-call(bf16[16,40,128]{2,1,0:T(8,128)(2,1)S(1)} %all_to_all.10.recv, bf16[16,1,512,256]{3,2,1,0:T(8,128)(2,1)S(1)} %copy-done.1, bf16[16,2,8192]{2,1,0:T(2,128)(2,1)S(1)} %copy-done.4, f32[1,8192]{1,0:T(1,128)S(1)} %get-tuple-element.20.gain, ...), custom_call_target="tpu_custom_call" | custom-call | flops 10000000000 | bytes 5242880 | tf_op jit(solution)/shard_map/attention/pallas_call | solution.py:273
  19.7 10.4 %all_to_all.11.recv = bf16[16,40,128]{2,1,0:T(8,128)(2,1)S(1)} all-to-all(bf16[16,40,128]{2,1,0:T(8,128)(2,1)S(1)} %get-tuple-element.23), channel_id=1, replica_groups=mesh['particle'=16,'tensor'=8] {'particle'}, dimensions={0} | all-to-all | bytes 327680 | tf_op jit(solution)/shard_map/all_to_all | solution.py:304
  30.1 0.0 slice-done
  30.1 0.0 slice-done.1
  30.1 0.0 slice-done.2
  30.2 0.0 slice-done.3
  30.2 0.0 copy-done
  30.2 1.8 %merge_project_sibling.1 = (bf16[3,32,1024]{2,1,0:T(8,128)(2,1)S(1)}, bf16[32,1024]{1,0:T(8,128)(2,1)S(1)}) custom-call(s32[16]{0:T(128)S(1)} %copy-done, bf16[16,40,128]{2,1,0:T(8,128)(2,1)S(1)} %all_to_all.11.recv, f32[256,128]{1,0:T(8,128)S(1)} %get-tuple-element.24.vec, f32[2,256,128]{2,1,0:T(8,128)S(1)} %get-tuple-element.25.stat, ...), custom_call_target="tpu_custom_call" | custom-call | flops 268435456 | bytes 8388608 | tf_op jit(solution)/shard_map/merge_project_sibling/pallas_call | solution.py:313
  32.0 3.2 %collective-permute-start = (bf16[3,32,1024]{2,1,0:T(8,128)(2,1)S(1)}, bf16[3,32,1024]{2,1,0:T(8,128)(2,1)S(1)}, u32[]{:S(2)}, u32[]{:S(2)}) collective-permute-start(bf16[3,32,1024]{2,1,0:T(8,128)(2,1)S(1)} %get-tuple-element.27), channel_id=1, source_target_pairs={{0,1},{1,0},{2,3},{3,2},{4,5},{5,4},{6,7},{7,6},{8,9},{9,8},{10,11... | collective-permute-start | bytes 589832 | tf_op jit(solution)/shard_map/ppermute | solution.py:332
  35.2 1.0 %project_own.1.mine = bf16[3,32,1024]{2,1,0:T(8,128)(2,1)S(1)} custom-call(bf16[32,1024]{1,0:T(8,128)(2,1)S(1)} %get-tuple-element.26.heads, bf16[1024,8192]{1,0:T(8,128)(2,1)S(1)} %bitcast.2), custom_call_target="tpu_custom_call" | custom-call | flops 268435456 | bytes 8388608 | tf_op jit(solution)/shard_map/project_own/pallas_call | solution.py:333
  36.2 0.1 collective-permute-done.given
  36.3 3.0 %collective-permute-start.1 = (bf16[32,1024]{1,0:T(8,128)(2,1)S(1)}, bf16[32,1024]{1,0:T(8,128)(2,1)S(1)}, u32[]{:S(2)}, u32[]{:S(2)}) collective-permute-start(bf16[32,1024]{1,0:T(8,128)(2,1)S(1)} %get-tuple-element.28), channel_id=1, source_target_pairs={{0,4},{1,5},{2,6},{3,7},{4,0},{5,1},{6,2},{7,3},{8,12},{9,13},{10,... | collective-permute-start | bytes 196616 | tf_op jit(solution)/shard_map/ppermute | solution.py:353
  39.3 0.8 %collective-permute-start.3 = (bf16[32,1024]{1,0:T(8,128)(2,1)S(1)}, bf16[32,1024]{1,0:T(8,128)(2,1)S(1)}, u32[]{:S(2)}, u32[]{:S(2)}) collective-permute-start(bf16[32,1024]{1,0:T(8,128)(2,1)S(1)} %get-tuple-element.31), channel_id=1, source_target_pairs={{0,6},{1,7},{2,4},{3,5},{4,2},{5,3},{6,0},{7,1},{8,14},{9,15},{10,... | collective-permute-start | bytes 196616 | tf_op jit(solution)/shard_map/ppermute | solution.py:353
  40.1 0.0 collective-permute-start.4
  40.1 0.9 %collective-permute-done.1.arrived = bf16[32,1024]{1,0:T(8,128)(2,1)S(1)} collective-permute-done((bf16[32,1024]{1,0:T(8,128)(2,1)S(1)}, bf16[32,1024]{1,0:T(8,128)(2,1)S(1)}, u32[]{:S(2)}, u32[]{:S(2)}) %collective-permute-start.1) | collective-permute-done | bytes 65568 | tf_op jit(solution)/shard_map/ppermute | solution.py:353
  41.0 0.7 %project_last.1 = (f32[32,1024]{1,0:T(8,128)S(1)}, bf16[32,1024]{1,0:T(8,128)(2,1)S(1)}) custom-call(bf16[32,1024]{1,0:T(8,128)(2,1)S(1)} %get-tuple-element.26.heads, bf16[1024,8192]{1,0:T(8,128)(2,1)S(1)} %bitcast.2, bf16[32,1024]{1,0:T(8,128)(2,1)S(1)} %collective-permute-done.1.arrived), custom_call_target="tpu_custom_call" | custom-call | flops 268435456 | bytes 8388608 | tf_op jit(solution)/shard_map/project_last/pallas_call | solution.py:354
  41.7 1.6 %collective-permute-start.2 = (bf16[32,1024]{1,0:T(8,128)(2,1)S(1)}, bf16[32,1024]{1,0:T(8,128)(2,1)S(1)}, u32[]{:S(2)}, u32[]{:S(2)}) collective-permute-start(bf16[32,1024]{1,0:T(8,128)(2,1)S(1)} %get-tuple-element.30), channel_id=1, source_target_pairs={{0,1},{1,0},{2,3},{3,2},{4,5},{5,4},{6,7},{7,6},{8,9},{9,8},{10,11... | collective-permute-start | bytes 196616 | tf_op jit(solution)/shard_map/ppermute | solution.py:363
  43.3 0.3 collective-permute-done.3
  43.6 0.0 collective-permute-done.4
  43.6 0.6 %collective-permute-done.2 = bf16[32,1024]{1,0:T(8,128)(2,1)S(1)} collective-permute-done((bf16[32,1024]{1,0:T(8,128)(2,1)S(1)}, bf16[32,1024]{1,0:T(8,128)(2,1)S(1)}, u32[]{:S(2)}, u32[]{:S(2)}) %collective-permute-start.2) | collective-permute-done | bytes 65568 | tf_op jit(solution)/shard_map/ppermute | solution.py:363
  44.3 0.7 %reshape.7 = bf16[16,2,1024]{2,1,0:T(2,128)(2,1)} reshape(bf16[32,1024]{1,0:T(8,128)(2,1)S(1)} %add_convert_fusion) | data formatting | bytes 131072 | tf_op jit(solution)/shard_map/reshape | solution.py:366
  (3 shorter events, 0.1 us)
Async XLA Ops:
  0.0 16.7 %copy-start.1 = (bf16[16,1,512,256]{3,2,1,0:T(8,128)(2,1)S(1)}, bf16[16,1,512,256]{3,2,1,0:T(8,128)(2,1)}, u32[]{:S(2)}) copy-start(bf16[16,1,512,256]{3,2,1,0:T(8,128)(2,1)} %kv.1) | copy-start | bytes 12582916
  0.0 16.7 %copy-start.2 = (bf16[8192,128]{1,0:T(8,128)(2,1)S(1)}, bf16[8192,128]{1,0:T(8,128)(2,1)}, u32[]{:S(2)}) copy-start(bf16[8192,128]{1,0:T(8,128)(2,1)} %wk.1) | copy-start | bytes 6291460
  0.0 16.7 %copy-start.3 = (bf16[8192,128]{1,0:T(8,128)(2,1)S(1)}, bf16[8192,128]{1,0:T(8,128)(2,1)}, u32[]{:S(2)}) copy-start(bf16[8192,128]{1,0:T(8,128)(2,1)} %wv.1) | copy-start | bytes 6291460
  0.0 16.7 %copy-start.4 = (bf16[16,2,8192]{2,1,0:T(2,128)(2,1)S(1)}, bf16[16,2,8192]{2,1,0:T(2,128)(2,1)}, u32[]{:S(2)}) copy-start(bf16[16,2,8192]{2,1,0:T(2,128)(2,1)} %x.1) | copy-start | bytes 1572868
  16.7 13.4 %slice-start = ((s8[16777216]{0:T(1024)(128)(4,1)}), s8[4194304]{0:T(1024)(128)(4,1)S(1)}, s32[]{:S(2)}) async-start(s8[16777216]{0:T(1024)(128)(4,1)} %bitcast.1), calls=%async_computation.2 | async-start | bytes 8388608
  16.7 13.4 %slice-start.1 = ((s8[16777216]{0:T(1024)(128)(4,1)}), s8[4194304]{0:T(1024)(128)(4,1)S(1)}, s32[]{:S(2)}) async-start(s8[16777216]{0:T(1024)(128)(4,1)} %bitcast.1), calls=%async_computation.3 | async-start | bytes 8388608
  16.8 13.4 %slice-start.2 = ((s8[16777216]{0:T(1024)(128)(4,1)}), s8[4194304]{0:T(1024)(128)(4,1)S(1)}, s32[]{:S(2)}) async-start(s8[16777216]{0:T(1024)(128)(4,1)} %bitcast.1), calls=%async_computation.4 | async-start | bytes 8388608
  16.8 13.4 %slice-start.3 = ((s8[16777216]{0:T(1024)(128)(4,1)}), s8[4194304]{0:T(1024)(128)(4,1)S(1)}, s32[]{:S(2)}) async-start(s8[16777216]{0:T(1024)(128)(4,1)} %bitcast.1), calls=%async_computation.5 | async-start | bytes 8388608
  16.8 13.4 %copy-start = (s32[16]{0:T(128)S(1)}, s32[16]{0:T(128)}, u32[]{:S(2)}) copy-start(s32[16]{0:T(128)} %anc.1) | copy-start | bytes 196
  32.0 4.3 %collective-permute-start = (bf16[3,32,1024]{2,1,0:T(8,128)(2,1)S(1)}, bf16[3,32,1024]{2,1,0:T(8,128)(2,1)S(1)}, u32[]{:S(2)}, u32[]{:S(2)}) collective-permute-start(bf16[3,32,1024]{2,1,0:T(8,128)(2,1)S(1)} %get-tuple-element.27), channel_id=1, source_target_pairs={{0,1},{1,0},{2,3},{3,2},{4,5},{5,4},{6,7},{7,6},{8,9},{9,8},{10,11... | collective-permute-start | bytes 589832 | tf_op jit(solution)/shard_map/ppermute | solution.py:332
  36.3 4.7 %collective-permute-start.1 = (bf16[32,1024]{1,0:T(8,128)(2,1)S(1)}, bf16[32,1024]{1,0:T(8,128)(2,1)S(1)}, u32[]{:S(2)}, u32[]{:S(2)}) collective-permute-start(bf16[32,1024]{1,0:T(8,128)(2,1)S(1)} %get-tuple-element.28), channel_id=1, source_target_pairs={{0,4},{1,5},{2,6},{3,7},{4,0},{5,1},{6,2},{7,3},{8,12},{9,13},{10,... | collective-permute-start | bytes 196616 | tf_op jit(solution)/shard_map/ppermute | solution.py:353
  39.3 4.3 %collective-permute-start.3 = (bf16[32,1024]{1,0:T(8,128)(2,1)S(1)}, bf16[32,1024]{1,0:T(8,128)(2,1)S(1)}, u32[]{:S(2)}, u32[]{:S(2)}) collective-permute-start(bf16[32,1024]{1,0:T(8,128)(2,1)S(1)} %get-tuple-element.31), channel_id=1, source_target_pairs={{0,6},{1,7},{2,4},{3,5},{4,2},{5,3},{6,0},{7,1},{8,14},{9,15},{10,... | collective-permute-start | bytes 196616 | tf_op jit(solution)/shard_map/ppermute | solution.py:353
  40.1 3.5 %collective-permute-start.4 = (bf16[32,1024]{1,0:T(8,128)(2,1)S(1)}, bf16[32,1024]{1,0:T(8,128)(2,1)S(1)}, u32[]{:S(2)}, u32[]{:S(2)}) collective-permute-start(bf16[32,1024]{1,0:T(8,128)(2,1)S(1)} %get-tuple-element.32), channel_id=1, source_target_pairs={{0,2},{1,3},{2,0},{3,1},{4,6},{5,7},{6,4},{7,5},{8,10},{9,11},{10,... | collective-permute-start | bytes 196616 | tf_op jit(solution)/shard_map/ppermute | solution.py:353
  41.7 2.5 %collective-permute-start.2 = (bf16[32,1024]{1,0:T(8,128)(2,1)S(1)}, bf16[32,1024]{1,0:T(8,128)(2,1)S(1)}, u32[]{:S(2)}, u32[]{:S(2)}) collective-permute-start(bf16[32,1024]{1,0:T(8,128)(2,1)S(1)} %get-tuple-element.30), channel_id=1, source_target_pairs={{0,1},{1,0},{2,3},{3,2},{4,5},{5,4},{6,7},{7,6},{8,9},{9,8},{10,11... | collective-permute-start | bytes 196616 | tf_op jit(solution)/shard_map/ppermute | solution.py:363

commit v13 on v12

--- a/solution.py
+++ b/solution.py
@@ -7,7 +7,6 @@
 from jax.sharding import PartitionSpec as P
 
 PAIR = 2
-PARTNERS = (2, 3, 1)
 MORE = 8
 THETA = 500000.0
 EPSILON = 1e-05
@@ -152,7 +151,8 @@
     index = lax.axis_index("tensor")
     y, core = lax.div(index, 2), lax.rem(index, 2)
     core = core if own else 1 - core
-    return [2 * lax.bitwise_xor(y, k) + core for k in (*PARTNERS, 0)]
+    served = lax.bitwise_xor(y, 2 + core)
+    return 2 * served + core, 2 * served + 1 - core, 2 * lax.bitwise_xor(y, 1) + core, 2 * y + core
 
 
 def product(wide, w, block, tokens, column):
@@ -213,16 +213,18 @@
     project(heads, w, out, True)
 
 
-def add_kernel(mine, given, *outs):
-    for k, out in enumerate(outs):
-        out[...] = (mine[k].astype(F32) + given[k].astype(F32)).astype(BF16)
+def add_kernel(mine, given, served, near):
+    served[...] = (mine[:2].astype(F32) + given[:2].astype(F32)).astype(BF16)
+    near[...] = (mine[2].astype(F32) + given[2].astype(F32)).astype(BF16)
 
 
 def last_kernel(heads, w, arrived, keep, crossing):
     tokens, column = keep.shape
     wide = widen(heads)
-    crossing[...] = product(wide, w, units(False)[-1], tokens, column).astype(BF16)
-    keep[...] = product(wide, w, units(True)[-1], tokens, column) + arrived[...].astype(F32)
+    crossing[...] = (
+        product(wide, w, units(False)[-1], tokens, column) + arrived[1].astype(F32)
+    ).astype(BF16)
+    keep[...] = product(wide, w, units(True)[-1], tokens, column) + arrived[0].astype(F32)
 
 
 def shards(inputs, norm_gain, query_proj, w_key, w_value, w_out, kv_cache, ancestors):
@@ -303,8 +305,7 @@
     )
     home = lax.all_to_all(back, "particle", split_axis=0, concat_axis=0, tiled=True)
 
-    away = len(PARTNERS)
-    block = jax.ShapeDtypeStruct((away, rows * steps, column), BF16)
+    block = jax.ShapeDtypeStruct((3, rows * steps, column), BF16)
     one = jax.ShapeDtypeStruct((rows * steps, column), BF16)
     params = pltpu.CompilerParams(vmem_limit_bytes=8 * MIB)
     cost = pl.CostEstimate(
@@ -339,18 +340,16 @@
         cost_estimate=cost,
         name="project_own",
     )(heads_out, w_out)
-    pair = pl.pallas_call(
+    served, near = pl.pallas_call(
         add_kernel,
-        out_shape=(one,) * away,
+        out_shape=(jax.ShapeDtypeStruct((2, *one.shape), BF16), one),
         in_specs=[vmem, vmem],
-        out_specs=(vmem,) * away,
+        out_specs=(vmem, vmem),
         compiler_params=params,
         name="add_sibling",
     )(mine, given)
-    arrived = []
-    for part, k in zip(pair, PARTNERS):
-        exchange = [(i, ((i // 2) ^ k) * 2 + i % 2) for i in range(tensor)]
-        arrived.append(lax.ppermute(part, "tensor", exchange))
+    arrived = lax.ppermute(served, "tensor", [(i, ((i // 2) ^ (2 + i % 2)) * 2 + i % 2) for i in range(tensor)])
+    from_near = lax.ppermute(near, "tensor", [(i, i ^ 2) for i in range(tensor)])
     keep, crossing = pl.pallas_call(
         last_kernel,
         out_shape=(jax.ShapeDtypeStruct(one.shape, F32), one),
@@ -359,10 +358,8 @@
         compiler_params=params,
         cost_estimate=cost,
         name="project_last",
-    )(heads_out, w_out, arrived[0])
-    total = keep + lax.ppermute(crossing, "tensor", sibling).astype(F32)
-    for part in arrived[1:]:
-        total = total + part.astype(F32)
+    )(heads_out, w_out, arrived)
+    total = keep + from_near.astype(F32) + lax.ppermute(crossing, "tensor", sibling).astype(F32)
     return total.astype(BF16).reshape(rows, steps, column)
 
 

time: 45.1 us -> 46.5 us (1.031)
  waiting for transfers between devices: 1.91 us -> 4.15 us
  starting transfers between devices: 8.59 us -> 7.76 us
    ppermute x4 -> x3, waiting for transfers between devices: 1.84 us -> 4.07 us  [the longest x1 3.17 us: shards(): lax.ppermute(served, 'tensor', [(i, (i // 2 ^ 2 + i % 2) * 2 + i % 2) for...]
    ppermute x4 -> x3, starting transfers between devices: 5.36 us -> 4.54 us  [the longest x1 2.8 us: shards(): lax.ppermute(served, 'tensor', [(i, (i // 2 ^ 2 + i % 2) * 2 + i % 2) for...]
  transfers between devices with their start and end apart: 5 -> 4, of which waited for: 4 -> 3; matrix products, arithmetic and copies ran while one was open for 0% -> 0% of each run, Pallas kernels for 4% -> 4%
where the time goes in v13:
time: 46.5 us; the launch traced here: 46.3 us
  blocking collectives  25.9 us (56%)
  starting transfers between devices  7.76 us (17%)
  Pallas kernels  7.64 us (16%)
  waiting for transfers between devices  4.15 us (9%)
  local copies, waits for them, and re-layouts  0.7 us (2%)
    all_to_all x1, blocking collectives, shards(): lax.all_to_all(send, 'particle', split_axis=0, concat_axis=0, tiled=True)  15.5 us
    all_to_all x1, blocking collectives, shards(): lax.all_to_all(back, 'particle', split_axis=0, concat_axis=0, tiled=True)  10.4 us
    ppermute x1, starting transfers between devices, shards(): given = lax.ppermute(other, 'tensor', sibling)  3.23 us
    ppermute x1, waiting for transfers between devices, shards(): lax.ppermute(served, 'tensor', [(i, (i // 2 ^ 2 + i % 2) * 2 + i % 2) for...  3.17 us
    pallas_call x1, Pallas kernels, shards(): pl.pallas_call(attend_kernel, out_shape=(jax.ShapeDtypeStruct(packed, BF1...  2.9 us
    ppermute x1, starting transfers between devices, shards(): lax.ppermute(served, 'tensor', [(i, (i // 2 ^ 2 + i % 2) * 2 + i % 2) for...  2.8 us
    pallas_call x1, Pallas kernels, shards(): pl.pallas_call(merge_kernel, out_shape=(block, jax.ShapeDtypeStruct((rows...  1.77 us
    ppermute x1, starting transfers between devices, shards(): lax.ppermute(crossing, 'tensor', sibling).astype(F32)  1.73 us
  transfers between devices with their start and end apart: 4, of which 3 were waited for; matrix products, arithmetic and copies ran while one was open for 0% of the time, Pallas kernels for 4%

profile of v13, /device:TPU:1, one launch (start us, length us, event | category | flops | bytes accessed | tf_op | source)
XLA Modules:
  0.0 46.3 jit_solution(7400214553705418121)
XLA Ops:
  0.0 0.0 copy-start.1
  0.0 0.0 copy-start.2
  0.0 0.0 copy-start.3
  0.0 0.0 copy-start.4
  0.0 1.2 %pack_queries.1 = (bf16[16,40,128]{2,1,0:T(8,128)(2,1)S(1)}, bf16[16,16,128]{2,1,0:T(8,128)(2,1)S(1)}, f32[2,16,128]{2,1,0:T(8,128)S(1)}, f32[1,8192]{1,0:T(1,128)S(1)}) custom-call(s32[16]{0:T(128)} %anc.1, bf16[16,2,1024]{2,1,0:T(2,128)(2,1)} %qp_hbm.1, f32[2,16,128]{2,1,0:T(8,128)} %constant.2.clone.tables_hbm, f32[1,8192]{1,0:T(1,128)} %bitcast.3), custom_call_target="tpu_custom_call" | custom-call | flops 10000000000 | bytes 1048576 | tf_op jit(solution)/shard_map/pack_queries/pallas_call | solution.py:249
  1.2 15.5 %all_to_all.10.recv = bf16[16,40,128]{2,1,0:T(8,128)(2,1)S(1)} all-to-all(bf16[16,40,128]{2,1,0:T(8,128)(2,1)S(1)} %get-tuple-element.18), channel_id=1, replica_groups=mesh['particle'=16,'tensor'=8] {'particle'}, dimensions={0} | all-to-all | bytes 327680 | tf_op jit(solution)/shard_map/all_to_all | solution.py:272
  16.7 0.0 slice-start
  16.7 0.0 copy-done.1
  16.7 0.0 copy-done.2
  16.7 0.0 copy-done.3
  16.7 0.0 copy-done.4
  16.7 0.0 slice-start.1
  16.8 0.0 slice-start.2
  16.8 0.0 slice-start.3
  16.8 0.0 copy-start
  16.8 2.9 %attention.1 = (bf16[16,40,128]{2,1,0:T(8,128)(2,1)S(1)}, f32[256,128]{1,0:T(8,128)S(1)}, f32[2,256,128]{2,1,0:T(8,128)S(1)}) custom-call(bf16[16,40,128]{2,1,0:T(8,128)(2,1)S(1)} %all_to_all.10.recv, bf16[16,1,512,256]{3,2,1,0:T(8,128)(2,1)S(1)} %copy-done.1, bf16[16,2,8192]{2,1,0:T(2,128)(2,1)S(1)} %copy-done.4, f32[1,8192]{1,0:T(1,128)S(1)} %get-tuple-element.19.gain, ...), custom_call_target="tpu_custom_call" | custom-call | flops 10000000000 | bytes 5242880 | tf_op jit(solution)/shard_map/attention/pallas_call | solution.py:275
  19.7 10.4 %all_to_all.11.recv = bf16[16,40,128]{2,1,0:T(8,128)(2,1)S(1)} all-to-all(bf16[16,40,128]{2,1,0:T(8,128)(2,1)S(1)} %get-tuple-element.22), channel_id=1, replica_groups=mesh['particle'=16,'tensor'=8] {'particle'}, dimensions={0} | all-to-all | bytes 327680 | tf_op jit(solution)/shard_map/all_to_all | solution.py:306
  30.1 0.0 slice-done
  30.1 0.0 slice-done.1
  30.1 0.0 slice-done.2
  30.2 0.0 slice-done.3
  30.2 0.0 copy-done
  30.2 1.8 %merge_project_sibling.1 = (bf16[3,32,1024]{2,1,0:T(8,128)(2,1)S(1)}, bf16[32,1024]{1,0:T(8,128)(2,1)S(1)}) custom-call(s32[16]{0:T(128)S(1)} %copy-done, bf16[16,40,128]{2,1,0:T(8,128)(2,1)S(1)} %all_to_all.11.recv, f32[256,128]{1,0:T(8,128)S(1)} %get-tuple-element.23.vec, f32[2,256,128]{2,1,0:T(8,128)S(1)} %get-tuple-element.24.stat, ...), custom_call_target="tpu_custom_call" | custom-call | flops 268435456 | bytes 8388608 | tf_op jit(solution)/shard_map/merge_project_sibling/pallas_call | solution.py:314
  32.0 3.2 %collective-permute-start = (bf16[3,32,1024]{2,1,0:T(8,128)(2,1)S(1)}, bf16[3,32,1024]{2,1,0:T(8,128)(2,1)S(1)}, u32[]{:S(2)}, u32[]{:S(2)}) collective-permute-start(bf16[3,32,1024]{2,1,0:T(8,128)(2,1)S(1)} %get-tuple-element.26), channel_id=1, source_target_pairs={{0,1},{1,0},{2,3},{3,2},{4,5},{5,4},{6,7},{7,6},{8,9},{9,8},{10,11... | collective-permute-start | bytes 589832 | tf_op jit(solution)/shard_map/ppermute | solution.py:333
  35.2 1.0 %project_own.1.mine = bf16[3,32,1024]{2,1,0:T(8,128)(2,1)S(1)} custom-call(bf16[32,1024]{1,0:T(8,128)(2,1)S(1)} %get-tuple-element.25.heads, bf16[1024,8192]{1,0:T(8,128)(2,1)S(1)} %bitcast.2), custom_call_target="tpu_custom_call" | custom-call | flops 268435456 | bytes 8388608 | tf_op jit(solution)/shard_map/project_own/pallas_call | solution.py:334
  36.2 0.1 collective-permute-done.given
  36.3 2.8 %collective-permute-start.1 = (bf16[2,32,1024]{2,1,0:T(8,128)(2,1)S(1)}, bf16[2,32,1024]{2,1,0:T(8,128)(2,1)S(1)}, u32[]{:S(2)}, u32[]{:S(2)}) collective-permute-start(bf16[2,32,1024]{2,1,0:T(8,128)(2,1)S(1)} %get-tuple-element.27), channel_id=1, source_target_pairs={{0,4},{1,7},{2,6},{3,5},{4,0},{5,3},{6,2},{7,1},{8,12},{9,15},{10,... | collective-permute-start | bytes 393224 | tf_op jit(solution)/shard_map/ppermute | solution.py:351
  39.1 0.0 collective-permute-start.2
  39.1 3.2 %collective-permute-done.1.arrived = bf16[2,32,1024]{2,1,0:T(8,128)(2,1)S(1)} collective-permute-done((bf16[2,32,1024]{2,1,0:T(8,128)(2,1)S(1)}, bf16[2,32,1024]{2,1,0:T(8,128)(2,1)S(1)}, u32[]{:S(2)}, u32[]{:S(2)}) %collective-permute-start.1) | collective-permute-done | bytes 131104 | tf_op jit(solution)/shard_map/ppermute | solution.py:351
  42.3 0.7 %project_last.1 = (f32[32,1024]{1,0:T(8,128)S(1)}, bf16[32,1024]{1,0:T(8,128)(2,1)S(1)}) custom-call(bf16[32,1024]{1,0:T(8,128)(2,1)S(1)} %get-tuple-element.25.heads, bf16[1024,8192]{1,0:T(8,128)(2,1)S(1)} %bitcast.2, bf16[2,32,1024]{2,1,0:T(8,128)(2,1)S(1)} %collective-permute-done.1.arrived), custom_call_target="tpu_custom_call" | custom-call | flops 268435456 | bytes 8388608 | tf_op jit(solution)/shard_map/project_last/pallas_call | solution.py:353
  43.0 1.7 %collective-permute-start.3 = (bf16[32,1024]{1,0:T(8,128)(2,1)S(1)}, bf16[32,1024]{1,0:T(8,128)(2,1)S(1)}, u32[]{:S(2)}, u32[]{:S(2)}) collective-permute-start(bf16[32,1024]{1,0:T(8,128)(2,1)S(1)} %get-tuple-element.30), channel_id=1, source_target_pairs={{0,1},{1,0},{2,3},{3,2},{4,5},{5,4},{6,7},{7,6},{8,9},{9,8},{10,11... | collective-permute-start | bytes 196616 | tf_op jit(solution)/shard_map/ppermute | solution.py:362
  44.7 0.0 collective-permute-done.2
  44.7 0.9 %collective-permute-done.3 = bf16[32,1024]{1,0:T(8,128)(2,1)S(1)} collective-permute-done((bf16[32,1024]{1,0:T(8,128)(2,1)S(1)}, bf16[32,1024]{1,0:T(8,128)(2,1)S(1)}, u32[]{:S(2)}, u32[]{:S(2)}) %collective-permute-start.3) | collective-permute-done | bytes 65568 | tf_op jit(solution)/shard_map/ppermute | solution.py:362
  45.7 0.7 %reshape.7 = bf16[16,2,1024]{2,1,0:T(2,128)(2,1)} reshape(bf16[32,1024]{1,0:T(8,128)(2,1)S(1)} %add_convert_fusion) | data formatting | bytes 131072 | tf_op jit(solution)/shard_map/reshape | solution.py:363
  (3 shorter events, 0.1 us)
Async XLA Ops:
  0.0 16.7 %copy-start.1 = (bf16[16,1,512,256]{3,2,1,0:T(8,128)(2,1)S(1)}, bf16[16,1,512,256]{3,2,1,0:T(8,128)(2,1)}, u32[]{:S(2)}) copy-start(bf16[16,1,512,256]{3,2,1,0:T(8,128)(2,1)} %kv.1) | copy-start | bytes 12582916
  0.0 16.7 %copy-start.2 = (bf16[8192,128]{1,0:T(8,128)(2,1)S(1)}, bf16[8192,128]{1,0:T(8,128)(2,1)}, u32[]{:S(2)}) copy-start(bf16[8192,128]{1,0:T(8,128)(2,1)} %wk.1) | copy-start | bytes 6291460
  0.0 16.7 %copy-start.3 = (bf16[8192,128]{1,0:T(8,128)(2,1)S(1)}, bf16[8192,128]{1,0:T(8,128)(2,1)}, u32[]{:S(2)}) copy-start(bf16[8192,128]{1,0:T(8,128)(2,1)} %wv.1) | copy-start | bytes 6291460
  0.0 16.7 %copy-start.4 = (bf16[16,2,8192]{2,1,0:T(2,128)(2,1)S(1)}, bf16[16,2,8192]{2,1,0:T(2,128)(2,1)}, u32[]{:S(2)}) copy-start(bf16[16,2,8192]{2,1,0:T(2,128)(2,1)} %x.1) | copy-start | bytes 1572868
  16.7 13.4 %slice-start = ((s8[16777216]{0:T(1024)(128)(4,1)}), s8[4194304]{0:T(1024)(128)(4,1)S(1)}, s32[]{:S(2)}) async-start(s8[16777216]{0:T(1024)(128)(4,1)} %bitcast.1), calls=%async_computation.2 | async-start | bytes 8388608
  16.7 13.4 %slice-start.1 = ((s8[16777216]{0:T(1024)(128)(4,1)}), s8[4194304]{0:T(1024)(128)(4,1)S(1)}, s32[]{:S(2)}) async-start(s8[16777216]{0:T(1024)(128)(4,1)} %bitcast.1), calls=%async_computation.3 | async-start | bytes 8388608
  16.8 13.4 %slice-start.2 = ((s8[16777216]{0:T(1024)(128)(4,1)}), s8[4194304]{0:T(1024)(128)(4,1)S(1)}, s32[]{:S(2)}) async-start(s8[16777216]{0:T(1024)(128)(4,1)} %bitcast.1), calls=%async_computation.4 | async-start | bytes 8388608
  16.8 13.4 %slice-start.3 = ((s8[16777216]{0:T(1024)(128)(4,1)}), s8[4194304]{0:T(1024)(128)(4,1)S(1)}, s32[]{:S(2)}) async-start(s8[16777216]{0:T(1024)(128)(4,1)} %bitcast.1), calls=%async_computation.5 | async-start | bytes 8388608
  16.8 13.4 %copy-start = (s32[16]{0:T(128)S(1)}, s32[16]{0:T(128)}, u32[]{:S(2)}) copy-start(s32[16]{0:T(128)} %anc.1) | copy-start | bytes 196
  32.0 4.3 %collective-permute-start = (bf16[3,32,1024]{2,1,0:T(8,128)(2,1)S(1)}, bf16[3,32,1024]{2,1,0:T(8,128)(2,1)S(1)}, u32[]{:S(2)}, u32[]{:S(2)}) collective-permute-start(bf16[3,32,1024]{2,1,0:T(8,128)(2,1)S(1)} %get-tuple-element.26), channel_id=1, source_target_pairs={{0,1},{1,0},{2,3},{3,2},{4,5},{5,4},{6,7},{7,6},{8,9},{9,8},{10,11... | collective-permute-start | bytes 589832 | tf_op jit(solution)/shard_map/ppermute | solution.py:333
  36.3 6.0 %collective-permute-start.1 = (bf16[2,32,1024]{2,1,0:T(8,128)(2,1)S(1)}, bf16[2,32,1024]{2,1,0:T(8,128)(2,1)S(1)}, u32[]{:S(2)}, u32[]{:S(2)}) collective-permute-start(bf16[2,32,1024]{2,1,0:T(8,128)(2,1)S(1)} %get-tuple-element.27), channel_id=1, source_target_pairs={{0,4},{1,7},{2,6},{3,5},{4,0},{5,3},{6,2},{7,1},{8,12},{9,15},{10,... | collective-permute-start | bytes 393224 | tf_op jit(solution)/shard_map/ppermute | solution.py:351
  39.1 5.6 %collective-permute-start.2 = (bf16[32,1024]{1,0:T(8,128)(2,1)S(1)}, bf16[32,1024]{1,0:T(8,128)(2,1)S(1)}, u32[]{:S(2)}, u32[]{:S(2)}) collective-permute-start(bf16[32,1024]{1,0:T(8,128)(2,1)S(1)} %get-tuple-element.29), channel_id=1, source_target_pairs={{0,2},{1,3},{2,0},{3,1},{4,6},{5,7},{6,4},{7,5},{8,10},{9,11},{10,... | collective-permute-start | bytes 196616 | tf_op jit(solution)/shard_map/ppermute | solution.py:352
  43.0 2.6 %collective-permute-start.3 = (bf16[32,1024]{1,0:T(8,128)(2,1)S(1)}, bf16[32,1024]{1,0:T(8,128)(2,1)S(1)}, u32[]{:S(2)}, u32[]{:S(2)}) collective-permute-start(bf16[32,1024]{1,0:T(8,128)(2,1)S(1)} %get-tuple-element.30), channel_id=1, source_target_pairs={{0,1},{1,0},{2,3},{3,2},{4,5},{5,4},{6,7},{7,6},{8,9},{9,8},{10,11... | collective-permute-start | bytes 196616 | tf_op jit(solution)/shard_map/ppermute | solution.py:362

commit v14 on v11

--- a/solution.py
+++ b/solution.py
@@ -50,7 +50,7 @@
         send[d] = jnp.zeros(send.shape[1:], BF16)
         count[d] = 0
         for j in range(PAIR):
-            spots[PAIR * d + j] = 0
+            spots[PAIR * d + j] = -1
         return 0
 
     lax.fori_loop(0, devices, clear, 0)
@@ -72,59 +72,70 @@
         ).astype(BF16)
 
 
-def slot_rows(chunks, i, per_row):
-    at = (i % PAIR) * per_row
-    return chunks[i // PAIR, at : at + per_row, :]
-
-
-def pack_statistics(tops, sums, back):
+def pack_statistics(tops, sums, places, back):
     devices, _, head_dim = back.shape
     per_row = tops.shape[1]
+    pieces = per_row // MORE
     lane = lax.broadcasted_iota(jnp.int32, (MORE, head_dim), 1)
-    quarter = head_dim * MORE // (PAIR * per_row)
+    quarter = head_dim // (PAIR * pieces)
+    piece_of, is_top, part_of = lax.div(lane, quarter), lax.rem(lane, quarter) < 4, lax.rem(lane, 4)
     for d in range(devices):
-        stat = jnp.zeros(lane.shape, F32)
+        value = jnp.zeros(lane.shape, F32)
         for j in range(PAIR):
-            i = d * PAIR + j
-            for g in range(per_row // MORE):
-                at_lane = (j * (per_row // MORE) + g) * quarter
-                for source, parts in ((tops, 3), (sums, 2)):
-                    value = source[i, g * MORE : (g + 1) * MORE, :]
-                    for _ in range(parts):
-                        part = value.astype(BF16).astype(F32)
-                        stat = jnp.where(lane == at_lane, part, stat)
-                        value = value - part
-                        at_lane += 1
-        back[d, PAIR * per_row :, :] = stat.astype(BF16)
+            place = places[d * PAIR + j]
+            for g in range(pieces):
+                at = slice(g * MORE, (g + 1) * MORE)
+                both = jnp.where(is_top, tops[place, at, :], sums[place, at, :])
+                value = jnp.where(piece_of == j * pieces + g, both, value)
+        first = value.astype(BF16).astype(F32)
+        second = (value - first).astype(BF16).astype(F32)
+        third = value - first - second
+        back[d, PAIR * per_row :, :] = jnp.where(
+            part_of == 0, first, jnp.where(part_of == 1, second, third)
+        ).astype(BF16)
 
 
 def attend_kernel(
     recv, kv, x, gain, wk, wv, queries, tables, back, vec, stat, *scratch
 ):
-    scores, expos, tops, sums, normed = scratch
+    scores, expos, tops, sums, vectors, normed, chosen, row_of = scratch
     devices, _, head_dim = recv.shape
     per_row = queries.shape[1]
     lane = lax.broadcasted_iota(jnp.int32, (per_row, head_dim), 1)
-    spots = []
+    slots = devices * PAIR
+    for k in range(slots):
+        chosen[k] = 0
+        row_of[k] = 0
+    used = jnp.int32(0)
+    places = []
     for d in range(devices):
         spot = recv[d, PAIR * per_row :, :].astype(F32)
         for j in range(PAIR):
-            spots.append(spot[0, j * (head_dim // PAIR)].astype(jnp.int32))
-    for i in range(devices * PAIR):
-        scores[i] = lax.dot_general(
-            slot_rows(recv, i, per_row), kv[spots[i], 0, :, :head_dim], NT, preferred_element_type=F32
-        ) * head_dim ** (-0.5)
-    for i in range(devices * PAIR):
-        top = jnp.max(scores[i], -1, keepdims=True)
-        expo = jnp.exp(scores[i] - top)
-        expos[i] = expo.astype(BF16)
-        tops[i] = jnp.broadcast_to(top, lane.shape)
-        sums[i] = jnp.broadcast_to(jnp.sum(expo, -1, keepdims=True), lane.shape)
-    for i in range(devices * PAIR):
-        vector = jnp.dot(expos[i], kv[spots[i], 0, :, head_dim:], preferred_element_type=F32)
-        at = (i % PAIR) * per_row
-        back[i // PAIR, at : at + per_row, :] = (vector / sums[i]).astype(BF16)
-    pack_statistics(tops, sums, back)
+            row = spot[0, j * (head_dim // PAIR)].astype(jnp.int32)
+            chosen[used] = d * PAIR + j
+            row_of[used] = jnp.maximum(row, 0)
+            places.append(used)
+            used = used + jnp.where(row >= 0, 1, 0)
+
+    def cached(first, last):
+        for k in range(first, last):
+            d, j = lax.div(chosen[k], PAIR), lax.rem(chosen[k], PAIR)
+            asked = recv[d, pl.ds(pl.multiple_of(j * per_row, per_row), per_row), :]
+            scores[k] = lax.dot_general(
+                asked, kv[row_of[k], 0, :, :head_dim], NT, preferred_element_type=F32
+            ) * head_dim ** (-0.5)
+        for k in range(first, last):
+            top = jnp.max(scores[k], -1, keepdims=True)
+            expo = jnp.exp(scores[k] - top)
+            expos[k] = expo.astype(BF16)
+            tops[k] = jnp.broadcast_to(top, lane.shape)
+            sums[k] = jnp.broadcast_to(jnp.sum(expo, -1, keepdims=True), lane.shape)
+        for k in range(first, last):
+            vector = jnp.dot(expos[k], kv[row_of[k], 0, :, head_dim:], preferred_element_type=F32)
+            vectors[k] = (vector / sums[k]).astype(BF16)
+
+    most = slots * 3 // 4
+    cached(0, most)
     rows, steps, width = x.shape
     tokens = rows * steps
     floats = x[...].reshape(tokens, width).astype(F32)
@@ -145,6 +156,15 @@
     vec[...] = jnp.dot(expo.astype(BF16), vals, preferred_element_type=F32)
     stat[0] = jnp.broadcast_to(top, stat.shape[1:])
     stat[1] = jnp.broadcast_to(jnp.sum(expo, -1, keepdims=True), stat.shape[1:])
+
+    @pl.when(used > most)
+    def _():
+        cached(most, slots)
+
+    for i in range(slots):
+        at = (i % PAIR) * per_row
+        back[i // PAIR, at : at + per_row, :] = vectors[places[i]]
+    pack_statistics(tops, sums, places, back)
 
 
 def units(own, groups):
@@ -191,7 +211,7 @@
     lane_from = lax.rem(lax.broadcasted_iota(jnp.int32, (head_dim, 2 * head_dim), 0), quarter)
     lane_to = lax.broadcasted_iota(jnp.int32, (head_dim, 2 * head_dim), 1)
     first = jnp.where(lane_from < 3, 1.0, 0.0)
-    second = jnp.where((lane_from >= 3) & (lane_from < 5), 1.0, 0.0)
+    second = jnp.where((lane_from >= 4) & (lane_from < 7), 1.0, 0.0)
     spread = jnp.where(lane_to < head_dim, first, second)
     both = jnp.dot(sums[...], spread.astype(BF16), preferred_element_type=F32)
     top_c, sum_c = both[:, :head_dim], both[:, head_dim:]
@@ -284,7 +304,10 @@
             pltpu.VMEM((slots, per_row, context), BF16),
             pltpu.VMEM((slots, per_row, head_dim), F32),
             pltpu.VMEM((slots, per_row, head_dim), F32),
+            pltpu.VMEM((slots, per_row, head_dim), BF16),
             pltpu.VMEM((rows * steps, width), BF16),
+            pltpu.SMEM((slots,), jnp.int32),
+            pltpu.SMEM((slots,), jnp.int32),
         ],
         compiler_params=pltpu.CompilerParams(vmem_limit_bytes=12 * MIB),
         cost_estimate=pl.CostEstimate(

time: 45.1 us -> 44.9 us (level)
  no operation moved by 1% of the time
where the time goes in v14:
time: 44.9 us; the launch traced here: 44.8 us
  blocking collectives  25.9 us (58%)
  starting transfers between devices  9.56 us (21%)
  Pallas kernels  7.45 us (17%)
  waiting for transfers between devices  0.97 us (2%)
  local copies, waits for them, and re-layouts  0.7 us (2%)
    all_to_all x1, blocking collectives, shards(): lax.all_to_all(send, 'particle', split_axis=0, concat_axis=0, tiled=True)  15.5 us
    all_to_all x1, blocking collectives, shards(): lax.all_to_all(back, 'particle', split_axis=0, concat_axis=0, tiled=True)  10.4 us
    ppermute x3, starting transfers between devices, shards(): arrived.append(lax.ppermute(pair[k - 1], 'tensor', ring))  5.04 us
    ppermute x1, starting transfers between devices, shards(): given = lax.ppermute(other, 'tensor', sibling)  3.22 us
    pallas_call x1, Pallas kernels, shards(): pl.pallas_call(attend_kernel, out_shape=(jax.ShapeDtypeStruct(packed, BF1...  2.71 us
    pallas_call x1, Pallas kernels, shards(): pl.pallas_call(merge_kernel, out_shape=(block, jax.ShapeDtypeStruct((rows...  1.77 us
    ppermute x1, starting transfers between devices, shards(): total = keep + lax.ppermute(crossing, 'tensor', sibling).astype(F32)  1.29 us
    pallas_call x1, Pallas kernels, shards(): pl.pallas_call(pack_kernel, out_shape=(jax.ShapeDtypeStruct(packed, BF16)...  1.21 us
  transfers between devices with their start and end apart: 5, of which 3 were waited for; matrix products, arithmetic and copies ran while one was open for 0% of the time, Pallas kernels for 4%

profile of v14, /device:TPU:1, one launch (start us, length us, event | category | flops | bytes accessed | tf_op | source)
XLA Modules:
  0.0 44.8 jit_solution(7724634172012175300)
XLA Ops:
  0.0 0.0 copy-start.1
  0.0 0.0 copy-start.2
  0.0 0.0 copy-start.3
  0.0 0.0 copy-start.4
  0.0 1.2 %pack_queries.1 = (bf16[16,40,128]{2,1,0:T(8,128)(2,1)S(1)}, bf16[16,16,128]{2,1,0:T(8,128)(2,1)S(1)}, f32[2,16,128]{2,1,0:T(8,128)S(1)}, f32[1,8192]{1,0:T(1,128)S(1)}) custom-call(s32[16]{0:T(128)} %anc.1, bf16[16,2,1024]{2,1,0:T(2,128)(2,1)} %qp_hbm.1, f32[2,16,128]{2,1,0:T(8,128)} %constant.2.clone.tables_hbm, f32[1,8192]{1,0:T(1,128)} %bitcast.3), custom_call_target="tpu_custom_call" | custom-call | flops 10000000000 | bytes 1048576 | tf_op jit(solution)/shard_map/pack_queries/pallas_call | solution.py:267
  1.2 15.5 %all_to_all.10.recv = bf16[16,40,128]{2,1,0:T(8,128)(2,1)S(1)} all-to-all(bf16[16,40,128]{2,1,0:T(8,128)(2,1)S(1)} %get-tuple-element.19), channel_id=1, replica_groups=mesh['particle'=16,'tensor'=8] {'particle'}, dimensions={0} | all-to-all | bytes 327680 | tf_op jit(solution)/shard_map/all_to_all | solution.py:290
  16.7 0.0 slice-start
  16.7 0.0 copy-done.1
  16.7 0.0 copy-done.2
  16.7 0.0 copy-done.3
  16.7 0.0 copy-done.4
  16.7 0.0 slice-start.1
  16.8 0.0 slice-start.2
  16.8 0.0 slice-start.3
  16.8 0.0 copy-start
  16.8 2.7 %attention.1 = (bf16[16,40,128]{2,1,0:T(8,128)(2,1)S(1)}, f32[256,128]{1,0:T(8,128)S(1)}, f32[2,256,128]{2,1,0:T(8,128)S(1)}) custom-call(bf16[16,40,128]{2,1,0:T(8,128)(2,1)S(1)} %all_to_all.10.recv, bf16[16,1,512,256]{3,2,1,0:T(8,128)(2,1)S(1)} %copy-done.1, bf16[16,2,8192]{2,1,0:T(2,128)(2,1)S(1)} %copy-done.4, f32[1,8192]{1,0:T(1,128)S(1)} %get-tuple-element.20.gain, ...), custom_call_target="tpu_custom_call" | custom-call | flops 10000000000 | bytes 5242880 | tf_op jit(solution)/shard_map/attention/pallas_call | solution.py:293
  19.5 10.4 %all_to_all.11.recv = bf16[16,40,128]{2,1,0:T(8,128)(2,1)S(1)} all-to-all(bf16[16,40,128]{2,1,0:T(8,128)(2,1)S(1)} %get-tuple-element.23), channel_id=1, replica_groups=mesh['particle'=16,'tensor'=8] {'particle'}, dimensions={0} | all-to-all | bytes 327680 | tf_op jit(solution)/shard_map/all_to_all | solution.py:327
  30.0 0.0 slice-done
  30.0 0.0 slice-done.1
  30.0 0.0 slice-done.2
  30.0 0.0 slice-done.3
  30.0 0.0 copy-done
  30.0 1.8 %merge_project_sibling.1 = (bf16[3,32,1024]{2,1,0:T(8,128)(2,1)S(1)}, bf16[32,1024]{1,0:T(8,128)(2,1)S(1)}) custom-call(s32[16]{0:T(128)S(1)} %copy-done, bf16[16,40,128]{2,1,0:T(8,128)(2,1)S(1)} %all_to_all.11.recv, f32[256,128]{1,0:T(8,128)S(1)} %get-tuple-element.24.vec, f32[2,256,128]{2,1,0:T(8,128)S(1)} %get-tuple-element.25.stat, ...), custom_call_target="tpu_custom_call" | custom-call | flops 268435456 | bytes 8388608 | tf_op jit(solution)/shard_map/merge_project_sibling/pallas_call | solution.py:337
  31.8 3.2 %collective-permute-start = (bf16[3,32,1024]{2,1,0:T(8,128)(2,1)S(1)}, bf16[3,32,1024]{2,1,0:T(8,128)(2,1)S(1)}, u32[]{:S(2)}, u32[]{:S(2)}) collective-permute-start(bf16[3,32,1024]{2,1,0:T(8,128)(2,1)S(1)} %get-tuple-element.27), channel_id=1, source_target_pairs={{0,1},{1,0},{2,3},{3,2},{4,5},{5,4},{6,7},{7,6},{8,9},{9,8},{10,11... | collective-permute-start | bytes 589832 | tf_op jit(solution)/shard_map/ppermute | solution.py:356
  35.0 1.0 %project_own.1.mine = bf16[3,32,1024]{2,1,0:T(8,128)(2,1)S(1)} custom-call(bf16[32,1024]{1,0:T(8,128)(2,1)S(1)} %get-tuple-element.26.heads, bf16[1024,8192]{1,0:T(8,128)(2,1)S(1)} %bitcast.2), custom_call_target="tpu_custom_call" | custom-call | flops 268435456 | bytes 8388608 | tf_op jit(solution)/shard_map/project_own/pallas_call | solution.py:357
  36.0 0.1 collective-permute-done.given
  36.1 1.4 %collective-permute-start.1 = (bf16[32,1024]{1,0:T(8,128)(2,1)S(1)}, bf16[32,1024]{1,0:T(8,128)(2,1)S(1)}, u32[]{:S(2)}, u32[]{:S(2)}) collective-permute-start(bf16[32,1024]{1,0:T(8,128)(2,1)S(1)} %get-tuple-element.28), channel_id=1, source_target_pairs={{0,2},{1,3},{2,4},{3,5},{4,6},{5,7},{6,0},{7,1},{8,10},{9,11},{10,... | collective-permute-start | bytes 196616 | tf_op jit(solution)/shard_map/ppermute | solution.py:377
  37.5 2.6 %collective-permute-start.3 = (bf16[32,1024]{1,0:T(8,128)(2,1)S(1)}, bf16[32,1024]{1,0:T(8,128)(2,1)S(1)}, u32[]{:S(2)}, u32[]{:S(2)}) collective-permute-start(bf16[32,1024]{1,0:T(8,128)(2,1)S(1)} %get-tuple-element.31), channel_id=1, source_target_pairs={{0,4},{1,5},{2,6},{3,7},{4,0},{5,1},{6,2},{7,3},{8,12},{9,13},{10,... | collective-permute-start | bytes 196616 | tf_op jit(solution)/shard_map/ppermute | solution.py:377
  40.1 1.1 %collective-permute-start.4 = (bf16[32,1024]{1,0:T(8,128)(2,1)S(1)}, bf16[32,1024]{1,0:T(8,128)(2,1)S(1)}, u32[]{:S(2)}, u32[]{:S(2)}) collective-permute-start(bf16[32,1024]{1,0:T(8,128)(2,1)S(1)} %get-tuple-element.32), channel_id=1, source_target_pairs={{0,6},{1,7},{2,0},{3,1},{4,2},{5,3},{6,4},{7,5},{8,14},{9,15},{10,... | collective-permute-start | bytes 196616 | tf_op jit(solution)/shard_map/ppermute | solution.py:377
  41.2 0.0 collective-permute-done.1.arrived
  41.2 0.7 %project_last.1 = (f32[32,1024]{1,0:T(8,128)S(1)}, bf16[32,1024]{1,0:T(8,128)(2,1)S(1)}) custom-call(bf16[32,1024]{1,0:T(8,128)(2,1)S(1)} %get-tuple-element.26.heads, bf16[1024,8192]{1,0:T(8,128)(2,1)S(1)} %bitcast.2, bf16[32,1024]{1,0:T(8,128)(2,1)S(1)} %collective-permute-done.1.arrived), custom_call_target="tpu_custom_call" | custom-call | flops 268435456 | bytes 8388608 | tf_op jit(solution)/shard_map/project_last/pallas_call | solution.py:378
  41.9 1.3 %collective-permute-start.2 = (bf16[32,1024]{1,0:T(8,128)(2,1)S(1)}, bf16[32,1024]{1,0:T(8,128)(2,1)S(1)}, u32[]{:S(2)}, u32[]{:S(2)}) collective-permute-start(bf16[32,1024]{1,0:T(8,128)(2,1)S(1)} %get-tuple-element.30), channel_id=1, source_target_pairs={{0,1},{1,0},{2,3},{3,2},{4,5},{5,4},{6,7},{7,6},{8,9},{9,8},{10,11... | collective-permute-start | bytes 196616 | tf_op jit(solution)/shard_map/ppermute | solution.py:387
  43.2 0.0 collective-permute-done.3
  43.2 0.3 collective-permute-done.4
  43.5 0.6 %collective-permute-done.2 = bf16[32,1024]{1,0:T(8,128)(2,1)S(1)} collective-permute-done((bf16[32,1024]{1,0:T(8,128)(2,1)S(1)}, bf16[32,1024]{1,0:T(8,128)(2,1)S(1)}, u32[]{:S(2)}, u32[]{:S(2)}) %collective-permute-start.2) | collective-permute-done | bytes 65568 | tf_op jit(solution)/shard_map/ppermute | solution.py:387
  44.1 0.7 %reshape.7 = bf16[16,2,1024]{2,1,0:T(2,128)(2,1)} reshape(bf16[32,1024]{1,0:T(8,128)(2,1)S(1)} %add_convert_fusion) | data formatting | bytes 131072 | tf_op jit(solution)/shard_map/reshape | solution.py:390
  (3 shorter events, 0.1 us)
Async XLA Ops:
  0.0 16.7 %copy-start.1 = (bf16[16,1,512,256]{3,2,1,0:T(8,128)(2,1)S(1)}, bf16[16,1,512,256]{3,2,1,0:T(8,128)(2,1)}, u32[]{:S(2)}) copy-start(bf16[16,1,512,256]{3,2,1,0:T(8,128)(2,1)} %kv.1) | copy-start | bytes 12582916
  0.0 16.7 %copy-start.2 = (bf16[8192,128]{1,0:T(8,128)(2,1)S(1)}, bf16[8192,128]{1,0:T(8,128)(2,1)}, u32[]{:S(2)}) copy-start(bf16[8192,128]{1,0:T(8,128)(2,1)} %wk.1) | copy-start | bytes 6291460
  0.0 16.7 %copy-start.3 = (bf16[8192,128]{1,0:T(8,128)(2,1)S(1)}, bf16[8192,128]{1,0:T(8,128)(2,1)}, u32[]{:S(2)}) copy-start(bf16[8192,128]{1,0:T(8,128)(2,1)} %wv.1) | copy-start | bytes 6291460
  0.0 16.7 %copy-start.4 = (bf16[16,2,8192]{2,1,0:T(2,128)(2,1)S(1)}, bf16[16,2,8192]{2,1,0:T(2,128)(2,1)}, u32[]{:S(2)}) copy-start(bf16[16,2,8192]{2,1,0:T(2,128)(2,1)} %x.1) | copy-start | bytes 1572868
  16.7 13.2 %slice-start = ((s8[16777216]{0:T(1024)(128)(4,1)}), s8[4194304]{0:T(1024)(128)(4,1)S(1)}, s32[]{:S(2)}) async-start(s8[16777216]{0:T(1024)(128)(4,1)} %bitcast.1), calls=%async_computation.2 | async-start | bytes 8388608
  16.7 13.2 %slice-start.1 = ((s8[16777216]{0:T(1024)(128)(4,1)}), s8[4194304]{0:T(1024)(128)(4,1)S(1)}, s32[]{:S(2)}) async-start(s8[16777216]{0:T(1024)(128)(4,1)} %bitcast.1), calls=%async_computation.3 | async-start | bytes 8388608
  16.8 13.2 %slice-start.2 = ((s8[16777216]{0:T(1024)(128)(4,1)}), s8[4194304]{0:T(1024)(128)(4,1)S(1)}, s32[]{:S(2)}) async-start(s8[16777216]{0:T(1024)(128)(4,1)} %bitcast.1), calls=%async_computation.4 | async-start | bytes 8388608
  16.8 13.2 %slice-start.3 = ((s8[16777216]{0:T(1024)(128)(4,1)}), s8[4194304]{0:T(1024)(128)(4,1)S(1)}, s32[]{:S(2)}) async-start(s8[16777216]{0:T(1024)(128)(4,1)} %bitcast.1), calls=%async_computation.5 | async-start | bytes 8388608
  16.8 13.2 %copy-start = (s32[16]{0:T(128)S(1)}, s32[16]{0:T(128)}, u32[]{:S(2)}) copy-start(s32[16]{0:T(128)} %anc.1) | copy-start | bytes 196
  31.8 4.3 %collective-permute-start = (bf16[3,32,1024]{2,1,0:T(8,128)(2,1)S(1)}, bf16[3,32,1024]{2,1,0:T(8,128)(2,1)S(1)}, u32[]{:S(2)}, u32[]{:S(2)}) collective-permute-start(bf16[3,32,1024]{2,1,0:T(8,128)(2,1)S(1)} %get-tuple-element.27), channel_id=1, source_target_pairs={{0,1},{1,0},{2,3},{3,2},{4,5},{5,4},{6,7},{7,6},{8,9},{9,8},{10,11... | collective-permute-start | bytes 589832 | tf_op jit(solution)/shard_map/ppermute | solution.py:356
  36.1 5.0 %collective-permute-start.1 = (bf16[32,1024]{1,0:T(8,128)(2,1)S(1)}, bf16[32,1024]{1,0:T(8,128)(2,1)S(1)}, u32[]{:S(2)}, u32[]{:S(2)}) collective-permute-start(bf16[32,1024]{1,0:T(8,128)(2,1)S(1)} %get-tuple-element.28), channel_id=1, source_target_pairs={{0,2},{1,3},{2,4},{3,5},{4,6},{5,7},{6,0},{7,1},{8,10},{9,11},{10,... | collective-permute-start | bytes 196616 | tf_op jit(solution)/shard_map/ppermute | solution.py:377
  37.5 5.7 %collective-permute-start.3 = (bf16[32,1024]{1,0:T(8,128)(2,1)S(1)}, bf16[32,1024]{1,0:T(8,128)(2,1)S(1)}, u32[]{:S(2)}, u32[]{:S(2)}) collective-permute-start(bf16[32,1024]{1,0:T(8,128)(2,1)S(1)} %get-tuple-element.31), channel_id=1, source_target_pairs={{0,4},{1,5},{2,6},{3,7},{4,0},{5,1},{6,2},{7,3},{8,12},{9,13},{10,... | collective-permute-start | bytes 196616 | tf_op jit(solution)/shard_map/ppermute | solution.py:377
  40.1 3.4 %collective-permute-start.4 = (bf16[32,1024]{1,0:T(8,128)(2,1)S(1)}, bf16[32,1024]{1,0:T(8,128)(2,1)S(1)}, u32[]{:S(2)}, u32[]{:S(2)}) collective-permute-start(bf16[32,1024]{1,0:T(8,128)(2,1)S(1)} %get-tuple-element.32), channel_id=1, source_target_pairs={{0,6},{1,7},{2,0},{3,1},{4,2},{5,3},{6,4},{7,5},{8,14},{9,15},{10,... | collective-permute-start | bytes 196616 | tf_op jit(solution)/shard_map/ppermute | solution.py:377
  41.9 2.2 %collective-permute-start.2 = (bf16[32,1024]{1,0:T(8,128)(2,1)S(1)}, bf16[32,1024]{1,0:T(8,128)(2,1)S(1)}, u32[]{:S(2)}, u32[]{:S(2)}) collective-permute-start(bf16[32,1024]{1,0:T(8,128)(2,1)S(1)} %get-tuple-element.30), channel_id=1, source_target_pairs={{0,1},{1,0},{2,3},{3,2},{4,5},{5,4},{6,7},{7,6},{8,9},{9,8},{10,11... | collective-permute-start | bytes 196616 | tf_op jit(solution)/shard_map/ppermute | solution.py:387

commit v15 on v14

--- a/solution.py
+++ b/solution.py
@@ -102,40 +102,6 @@
     devices, _, head_dim = recv.shape
     per_row = queries.shape[1]
     lane = lax.broadcasted_iota(jnp.int32, (per_row, head_dim), 1)
-    slots = devices * PAIR
-    for k in range(slots):
-        chosen[k] = 0
-        row_of[k] = 0
-    used = jnp.int32(0)
-    places = []
-    for d in range(devices):
-        spot = recv[d, PAIR * per_row :, :].astype(F32)
-        for j in range(PAIR):
-            row = spot[0, j * (head_dim // PAIR)].astype(jnp.int32)
-            chosen[used] = d * PAIR + j
-            row_of[used] = jnp.maximum(row, 0)
-            places.append(used)
-            used = used + jnp.where(row >= 0, 1, 0)
-
-    def cached(first, last):
-        for k in range(first, last):
-            d, j = lax.div(chosen[k], PAIR), lax.rem(chosen[k], PAIR)
-            asked = recv[d, pl.ds(pl.multiple_of(j * per_row, per_row), per_row), :]
-            scores[k] = lax.dot_general(
-                asked, kv[row_of[k], 0, :, :head_dim], NT, preferred_element_type=F32
-            ) * head_dim ** (-0.5)
-        for k in range(first, last):
-            top = jnp.max(scores[k], -1, keepdims=True)
-            expo = jnp.exp(scores[k] - top)
-            expos[k] = expo.astype(BF16)
-            tops[k] = jnp.broadcast_to(top, lane.shape)
-            sums[k] = jnp.broadcast_to(jnp.sum(expo, -1, keepdims=True), lane.shape)
-        for k in range(first, last):
-            vector = jnp.dot(expos[k], kv[row_of[k], 0, :, head_dim:], preferred_element_type=F32)
-            vectors[k] = (vector / sums[k]).astype(BF16)
-
-    most = slots * 3 // 4
-    cached(0, most)
     rows, steps, width = x.shape
     tokens = rows * steps
     floats = x[...].reshape(tokens, width).astype(F32)
@@ -156,6 +122,41 @@
     vec[...] = jnp.dot(expo.astype(BF16), vals, preferred_element_type=F32)
     stat[0] = jnp.broadcast_to(top, stat.shape[1:])
     stat[1] = jnp.broadcast_to(jnp.sum(expo, -1, keepdims=True), stat.shape[1:])
+    slots = devices * PAIR
+    for k in range(slots):
+        chosen[k] = 0
+        row_of[k] = 0
+    used = jnp.int32(0)
+    places = []
+    for d in range(devices):
+        spot = recv[d, PAIR * per_row :, :].astype(F32)
+        for j in range(PAIR):
+            row = spot[0, j * (head_dim // PAIR)].astype(jnp.int32)
+            chosen[used] = d * PAIR + j
+            row_of[used] = jnp.maximum(row, 0)
+            places.append(used)
+            used = used + jnp.where(row >= 0, 1, 0)
+
+    def cached(first, last):
+        for k in range(first, last):
+            d = lax.shift_right_logical(chosen[k], PAIR.bit_length() - 1)
+            j = lax.bitwise_and(chosen[k], PAIR - 1)
+            asked = recv[d, pl.ds(pl.multiple_of(j * per_row, per_row), per_row), :]
+            scores[k] = lax.dot_general(
+                asked, kv[row_of[k], 0, :, :head_dim], NT, preferred_element_type=F32
+            ) * head_dim ** (-0.5)
+        for k in range(first, last):
+            top = jnp.max(scores[k], -1, keepdims=True)
+            expo = jnp.exp(scores[k] - top)
+            expos[k] = expo.astype(BF16)
+            tops[k] = jnp.broadcast_to(top, lane.shape)
+            sums[k] = jnp.broadcast_to(jnp.sum(expo, -1, keepdims=True), lane.shape)
+        for k in range(first, last):
+            vector = jnp.dot(expos[k], kv[row_of[k], 0, :, head_dim:], preferred_element_type=F32)
+            vectors[k] = (vector / sums[k]).astype(BF16)
+
+    most = slots * 3 // 4
+    cached(0, most)
 
     @pl.when(used > most)
     def _():
@@ -190,7 +191,7 @@
         out[k] = product(wide, w, block, tokens, column).astype(BF16)
 
 
-def merge_kernel(anc, recv, vec, stat, w, out, heads, grid_ref, sums, lined, count):
+def merge_kernel(anc, recv, vec, stat, w, out, heads, grid_ref, sums, count):
     devices, chunk, head_dim = recv.shape
     per_row = (chunk - MORE) // PAIR
     rows = vec.shape[0] // per_row
@@ -223,8 +224,9 @@
     grid_ref[...] = (grid_ref[...] * factor_c + vec[...] * factor_f) * share
     for h in range(per_row // steps):
         for s in range(steps):
-            lined[h, pl.ds(s, rows, stride=steps), :] = grid_ref[pl.ds(h * steps + s, rows, stride=per_row), :]
-        heads[:, pl.ds(h * head_dim, head_dim)] = lined[h].astype(BF16)
+            heads[pl.ds(s * rows, rows), pl.ds(h * head_dim, head_dim)] = grid_ref[
+                pl.ds(h * steps + s, rows, stride=per_row), :
+            ].astype(BF16)
     project(heads, w, out, False)
 
 
@@ -345,7 +347,6 @@
         scratch_shapes=[
             pltpu.VMEM((rows * per_row, head_dim), F32),
             pltpu.VMEM((rows * per_row, head_dim), BF16),
-            pltpu.VMEM((heads, rows * steps, head_dim), F32),
             pltpu.SMEM((devices,), jnp.int32),
         ],
         compiler_params=params,
@@ -387,7 +388,7 @@
     total = keep + lax.ppermute(crossing, "tensor", sibling).astype(F32)
     for part in arrived[1:]:
         total = total + part.astype(F32)
-    return total.astype(BF16).reshape(rows, steps, column)
+    return total.astype(BF16).reshape(steps, rows, column).swapaxes(0, 1)
 
 
 def solution(mesh):

time: 44.9 us -> 44.8 us (level)
  no operation moved by 1% of the time
where the time goes in v15:
time: 44.8 us; the launch traced here: 44.7 us
  blocking collectives  25.9 us (58%)
  starting transfers between devices  9.56 us (21%)
  Pallas kernels  7.29 us (16%)
  waiting for transfers between devices  0.98 us (2%)
  local copies, waits for them, and re-layouts  0.74 us (2%)
    all_to_all x1, blocking collectives, shards(): lax.all_to_all(send, 'particle', split_axis=0, concat_axis=0, tiled=True)  15.5 us
    all_to_all x1, blocking collectives, shards(): lax.all_to_all(back, 'particle', split_axis=0, concat_axis=0, tiled=True)  10.5 us
    ppermute x3, starting transfers between devices, shards(): arrived.append(lax.ppermute(pair[k - 1], 'tensor', ring))  5.05 us
    ppermute x1, starting transfers between devices, shards(): given = lax.ppermute(other, 'tensor', sibling)  3.22 us
    pallas_call x1, Pallas kernels, shards(): pl.pallas_call(attend_kernel, out_shape=(jax.ShapeDtypeStruct(packed, BF1...  2.55 us
    pallas_call x1, Pallas kernels, shards(): pl.pallas_call(merge_kernel, out_shape=(block, jax.ShapeDtypeStruct((rows...  1.77 us
    ppermute x1, starting transfers between devices, shards(): total = keep + lax.ppermute(crossing, 'tensor', sibling).astype(F32)  1.29 us
    pallas_call x1, Pallas kernels, shards(): pl.pallas_call(pack_kernel, out_shape=(jax.ShapeDtypeStruct(packed, BF16)...  1.21 us
  transfers between devices with their start and end apart: 5, of which 3 were waited for; matrix products, arithmetic and copies ran while one was open for 0% of the time, Pallas kernels for 4%

profile of v15, /device:TPU:1, one launch (start us, length us, event | category | flops | bytes accessed | tf_op | source)
XLA Modules:
  0.0 44.7 jit_solution(9276894420475008113)
XLA Ops:
  0.0 0.0 copy-start.1
  0.0 0.0 copy-start.2
  0.0 0.0 copy-start.3
  0.0 0.0 copy-start.4
  0.0 1.2 %pack_queries.1 = (bf16[16,40,128]{2,1,0:T(8,128)(2,1)S(1)}, bf16[16,16,128]{2,1,0:T(8,128)(2,1)S(1)}, f32[2,16,128]{2,1,0:T(8,128)S(1)}, f32[1,8192]{1,0:T(1,128)S(1)}) custom-call(s32[16]{0:T(128)} %anc.1, bf16[16,2,1024]{2,1,0:T(2,128)(2,1)} %qp_hbm.1, f32[2,16,128]{2,1,0:T(8,128)} %constant.2.clone.tables_hbm, f32[1,8192]{1,0:T(1,128)} %bitcast.8), custom_call_target="tpu_custom_call" | custom-call | flops 10000000000 | bytes 1048576 | tf_op jit(solution)/shard_map/pack_queries/pallas_call | solution.py:269
  1.2 15.5 %all_to_all.10.recv = bf16[16,40,128]{2,1,0:T(8,128)(2,1)S(1)} all-to-all(bf16[16,40,128]{2,1,0:T(8,128)(2,1)S(1)} %get-tuple-element.19), channel_id=1, replica_groups=mesh['particle'=16,'tensor'=8] {'particle'}, dimensions={0} | all-to-all | bytes 327680 | tf_op jit(solution)/shard_map/all_to_all | solution.py:292
  16.7 0.0 slice-start
  16.7 0.0 copy-done.1
  16.7 0.0 copy-done.2
  16.7 0.0 copy-done.3
  16.7 0.0 copy-done.4
  16.7 0.0 slice-start.1
  16.8 0.0 slice-start.2
  16.8 0.0 slice-start.3
  16.8 0.0 copy-start
  16.8 2.5 %attention.1 = (bf16[16,40,128]{2,1,0:T(8,128)(2,1)S(1)}, f32[256,128]{1,0:T(8,128)S(1)}, f32[2,256,128]{2,1,0:T(8,128)S(1)}) custom-call(bf16[16,40,128]{2,1,0:T(8,128)(2,1)S(1)} %all_to_all.10.recv, bf16[16,1,512,256]{3,2,1,0:T(8,128)(2,1)S(1)} %copy-done.1, bf16[16,2,8192]{2,1,0:T(2,128)(2,1)S(1)} %copy-done.4, f32[1,8192]{1,0:T(1,128)S(1)} %get-tuple-element.20.gain, ...), custom_call_target="tpu_custom_call" | custom-call | flops 10000000000 | bytes 5242880 | tf_op jit(solution)/shard_map/attention/pallas_call | solution.py:295
  19.3 10.5 %all_to_all.11.recv = bf16[16,40,128]{2,1,0:T(8,128)(2,1)S(1)} all-to-all(bf16[16,40,128]{2,1,0:T(8,128)(2,1)S(1)} %get-tuple-element.23), channel_id=1, replica_groups=mesh['particle'=16,'tensor'=8] {'particle'}, dimensions={0} | all-to-all | bytes 327680 | tf_op jit(solution)/shard_map/all_to_all | solution.py:329
  29.8 0.0 slice-done
  29.8 0.0 slice-done.1
  29.8 0.0 slice-done.2
  29.8 0.0 slice-done.3
  29.8 0.0 copy-done
  29.8 1.8 %merge_project_sibling.1 = (bf16[3,32,1024]{2,1,0:T(8,128)(2,1)S(1)}, bf16[32,1024]{1,0:T(8,128)(2,1)S(1)}) custom-call(s32[16]{0:T(128)S(1)} %copy-done, bf16[16,40,128]{2,1,0:T(8,128)(2,1)S(1)} %all_to_all.11.recv, f32[256,128]{1,0:T(8,128)S(1)} %get-tuple-element.24.vec, f32[2,256,128]{2,1,0:T(8,128)S(1)} %get-tuple-element.25.stat, ...), custom_call_target="tpu_custom_call" | custom-call | flops 268435456 | bytes 8388608 | tf_op jit(solution)/shard_map/merge_project_sibling/pallas_call | solution.py:339
  31.6 3.2 %collective-permute-start = (bf16[3,32,1024]{2,1,0:T(8,128)(2,1)S(1)}, bf16[3,32,1024]{2,1,0:T(8,128)(2,1)S(1)}, u32[]{:S(2)}, u32[]{:S(2)}) collective-permute-start(bf16[3,32,1024]{2,1,0:T(8,128)(2,1)S(1)} %get-tuple-element.27), channel_id=1, source_target_pairs={{0,1},{1,0},{2,3},{3,2},{4,5},{5,4},{6,7},{7,6},{8,9},{9,8},{10,11... | collective-permute-start | bytes 589832 | tf_op jit(solution)/shard_map/ppermute | solution.py:357
  34.8 1.0 %project_own.1.mine = bf16[3,32,1024]{2,1,0:T(8,128)(2,1)S(1)} custom-call(bf16[32,1024]{1,0:T(8,128)(2,1)S(1)} %get-tuple-element.26.heads, bf16[1024,8192]{1,0:T(8,128)(2,1)S(1)} %bitcast.6), custom_call_target="tpu_custom_call" | custom-call | flops 268435456 | bytes 8388608 | tf_op jit(solution)/shard_map/project_own/pallas_call | solution.py:358
  35.8 0.1 collective-permute-done.given
  36.0 1.4 %collective-permute-start.1 = (bf16[32,1024]{1,0:T(8,128)(2,1)S(1)}, bf16[32,1024]{1,0:T(8,128)(2,1)S(1)}, u32[]{:S(2)}, u32[]{:S(2)}) collective-permute-start(bf16[32,1024]{1,0:T(8,128)(2,1)S(1)} %get-tuple-element.28), channel_id=1, source_target_pairs={{0,2},{1,3},{2,4},{3,5},{4,6},{5,7},{6,0},{7,1},{8,10},{9,11},{10,... | collective-permute-start | bytes 196616 | tf_op jit(solution)/shard_map/ppermute | solution.py:378
  37.3 2.6 %collective-permute-start.3 = (bf16[32,1024]{1,0:T(8,128)(2,1)S(1)}, bf16[32,1024]{1,0:T(8,128)(2,1)S(1)}, u32[]{:S(2)}, u32[]{:S(2)}) collective-permute-start(bf16[32,1024]{1,0:T(8,128)(2,1)S(1)} %get-tuple-element.31), channel_id=1, source_target_pairs={{0,4},{1,5},{2,6},{3,7},{4,0},{5,1},{6,2},{7,3},{8,12},{9,13},{10,... | collective-permute-start | bytes 196616 | tf_op jit(solution)/shard_map/ppermute | solution.py:378
  39.9 1.1 %collective-permute-start.4 = (bf16[32,1024]{1,0:T(8,128)(2,1)S(1)}, bf16[32,1024]{1,0:T(8,128)(2,1)S(1)}, u32[]{:S(2)}, u32[]{:S(2)}) collective-permute-start(bf16[32,1024]{1,0:T(8,128)(2,1)S(1)} %get-tuple-element.32), channel_id=1, source_target_pairs={{0,6},{1,7},{2,0},{3,1},{4,2},{5,3},{6,4},{7,5},{8,14},{9,15},{10,... | collective-permute-start | bytes 196616 | tf_op jit(solution)/shard_map/ppermute | solution.py:378
  41.0 0.0 collective-permute-done.1.arrived
  41.0 0.7 %project_last.1 = (f32[32,1024]{1,0:T(8,128)S(1)}, bf16[32,1024]{1,0:T(8,128)(2,1)S(1)}) custom-call(bf16[32,1024]{1,0:T(8,128)(2,1)S(1)} %get-tuple-element.26.heads, bf16[1024,8192]{1,0:T(8,128)(2,1)S(1)} %bitcast.6, bf16[32,1024]{1,0:T(8,128)(2,1)S(1)} %collective-permute-done.1.arrived), custom_call_target="tpu_custom_call" | custom-call | flops 268435456 | bytes 8388608 | tf_op jit(solution)/shard_map/project_last/pallas_call | solution.py:379
  41.7 1.3 %collective-permute-start.2 = (bf16[32,1024]{1,0:T(8,128)(2,1)S(1)}, bf16[32,1024]{1,0:T(8,128)(2,1)S(1)}, u32[]{:S(2)}, u32[]{:S(2)}) collective-permute-start(bf16[32,1024]{1,0:T(8,128)(2,1)S(1)} %get-tuple-element.30), channel_id=1, source_target_pairs={{0,1},{1,0},{2,3},{3,2},{4,5},{5,4},{6,7},{7,6},{8,9},{9,8},{10,11... | collective-permute-start | bytes 196616 | tf_op jit(solution)/shard_map/ppermute | solution.py:388
  43.0 0.0 collective-permute-done.3
  43.0 0.3 collective-permute-done.4
  43.4 0.6 %collective-permute-done.2 = bf16[32,1024]{1,0:T(8,128)(2,1)S(1)} collective-permute-done((bf16[32,1024]{1,0:T(8,128)(2,1)S(1)}, bf16[32,1024]{1,0:T(8,128)(2,1)S(1)}, u32[]{:S(2)}, u32[]{:S(2)}) %collective-permute-start.2) | collective-permute-done | bytes 65568 | tf_op jit(solution)/shard_map/ppermute | solution.py:388
  44.0 0.7 %copy.12 = bf16[2,16,1024]{2,0,1:T(2,128)(2,1)} copy(bf16[2,16,1024]{2,1,0:T(8,128)(2,1)S(1)} %bitcast.7) | data formatting | bytes 131072 | tf_op jit(solution)/shard_map/reshape | solution.py:391
  (3 shorter events, 0.1 us)
Async XLA Ops:
  0.0 16.7 %copy-start.1 = (bf16[16,1,512,256]{3,2,1,0:T(8,128)(2,1)S(1)}, bf16[16,1,512,256]{3,2,1,0:T(8,128)(2,1)}, u32[]{:S(2)}) copy-start(bf16[16,1,512,256]{3,2,1,0:T(8,128)(2,1)} %kv.1) | copy-start | bytes 12582916
  0.0 16.7 %copy-start.2 = (bf16[8192,128]{1,0:T(8,128)(2,1)S(1)}, bf16[8192,128]{1,0:T(8,128)(2,1)}, u32[]{:S(2)}) copy-start(bf16[8192,128]{1,0:T(8,128)(2,1)} %wk.1) | copy-start | bytes 6291460
  0.0 16.7 %copy-start.3 = (bf16[8192,128]{1,0:T(8,128)(2,1)S(1)}, bf16[8192,128]{1,0:T(8,128)(2,1)}, u32[]{:S(2)}) copy-start(bf16[8192,128]{1,0:T(8,128)(2,1)} %wv.1) | copy-start | bytes 6291460
  0.0 16.7 %copy-start.4 = (bf16[16,2,8192]{2,1,0:T(2,128)(2,1)S(1)}, bf16[16,2,8192]{2,1,0:T(2,128)(2,1)}, u32[]{:S(2)}) copy-start(bf16[16,2,8192]{2,1,0:T(2,128)(2,1)} %x.1) | copy-start | bytes 1572868
  16.7 13.1 %slice-start = ((s8[16777216]{0:T(1024)(128)(4,1)}), s8[4194304]{0:T(1024)(128)(4,1)S(1)}, s32[]{:S(2)}) async-start(s8[16777216]{0:T(1024)(128)(4,1)} %bitcast.5), calls=%async_computation.2 | async-start | bytes 8388608
  16.7 13.1 %slice-start.1 = ((s8[16777216]{0:T(1024)(128)(4,1)}), s8[4194304]{0:T(1024)(128)(4,1)S(1)}, s32[]{:S(2)}) async-start(s8[16777216]{0:T(1024)(128)(4,1)} %bitcast.5), calls=%async_computation.3 | async-start | bytes 8388608
  16.8 13.0 %slice-start.2 = ((s8[16777216]{0:T(1024)(128)(4,1)}), s8[4194304]{0:T(1024)(128)(4,1)S(1)}, s32[]{:S(2)}) async-start(s8[16777216]{0:T(1024)(128)(4,1)} %bitcast.5), calls=%async_computation.4 | async-start | bytes 8388608
  16.8 13.0 %slice-start.3 = ((s8[16777216]{0:T(1024)(128)(4,1)}), s8[4194304]{0:T(1024)(128)(4,1)S(1)}, s32[]{:S(2)}) async-start(s8[16777216]{0:T(1024)(128)(4,1)} %bitcast.5), calls=%async_computation.5 | async-start | bytes 8388608
  16.8 13.0 %copy-start = (s32[16]{0:T(128)S(1)}, s32[16]{0:T(128)}, u32[]{:S(2)}) copy-start(s32[16]{0:T(128)} %anc.1) | copy-start | bytes 196
  31.6 4.3 %collective-permute-start = (bf16[3,32,1024]{2,1,0:T(8,128)(2,1)S(1)}, bf16[3,32,1024]{2,1,0:T(8,128)(2,1)S(1)}, u32[]{:S(2)}, u32[]{:S(2)}) collective-permute-start(bf16[3,32,1024]{2,1,0:T(8,128)(2,1)S(1)} %get-tuple-element.27), channel_id=1, source_target_pairs={{0,1},{1,0},{2,3},{3,2},{4,5},{5,4},{6,7},{7,6},{8,9},{9,8},{10,11... | collective-permute-start | bytes 589832 | tf_op jit(solution)/shard_map/ppermute | solution.py:357
  36.0 5.1 %collective-permute-start.1 = (bf16[32,1024]{1,0:T(8,128)(2,1)S(1)}, bf16[32,1024]{1,0:T(8,128)(2,1)S(1)}, u32[]{:S(2)}, u32[]{:S(2)}) collective-permute-start(bf16[32,1024]{1,0:T(8,128)(2,1)S(1)} %get-tuple-element.28), channel_id=1, source_target_pairs={{0,2},{1,3},{2,4},{3,5},{4,6},{5,7},{6,0},{7,1},{8,10},{9,11},{10,... | collective-permute-start | bytes 196616 | tf_op jit(solution)/shard_map/ppermute | solution.py:378
  37.3 5.7 %collective-permute-start.3 = (bf16[32,1024]{1,0:T(8,128)(2,1)S(1)}, bf16[32,1024]{1,0:T(8,128)(2,1)S(1)}, u32[]{:S(2)}, u32[]{:S(2)}) collective-permute-start(bf16[32,1024]{1,0:T(8,128)(2,1)S(1)} %get-tuple-element.31), channel_id=1, source_target_pairs={{0,4},{1,5},{2,6},{3,7},{4,0},{5,1},{6,2},{7,3},{8,12},{9,13},{10,... | collective-permute-start | bytes 196616 | tf_op jit(solution)/shard_map/ppermute | solution.py:378
  39.9 3.4 %collective-permute-start.4 = (bf16[32,1024]{1,0:T(8,128)(2,1)S(1)}, bf16[32,1024]{1,0:T(8,128)(2,1)S(1)}, u32[]{:S(2)}, u32[]{:S(2)}) collective-permute-start(bf16[32,1024]{1,0:T(8,128)(2,1)S(1)} %get-tuple-element.32), channel_id=1, source_target_pairs={{0,6},{1,7},{2,0},{3,1},{4,2},{5,3},{6,4},{7,5},{8,14},{9,15},{10,... | collective-permute-start | bytes 196616 | tf_op jit(solution)/shard_map/ppermute | solution.py:378
  41.7 2.2 %collective-permute-start.2 = (bf16[32,1024]{1,0:T(8,128)(2,1)S(1)}, bf16[32,1024]{1,0:T(8,128)(2,1)S(1)}, u32[]{:S(2)}, u32[]{:S(2)}) collective-permute-start(bf16[32,1024]{1,0:T(8,128)(2,1)S(1)} %get-tuple-element.30), channel_id=1, source_target_pairs={{0,1},{1,0},{2,3},{3,2},{4,5},{5,4},{6,7},{7,6},{8,9},{9,8},{10,11... | collective-permute-start | bytes 196616 | tf_op jit(solution)/shard_map/ppermute | solution.py:388

commit v16 on v15

--- a/solution.py
+++ b/solution.py
@@ -7,6 +7,7 @@
 from jax.sharding import PartitionSpec as P
 
 PAIR = 2
+PARTNERS = (3, 2, 1)
 MORE = 8
 THETA = 500000.0
 EPSILON = 1e-05
@@ -168,11 +169,11 @@
     pack_statistics(tops, sums, places, back)
 
 
-def units(own, groups):
+def units(own):
     index = lax.axis_index("tensor")
     y, core = lax.div(index, 2), lax.rem(index, 2)
     core = core if own else 1 - core
-    return [2 * lax.rem(y + k, groups) + core for k in (*range(1, groups), 0)]
+    return [2 * lax.bitwise_xor(y, k) + core for k in (*PARTNERS, 0)]
 
 
 def product(wide, w, block, tokens, column):
@@ -187,7 +188,7 @@
 def project(heads, w, out, own):
     away, tokens, column = out.shape
     wide = widen(heads)
-    for k, block in enumerate(units(own, away + 1)[:away]):
+    for k, block in enumerate(units(own)[:away]):
         out[k] = product(wide, w, block, tokens, column).astype(BF16)
 
 
@@ -241,10 +242,9 @@
 
 def last_kernel(heads, w, arrived, keep, crossing):
     tokens, column = keep.shape
-    groups = w.shape[1] // column // 2
     wide = widen(heads)
-    crossing[...] = product(wide, w, units(False, groups)[-1], tokens, column).astype(BF16)
-    keep[...] = product(wide, w, units(True, groups)[-1], tokens, column) + arrived[...].astype(F32)
+    crossing[...] = product(wide, w, units(False)[-1], tokens, column).astype(BF16)
+    keep[...] = product(wide, w, units(True)[-1], tokens, column) + arrived[...].astype(F32)
 
 
 def shards(inputs, norm_gain, query_proj, w_key, w_value, w_out, kv_cache, ancestors):
@@ -328,8 +328,7 @@
     )
     home = lax.all_to_all(back, "particle", split_axis=0, concat_axis=0, tiled=True)
 
-    groups = tensor // 2
-    away = groups - 1
+    away = len(PARTNERS)
     block = jax.ShapeDtypeStruct((away, rows * steps, column), BF16)
     one = jax.ShapeDtypeStruct((rows * steps, column), BF16)
     params = pltpu.CompilerParams(vmem_limit_bytes=8 * MIB)
@@ -373,9 +372,9 @@
         name="add_sibling",
     )(mine, given)
     arrived = []
-    for k in range(1, groups):
-        ring = [(i, ((i // 2 + k) % groups) * 2 + i % 2) for i in range(tensor)]
-        arrived.append(lax.ppermute(pair[k - 1], "tensor", ring))
+    for part, k in zip(pair, PARTNERS):
+        exchange = [(i, ((i // 2) ^ k) * 2 + i % 2) for i in range(tensor)]
+        arrived.append(lax.ppermute(part, "tensor", exchange))
     keep, crossing = pl.pallas_call(
         last_kernel,
         out_shape=(jax.ShapeDtypeStruct(one.shape, F32), one),

time: 44.8 us -> 45.1 us (level)
  waiting for transfers between devices: 0.98 us -> 2.32 us
  starting transfers between devices: 9.56 us -> 8.51 us
    ppermute x3, starting transfers between devices: 5.05 us -> 3.48 us  [shards(): arrived.append(lax.ppermute(part, 'tensor', exchange))]
    ppermute x3, waiting for transfers between devices: 0.32 us -> 1.41 us  [shards(): arrived.append(lax.ppermute(part, 'tensor', exchange))]
    ppermute x1, starting transfers between devices: 1.29 us -> 1.81 us  [shards(): total = keep + lax.ppermute(crossing, 'tensor', sibling).astype(F32)]
  transfers between devices with their start and end apart: 5 -> 5, of which waited for: 3 -> 4; matrix products, arithmetic and copies ran while one was open for 0% -> 0% of each run, Pallas kernels for 4% -> 4%
where the time goes in v16:
time: 45.1 us; the launch traced here: 45 us
  blocking collectives  25.9 us (57%)
  starting transfers between devices  8.51 us (19%)
  Pallas kernels  7.29 us (16%)
  waiting for transfers between devices  2.32 us (5%)
  local copies, waits for them, and re-layouts  0.74 us (2%)
    all_to_all x1, blocking collectives, shards(): lax.all_to_all(send, 'particle', split_axis=0, concat_axis=0, tiled=True)  15.5 us
    all_to_all x1, blocking collectives, shards(): lax.all_to_all(back, 'particle', split_axis=0, concat_axis=0, tiled=True)  10.5 us
    ppermute x3, starting transfers between devices, shards(): arrived.append(lax.ppermute(part, 'tensor', exchange))  3.48 us
    ppermute x1, starting transfers between devices, shards(): given = lax.ppermute(other, 'tensor', sibling)  3.21 us
    pallas_call x1, Pallas kernels, shards(): pl.pallas_call(attend_kernel, out_shape=(jax.ShapeDtypeStruct(packed, BF1...  2.55 us
    ppermute x1, starting transfers between devices, shards(): total = keep + lax.ppermute(crossing, 'tensor', sibling).astype(F32)  1.81 us
    pallas_call x1, Pallas kernels, shards(): pl.pallas_call(merge_kernel, out_shape=(block, jax.ShapeDtypeStruct((rows...  1.77 us
    ppermute x3, waiting for transfers between devices, shards(): arrived.append(lax.ppermute(part, 'tensor', exchange))  1.41 us
  transfers between devices with their start and end apart: 5, of which 4 were waited for; matrix products, arithmetic and copies ran while one was open for 0% of the time, Pallas kernels for 4%

profile of v16, /device:TPU:1, one launch (start us, length us, event | category | flops | bytes accessed | tf_op | source)
XLA Modules:
  0.0 45.0 jit_solution(17914235804326212091)
XLA Ops:
  0.0 0.0 copy-start.1
  0.0 0.0 copy-start.2
  0.0 0.0 copy-start.3
  0.0 0.0 copy-start.4
  0.0 1.2 %pack_queries.1 = (bf16[16,40,128]{2,1,0:T(8,128)(2,1)S(1)}, bf16[16,16,128]{2,1,0:T(8,128)(2,1)S(1)}, f32[2,16,128]{2,1,0:T(8,128)S(1)}, f32[1,8192]{1,0:T(1,128)S(1)}) custom-call(s32[16]{0:T(128)} %anc.1, bf16[16,2,1024]{2,1,0:T(2,128)(2,1)} %qp_hbm.1, f32[2,16,128]{2,1,0:T(8,128)} %constant.2.clone.tables_hbm, f32[1,8192]{1,0:T(1,128)} %bitcast.8), custom_call_target="tpu_custom_call" | custom-call | flops 10000000000 | bytes 1048576 | tf_op jit(solution)/shard_map/pack_queries/pallas_call | solution.py:269
  1.2 15.5 %all_to_all.10.recv = bf16[16,40,128]{2,1,0:T(8,128)(2,1)S(1)} all-to-all(bf16[16,40,128]{2,1,0:T(8,128)(2,1)S(1)} %get-tuple-element.19), channel_id=1, replica_groups=mesh['particle'=16,'tensor'=8] {'particle'}, dimensions={0} | all-to-all | bytes 327680 | tf_op jit(solution)/shard_map/all_to_all | solution.py:292
  16.7 0.0 slice-start
  16.7 0.0 copy-done.1
  16.7 0.0 copy-done.2
  16.7 0.0 copy-done.3
  16.7 0.0 copy-done.4
  16.7 0.0 slice-start.1
  16.8 0.0 slice-start.2
  16.8 0.0 slice-start.3
  16.8 0.0 copy-start
  16.8 2.5 %attention.1 = (bf16[16,40,128]{2,1,0:T(8,128)(2,1)S(1)}, f32[256,128]{1,0:T(8,128)S(1)}, f32[2,256,128]{2,1,0:T(8,128)S(1)}) custom-call(bf16[16,40,128]{2,1,0:T(8,128)(2,1)S(1)} %all_to_all.10.recv, bf16[16,1,512,256]{3,2,1,0:T(8,128)(2,1)S(1)} %copy-done.1, bf16[16,2,8192]{2,1,0:T(2,128)(2,1)S(1)} %copy-done.4, f32[1,8192]{1,0:T(1,128)S(1)} %get-tuple-element.20.gain, ...), custom_call_target="tpu_custom_call" | custom-call | flops 10000000000 | bytes 5242880 | tf_op jit(solution)/shard_map/attention/pallas_call | solution.py:295
  19.3 10.5 %all_to_all.11.recv = bf16[16,40,128]{2,1,0:T(8,128)(2,1)S(1)} all-to-all(bf16[16,40,128]{2,1,0:T(8,128)(2,1)S(1)} %get-tuple-element.23), channel_id=1, replica_groups=mesh['particle'=16,'tensor'=8] {'particle'}, dimensions={0} | all-to-all | bytes 327680 | tf_op jit(solution)/shard_map/all_to_all | solution.py:329
  29.8 0.0 slice-done
  29.8 0.0 slice-done.1
  29.8 0.0 slice-done.2
  29.8 0.0 slice-done.3
  29.8 0.0 copy-done
  29.8 1.8 %merge_project_sibling.1 = (bf16[3,32,1024]{2,1,0:T(8,128)(2,1)S(1)}, bf16[32,1024]{1,0:T(8,128)(2,1)S(1)}) custom-call(s32[16]{0:T(128)S(1)} %copy-done, bf16[16,40,128]{2,1,0:T(8,128)(2,1)S(1)} %all_to_all.11.recv, f32[256,128]{1,0:T(8,128)S(1)} %get-tuple-element.24.vec, f32[2,256,128]{2,1,0:T(8,128)S(1)} %get-tuple-element.25.stat, ...), custom_call_target="tpu_custom_call" | custom-call | flops 268435456 | bytes 8388608 | tf_op jit(solution)/shard_map/merge_project_sibling/pallas_call | solution.py:338
  31.6 3.2 %collective-permute-start = (bf16[3,32,1024]{2,1,0:T(8,128)(2,1)S(1)}, bf16[3,32,1024]{2,1,0:T(8,128)(2,1)S(1)}, u32[]{:S(2)}, u32[]{:S(2)}) collective-permute-start(bf16[3,32,1024]{2,1,0:T(8,128)(2,1)S(1)} %get-tuple-element.27), channel_id=1, source_target_pairs={{0,1},{1,0},{2,3},{3,2},{4,5},{5,4},{6,7},{7,6},{8,9},{9,8},{10,11... | collective-permute-start | bytes 589832 | tf_op jit(solution)/shard_map/ppermute | solution.py:356
  34.8 1.0 %project_own.1.mine = bf16[3,32,1024]{2,1,0:T(8,128)(2,1)S(1)} custom-call(bf16[32,1024]{1,0:T(8,128)(2,1)S(1)} %get-tuple-element.26.heads, bf16[1024,8192]{1,0:T(8,128)(2,1)S(1)} %bitcast.6), custom_call_target="tpu_custom_call" | custom-call | flops 268435456 | bytes 8388608 | tf_op jit(solution)/shard_map/project_own/pallas_call | solution.py:357
  35.8 0.1 collective-permute-done.given
  36.0 2.8 %collective-permute-start.1 = (bf16[32,1024]{1,0:T(8,128)(2,1)S(1)}, bf16[32,1024]{1,0:T(8,128)(2,1)S(1)}, u32[]{:S(2)}, u32[]{:S(2)}) collective-permute-start(bf16[32,1024]{1,0:T(8,128)(2,1)S(1)} %get-tuple-element.28), channel_id=1, source_target_pairs={{0,6},{1,7},{2,4},{3,5},{4,2},{5,3},{6,0},{7,1},{8,14},{9,15},{10,... | collective-permute-start | bytes 196616 | tf_op jit(solution)/shard_map/ppermute | solution.py:377
  38.8 0.4 collective-permute-start.3
  39.1 0.3 collective-permute-start.4
  39.4 1.3 %collective-permute-done.1.arrived = bf16[32,1024]{1,0:T(8,128)(2,1)S(1)} collective-permute-done((bf16[32,1024]{1,0:T(8,128)(2,1)S(1)}, bf16[32,1024]{1,0:T(8,128)(2,1)S(1)}, u32[]{:S(2)}, u32[]{:S(2)}) %collective-permute-start.1) | collective-permute-done | bytes 65568 | tf_op jit(solution)/shard_map/ppermute | solution.py:377
  40.8 0.7 %project_last.1 = (f32[32,1024]{1,0:T(8,128)S(1)}, bf16[32,1024]{1,0:T(8,128)(2,1)S(1)}) custom-call(bf16[32,1024]{1,0:T(8,128)(2,1)S(1)} %get-tuple-element.26.heads, bf16[1024,8192]{1,0:T(8,128)(2,1)S(1)} %bitcast.6, bf16[32,1024]{1,0:T(8,128)(2,1)S(1)} %collective-permute-done.1.arrived), custom_call_target="tpu_custom_call" | custom-call | flops 268435456 | bytes 8388608 | tf_op jit(solution)/shard_map/project_last/pallas_call | solution.py:378
  41.5 1.8 %collective-permute-start.2 = (bf16[32,1024]{1,0:T(8,128)(2,1)S(1)}, bf16[32,1024]{1,0:T(8,128)(2,1)S(1)}, u32[]{:S(2)}, u32[]{:S(2)}) collective-permute-start(bf16[32,1024]{1,0:T(8,128)(2,1)S(1)} %get-tuple-element.30), channel_id=1, source_target_pairs={{0,1},{1,0},{2,3},{3,2},{4,5},{5,4},{6,7},{7,6},{8,9},{9,8},{10,11... | collective-permute-start | bytes 196616 | tf_op jit(solution)/shard_map/ppermute | solution.py:387
  43.3 0.1 collective-permute-done.3
  43.4 0.0 collective-permute-done.4
  43.4 0.8 %collective-permute-done.2 = bf16[32,1024]{1,0:T(8,128)(2,1)S(1)} collective-permute-done((bf16[32,1024]{1,0:T(8,128)(2,1)S(1)}, bf16[32,1024]{1,0:T(8,128)(2,1)S(1)}, u32[]{:S(2)}, u32[]{:S(2)}) %collective-permute-start.2) | collective-permute-done | bytes 65568 | tf_op jit(solution)/shard_map/ppermute | solution.py:387
  44.3 0.7 %copy.12 = bf16[2,16,1024]{2,0,1:T(2,128)(2,1)} copy(bf16[2,16,1024]{2,1,0:T(8,128)(2,1)S(1)} %bitcast.7) | data formatting | bytes 131072 | tf_op jit(solution)/shard_map/reshape | solution.py:390
  (3 shorter events, 0.1 us)
Async XLA Ops:
  0.0 16.7 %copy-start.1 = (bf16[16,1,512,256]{3,2,1,0:T(8,128)(2,1)S(1)}, bf16[16,1,512,256]{3,2,1,0:T(8,128)(2,1)}, u32[]{:S(2)}) copy-start(bf16[16,1,512,256]{3,2,1,0:T(8,128)(2,1)} %kv.1) | copy-start | bytes 12582916
  0.0 16.7 %copy-start.2 = (bf16[8192,128]{1,0:T(8,128)(2,1)S(1)}, bf16[8192,128]{1,0:T(8,128)(2,1)}, u32[]{:S(2)}) copy-start(bf16[8192,128]{1,0:T(8,128)(2,1)} %wk.1) | copy-start | bytes 6291460
  0.0 16.7 %copy-start.3 = (bf16[8192,128]{1,0:T(8,128)(2,1)S(1)}, bf16[8192,128]{1,0:T(8,128)(2,1)}, u32[]{:S(2)}) copy-start(bf16[8192,128]{1,0:T(8,128)(2,1)} %wv.1) | copy-start | bytes 6291460
  0.0 16.7 %copy-start.4 = (bf16[16,2,8192]{2,1,0:T(2,128)(2,1)S(1)}, bf16[16,2,8192]{2,1,0:T(2,128)(2,1)}, u32[]{:S(2)}) copy-start(bf16[16,2,8192]{2,1,0:T(2,128)(2,1)} %x.1) | copy-start | bytes 1572868
  16.7 13.1 %slice-start = ((s8[16777216]{0:T(1024)(128)(4,1)}), s8[4194304]{0:T(1024)(128)(4,1)S(1)}, s32[]{:S(2)}) async-start(s8[16777216]{0:T(1024)(128)(4,1)} %bitcast.5), calls=%async_computation.2 | async-start | bytes 8388608
  16.7 13.1 %slice-start.1 = ((s8[16777216]{0:T(1024)(128)(4,1)}), s8[4194304]{0:T(1024)(128)(4,1)S(1)}, s32[]{:S(2)}) async-start(s8[16777216]{0:T(1024)(128)(4,1)} %bitcast.5), calls=%async_computation.3 | async-start | bytes 8388608
  16.8 13.0 %slice-start.2 = ((s8[16777216]{0:T(1024)(128)(4,1)}), s8[4194304]{0:T(1024)(128)(4,1)S(1)}, s32[]{:S(2)}) async-start(s8[16777216]{0:T(1024)(128)(4,1)} %bitcast.5), calls=%async_computation.4 | async-start | bytes 8388608
  16.8 13.0 %slice-start.3 = ((s8[16777216]{0:T(1024)(128)(4,1)}), s8[4194304]{0:T(1024)(128)(4,1)S(1)}, s32[]{:S(2)}) async-start(s8[16777216]{0:T(1024)(128)(4,1)} %bitcast.5), calls=%async_computation.5 | async-start | bytes 8388608
  16.8 13.0 %copy-start = (s32[16]{0:T(128)S(1)}, s32[16]{0:T(128)}, u32[]{:S(2)}) copy-start(s32[16]{0:T(128)} %anc.1) | copy-start | bytes 196
  31.6 4.3 %collective-permute-start = (bf16[3,32,1024]{2,1,0:T(8,128)(2,1)S(1)}, bf16[3,32,1024]{2,1,0:T(8,128)(2,1)S(1)}, u32[]{:S(2)}, u32[]{:S(2)}) collective-permute-start(bf16[3,32,1024]{2,1,0:T(8,128)(2,1)S(1)} %get-tuple-element.27), channel_id=1, source_target_pairs={{0,1},{1,0},{2,3},{3,2},{4,5},{5,4},{6,7},{7,6},{8,9},{9,8},{10,11... | collective-permute-start | bytes 589832 | tf_op jit(solution)/shard_map/ppermute | solution.py:356
  36.0 4.8 %collective-permute-start.1 = (bf16[32,1024]{1,0:T(8,128)(2,1)S(1)}, bf16[32,1024]{1,0:T(8,128)(2,1)S(1)}, u32[]{:S(2)}, u32[]{:S(2)}) collective-permute-start(bf16[32,1024]{1,0:T(8,128)(2,1)S(1)} %get-tuple-element.28), channel_id=1, source_target_pairs={{0,6},{1,7},{2,4},{3,5},{4,2},{5,3},{6,0},{7,1},{8,14},{9,15},{10,... | collective-permute-start | bytes 196616 | tf_op jit(solution)/shard_map/ppermute | solution.py:377
  38.8 4.6 %collective-permute-start.3 = (bf16[32,1024]{1,0:T(8,128)(2,1)S(1)}, bf16[32,1024]{1,0:T(8,128)(2,1)S(1)}, u32[]{:S(2)}, u32[]{:S(2)}) collective-permute-start(bf16[32,1024]{1,0:T(8,128)(2,1)S(1)} %get-tuple-element.31), channel_id=1, source_target_pairs={{0,4},{1,5},{2,6},{3,7},{4,0},{5,1},{6,2},{7,3},{8,12},{9,13},{10,... | collective-permute-start | bytes 196616 | tf_op jit(solution)/shard_map/ppermute | solution.py:377
  39.1 4.3 %collective-permute-start.4 = (bf16[32,1024]{1,0:T(8,128)(2,1)S(1)}, bf16[32,1024]{1,0:T(8,128)(2,1)S(1)}, u32[]{:S(2)}, u32[]{:S(2)}) collective-permute-start(bf16[32,1024]{1,0:T(8,128)(2,1)S(1)} %get-tuple-element.32), channel_id=1, source_target_pairs={{0,2},{1,3},{2,0},{3,1},{4,6},{5,7},{6,4},{7,5},{8,10},{9,11},{10,... | collective-permute-start | bytes 196616 | tf_op jit(solution)/shard_map/ppermute | solution.py:377
  41.5 2.7 %collective-permute-start.2 = (bf16[32,1024]{1,0:T(8,128)(2,1)S(1)}, bf16[32,1024]{1,0:T(8,128)(2,1)S(1)}, u32[]{:S(2)}, u32[]{:S(2)}) collective-permute-start(bf16[32,1024]{1,0:T(8,128)(2,1)S(1)} %get-tuple-element.30), channel_id=1, source_target_pairs={{0,1},{1,0},{2,3},{3,2},{4,5},{5,4},{6,7},{7,6},{8,9},{9,8},{10,11... | collective-permute-start | bytes 196616 | tf_op jit(solution)/shard_map/ppermute | solution.py:387

commit v17 on v15

--- a/solution.py
+++ b/solution.py
@@ -373,7 +373,7 @@
         name="add_sibling",
     )(mine, given)
     arrived = []
-    for k in range(1, groups):
+    for k in range(groups - 1, 0, -1):
         ring = [(i, ((i // 2 + k) % groups) * 2 + i % 2) for i in range(tensor)]
         arrived.append(lax.ppermute(pair[k - 1], "tensor", ring))
     keep, crossing = pl.pallas_call(

time: 44.8 us -> 46 us (1.027)
  waiting for transfers between devices: 0.98 us -> 2.15 us
    ppermute x3, waiting for transfers between devices: 0.32 us -> 2.07 us  [shards(): arrived.append(lax.ppermute(pair[k - 1], 'tensor', ring))]
    ppermute x1, starting transfers between devices: 1.29 us -> 2.55 us  [shards(): total = keep + lax.ppermute(crossing, 'tensor', sibling).astype(F32)]
    ppermute x3, starting transfers between devices: 5.05 us -> 3.84 us  [shards(): arrived.append(lax.ppermute(pair[k - 1], 'tensor', ring))]
    ppermute x1, waiting for transfers between devices: 0.58 us -> 0.01 us  [shards(): total = keep + lax.ppermute(crossing, 'tensor', sibling).astype(F32)]
  transfers between devices with their start and end apart: 5 -> 5, of which waited for: 3 -> 4; matrix products, arithmetic and copies ran while one was open for 0% -> 0% of each run, Pallas kernels for 4% -> 4%
where the time goes in v17:
time: 46 us; the launch traced here: 45.9 us
  blocking collectives  25.9 us (56%)
  starting transfers between devices  9.6 us (21%)
  Pallas kernels  7.28 us (16%)
  waiting for transfers between devices  2.15 us (5%)
  local copies, waits for them, and re-layouts  0.74 us (2%)
    all_to_all x1, blocking collectives, shards(): lax.all_to_all(send, 'particle', split_axis=0, concat_axis=0, tiled=True)  15.5 us
    all_to_all x1, blocking collectives, shards(): lax.all_to_all(back, 'particle', split_axis=0, concat_axis=0, tiled=True)  10.5 us
    ppermute x3, starting transfers between devices, shards(): arrived.append(lax.ppermute(pair[k - 1], 'tensor', ring))  3.84 us
    ppermute x1, starting transfers between devices, shards(): given = lax.ppermute(other, 'tensor', sibling)  3.22 us
    pallas_call x1, Pallas kernels, shards(): pl.pallas_call(attend_kernel, out_shape=(jax.ShapeDtypeStruct(packed, BF1...  2.55 us
    ppermute x1, starting transfers between devices, shards(): total = keep + lax.ppermute(crossing, 'tensor', sibling).astype(F32)  2.55 us
    ppermute x3, waiting for transfers between devices, shards(): arrived.append(lax.ppermute(pair[k - 1], 'tensor', ring))  2.07 us
    pallas_call x1, Pallas kernels, shards(): pl.pallas_call(merge_kernel, out_shape=(block, jax.ShapeDtypeStruct((rows...  1.77 us
  transfers between devices with their start and end apart: 5, of which 4 were waited for; matrix products, arithmetic and copies ran while one was open for 0% of the time, Pallas kernels for 4%

profile of v17, /device:TPU:1, one launch (start us, length us, event | category | flops | bytes accessed | tf_op | source)
XLA Modules:
  0.0 45.9 jit_solution(18245060009714875982)
XLA Ops:
  0.0 0.0 copy-start.1
  0.0 0.0 copy-start.2
  0.0 0.0 copy-start.3
  0.0 0.0 copy-start.4
  0.0 1.2 %pack_queries.1 = (bf16[16,40,128]{2,1,0:T(8,128)(2,1)S(1)}, bf16[16,16,128]{2,1,0:T(8,128)(2,1)S(1)}, f32[2,16,128]{2,1,0:T(8,128)S(1)}, f32[1,8192]{1,0:T(1,128)S(1)}) custom-call(s32[16]{0:T(128)} %anc.1, bf16[16,2,1024]{2,1,0:T(2,128)(2,1)} %qp_hbm.1, f32[2,16,128]{2,1,0:T(8,128)} %constant.2.clone.tables_hbm, f32[1,8192]{1,0:T(1,128)} %bitcast.8), custom_call_target="tpu_custom_call" | custom-call | flops 10000000000 | bytes 1048576 | tf_op jit(solution)/shard_map/pack_queries/pallas_call | solution.py:269
  1.2 15.5 %all_to_all.10.recv = bf16[16,40,128]{2,1,0:T(8,128)(2,1)S(1)} all-to-all(bf16[16,40,128]{2,1,0:T(8,128)(2,1)S(1)} %get-tuple-element.19), channel_id=1, replica_groups=mesh['particle'=16,'tensor'=8] {'particle'}, dimensions={0} | all-to-all | bytes 327680 | tf_op jit(solution)/shard_map/all_to_all | solution.py:292
  16.7 0.0 slice-start
  16.7 0.0 copy-done.1
  16.7 0.0 copy-done.2
  16.7 0.0 copy-done.3
  16.7 0.0 copy-done.4
  16.7 0.0 slice-start.1
  16.8 0.0 slice-start.2
  16.8 0.0 slice-start.3
  16.8 0.0 copy-start
  16.8 2.5 %attention.1 = (bf16[16,40,128]{2,1,0:T(8,128)(2,1)S(1)}, f32[256,128]{1,0:T(8,128)S(1)}, f32[2,256,128]{2,1,0:T(8,128)S(1)}) custom-call(bf16[16,40,128]{2,1,0:T(8,128)(2,1)S(1)} %all_to_all.10.recv, bf16[16,1,512,256]{3,2,1,0:T(8,128)(2,1)S(1)} %copy-done.1, bf16[16,2,8192]{2,1,0:T(2,128)(2,1)S(1)} %copy-done.4, f32[1,8192]{1,0:T(1,128)S(1)} %get-tuple-element.20.gain, ...), custom_call_target="tpu_custom_call" | custom-call | flops 10000000000 | bytes 5242880 | tf_op jit(solution)/shard_map/attention/pallas_call | solution.py:295
  19.3 10.5 %all_to_all.11.recv = bf16[16,40,128]{2,1,0:T(8,128)(2,1)S(1)} all-to-all(bf16[16,40,128]{2,1,0:T(8,128)(2,1)S(1)} %get-tuple-element.23), channel_id=1, replica_groups=mesh['particle'=16,'tensor'=8] {'particle'}, dimensions={0} | all-to-all | bytes 327680 | tf_op jit(solution)/shard_map/all_to_all | solution.py:329
  29.8 0.0 slice-done
  29.8 0.0 slice-done.1
  29.8 0.0 slice-done.2
  29.8 0.0 slice-done.3
  29.8 0.0 copy-done
  29.8 1.8 %merge_project_sibling.1 = (bf16[3,32,1024]{2,1,0:T(8,128)(2,1)S(1)}, bf16[32,1024]{1,0:T(8,128)(2,1)S(1)}) custom-call(s32[16]{0:T(128)S(1)} %copy-done, bf16[16,40,128]{2,1,0:T(8,128)(2,1)S(1)} %all_to_all.11.recv, f32[256,128]{1,0:T(8,128)S(1)} %get-tuple-element.24.vec, f32[2,256,128]{2,1,0:T(8,128)S(1)} %get-tuple-element.25.stat, ...), custom_call_target="tpu_custom_call" | custom-call | flops 268435456 | bytes 8388608 | tf_op jit(solution)/shard_map/merge_project_sibling/pallas_call | solution.py:339
  31.6 3.2 %collective-permute-start = (bf16[3,32,1024]{2,1,0:T(8,128)(2,1)S(1)}, bf16[3,32,1024]{2,1,0:T(8,128)(2,1)S(1)}, u32[]{:S(2)}, u32[]{:S(2)}) collective-permute-start(bf16[3,32,1024]{2,1,0:T(8,128)(2,1)S(1)} %get-tuple-element.27), channel_id=1, source_target_pairs={{0,1},{1,0},{2,3},{3,2},{4,5},{5,4},{6,7},{7,6},{8,9},{9,8},{10,11... | collective-permute-start | bytes 589832 | tf_op jit(solution)/shard_map/ppermute | solution.py:357
  34.8 1.0 %project_own.1.mine = bf16[3,32,1024]{2,1,0:T(8,128)(2,1)S(1)} custom-call(bf16[32,1024]{1,0:T(8,128)(2,1)S(1)} %get-tuple-element.26.heads, bf16[1024,8192]{1,0:T(8,128)(2,1)S(1)} %bitcast.6), custom_call_target="tpu_custom_call" | custom-call | flops 268435456 | bytes 8388608 | tf_op jit(solution)/shard_map/project_own/pallas_call | solution.py:358
  35.8 0.1 collective-permute-done.given
  36.0 2.8 %collective-permute-start.1 = (bf16[32,1024]{1,0:T(8,128)(2,1)S(1)}, bf16[32,1024]{1,0:T(8,128)(2,1)S(1)}, u32[]{:S(2)}, u32[]{:S(2)}) collective-permute-start(bf16[32,1024]{1,0:T(8,128)(2,1)S(1)} %get-tuple-element.28), channel_id=1, source_target_pairs={{0,6},{1,7},{2,0},{3,1},{4,2},{5,3},{6,4},{7,5},{8,14},{9,15},{10,... | collective-permute-start | bytes 196616 | tf_op jit(solution)/shard_map/ppermute | solution.py:378
  38.8 0.3 collective-permute-start.3
  39.1 0.7 %collective-permute-start.4 = (bf16[32,1024]{1,0:T(8,128)(2,1)S(1)}, bf16[32,1024]{1,0:T(8,128)(2,1)S(1)}, u32[]{:S(2)}, u32[]{:S(2)}) collective-permute-start(bf16[32,1024]{1,0:T(8,128)(2,1)S(1)} %get-tuple-element.32), channel_id=1, source_target_pairs={{0,2},{1,3},{2,4},{3,5},{4,6},{5,7},{6,0},{7,1},{8,10},{9,11},{10,... | collective-permute-start | bytes 196616 | tf_op jit(solution)/shard_map/ppermute | solution.py:378
  39.8 0.3 collective-permute-done.1.arrived
  40.1 0.7 %project_last.1 = (f32[32,1024]{1,0:T(8,128)S(1)}, bf16[32,1024]{1,0:T(8,128)(2,1)S(1)}) custom-call(bf16[32,1024]{1,0:T(8,128)(2,1)S(1)} %get-tuple-element.26.heads, bf16[1024,8192]{1,0:T(8,128)(2,1)S(1)} %bitcast.6, bf16[32,1024]{1,0:T(8,128)(2,1)S(1)} %collective-permute-done.1.arrived), custom_call_target="tpu_custom_call" | custom-call | flops 268435456 | bytes 8388608 | tf_op jit(solution)/shard_map/project_last/pallas_call | solution.py:379
  40.8 2.5 %collective-permute-start.2 = (bf16[32,1024]{1,0:T(8,128)(2,1)S(1)}, bf16[32,1024]{1,0:T(8,128)(2,1)S(1)}, u32[]{:S(2)}, u32[]{:S(2)}) collective-permute-start(bf16[32,1024]{1,0:T(8,128)(2,1)S(1)} %get-tuple-element.30), channel_id=1, source_target_pairs={{0,1},{1,0},{2,3},{3,2},{4,5},{5,4},{6,7},{7,6},{8,9},{9,8},{10,11... | collective-permute-start | bytes 196616 | tf_op jit(solution)/shard_map/ppermute | solution.py:388
  43.4 0.1 collective-permute-done.3
  43.4 1.7 %collective-permute-done.4 = bf16[32,1024]{1,0:T(8,128)(2,1)S(1)} collective-permute-done((bf16[32,1024]{1,0:T(8,128)(2,1)S(1)}, bf16[32,1024]{1,0:T(8,128)(2,1)S(1)}, u32[]{:S(2)}, u32[]{:S(2)}) %collective-permute-start.4) | collective-permute-done | bytes 65568 | tf_op jit(solution)/shard_map/ppermute | solution.py:378
  45.1 0.0 collective-permute-done.2
  45.2 0.7 %copy.12 = bf16[2,16,1024]{2,0,1:T(2,128)(2,1)} copy(bf16[2,16,1024]{2,1,0:T(8,128)(2,1)S(1)} %bitcast.7) | data formatting | bytes 131072 | tf_op jit(solution)/shard_map/reshape | solution.py:391
  (3 shorter events, 0.1 us)
Async XLA Ops:
  0.0 16.7 %copy-start.1 = (bf16[16,1,512,256]{3,2,1,0:T(8,128)(2,1)S(1)}, bf16[16,1,512,256]{3,2,1,0:T(8,128)(2,1)}, u32[]{:S(2)}) copy-start(bf16[16,1,512,256]{3,2,1,0:T(8,128)(2,1)} %kv.1) | copy-start | bytes 12582916
  0.0 16.7 %copy-start.2 = (bf16[8192,128]{1,0:T(8,128)(2,1)S(1)}, bf16[8192,128]{1,0:T(8,128)(2,1)}, u32[]{:S(2)}) copy-start(bf16[8192,128]{1,0:T(8,128)(2,1)} %wk.1) | copy-start | bytes 6291460
  0.0 16.7 %copy-start.3 = (bf16[8192,128]{1,0:T(8,128)(2,1)S(1)}, bf16[8192,128]{1,0:T(8,128)(2,1)}, u32[]{:S(2)}) copy-start(bf16[8192,128]{1,0:T(8,128)(2,1)} %wv.1) | copy-start | bytes 6291460
  0.0 16.7 %copy-start.4 = (bf16[16,2,8192]{2,1,0:T(2,128)(2,1)S(1)}, bf16[16,2,8192]{2,1,0:T(2,128)(2,1)}, u32[]{:S(2)}) copy-start(bf16[16,2,8192]{2,1,0:T(2,128)(2,1)} %x.1) | copy-start | bytes 1572868
  16.7 13.1 %slice-start = ((s8[16777216]{0:T(1024)(128)(4,1)}), s8[4194304]{0:T(1024)(128)(4,1)S(1)}, s32[]{:S(2)}) async-start(s8[16777216]{0:T(1024)(128)(4,1)} %bitcast.5), calls=%async_computation.2 | async-start | bytes 8388608
  16.7 13.1 %slice-start.1 = ((s8[16777216]{0:T(1024)(128)(4,1)}), s8[4194304]{0:T(1024)(128)(4,1)S(1)}, s32[]{:S(2)}) async-start(s8[16777216]{0:T(1024)(128)(4,1)} %bitcast.5), calls=%async_computation.3 | async-start | bytes 8388608
  16.8 13.0 %slice-start.2 = ((s8[16777216]{0:T(1024)(128)(4,1)}), s8[4194304]{0:T(1024)(128)(4,1)S(1)}, s32[]{:S(2)}) async-start(s8[16777216]{0:T(1024)(128)(4,1)} %bitcast.5), calls=%async_computation.4 | async-start | bytes 8388608
  16.8 13.0 %slice-start.3 = ((s8[16777216]{0:T(1024)(128)(4,1)}), s8[4194304]{0:T(1024)(128)(4,1)S(1)}, s32[]{:S(2)}) async-start(s8[16777216]{0:T(1024)(128)(4,1)} %bitcast.5), calls=%async_computation.5 | async-start | bytes 8388608
  16.8 13.0 %copy-start = (s32[16]{0:T(128)S(1)}, s32[16]{0:T(128)}, u32[]{:S(2)}) copy-start(s32[16]{0:T(128)} %anc.1) | copy-start | bytes 196
  31.6 4.3 %collective-permute-start = (bf16[3,32,1024]{2,1,0:T(8,128)(2,1)S(1)}, bf16[3,32,1024]{2,1,0:T(8,128)(2,1)S(1)}, u32[]{:S(2)}, u32[]{:S(2)}) collective-permute-start(bf16[3,32,1024]{2,1,0:T(8,128)(2,1)S(1)} %get-tuple-element.27), channel_id=1, source_target_pairs={{0,1},{1,0},{2,3},{3,2},{4,5},{5,4},{6,7},{7,6},{8,9},{9,8},{10,11... | collective-permute-start | bytes 589832 | tf_op jit(solution)/shard_map/ppermute | solution.py:357
  36.0 4.1 %collective-permute-start.1 = (bf16[32,1024]{1,0:T(8,128)(2,1)S(1)}, bf16[32,1024]{1,0:T(8,128)(2,1)S(1)}, u32[]{:S(2)}, u32[]{:S(2)}) collective-permute-start(bf16[32,1024]{1,0:T(8,128)(2,1)S(1)} %get-tuple-element.28), channel_id=1, source_target_pairs={{0,6},{1,7},{2,0},{3,1},{4,2},{5,3},{6,4},{7,5},{8,14},{9,15},{10,... | collective-permute-start | bytes 196616 | tf_op jit(solution)/shard_map/ppermute | solution.py:378
  38.8 4.7 %collective-permute-start.3 = (bf16[32,1024]{1,0:T(8,128)(2,1)S(1)}, bf16[32,1024]{1,0:T(8,128)(2,1)S(1)}, u32[]{:S(2)}, u32[]{:S(2)}) collective-permute-start(bf16[32,1024]{1,0:T(8,128)(2,1)S(1)} %get-tuple-element.31), channel_id=1, source_target_pairs={{0,4},{1,5},{2,6},{3,7},{4,0},{5,1},{6,2},{7,3},{8,12},{9,13},{10,... | collective-permute-start | bytes 196616 | tf_op jit(solution)/shard_map/ppermute | solution.py:378
  39.1 6.0 %collective-permute-start.4 = (bf16[32,1024]{1,0:T(8,128)(2,1)S(1)}, bf16[32,1024]{1,0:T(8,128)(2,1)S(1)}, u32[]{:S(2)}, u32[]{:S(2)}) collective-permute-start(bf16[32,1024]{1,0:T(8,128)(2,1)S(1)} %get-tuple-element.32), channel_id=1, source_target_pairs={{0,2},{1,3},{2,4},{3,5},{4,6},{5,7},{6,0},{7,1},{8,10},{9,11},{10,... | collective-permute-start | bytes 196616 | tf_op jit(solution)/shard_map/ppermute | solution.py:378
  40.8 4.3 %collective-permute-start.2 = (bf16[32,1024]{1,0:T(8,128)(2,1)S(1)}, bf16[32,1024]{1,0:T(8,128)(2,1)S(1)}, u32[]{:S(2)}, u32[]{:S(2)}) collective-permute-start(bf16[32,1024]{1,0:T(8,128)(2,1)S(1)} %get-tuple-element.30), channel_id=1, source_target_pairs={{0,1},{1,0},{2,3},{3,2},{4,5},{5,4},{6,7},{7,6},{8,9},{9,8},{10,11... | collective-permute-start | bytes 196616 | tf_op jit(solution)/shard_map/ppermute | solution.py:388

commit v18 on v15

--- a/solution.py
+++ b/solution.py
@@ -28,11 +28,15 @@
     )
 
 
-def slot_of(anc, row, rows, count):
-    source = lax.div(anc[row], rows)
-    rank = count[source]
-    count[source] = rank + 1
-    return source, rank
+def slots_of(anc, rows):
+    sources = [lax.div(anc[r], rows) for r in range(rows)]
+    ranks = []
+    for r in range(rows):
+        rank = jnp.int32(0)
+        for q in range(r):
+            rank = rank + jnp.where(sources[q] == sources[r], 1, 0)
+        ranks.append(rank)
+    return list(zip(sources, ranks))
 
 
 def pack_kernel(
@@ -58,8 +62,7 @@
         copy.wait()
     for h in range(width // head_dim):
         grid_ref[:, steps * h : steps * (h + 1), :] = qp[:, :, head_dim * h : head_dim * (h + 1)].astype(F32)
-    for r in range(rows):
-        source, rank = slot_of(anc, r, rows, count)
+    for r, (source, rank) in enumerate(slots_of(anc, rows)):
         spots[source * PAIR + rank] = lax.rem(anc[r], rows)
         plain = grid_ref[r]
         turned = (plain * tables[0] + pltpu.roll(plain, head_dim // 2, 1) * tables[1]).astype(BF16)
@@ -201,8 +204,7 @@
     for d in range(devices):
         count[d] = 0
     part_of = lax.div(lax.broadcasted_iota(jnp.int32, (MORE, head_dim), 1), quarter)
-    for r in range(rows):
-        source, rank = slot_of(anc, r, rows, count)
+    for r, (source, rank) in enumerate(slots_of(anc, rows)):
         at = pl.multiple_of(rank * per_row, per_row)
         grid_ref[pl.ds(r * per_row, per_row), :] = recv[source, pl.ds(at, per_row), :].astype(F32)
         parts = recv[source, PAIR * per_row :, :].astype(F32)

time: 44.8 us -> 45 us (level)
  no operation moved by 1% of the time
where the time goes in v18:
time: 45 us; the launch traced here: 44.8 us
  blocking collectives  25.9 us (58%)
  starting transfers between devices  9.56 us (21%)
  Pallas kernels  7.46 us (17%)
  waiting for transfers between devices  0.98 us (2%)
  local copies, waits for them, and re-layouts  0.74 us (2%)
    all_to_all x1, blocking collectives, shards(): lax.all_to_all(send, 'particle', split_axis=0, concat_axis=0, tiled=True)  15.5 us
    all_to_all x1, blocking collectives, shards(): lax.all_to_all(back, 'particle', split_axis=0, concat_axis=0, tiled=True)  10.4 us
    ppermute x3, starting transfers between devices, shards(): arrived.append(lax.ppermute(pair[k - 1], 'tensor', ring))  5.05 us
    ppermute x1, starting transfers between devices, shards(): given = lax.ppermute(other, 'tensor', sibling)  3.21 us
    pallas_call x1, Pallas kernels, shards(): pl.pallas_call(attend_kernel, out_shape=(jax.ShapeDtypeStruct(packed, BF1...  2.55 us
    pallas_call x1, Pallas kernels, shards(): pl.pallas_call(merge_kernel, out_shape=(block, jax.ShapeDtypeStruct((rows...  1.84 us
    pallas_call x1, Pallas kernels, shards(): pl.pallas_call(pack_kernel, out_shape=(jax.ShapeDtypeStruct(packed, BF16)...  1.32 us
    ppermute x1, starting transfers between devices, shards(): total = keep + lax.ppermute(crossing, 'tensor', sibling).astype(F32)  1.29 us
  transfers between devices with their start and end apart: 5, of which 3 were waited for; matrix products, arithmetic and copies ran while one was open for 0% of the time, Pallas kernels for 4%

profile of v18, /device:TPU:1, one launch (start us, length us, event | category | flops | bytes accessed | tf_op | source)
XLA Modules:
  0.0 44.8 jit_solution(11154465697397658621)
XLA Ops:
  0.0 0.0 copy-start.1
  0.0 0.0 copy-start.2
  0.0 0.0 copy-start.3
  0.0 0.0 copy-start.4
  0.0 1.3 %pack_queries.1 = (bf16[16,40,128]{2,1,0:T(8,128)(2,1)S(1)}, bf16[16,16,128]{2,1,0:T(8,128)(2,1)S(1)}, f32[2,16,128]{2,1,0:T(8,128)S(1)}, f32[1,8192]{1,0:T(1,128)S(1)}) custom-call(s32[16]{0:T(128)} %anc.1, bf16[16,2,1024]{2,1,0:T(2,128)(2,1)} %qp_hbm.1, f32[2,16,128]{2,1,0:T(8,128)} %constant.2.clone.tables_hbm, f32[1,8192]{1,0:T(1,128)} %bitcast.8), custom_call_target="tpu_custom_call" | custom-call | flops 10000000000 | bytes 1048576 | tf_op jit(solution)/shard_map/pack_queries/pallas_call | solution.py:271
  1.3 15.5 %all_to_all.10.recv = bf16[16,40,128]{2,1,0:T(8,128)(2,1)S(1)} all-to-all(bf16[16,40,128]{2,1,0:T(8,128)(2,1)S(1)} %get-tuple-element.19), channel_id=1, replica_groups=mesh['particle'=16,'tensor'=8] {'particle'}, dimensions={0} | all-to-all | bytes 327680 | tf_op jit(solution)/shard_map/all_to_all | solution.py:294
  16.8 0.0 slice-start
  16.8 0.0 copy-done.1
  16.8 0.0 copy-done.2
  16.8 0.0 copy-done.3
  16.8 0.0 copy-done.4
  16.9 0.0 slice-start.1
  16.9 0.0 slice-start.2
  16.9 0.0 slice-start.3
  16.9 0.0 copy-start
  16.9 2.6 %attention.1 = (bf16[16,40,128]{2,1,0:T(8,128)(2,1)S(1)}, f32[256,128]{1,0:T(8,128)S(1)}, f32[2,256,128]{2,1,0:T(8,128)S(1)}) custom-call(bf16[16,40,128]{2,1,0:T(8,128)(2,1)S(1)} %all_to_all.10.recv, bf16[16,1,512,256]{3,2,1,0:T(8,128)(2,1)S(1)} %copy-done.1, bf16[16,2,8192]{2,1,0:T(2,128)(2,1)S(1)} %copy-done.4, f32[1,8192]{1,0:T(1,128)S(1)} %get-tuple-element.20.gain, ...), custom_call_target="tpu_custom_call" | custom-call | flops 10000000000 | bytes 5242880 | tf_op jit(solution)/shard_map/attention/pallas_call | solution.py:297
  19.5 10.4 %all_to_all.11.recv = bf16[16,40,128]{2,1,0:T(8,128)(2,1)S(1)} all-to-all(bf16[16,40,128]{2,1,0:T(8,128)(2,1)S(1)} %get-tuple-element.23), channel_id=1, replica_groups=mesh['particle'=16,'tensor'=8] {'particle'}, dimensions={0} | all-to-all | bytes 327680 | tf_op jit(solution)/shard_map/all_to_all | solution.py:331
  29.9 0.0 slice-done
  29.9 0.0 slice-done.1
  29.9 0.0 slice-done.2
  29.9 0.0 slice-done.3
  29.9 0.0 copy-done
  29.9 1.8 %merge_project_sibling.1 = (bf16[3,32,1024]{2,1,0:T(8,128)(2,1)S(1)}, bf16[32,1024]{1,0:T(8,128)(2,1)S(1)}) custom-call(s32[16]{0:T(128)S(1)} %copy-done, bf16[16,40,128]{2,1,0:T(8,128)(2,1)S(1)} %all_to_all.11.recv, f32[256,128]{1,0:T(8,128)S(1)} %get-tuple-element.24.vec, f32[2,256,128]{2,1,0:T(8,128)S(1)} %get-tuple-element.25.stat, ...), custom_call_target="tpu_custom_call" | custom-call | flops 268435456 | bytes 8388608 | tf_op jit(solution)/shard_map/merge_project_sibling/pallas_call | solution.py:341
  31.8 3.2 %collective-permute-start = (bf16[3,32,1024]{2,1,0:T(8,128)(2,1)S(1)}, bf16[3,32,1024]{2,1,0:T(8,128)(2,1)S(1)}, u32[]{:S(2)}, u32[]{:S(2)}) collective-permute-start(bf16[3,32,1024]{2,1,0:T(8,128)(2,1)S(1)} %get-tuple-element.27), channel_id=1, source_target_pairs={{0,1},{1,0},{2,3},{3,2},{4,5},{5,4},{6,7},{7,6},{8,9},{9,8},{10,11... | collective-permute-start | bytes 589832 | tf_op jit(solution)/shard_map/ppermute | solution.py:359
  35.0 1.0 %project_own.1.mine = bf16[3,32,1024]{2,1,0:T(8,128)(2,1)S(1)} custom-call(bf16[32,1024]{1,0:T(8,128)(2,1)S(1)} %get-tuple-element.26.heads, bf16[1024,8192]{1,0:T(8,128)(2,1)S(1)} %bitcast.6), custom_call_target="tpu_custom_call" | custom-call | flops 268435456 | bytes 8388608 | tf_op jit(solution)/shard_map/project_own/pallas_call | solution.py:360
  36.0 0.1 collective-permute-done.given
  36.1 1.4 %collective-permute-start.1 = (bf16[32,1024]{1,0:T(8,128)(2,1)S(1)}, bf16[32,1024]{1,0:T(8,128)(2,1)S(1)}, u32[]{:S(2)}, u32[]{:S(2)}) collective-permute-start(bf16[32,1024]{1,0:T(8,128)(2,1)S(1)} %get-tuple-element.28), channel_id=1, source_target_pairs={{0,2},{1,3},{2,4},{3,5},{4,6},{5,7},{6,0},{7,1},{8,10},{9,11},{10,... | collective-permute-start | bytes 196616 | tf_op jit(solution)/shard_map/ppermute | solution.py:380
  37.5 2.6 %collective-permute-start.3 = (bf16[32,1024]{1,0:T(8,128)(2,1)S(1)}, bf16[32,1024]{1,0:T(8,128)(2,1)S(1)}, u32[]{:S(2)}, u32[]{:S(2)}) collective-permute-start(bf16[32,1024]{1,0:T(8,128)(2,1)S(1)} %get-tuple-element.31), channel_id=1, source_target_pairs={{0,4},{1,5},{2,6},{3,7},{4,0},{5,1},{6,2},{7,3},{8,12},{9,13},{10,... | collective-permute-start | bytes 196616 | tf_op jit(solution)/shard_map/ppermute | solution.py:380
  40.1 1.1 %collective-permute-start.4 = (bf16[32,1024]{1,0:T(8,128)(2,1)S(1)}, bf16[32,1024]{1,0:T(8,128)(2,1)S(1)}, u32[]{:S(2)}, u32[]{:S(2)}) collective-permute-start(bf16[32,1024]{1,0:T(8,128)(2,1)S(1)} %get-tuple-element.32), channel_id=1, source_target_pairs={{0,6},{1,7},{2,0},{3,1},{4,2},{5,3},{6,4},{7,5},{8,14},{9,15},{10,... | collective-permute-start | bytes 196616 | tf_op jit(solution)/shard_map/ppermute | solution.py:380
  41.2 0.0 collective-permute-done.1.arrived
  41.2 0.7 %project_last.1 = (f32[32,1024]{1,0:T(8,128)S(1)}, bf16[32,1024]{1,0:T(8,128)(2,1)S(1)}) custom-call(bf16[32,1024]{1,0:T(8,128)(2,1)S(1)} %get-tuple-element.26.heads, bf16[1024,8192]{1,0:T(8,128)(2,1)S(1)} %bitcast.6, bf16[32,1024]{1,0:T(8,128)(2,1)S(1)} %collective-permute-done.1.arrived), custom_call_target="tpu_custom_call" | custom-call | flops 268435456 | bytes 8388608 | tf_op jit(solution)/shard_map/project_last/pallas_call | solution.py:381
  41.9 1.3 %collective-permute-start.2 = (bf16[32,1024]{1,0:T(8,128)(2,1)S(1)}, bf16[32,1024]{1,0:T(8,128)(2,1)S(1)}, u32[]{:S(2)}, u32[]{:S(2)}) collective-permute-start(bf16[32,1024]{1,0:T(8,128)(2,1)S(1)} %get-tuple-element.30), channel_id=1, source_target_pairs={{0,1},{1,0},{2,3},{3,2},{4,5},{5,4},{6,7},{7,6},{8,9},{9,8},{10,11... | collective-permute-start | bytes 196616 | tf_op jit(solution)/shard_map/ppermute | solution.py:390
  43.2 0.0 collective-permute-done.3
  43.2 0.3 collective-permute-done.4
  43.5 0.6 %collective-permute-done.2 = bf16[32,1024]{1,0:T(8,128)(2,1)S(1)} collective-permute-done((bf16[32,1024]{1,0:T(8,128)(2,1)S(1)}, bf16[32,1024]{1,0:T(8,128)(2,1)S(1)}, u32[]{:S(2)}, u32[]{:S(2)}) %collective-permute-start.2) | collective-permute-done | bytes 65568 | tf_op jit(solution)/shard_map/ppermute | solution.py:390
  44.1 0.7 %copy.12 = bf16[2,16,1024]{2,0,1:T(2,128)(2,1)} copy(bf16[2,16,1024]{2,1,0:T(8,128)(2,1)S(1)} %bitcast.7) | data formatting | bytes 131072 | tf_op jit(solution)/shard_map/reshape | solution.py:393
  (3 shorter events, 0.1 us)
Async XLA Ops:
  0.0 16.8 %copy-start.1 = (bf16[16,1,512,256]{3,2,1,0:T(8,128)(2,1)S(1)}, bf16[16,1,512,256]{3,2,1,0:T(8,128)(2,1)}, u32[]{:S(2)}) copy-start(bf16[16,1,512,256]{3,2,1,0:T(8,128)(2,1)} %kv.1) | copy-start | bytes 12582916
  0.0 16.8 %copy-start.2 = (bf16[8192,128]{1,0:T(8,128)(2,1)S(1)}, bf16[8192,128]{1,0:T(8,128)(2,1)}, u32[]{:S(2)}) copy-start(bf16[8192,128]{1,0:T(8,128)(2,1)} %wk.1) | copy-start | bytes 6291460
  0.0 16.8 %copy-start.3 = (bf16[8192,128]{1,0:T(8,128)(2,1)S(1)}, bf16[8192,128]{1,0:T(8,128)(2,1)}, u32[]{:S(2)}) copy-start(bf16[8192,128]{1,0:T(8,128)(2,1)} %wv.1) | copy-start | bytes 6291460
  0.0 16.8 %copy-start.4 = (bf16[16,2,8192]{2,1,0:T(2,128)(2,1)S(1)}, bf16[16,2,8192]{2,1,0:T(2,128)(2,1)}, u32[]{:S(2)}) copy-start(bf16[16,2,8192]{2,1,0:T(2,128)(2,1)} %x.1) | copy-start | bytes 1572868
  16.8 13.1 %slice-start = ((s8[16777216]{0:T(1024)(128)(4,1)}), s8[4194304]{0:T(1024)(128)(4,1)S(1)}, s32[]{:S(2)}) async-start(s8[16777216]{0:T(1024)(128)(4,1)} %bitcast.5), calls=%async_computation.2 | async-start | bytes 8388608
  16.9 13.1 %slice-start.1 = ((s8[16777216]{0:T(1024)(128)(4,1)}), s8[4194304]{0:T(1024)(128)(4,1)S(1)}, s32[]{:S(2)}) async-start(s8[16777216]{0:T(1024)(128)(4,1)} %bitcast.5), calls=%async_computation.3 | async-start | bytes 8388608
  16.9 13.0 %slice-start.2 = ((s8[16777216]{0:T(1024)(128)(4,1)}), s8[4194304]{0:T(1024)(128)(4,1)S(1)}, s32[]{:S(2)}) async-start(s8[16777216]{0:T(1024)(128)(4,1)} %bitcast.5), calls=%async_computation.4 | async-start | bytes 8388608
  16.9 13.0 %slice-start.3 = ((s8[16777216]{0:T(1024)(128)(4,1)}), s8[4194304]{0:T(1024)(128)(4,1)S(1)}, s32[]{:S(2)}) async-start(s8[16777216]{0:T(1024)(128)(4,1)} %bitcast.5), calls=%async_computation.5 | async-start | bytes 8388608
  16.9 13.0 %copy-start = (s32[16]{0:T(128)S(1)}, s32[16]{0:T(128)}, u32[]{:S(2)}) copy-start(s32[16]{0:T(128)} %anc.1) | copy-start | bytes 196
  31.8 4.3 %collective-permute-start = (bf16[3,32,1024]{2,1,0:T(8,128)(2,1)S(1)}, bf16[3,32,1024]{2,1,0:T(8,128)(2,1)S(1)}, u32[]{:S(2)}, u32[]{:S(2)}) collective-permute-start(bf16[3,32,1024]{2,1,0:T(8,128)(2,1)S(1)} %get-tuple-element.27), channel_id=1, source_target_pairs={{0,1},{1,0},{2,3},{3,2},{4,5},{5,4},{6,7},{7,6},{8,9},{9,8},{10,11... | collective-permute-start | bytes 589832 | tf_op jit(solution)/shard_map/ppermute | solution.py:359
  36.1 5.1 %collective-permute-start.1 = (bf16[32,1024]{1,0:T(8,128)(2,1)S(1)}, bf16[32,1024]{1,0:T(8,128)(2,1)S(1)}, u32[]{:S(2)}, u32[]{:S(2)}) collective-permute-start(bf16[32,1024]{1,0:T(8,128)(2,1)S(1)} %get-tuple-element.28), channel_id=1, source_target_pairs={{0,2},{1,3},{2,4},{3,5},{4,6},{5,7},{6,0},{7,1},{8,10},{9,11},{10,... | collective-permute-start | bytes 196616 | tf_op jit(solution)/shard_map/ppermute | solution.py:380
  37.5 5.7 %collective-permute-start.3 = (bf16[32,1024]{1,0:T(8,128)(2,1)S(1)}, bf16[32,1024]{1,0:T(8,128)(2,1)S(1)}, u32[]{:S(2)}, u32[]{:S(2)}) collective-permute-start(bf16[32,1024]{1,0:T(8,128)(2,1)S(1)} %get-tuple-element.31), channel_id=1, source_target_pairs={{0,4},{1,5},{2,6},{3,7},{4,0},{5,1},{6,2},{7,3},{8,12},{9,13},{10,... | collective-permute-start | bytes 196616 | tf_op jit(solution)/shard_map/ppermute | solution.py:380
  40.1 3.4 %collective-permute-start.4 = (bf16[32,1024]{1,0:T(8,128)(2,1)S(1)}, bf16[32,1024]{1,0:T(8,128)(2,1)S(1)}, u32[]{:S(2)}, u32[]{:S(2)}) collective-permute-start(bf16[32,1024]{1,0:T(8,128)(2,1)S(1)} %get-tuple-element.32), channel_id=1, source_target_pairs={{0,6},{1,7},{2,0},{3,1},{4,2},{5,3},{6,4},{7,5},{8,14},{9,15},{10,... | collective-permute-start | bytes 196616 | tf_op jit(solution)/shard_map/ppermute | solution.py:380
  41.9 2.2 %collective-permute-start.2 = (bf16[32,1024]{1,0:T(8,128)(2,1)S(1)}, bf16[32,1024]{1,0:T(8,128)(2,1)S(1)}, u32[]{:S(2)}, u32[]{:S(2)}) collective-permute-start(bf16[32,1024]{1,0:T(8,128)(2,1)S(1)} %get-tuple-element.30), channel_id=1, source_target_pairs={{0,1},{1,0},{2,3},{3,2},{4,5},{5,4},{6,7},{7,6},{8,9},{9,8},{10,11... | collective-permute-start | bytes 196616 | tf_op jit(solution)/shard_map/ppermute | solution.py:390

commit v19 on v15

--- a/solution.py
+++ b/solution.py
@@ -191,7 +191,7 @@
         out[k] = product(wide, w, block, tokens, column).astype(BF16)
 
 
-def merge_kernel(anc, recv, vec, stat, w, out, heads, grid_ref, sums, count):
+def merge_kernel(anc, recv, vec, stat, w, out, heads, grid_ref, sums, lined, count):
     devices, chunk, head_dim = recv.shape
     per_row = (chunk - MORE) // PAIR
     rows = vec.shape[0] // per_row
@@ -224,9 +224,8 @@
     grid_ref[...] = (grid_ref[...] * factor_c + vec[...] * factor_f) * share
     for h in range(per_row // steps):
         for s in range(steps):
-            heads[pl.ds(s * rows, rows), pl.ds(h * head_dim, head_dim)] = grid_ref[
-                pl.ds(h * steps + s, rows, stride=per_row), :
-            ].astype(BF16)
+            lined[h, pl.ds(s, rows, stride=steps), :] = grid_ref[pl.ds(h * steps + s, rows, stride=per_row), :]
+        heads[:, pl.ds(h * head_dim, head_dim)] = lined[h].astype(BF16)
     project(heads, w, out, False)
 
 
@@ -347,6 +346,7 @@
         scratch_shapes=[
             pltpu.VMEM((rows * per_row, head_dim), F32),
             pltpu.VMEM((rows * per_row, head_dim), BF16),
+            pltpu.VMEM((heads, rows * steps, head_dim), F32),
             pltpu.SMEM((devices,), jnp.int32),
         ],
         compiler_params=params,
@@ -388,7 +388,7 @@
     total = keep + lax.ppermute(crossing, "tensor", sibling).astype(F32)
     for part in arrived[1:]:
         total = total + part.astype(F32)
-    return total.astype(BF16).reshape(steps, rows, column).swapaxes(0, 1)
+    return total.astype(BF16).reshape(rows, steps, column)
 
 
 def solution(mesh):

time: 44.8 us -> 44.8 us (level)
  no operation moved by 1% of the time
where the time goes in v19:
time: 44.8 us; the launch traced here: 44.6 us
  blocking collectives  25.9 us (58%)
  starting transfers between devices  9.56 us (21%)
  Pallas kernels  7.29 us (16%)
  waiting for transfers between devices  0.98 us (2%)
  local copies, waits for them, and re-layouts  0.7 us (2%)
    all_to_all x1, blocking collectives, shards(): lax.all_to_all(send, 'particle', split_axis=0, concat_axis=0, tiled=True)  15.5 us
    all_to_all x1, blocking collectives, shards(): lax.all_to_all(back, 'particle', split_axis=0, concat_axis=0, tiled=True)  10.4 us
    ppermute x3, starting transfers between devices, shards(): arrived.append(lax.ppermute(pair[k - 1], 'tensor', ring))  5.05 us
    ppermute x1, starting transfers between devices, shards(): given = lax.ppermute(other, 'tensor', sibling)  3.22 us
    pallas_call x1, Pallas kernels, shards(): pl.pallas_call(attend_kernel, out_shape=(jax.ShapeDtypeStruct(packed, BF1...  2.55 us
    pallas_call x1, Pallas kernels, shards(): pl.pallas_call(merge_kernel, out_shape=(block, jax.ShapeDtypeStruct((rows...  1.77 us
    ppermute x1, starting transfers between devices, shards(): total = keep + lax.ppermute(crossing, 'tensor', sibling).astype(F32)  1.29 us
    pallas_call x1, Pallas kernels, shards(): pl.pallas_call(pack_kernel, out_shape=(jax.ShapeDtypeStruct(packed, BF16)...  1.21 us
  transfers between devices with their start and end apart: 5, of which 3 were waited for; matrix products, arithmetic and copies ran while one was open for 0% of the time, Pallas kernels for 4%

profile of v19, /device:TPU:1, one launch (start us, length us, event | category | flops | bytes accessed | tf_op | source)
XLA Modules:
  0.0 44.6 jit_solution(650360694943317949)
XLA Ops:
  0.0 0.0 copy-start.1
  0.0 0.0 copy-start.2
  0.0 0.0 copy-start.3
  0.0 0.0 copy-start.4
  0.0 1.2 %pack_queries.1 = (bf16[16,40,128]{2,1,0:T(8,128)(2,1)S(1)}, bf16[16,16,128]{2,1,0:T(8,128)(2,1)S(1)}, f32[2,16,128]{2,1,0:T(8,128)S(1)}, f32[1,8192]{1,0:T(1,128)S(1)}) custom-call(s32[16]{0:T(128)} %anc.1, bf16[16,2,1024]{2,1,0:T(2,128)(2,1)} %qp_hbm.1, f32[2,16,128]{2,1,0:T(8,128)} %constant.2.clone.tables_hbm, f32[1,8192]{1,0:T(1,128)} %bitcast.3), custom_call_target="tpu_custom_call" | custom-call | flops 10000000000 | bytes 1048576 | tf_op jit(solution)/shard_map/pack_queries/pallas_call | solution.py:268
  1.2 15.5 %all_to_all.10.recv = bf16[16,40,128]{2,1,0:T(8,128)(2,1)S(1)} all-to-all(bf16[16,40,128]{2,1,0:T(8,128)(2,1)S(1)} %get-tuple-element.19), channel_id=1, replica_groups=mesh['particle'=16,'tensor'=8] {'particle'}, dimensions={0} | all-to-all | bytes 327680 | tf_op jit(solution)/shard_map/all_to_all | solution.py:291
  16.7 0.0 slice-start
  16.7 0.0 copy-done.1
  16.7 0.0 copy-done.2
  16.7 0.0 copy-done.3
  16.7 0.0 copy-done.4
  16.7 0.0 slice-start.1
  16.8 0.0 slice-start.2
  16.8 0.0 slice-start.3
  16.8 0.0 copy-start
  16.8 2.6 %attention.1 = (bf16[16,40,128]{2,1,0:T(8,128)(2,1)S(1)}, f32[256,128]{1,0:T(8,128)S(1)}, f32[2,256,128]{2,1,0:T(8,128)S(1)}) custom-call(bf16[16,40,128]{2,1,0:T(8,128)(2,1)S(1)} %all_to_all.10.recv, bf16[16,1,512,256]{3,2,1,0:T(8,128)(2,1)S(1)} %copy-done.1, bf16[16,2,8192]{2,1,0:T(2,128)(2,1)S(1)} %copy-done.4, f32[1,8192]{1,0:T(1,128)S(1)} %get-tuple-element.20.gain, ...), custom_call_target="tpu_custom_call" | custom-call | flops 10000000000 | bytes 5242880 | tf_op jit(solution)/shard_map/attention/pallas_call | solution.py:294
  19.4 10.4 %all_to_all.11.recv = bf16[16,40,128]{2,1,0:T(8,128)(2,1)S(1)} all-to-all(bf16[16,40,128]{2,1,0:T(8,128)(2,1)S(1)} %get-tuple-element.23), channel_id=1, replica_groups=mesh['particle'=16,'tensor'=8] {'particle'}, dimensions={0} | all-to-all | bytes 327680 | tf_op jit(solution)/shard_map/all_to_all | solution.py:328
  29.8 0.0 slice-done
  29.8 0.0 slice-done.1
  29.8 0.0 slice-done.2
  29.8 0.0 slice-done.3
  29.8 0.0 copy-done
  29.8 1.8 %merge_project_sibling.1 = (bf16[3,32,1024]{2,1,0:T(8,128)(2,1)S(1)}, bf16[32,1024]{1,0:T(8,128)(2,1)S(1)}) custom-call(s32[16]{0:T(128)S(1)} %copy-done, bf16[16,40,128]{2,1,0:T(8,128)(2,1)S(1)} %all_to_all.11.recv, f32[256,128]{1,0:T(8,128)S(1)} %get-tuple-element.24.vec, f32[2,256,128]{2,1,0:T(8,128)S(1)} %get-tuple-element.25.stat, ...), custom_call_target="tpu_custom_call" | custom-call | flops 268435456 | bytes 8388608 | tf_op jit(solution)/shard_map/merge_project_sibling/pallas_call | solution.py:338
  31.6 3.2 %collective-permute-start = (bf16[3,32,1024]{2,1,0:T(8,128)(2,1)S(1)}, bf16[3,32,1024]{2,1,0:T(8,128)(2,1)S(1)}, u32[]{:S(2)}, u32[]{:S(2)}) collective-permute-start(bf16[3,32,1024]{2,1,0:T(8,128)(2,1)S(1)} %get-tuple-element.27), channel_id=1, source_target_pairs={{0,1},{1,0},{2,3},{3,2},{4,5},{5,4},{6,7},{7,6},{8,9},{9,8},{10,11... | collective-permute-start | bytes 589832 | tf_op jit(solution)/shard_map/ppermute | solution.py:357
  34.8 1.0 %project_own.1.mine = bf16[3,32,1024]{2,1,0:T(8,128)(2,1)S(1)} custom-call(bf16[32,1024]{1,0:T(8,128)(2,1)S(1)} %get-tuple-element.26.heads, bf16[1024,8192]{1,0:T(8,128)(2,1)S(1)} %bitcast.2), custom_call_target="tpu_custom_call" | custom-call | flops 268435456 | bytes 8388608 | tf_op jit(solution)/shard_map/project_own/pallas_call | solution.py:358
  35.8 0.1 collective-permute-done.given
  36.0 1.4 %collective-permute-start.1 = (bf16[32,1024]{1,0:T(8,128)(2,1)S(1)}, bf16[32,1024]{1,0:T(8,128)(2,1)S(1)}, u32[]{:S(2)}, u32[]{:S(2)}) collective-permute-start(bf16[32,1024]{1,0:T(8,128)(2,1)S(1)} %get-tuple-element.28), channel_id=1, source_target_pairs={{0,2},{1,3},{2,4},{3,5},{4,6},{5,7},{6,0},{7,1},{8,10},{9,11},{10,... | collective-permute-start | bytes 196616 | tf_op jit(solution)/shard_map/ppermute | solution.py:378
  37.3 2.6 %collective-permute-start.3 = (bf16[32,1024]{1,0:T(8,128)(2,1)S(1)}, bf16[32,1024]{1,0:T(8,128)(2,1)S(1)}, u32[]{:S(2)}, u32[]{:S(2)}) collective-permute-start(bf16[32,1024]{1,0:T(8,128)(2,1)S(1)} %get-tuple-element.31), channel_id=1, source_target_pairs={{0,4},{1,5},{2,6},{3,7},{4,0},{5,1},{6,2},{7,3},{8,12},{9,13},{10,... | collective-permute-start | bytes 196616 | tf_op jit(solution)/shard_map/ppermute | solution.py:378
  39.9 1.1 %collective-permute-start.4 = (bf16[32,1024]{1,0:T(8,128)(2,1)S(1)}, bf16[32,1024]{1,0:T(8,128)(2,1)S(1)}, u32[]{:S(2)}, u32[]{:S(2)}) collective-permute-start(bf16[32,1024]{1,0:T(8,128)(2,1)S(1)} %get-tuple-element.32), channel_id=1, source_target_pairs={{0,6},{1,7},{2,0},{3,1},{4,2},{5,3},{6,4},{7,5},{8,14},{9,15},{10,... | collective-permute-start | bytes 196616 | tf_op jit(solution)/shard_map/ppermute | solution.py:378
  41.0 0.0 collective-permute-done.1.arrived
  41.0 0.7 %project_last.1 = (f32[32,1024]{1,0:T(8,128)S(1)}, bf16[32,1024]{1,0:T(8,128)(2,1)S(1)}) custom-call(bf16[32,1024]{1,0:T(8,128)(2,1)S(1)} %get-tuple-element.26.heads, bf16[1024,8192]{1,0:T(8,128)(2,1)S(1)} %bitcast.2, bf16[32,1024]{1,0:T(8,128)(2,1)S(1)} %collective-permute-done.1.arrived), custom_call_target="tpu_custom_call" | custom-call | flops 268435456 | bytes 8388608 | tf_op jit(solution)/shard_map/project_last/pallas_call | solution.py:379
  41.7 1.3 %collective-permute-start.2 = (bf16[32,1024]{1,0:T(8,128)(2,1)S(1)}, bf16[32,1024]{1,0:T(8,128)(2,1)S(1)}, u32[]{:S(2)}, u32[]{:S(2)}) collective-permute-start(bf16[32,1024]{1,0:T(8,128)(2,1)S(1)} %get-tuple-element.30), channel_id=1, source_target_pairs={{0,1},{1,0},{2,3},{3,2},{4,5},{5,4},{6,7},{7,6},{8,9},{9,8},{10,11... | collective-permute-start | bytes 196616 | tf_op jit(solution)/shard_map/ppermute | solution.py:388
  43.0 0.0 collective-permute-done.3
  43.0 0.3 collective-permute-done.4
  43.4 0.6 %collective-permute-done.2 = bf16[32,1024]{1,0:T(8,128)(2,1)S(1)} collective-permute-done((bf16[32,1024]{1,0:T(8,128)(2,1)S(1)}, bf16[32,1024]{1,0:T(8,128)(2,1)S(1)}, u32[]{:S(2)}, u32[]{:S(2)}) %collective-permute-start.2) | collective-permute-done | bytes 65568 | tf_op jit(solution)/shard_map/ppermute | solution.py:388
  44.0 0.7 %reshape.7 = bf16[16,2,1024]{2,1,0:T(2,128)(2,1)} reshape(bf16[32,1024]{1,0:T(8,128)(2,1)S(1)} %add_convert_fusion) | data formatting | bytes 131072 | tf_op jit(solution)/shard_map/reshape | solution.py:391
  (3 shorter events, 0.1 us)
Async XLA Ops:
  0.0 16.7 %copy-start.1 = (bf16[16,1,512,256]{3,2,1,0:T(8,128)(2,1)S(1)}, bf16[16,1,512,256]{3,2,1,0:T(8,128)(2,1)}, u32[]{:S(2)}) copy-start(bf16[16,1,512,256]{3,2,1,0:T(8,128)(2,1)} %kv.1) | copy-start | bytes 12582916
  0.0 16.7 %copy-start.2 = (bf16[8192,128]{1,0:T(8,128)(2,1)S(1)}, bf16[8192,128]{1,0:T(8,128)(2,1)}, u32[]{:S(2)}) copy-start(bf16[8192,128]{1,0:T(8,128)(2,1)} %wk.1) | copy-start | bytes 6291460
  0.0 16.7 %copy-start.3 = (bf16[8192,128]{1,0:T(8,128)(2,1)S(1)}, bf16[8192,128]{1,0:T(8,128)(2,1)}, u32[]{:S(2)}) copy-start(bf16[8192,128]{1,0:T(8,128)(2,1)} %wv.1) | copy-start | bytes 6291460
  0.0 16.7 %copy-start.4 = (bf16[16,2,8192]{2,1,0:T(2,128)(2,1)S(1)}, bf16[16,2,8192]{2,1,0:T(2,128)(2,1)}, u32[]{:S(2)}) copy-start(bf16[16,2,8192]{2,1,0:T(2,128)(2,1)} %x.1) | copy-start | bytes 1572868
  16.7 13.1 %slice-start = ((s8[16777216]{0:T(1024)(128)(4,1)}), s8[4194304]{0:T(1024)(128)(4,1)S(1)}, s32[]{:S(2)}) async-start(s8[16777216]{0:T(1024)(128)(4,1)} %bitcast.1), calls=%async_computation.2 | async-start | bytes 8388608
  16.7 13.1 %slice-start.1 = ((s8[16777216]{0:T(1024)(128)(4,1)}), s8[4194304]{0:T(1024)(128)(4,1)S(1)}, s32[]{:S(2)}) async-start(s8[16777216]{0:T(1024)(128)(4,1)} %bitcast.1), calls=%async_computation.3 | async-start | bytes 8388608
  16.8 13.0 %slice-start.2 = ((s8[16777216]{0:T(1024)(128)(4,1)}), s8[4194304]{0:T(1024)(128)(4,1)S(1)}, s32[]{:S(2)}) async-start(s8[16777216]{0:T(1024)(128)(4,1)} %bitcast.1), calls=%async_computation.4 | async-start | bytes 8388608
  16.8 13.0 %slice-start.3 = ((s8[16777216]{0:T(1024)(128)(4,1)}), s8[4194304]{0:T(1024)(128)(4,1)S(1)}, s32[]{:S(2)}) async-start(s8[16777216]{0:T(1024)(128)(4,1)} %bitcast.1), calls=%async_computation.5 | async-start | bytes 8388608
  16.8 13.0 %copy-start = (s32[16]{0:T(128)S(1)}, s32[16]{0:T(128)}, u32[]{:S(2)}) copy-start(s32[16]{0:T(128)} %anc.1) | copy-start | bytes 196
  31.6 4.3 %collective-permute-start = (bf16[3,32,1024]{2,1,0:T(8,128)(2,1)S(1)}, bf16[3,32,1024]{2,1,0:T(8,128)(2,1)S(1)}, u32[]{:S(2)}, u32[]{:S(2)}) collective-permute-start(bf16[3,32,1024]{2,1,0:T(8,128)(2,1)S(1)} %get-tuple-element.27), channel_id=1, source_target_pairs={{0,1},{1,0},{2,3},{3,2},{4,5},{5,4},{6,7},{7,6},{8,9},{9,8},{10,11... | collective-permute-start | bytes 589832 | tf_op jit(solution)/shard_map/ppermute | solution.py:357
  36.0 5.1 %collective-permute-start.1 = (bf16[32,1024]{1,0:T(8,128)(2,1)S(1)}, bf16[32,1024]{1,0:T(8,128)(2,1)S(1)}, u32[]{:S(2)}, u32[]{:S(2)}) collective-permute-start(bf16[32,1024]{1,0:T(8,128)(2,1)S(1)} %get-tuple-element.28), channel_id=1, source_target_pairs={{0,2},{1,3},{2,4},{3,5},{4,6},{5,7},{6,0},{7,1},{8,10},{9,11},{10,... | collective-permute-start | bytes 196616 | tf_op jit(solution)/shard_map/ppermute | solution.py:378
  37.3 5.7 %collective-permute-start.3 = (bf16[32,1024]{1,0:T(8,128)(2,1)S(1)}, bf16[32,1024]{1,0:T(8,128)(2,1)S(1)}, u32[]{:S(2)}, u32[]{:S(2)}) collective-permute-start(bf16[32,1024]{1,0:T(8,128)(2,1)S(1)} %get-tuple-element.31), channel_id=1, source_target_pairs={{0,4},{1,5},{2,6},{3,7},{4,0},{5,1},{6,2},{7,3},{8,12},{9,13},{10,... | collective-permute-start | bytes 196616 | tf_op jit(solution)/shard_map/ppermute | solution.py:378
  39.9 3.4 %collective-permute-start.4 = (bf16[32,1024]{1,0:T(8,128)(2,1)S(1)}, bf16[32,1024]{1,0:T(8,128)(2,1)S(1)}, u32[]{:S(2)}, u32[]{:S(2)}) collective-permute-start(bf16[32,1024]{1,0:T(8,128)(2,1)S(1)} %get-tuple-element.32), channel_id=1, source_target_pairs={{0,6},{1,7},{2,0},{3,1},{4,2},{5,3},{6,4},{7,5},{8,14},{9,15},{10,... | collective-permute-start | bytes 196616 | tf_op jit(solution)/shard_map/ppermute | solution.py:378
  41.7 2.2 %collective-permute-start.2 = (bf16[32,1024]{1,0:T(8,128)(2,1)S(1)}, bf16[32,1024]{1,0:T(8,128)(2,1)S(1)}, u32[]{:S(2)}, u32[]{:S(2)}) collective-permute-start(bf16[32,1024]{1,0:T(8,128)(2,1)S(1)} %get-tuple-element.30), channel_id=1, source_target_pairs={{0,1},{1,0},{2,3},{3,2},{4,5},{5,4},{6,7},{7,6},{8,9},{9,8},{10,11... | collective-permute-start | bytes 196616 | tf_op jit(solution)/shard_map/ppermute | solution.py:388
